TPU v7x, 32 devices: a whole 2x2x4 slice. The times are simulated.
32 devices in a mesh: region: 2 (over y), tile: 4 (over z), epoch: 2 (over x), band: 2 (over core).
Axes of the slice: x: 2, y: 2, z: 4, core: 2. Of those that a mesh axis runs over, the one named last changes fastest.
Arguments:
- source_params: float32 [64, 44, 128], P(('region', 'tile')), parts along dimension 0, as said below
- pixel_data: float32 [16, 2, 2, 128, 128], P(('region', 'tile'), 'epoch', 'band'), parts along dimension 0, may hold values from -6 to 6
- pixel_weight: float32 [16, 2, 2, 128, 128], P(('region', 'tile'), 'epoch', 'band'), parts along dimension 0, may hold values from 0.5 to 2
- psf_width: float32 [4, 2], P(('region', 'epoch'), 'band'), parts along dimension 0, may hold values from 0.8 to 2
- block_lists: int32 [16, 8], P(('region', 'tile')), parts along dimension 0, may hold values from 0 to 31, as said below
- block_counts: int32 [16], P(('region', 'tile')), parts along dimension 0, may hold values from 1 to 8, as said below
- block_offsets: int32 [16, 8, 2], P(('region', 'tile')), parts along dimension 0, may hold values from 0 to 63
Outputs:
- updated_params: float32 [64, 44, 128], P(('region', 'tile')), parts along dimension 0
There are 2 independent parts, one for each index of `region`. A program takes and returns all parts, laid end to end along the dimension named above; each array names one. Nothing has to cross between parts.
Inputs may be any that keep to these rules, and one draw needn't show every extreme that they name: `block_lists`: block g is owned by tile index g // 8. Among the 2 x 8 slots of one tile index no id repeats and no owner appears more than 4 times; on every tile index some owner appears exactly 4 times. `block_counts`: slots of a tile beyond its count are unused. `source_params`: rows 0 and 1 lie in 0 to 4; rows 2 + 6c + 2 lie in 0 to 1.4 and rows 2 + 6c + 3 in -0.3 to 0.3.
All inputs are finite; a program needn't handle non-finite values.
Results may differ from a plain program's by a relative error of at most 0.0003.
Values sent between devices are 32-bit elements; how exact they have to be, the bound alone decides.
No kernel may reach another device: no remote copies, remote signals or barrier semaphores. Data moves between devices by JAX's collectives and lax.ppermute only.
A program may use at most 64 MiB of HBM per device.

v0:
```python
import jax
import jax.numpy as jnp
from jax import lax
from jax.sharding import PartitionSpec as P

ITERS = 2


step_scale = 0.005


def render(block_params, offset_pair, psf_value, band_index, pixels):
    components = block_params[2:].reshape(7, 6, block_params.shape[-1])
    spacing = pixels / 8.0
    centre_x = spacing * block_params[0] + components[:, 0] + offset_pair[0]
    centre_y = spacing * block_params[1] + components[:, 1] + offset_pair[1]
    variance_x = jnp.exp(2.0 * (components[:, 2] + components[:, 3])) + psf_value * psf_value
    variance_y = jnp.exp(2.0 * (components[:, 2] - components[:, 3])) + psf_value * psf_value
    amplitude = lax.dynamic_index_in_dim(components, 4 + band_index, 1, keepdims=False)
    pixel_grid = jnp.arange(pixels).astype(jnp.float32)
    profile_x = jnp.exp(
        -0.5 * (pixel_grid[None, None, :] - centre_x[:, :, None]) ** 2 / variance_x[:, :, None]
    )
    profile_y = amplitude[:, :, None] * jnp.exp(
        -0.5 * (pixel_grid[None, None, :] - centre_y[:, :, None]) ** 2 / variance_y[:, :, None]
    )
    return jnp.einsum("csi,csj->ij", profile_x, profile_y, precision=lax.Precision.HIGHEST)


def local_gradients(
    slot_params, pixel_data, pixel_weight, psf_value, band_index, block_counts, block_offsets
):
    tiles_here, slot_count = (block_offsets.shape[0], block_offsets.shape[1])
    pixels = pixel_data.shape[-1]
    pieces = []
    for tile_index in range(tiles_here):
        first_slot = tile_index * slot_count
        used_slots = block_counts[tile_index]
        offset_rows = block_offsets[tile_index].astype(jnp.float32)

        def slot_block(slot_index):
            return lax.dynamic_index_in_dim(slot_params, first_slot + slot_index, 0, keepdims=False)

        def add_slot(slot_index, image_sum):
            return image_sum + render(
                slot_block(slot_index), offset_rows[slot_index], psf_value, band_index, pixels
            )

        model_image = lax.fori_loop(
            0, used_slots, add_slot, jnp.zeros((pixels, pixels), jnp.float32)
        )
        cotangent = pixel_weight[tile_index, 0, 0] * (model_image - pixel_data[tile_index, 0, 0])

        def grad_slot(slot_index, buffer_grads):
            unused, pullback = jax.vjp(
                lambda block_value: render(
                    block_value, offset_rows[slot_index], psf_value, band_index, pixels
                ),
                slot_block(slot_index),
            )
            return lax.dynamic_update_index_in_dim(
                buffer_grads, pullback(cotangent)[0], slot_index, 0
            )

        empty_grads = jnp.zeros((slot_count,) + slot_params.shape[1:], jnp.float32)
        pieces.append(lax.fori_loop(0, used_slots, grad_slot, empty_grads))
    return jnp.concatenate(pieces, axis=0)


def shards(
    source_params, pixel_data, pixel_weight, psf_width, block_lists, block_counts, block_offsets
):
    owners = lax.axis_size("tile")
    blocks_here, param_rows, block_sources = source_params.shape
    band_index = lax.axis_index("band")
    psf_value = psf_width[0, 0]
    flat_ids = block_lists.reshape(-1)
    row_scale = (step_scale * jnp.where(jnp.arange(param_rows) < 2, 1.0 / 64.0, 1.0)).astype(
        jnp.float32
    )[:, None]
    current = source_params
    for section_index in range(ITERS):
        everything = lax.all_gather(current, "tile", axis=0, tiled=True)
        slot_params = jnp.take(everything, flat_ids, axis=0)
        slot_grads = local_gradients(
            slot_params,
            pixel_data,
            pixel_weight,
            psf_value,
            band_index,
            block_counts,
            block_offsets,
        )
        dense_grads = (
            jnp.zeros((owners * blocks_here, param_rows, block_sources), jnp.float32)
            .at[flat_ids]
            .add(slot_grads)
        )
        own_grads = lax.psum_scatter(dense_grads, "tile", scatter_dimension=0, tiled=True)
        summed = lax.psum(own_grads, ("epoch", "band"))
        current = current - row_scale * summed
    return current


def solution(mesh):
    return jax.shard_map(
        shards,
        mesh=mesh,
        in_specs=(
            P(("region", "tile"), None, None),
            P(("region", "tile"), "epoch", "band", None, None),
            P(("region", "tile"), "epoch", "band", None, None),
            P(("region", "epoch"), "band"),
            P(("region", "tile"), None),
            P(("region", "tile")),
            P(("region", "tile"), None, None),
        ),
        out_specs=P(("region", "tile"), None, None),
        check_vma=False,
    )
```

profile of v0, /device:TPU:0, one launch (start us, length us, event | category | flops | bytes accessed | tf_op | source)
XLA Modules:
  0.0 453.9 jit_solution(256327121307471743)
XLA Ops:
  7.4 20.8 %all_gather.6 = f32[32,44,128]{2,0,1:T(8,128)S(1)} all-gather(f32[8,44,128]{2,0,1:T(8,128)} %param.25), channel_id=1, replica_groups=mesh['region'=2,'tile'=4,'epoch'=2,'band'=2] {'tile'}, dimensions={0}, use_global_device_ids=true | all-gather | bytes 901120 | tf_op jit(solution)/shard_map/all_gather | solution.py:83
  30.7 29.3 %while.96 = (s32[]{:T(128)}, f32[128,128]{1,0:T(8,128)S(1)}, s32[]{:T(128)}, f32[16,44,128]{2,1,0:T(8,128)S(1)}, f32[8,2]{0,1:T(2,128)S(1)}, /*index=5*/f32[]{:T...) while((s32[]{:T(128)}, f32[128,128]{1,0:T(8,128)S(1)}, s32[]{:T(128)}, ...), condition=%wide.region_1.3_spmd, body=%wide.region_0.2_spmd.sunk | while | flops 177218688 | bytes 311060 | solution.py:49
  60.1 29.5 %while.98 = (s32[]{:T(128)}, f32[128,128]{1,0:T(8,128)S(1)}, s32[]{:T(128)}, f32[16,44,128]{2,1,0:T(8,128)S(1)}, f32[8,2]{0,1:T(2,128)S(1)}, /*index=5*/f32[]{:T...) while((s32[]{:T(128)}, f32[128,128]{1,0:T(8,128)S(1)}, ...), condition=%wide.region_12.14_spmd, body=%wide.region_11.13_spmd.sunk | while | flops 177218704 | bytes 311069 | solution.py:49
  61.6 1.3 fusion.357
  65.2 1.3 fusion.357
  68.8 1.3 fusion.357
  72.4 1.3 fusion.357
  76.0 1.3 fusion.357
  79.6 1.3 fusion.357
  83.2 1.3 fusion.357
  89.7 40.2 %while.97 = (s32[]{:T(128)}, f32[8,44,128]{2,1,0:T(8,128)S(1)}, s32[]{:T(128)}, f32[16,44,128]{2,1,0:T(8,128)S(1)}, s32[]{:T(128)}, /*index=5*/f32[8,2]{1,0:T(8,...) while((s32[]{:T(128)}, f32[8,44,128]{2,1,0:T(8,128)S(1)}, ...), condition=%wide.region_10.12_spmd, body=%wide.region_2.11_spmd.sunk | while | flops 357309824 | bytes 3389756 | solution.py:66
  129.9 41.2 %while.99 = (s32[]{:T(128)}, f32[8,44,128]{2,1,0:T(8,128)S(1)}, s32[]{:T(128)}, f32[16,44,128]{2,1,0:T(8,128)S(1)}, s32[]{:T(128)}, /*index=5*/f32[8,2]{1,0:T(8,...) while((s32[]{:T(128)}, f32[8,44,128]{2,1,0:T(8,128)S(1)}, ...), condition=%wide.region_21.23_spmd, body=%wide.region_13.22_spmd.sunk | while | flops 357309824 | bytes 3389765 | solution.py:66
  171.1 1.4 scatter_fusion
  173.7 21.2 %reduce-scatter.3.cloned.1.call-done = f32[8,44,128]{2,0,1:T(8,128)} async-done(((f32[32,44,128]{2,0,1:T(8,128)}), f32[8,44,128]{2,0,1:T(8,128)}) %reduce-scatter.3.cloned.1.call-update) | async-done | bytes 180240 | tf_op jit(solution)/shard_map/reduce_scatter | solution.py:99
  195.1 32.3 %all-reduce.39.cloned.1.call-done = f32[8,44,128]{2,0,1:T(8,128)} async-done(((f32[8,44,128]{2,0,1:T(8,128)}), f32[8,44,128]{2,0,1:T(8,128)}) %all-reduce.39.cloned.1.call-update) | async-done | bytes 180240 | tf_op jit(solution)/shard_map/psum | solution.py:100
  228.4 18.9 %all_gather.7 = f32[32,44,128]{2,0,1:T(8,128)S(1)} all-gather(f32[8,44,128]{2,0,1:T(8,128)S(1)} %multiply_subtract_fusion.1), channel_id=1, replica_groups=mesh['region'=2,'tile'=4,'epoch'=2,'band'=2] {'tile'}, dimensions={0}, use_global_device_ids=true | all-gather | bytes 901120 | tf_op jit(solution)/shard_map/all_gather | solution.py:83
  248.4 29.5 %while.100 = (s32[]{:T(128)}, f32[128,128]{1,0:T(8,128)S(1)}, s32[]{:T(128)}, f32[16,44,128]{2,1,0:T(8,128)S(1)}, f32[8,2]{0,1:T(2,128)S(1)}, /*index=5*/f32[]{:...) while((s32[]{:T(128)}, f32[128,128]{1,0:T(8,128)S(1)}, ...), condition=%wide.region_26.28_spmd, body=%wide.region_25.27_spmd.sunk | while | flops 177218688 | bytes 311060 | solution.py:49
  278.0 29.4 %while.102 = (s32[]{:T(128)}, f32[128,128]{1,0:T(8,128)S(1)}, s32[]{:T(128)}, f32[16,44,128]{2,1,0:T(8,128)S(1)}, f32[8,2]{0,1:T(2,128)S(1)}, /*index=5*/f32[]{:...) while((s32[]{:T(128)}, f32[128,128]{1,0:T(8,128)S(1)}, ...), condition=%wide.region_37.39_spmd, body=%wide.region_36.38_spmd.sunk | while | flops 177218704 | bytes 311069 | solution.py:49
  307.4 41.5 %while.101 = (s32[]{:T(128)}, f32[8,44,128]{2,1,0:T(8,128)S(1)}, s32[]{:T(128)}, f32[16,44,128]{2,1,0:T(8,128)S(1)}, s32[]{:T(128)}, /*index=5*/f32[8,2]{1,0:T(8...) while((s32[]{:T(128)}, f32[8,44,128]{2,1,0:T(8,128)S(1)}, ...), condition=%wide.region_35.37_spmd, body=%wide.region_27.36_spmd.sunk | while | flops 357309824 | bytes 3389756 | solution.py:66
  349.0 41.2 %while.103 = (s32[]{:T(128)}, f32[8,44,128]{2,1,0:T(8,128)S(1)}, s32[]{:T(128)}, f32[16,44,128]{2,1,0:T(8,128)S(1)}, s32[]{:T(128)}, /*index=5*/f32[8,2]{1,0:T(8...) while((s32[]{:T(128)}, f32[8,44,128]{2,1,0:T(8,128)S(1)}, ...), condition=%wide.region_46.48_spmd, body=%wide.region_38.0_spmd.sunk | while | flops 357309824 | bytes 3389765 | solution.py:66
  390.3 1.4 scatter_fusion.1
  392.9 20.4 %reduce-scatter.5.cloned.1.call-done = f32[8,44,128]{2,0,1:T(8,128)} async-done(((f32[32,44,128]{2,0,1:T(8,128)}), f32[8,44,128]{2,0,1:T(8,128)}) %reduce-scatter.5.cloned.1.call-update) | async-done | bytes 180240 | tf_op jit(solution)/shard_map/reduce_scatter | solution.py:99
  413.4 32.3 %all-reduce.41.cloned.1.call-done = f32[8,44,128]{2,0,1:T(8,128)} async-done(((f32[8,44,128]{2,0,1:T(8,128)}), f32[8,44,128]{2,0,1:T(8,128)}) %all-reduce.41.cloned.1.call-update) | async-done | bytes 180240 | tf_op jit(solution)/shard_map/psum | solution.py:100
  445.7 1.7 multiply_subtract_fusion
  (1391 shorter events, 226.1 us)
Async XLA Ops:
  6.5 0.7 copy-start.5
  6.5 188.4 %reduce-scatter.3.cloned.1.call-start = ((), (), s32[]{:S(2)}) async-start(), calls=%async_computation.2 | async-start | bytes 901120 | tf_op jit(solution)/shard_map/reduce_scatter | solution.py:99
  28.2 1.1 copy-start.4
  29.2 0.7 copy-start.3
  60.1 29.5 %copy-start.1 = (f32[2,1,1,128,128]{4,3,2,1,0:T(8,128)S(1)}, f32[2,1,1,128,128]{4,3,2,1,0:T(8,128)}, u32[]{:S(2)}) copy-start(f32[2,1,1,128,128]{4,3,2,1,0:T(8,128)} %param.26) | copy-start | bytes 393220
  60.1 29.5 %copy-start.2 = (f32[2,1,1,128,128]{4,3,2,1,0:T(8,128)S(1)}, f32[2,1,1,128,128]{4,3,2,1,0:T(8,128)}, u32[]{:S(2)}) copy-start(f32[2,1,1,128,128]{4,3,2,1,0:T(8,128)} %param.27) | copy-start | bytes 393220
  173.7 53.7 %copy-start = (f32[8,44,128]{2,0,1:T(8,128)S(1)}, f32[8,44,128]{2,0,1:T(8,128)}, u32[]{:S(2)}) copy-start(f32[8,44,128]{2,0,1:T(8,128)} %param.25) | copy-start | bytes 540676
  173.7 53.7 %all-reduce.39.cloned.1.call-start = ((), (), s32[]{:S(2)}) async-start(), calls=%async_computation.3 | async-start | bytes 360448 | tf_op jit(solution)/shard_map/psum | solution.py:100
  195.0 218.3 %reduce-scatter.5.cloned.1.call-start = ((), (), s32[]{:S(2)}) async-start(), calls=%async_computation.4 | async-start | bytes 901120 | tf_op jit(solution)/shard_map/reduce_scatter | solution.py:99
  392.9 52.8 %all-reduce.41.cloned.1.call-start = ((), (), s32[]{:S(2)}) async-start(), calls=%async_computation.5 | async-start | bytes 360448 | tf_op jit(solution)/shard_map/psum | solution.py:100
Sparse Core Ops, SparseCore 0:
  173.8 21.1 reduce-scatter.2
  197.3 29.9 all-reduce.38
  393.0 20.3 reduce-scatter.4
  415.6 30.0 all-reduce.40
where the time goes:
time: 456 us; the launch traced here: 454 us
  waiting for transfers between devices  106 us (23%)
  other arithmetic  101 us (22%)
  matrix products  86.4 us (19%)
  loops' own time  54.3 us (12%)
  local copies, waits for them, and re-layouts  52 us (11%)
  blocking collectives  39.7 us (9%)
  between operations  14.1 us (3%)
    dot_general x96, matrix products, render(): jnp.einsum('csi,csj->ij', profile_x, profile_y, precision=lax.Precision.H...  86.4 us
    add x64, other arithmetic, render(): centre_y = spacing * block_params[1] + components[:, 1] + offset_pair[1]  79.7 us
    psum x2, waiting for transfers between devices, shards(): summed = lax.psum(own_grads, ('epoch', 'band'))  64.6 us
    reduce_scatter x2, waiting for transfers between devices, shards(): lax.psum_scatter(dense_grads, 'tile', scatter_dimension=0, tiled=True)  41.7 us
    all_gather x2, blocking collectives, shards(): everything = lax.all_gather(current, 'tile', axis=0, tiled=True)  39.7 us
    another operation x4, loops' own time, local_gradients(): pieces.append(lax.fori_loop(0, used_slots, grad_slot, empty_grads))  29.1 us
    another operation x4, loops' own time, local_gradients(): lax.fori_loop(0, used_slots, add_slot, jnp.zeros((pixels, pixels), jnp.fl...  25.3 us
    slice x32, local copies, waits for them, and re-layouts, render(): centre_y = spacing * block_params[1] + components[:, 1] + offset_pair[1]  20.5 us
  transfers between devices with their start and end apart: 4, of which 4 were waited for; matrix products, arithmetic and copies ran while one was open for 0% of the time, Pallas kernels for 0%

commit v1 on v0

v1 whole, which is shorter than its diff:
```python
import functools
import math

import jax
import jax.numpy as jnp
from jax import lax
from jax.experimental import pallas as pl
from jax.experimental.pallas import tpu as pltpu
from jax.sharding import PartitionSpec as P

ITERS = 2
STEP = 0.005
COMPS = 7
BANDS = 2
SHARED = [0, 1] + [2 + 6 * c + k for k in range(4) for c in range(COMPS)]
HALF = len(SHARED) // BANDS
LOG2E = math.log2(math.e)
F32 = jnp.float32
BF16 = jnp.bfloat16
VMEM_LIMIT = 56 * 1024 * 1024


def quarter_layout(epochs):
    shared_rows = -(-HALF // epochs)
    rows = -(-(HALF + COMPS) // epochs)
    pieces, amp = [], 0
    for q in range(epochs):
        piece = [("s", i) for i in range(q * shared_rows, min((q + 1) * shared_rows, HALF))]
        while len(piece) < rows and amp < COMPS:
            piece.append(("a", amp))
            amp += 1
        pieces.append(piece + [None] * (rows - len(piece)))
    return shared_rows, rows, pieces


def row_of(band, entry):
    if entry is None:
        return 0
    kind, i = entry
    return SHARED[HALF * band + i] if kind == "s" else 2 + 6 * i + 4 + band


def split3(x):
    hi = x.astype(BF16)
    rest = x - hi.astype(F32)
    mid = rest.astype(BF16)
    low = (rest - mid.astype(F32)).astype(BF16)
    return jnp.concatenate([hi, mid, low], axis=0)


def pick(matrix, rows):
    wide = jnp.concatenate([matrix, matrix, matrix], axis=1).astype(BF16)
    return jnp.dot(wide, split3(rows), preferred_element_type=F32)


def vmem():
    return pl.BlockSpec(memory_space=pltpu.VMEM)


def smem():
    return pl.BlockSpec(memory_space=pltpu.SMEM)


def f32(*shape):
    return jax.ShapeDtypeStruct(shape, F32)


def params():
    return pltpu.CompilerParams(vmem_limit_bytes=VMEM_LIMIT)


def pack_kernel(layout, lists_ref, params_ref, out_ref):
    shared_rows, rows, pieces = layout
    band, epoch = lax.axis_index("band"), lax.axis_index("epoch")
    for b in range(BANDS):
        for q in range(len(pieces)):

            @pl.when((band == b) & (epoch == q))
            def _():
                for p, entry in enumerate(pieces[q]):
                    out_ref[p] = params_ref[row_of(b, entry)]

    tiles, slots = lists_ref.shape
    lane = lax.broadcasted_iota(jnp.int32, (8, 128), 1) % slots
    line = lax.broadcasted_iota(jnp.int32, (8, 128), 0)
    ids = jnp.zeros((8, 128), jnp.int32)
    for t in range(tiles):
        for s in range(slots):
            ids = jnp.where((line == t) & (lane == s), lists_ref[t, s], ids)
    out_ref[rows] = ids.astype(F32)


def select_kernel(layout, lists_ref, *refs):
    shared_rows, rows, pieces = layout
    out_ref, match_ref = refs[-2:]
    got = refs[:-2]
    owners = len(got)
    tiles, slots = lists_ref.shape
    blocks = got[0].shape[1]
    wide = tiles * slots
    me = lax.axis_index("tile")

    def slot_ids(shape):
        line = lax.broadcasted_iota(jnp.int32, shape, 0)
        ids = jnp.zeros(shape, jnp.int32)
        for t in range(tiles):
            for s in range(slots):
                ids = jnp.where(line == t * slots + s, lists_ref[t, s], ids)
        return ids

    shape = (wide, owners * blocks)
    lane = lax.broadcasted_iota(jnp.int32, shape, 1)
    held = lax.rem(me - lane // blocks + owners, owners) * blocks + lane % blocks
    choose = (slot_ids(shape) == held).astype(F32)
    for p in range(rows):
        everything = jnp.concatenate([ref[p] for ref in got], axis=0)
        out_ref[p] = pick(choose, everything)

    shape = (wide + blocks, tiles * owners * slots)
    line = lax.broadcasted_iota(jnp.int32, shape, 0)
    own = jnp.where(line < wide, slot_ids(shape), me * blocks + line - wide).astype(F32)
    sent = jnp.concatenate(
        [got[k][rows, t : t + 1, :slots] for t in range(tiles) for k in range(owners)], axis=1
    )
    match_ref[...] = (own == sent).astype(F32)


def tile_kernel(layout, tile, counts_ref, offsets_ref, psf_ref, data_ref, weight_ref, *refs):
    shared_rows, rows, pieces = layout
    epochs = len(pieces)
    ins, refs = refs[: 2 * epochs], refs[2 * epochs :]
    outs, refs = refs[: 2 * epochs], refs[2 * epochs :]
    shared, amps, derived, prof_x, prof_y, pieces_x, pieces_y, image, sums, half_out, other_out = refs
    band, epoch = lax.axis_index("band"), lax.axis_index("epoch")
    slots = shared.shape[2]
    pixels = data_ref.shape[-1]
    used = counts_ref[tile]

    for k in range(epochs):
        half_out[lax.rem(epoch - k + epochs, epochs)] = ins[k][...]
        other_out[lax.rem(epoch - k + epochs, epochs)] = ins[epochs + k][...]
    for q, piece in enumerate(pieces):
        for p, entry in enumerate(piece):
            if entry is None:
                continue
            kind, i = entry
            if kind == "s":
                shared[band, i] = half_out[q, p]
                shared[1 - band, i] = other_out[q, p]
            else:
                amps[i] = half_out[q, p]

    def shared_row(r):
        return shared[r // HALF, r % HALF]

    psf = psf_ref[0, 0]
    spacing = pixels / 8.0
    lead = [2 + k * COMPS for k in range(4)]
    for c in range(COMPS):
        dx, dy, lw, an = (shared_row(lead[k] + c) for k in range(4))
        derived[0, c] = spacing * shared_row(0) + dx
        derived[1, c] = spacing * shared_row(1) + dy
        derived[2, c] = (-0.5 * LOG2E) / (jnp.exp(2.0 * (lw + an)) + psf * psf)
        derived[3, c] = (-0.5 * LOG2E) / (jnp.exp(2.0 * (lw - an)) + psf * psf)
        derived[4, c] = amps[c]

    grid = lax.broadcasted_iota(jnp.int32, (pixels, 128), 0).astype(F32)

    def line(index, c, s):
        return derived[index, c, pl.ds(s, 1), :]

    def cut(x):
        hi = x.astype(BF16)
        return jnp.concatenate([hi, (x - hi.astype(F32)).astype(BF16)], axis=0)

    image[...] = jnp.zeros_like(image)

    def render(s, carry):
        off_x = offsets_ref[tile, s, 0].astype(F32)
        off_y = offsets_ref[tile, s, 1].astype(F32)
        for first in range(0, COMPS, 2):
            cut_x, cut_y = [], []
            for c in range(first, min(first + 2, COMPS)):
                d = grid - (line(0, c, s) + off_x)
                e = jnp.exp2(d * d * line(2, c, s))
                prof_x[s * COMPS + c] = e
                cut_x.append(cut(e))
                d = grid - (line(1, c, s) + off_y)
                e = jnp.exp2(d * d * line(3, c, s))
                prof_y[s * COMPS + c] = e
                cut_y.append(cut(e * line(4, c, s)))
            span = pl.ds(first * 128, 128 * len(cut_x))
            both_x, both_y = jnp.concatenate(cut_x, axis=1), jnp.concatenate(cut_y, axis=1)
            pieces_x[s, :, span] = both_x
            pieces_y[s, :, span] = both_y
            image[...] += lax.dot_general(
                both_x, both_y, (((1,), (1,)), ((), ())), preferred_element_type=F32
            )
        return carry

    lax.fori_loop(0, used, render, 0)

    model = (image[:pixels, :pixels] + image[pixels:, pixels:]) + (
        image[:pixels, pixels:] + image[pixels:, :pixels]
    )
    cotangent = weight_ref[0, 0, 0] * (model - data_ref[0, 0, 0])

    def stack(x):
        both = cut(x)
        return jnp.concatenate([both, both], axis=1)

    left_x, left_y = stack(cotangent), stack(cotangent.T)
    sums[...] = jnp.zeros_like(sums)

    def total(x):
        return jnp.sum(x, axis=0, keepdims=True)

    def pull(s, carry):
        off_x = offsets_ref[tile, s, 0].astype(F32)
        off_y = offsets_ref[tile, s, 1].astype(F32)
        for first in range(0, COMPS, 2):
            here = min(2, COMPS - first)
            span = pl.ds(first * 128, 128 * here)
            by_x = jnp.dot(left_x, pieces_y[s, :, span], preferred_element_type=F32)
            by_y = jnp.dot(left_y, pieces_x[s, :, span], preferred_element_type=F32)
            by_x = by_x[:pixels] + by_x[pixels:]
            by_y = by_y[:pixels] + by_y[pixels:]
            for n in range(here):
                c = first + n
                d = grid - (line(0, c, s) + off_x)
                g = prof_x[s * COMPS + c] * by_x[:, n * 128 : (n + 1) * 128]
                g1 = g * d
                sums[0, c, pl.ds(s, 1), :] = total(g1)
                sums[1, c, pl.ds(s, 1), :] = total(g1 * d)
                d = grid - (line(1, c, s) + off_y)
                g = prof_y[s * COMPS + c] * by_y[:, n * 128 : (n + 1) * 128]
                g1 = g * d
                sums[2, c, pl.ds(s, 1), :] = total(g1)
                sums[3, c, pl.ds(s, 1), :] = total(g1 * d)
                sums[4, c, pl.ds(s, 1), :] = total(g)
        return carry

    lax.fori_loop(0, used, pull, 0)

    live = lax.broadcasted_iota(jnp.int32, (slots, 128), 0) < used

    def keep(x):
        return jnp.where(live, x, 0.0)

    sum_x = sum_y = 0.0
    grads = {}
    for c in range(COMPS):
        lw, an = shared_row(lead[2] + c), shared_row(lead[3] + c)
        wide_x, wide_y = jnp.exp(2.0 * (lw + an)), jnp.exp(2.0 * (lw - an))
        inv_x, inv_y = 1.0 / (wide_x + psf * psf), 1.0 / (wide_y + psf * psf)
        amp = amps[c]
        dx = keep(sums[0, c] * inv_x)
        dy = keep(amp * sums[2, c] * inv_y)
        var_x = keep(sums[1, c] * inv_x * inv_x * wide_x)
        var_y = keep(amp * sums[3, c] * inv_y * inv_y * wide_y)
        sum_x, sum_y = sum_x + dx, sum_y + dy
        for k, value in enumerate((dx, dy, var_x + var_y, var_x - var_y)):
            grads[lead[k] + c] = value
    grads[0], grads[1] = spacing * sum_x, spacing * sum_y
    for r, value in grads.items():
        shared[r // HALF, r % HALF] = value
    for q, piece in enumerate(pieces):
        for p, entry in enumerate(piece):
            if entry is None:
                half_out[q, p] = jnp.zeros((slots, 128), F32)
            elif entry[0] == "s":
                half_out[q, p] = shared[band, entry[1]]
            else:
                half_out[q, p] = keep(sums[4, entry[1]])
            if p < shared_rows:
                if entry is not None and entry[0] == "s":
                    other_out[q, p] = shared[1 - band, entry[1]]
                else:
                    other_out[q, p] = jnp.zeros((slots, 128), F32)
    for k in range(epochs):
        outs[k][...] = half_out[lax.rem(epoch + k, epochs)]
        outs[epochs + k][...] = other_out[lax.rem(epoch + k, epochs)]


def tile_gradient(layout, tile, counts, offsets, psf, data, weight, slot_rows):
    shared_rows, rows, pieces = layout
    epochs = len(pieces)
    slots = offsets.shape[1]
    pixels = data.shape[-1]
    shapes = [(rows, slots, 128)] * epochs + [(shared_rows, slots, 128)] * epochs
    image = pl.BlockSpec((1, 1, 1, pixels, pixels), lambda i: (tile, 0, 0, 0, 0))
    return pl.pallas_call(
        functools.partial(tile_kernel, layout, tile),
        grid=(1,),
        out_shape=[f32(*s) for s in shapes],
        in_specs=[smem(), smem(), smem(), image, image]
        + [pl.BlockSpec(s, lambda i: (0, tile, 0)) for s in shapes],
        out_specs=[pl.BlockSpec(s, lambda i: (0, 0, 0)) for s in shapes],
        scratch_shapes=[
            pltpu.VMEM((BANDS, HALF, slots, 128), F32),
            pltpu.VMEM((COMPS, slots, 128), F32),
            pltpu.VMEM((5, COMPS, slots, 128), F32),
            pltpu.VMEM((slots * COMPS, pixels, 128), F32),
            pltpu.VMEM((slots * COMPS, pixels, 128), F32),
            pltpu.VMEM((slots, 2 * pixels, COMPS * 128), BF16),
            pltpu.VMEM((slots, 2 * pixels, COMPS * 128), BF16),
            pltpu.VMEM((2 * pixels, 2 * pixels), F32),
            pltpu.VMEM((5, COMPS, slots, 128), F32),
            pltpu.VMEM((epochs, rows, slots, 128), F32),
            pltpu.VMEM((epochs, shared_rows, slots, 128), F32),
        ],
        compiler_params=params(),
        name=f"tile_{tile}",
    )(counts, offsets, psf, data, weight, *slot_rows)


def scale_of(p):
    first = (lax.axis_index("band") == 0) & (lax.axis_index("epoch") == 0)
    if p < 2:
        return jnp.where(first, F32(STEP / 64.0), F32(STEP))
    return F32(STEP)


def combine_kernel(rows, tiles, match_ref, slots_ref, own_ref, *refs):
    got, (new_slots, new_own) = refs[:-2], refs[-2:]
    wide = slots_ref.shape[1]
    match = match_ref[...]
    for p in range(rows):
        both = pick(match, jnp.concatenate([ref[p] for ref in got], axis=0)) * scale_of(p)
        new_slots[p] = slots_ref[p] - both[:wide]
        new_own[p] = own_ref[p] - both[wide:]


def dense_kernel(rows, lists_ref, *refs):
    tiles, slots = lists_ref.shape
    grads, outs = refs[:tiles], refs[tiles:]
    owners, blocks = len(outs), outs[0].shape[1]
    shape = (owners * blocks, tiles * slots)
    line = lax.broadcasted_iota(jnp.int32, shape, 0)
    lane = lax.broadcasted_iota(jnp.int32, shape, 1)
    me = lax.axis_index("tile")
    target = lax.rem(me + line // blocks, owners) * blocks + line % blocks
    ids = jnp.zeros(shape, jnp.int32)
    for t in range(tiles):
        for s in range(slots):
            ids = jnp.where(lane == t * slots + s, lists_ref[t, s], ids)
    match = (ids == target).astype(F32)
    for p in range(rows):
        dense = pick(match, jnp.concatenate([ref[p] for ref in grads], axis=0))
        for k, out in enumerate(outs):
            out[p] = dense[k * blocks : (k + 1) * blocks]


def update_kernel(rows, own_ref, *refs):
    got, out_ref = refs[:-1], refs[-1]
    for p in range(rows):
        out_ref[p] = own_ref[p] - scale_of(p) * functools.reduce(lambda a, b: a + b, [g[p] for g in got])


def final_kernel(layout, *refs):
    shared_rows, rows, pieces = layout
    epochs = len(pieces)
    ins, (out_ref, held) = refs[: 2 * epochs], refs[2 * epochs :]
    band, epoch = lax.axis_index("band"), lax.axis_index("epoch")
    for k in range(epochs):
        q = lax.rem(epoch - k + epochs, epochs)
        held[band, q] = ins[k][...]
        held[1 - band, q] = ins[epochs + k][...]
    for b in range(BANDS):
        for q, piece in enumerate(pieces):
            for p, entry in enumerate(piece):
                if entry is not None:
                    out_ref[row_of(b, entry)] = held[b, q, p]


def shards(source_params, pixel_data, pixel_weight, psf_width, block_lists, block_counts, block_offsets):
    owners, epochs = lax.axis_size("tile"), lax.axis_size("epoch")
    blocks, param_rows, sources = source_params.shape
    tiles, slots = block_lists.shape
    wide = tiles * slots
    layout = quarter_layout(epochs)
    shared_rows, rows, pieces = layout

    def to_peers(same, other):
        kept = [same[0]]
        for k in range(1, epochs):
            kept.append(lax.ppermute(same[k], "epoch", [(i, (i + k) % epochs) for i in range(epochs)]))
        for k in range(epochs):
            pairs = [
                (i * BANDS + b, (i + k) % epochs * BANDS + 1 - b)
                for i in range(epochs)
                for b in range(BANDS)
            ]
            kept.append(lax.ppermute(other[k], ("epoch", "band"), pairs))
        return kept

    def round_tiles(arrays):
        return [arrays[0]] + [
            lax.ppermute(arrays[k], "tile", [(i, (i + k) % owners) for i in range(owners)])
            for k in range(1, owners)
        ]

    def spread(piece, other_rows):
        return to_peers([piece] * epochs, [piece[:other_rows]] * epochs)

    def summed(parts):
        near = functools.reduce(lambda a, b: a + b, parts[:epochs])
        far = functools.reduce(lambda a, b: a + b, parts[epochs:])
        return near + jnp.pad(far, ((0, rows - shared_rows), (0, 0), (0, 0)))

    by_row = jnp.transpose(source_params, (1, 0, 2))
    packed = pl.pallas_call(
        functools.partial(pack_kernel, layout),
        out_shape=f32(rows + 1, blocks, sources),
        in_specs=[smem(), vmem()],
        out_specs=vmem(),
        compiler_params=params(),
        name="pack",
    )(block_lists, by_row)
    got = round_tiles([packed] * owners)
    slot_piece, match = pl.pallas_call(
        functools.partial(select_kernel, layout),
        out_shape=[f32(rows, wide, sources), f32(wide + blocks, owners * wide)],
        in_specs=[smem()] + [vmem()] * owners,
        out_specs=[vmem()] * 2,
        compiler_params=params(),
        name="select",
    )(block_lists, *got)
    own_piece = packed[:rows]

    for step in range(ITERS):
        slot_rows = spread(slot_piece, shared_rows)
        tile_sums = []
        for t in range(tiles):
            parts = tile_gradient(
                layout, t, block_counts, block_offsets, psf_width, pixel_data, pixel_weight, slot_rows
            )
            tile_sums.append(summed(to_peers(parts[:epochs], parts[epochs:])))
        if step < ITERS - 1:
            got = []
            for t in range(tiles):
                got += round_tiles([tile_sums[t]] * owners)
            slot_piece, own_piece = pl.pallas_call(
                functools.partial(combine_kernel, rows, tiles),
                out_shape=[f32(rows, wide, sources), f32(rows, blocks, sources)],
                in_specs=[vmem()] * (3 + len(got)),
                out_specs=[vmem()] * 2,
                compiler_params=params(),
                name="combine",
            )(match, slot_piece, own_piece, *got)
        else:
            dense = pl.pallas_call(
                functools.partial(dense_kernel, rows),
                out_shape=[f32(rows, blocks, sources)] * owners,
                in_specs=[smem()] + [vmem()] * tiles,
                out_specs=[vmem()] * owners,
                compiler_params=params(),
                name="dense",
            )(block_lists, *tile_sums)
            got = round_tiles(dense)
            own_piece = pl.pallas_call(
                functools.partial(update_kernel, rows),
                out_shape=f32(rows, blocks, sources),
                in_specs=[vmem()] * (1 + owners),
                out_specs=vmem(),
                compiler_params=params(),
                name="update",
            )(own_piece, *got)
    whole = pl.pallas_call(
        functools.partial(final_kernel, layout),
        out_shape=f32(param_rows, blocks, sources),
        in_specs=[vmem()] * (2 * epochs),
        out_specs=vmem(),
        scratch_shapes=[pltpu.VMEM((BANDS, epochs, rows, blocks, sources), F32)],
        compiler_params=params(),
        name="final",
    )(*spread(own_piece, rows))
    return jnp.transpose(whole, (1, 0, 2))


def solution(mesh):
    return jax.shard_map(
        shards,
        mesh=mesh,
        in_specs=(
            P(("region", "tile"), None, None),
            P(("region", "tile"), "epoch", "band", None, None),
            P(("region", "tile"), "epoch", "band", None, None),
            P(("region", "epoch"), "band"),
            P(("region", "tile"), None),
            P(("region", "tile")),
            P(("region", "tile"), None, None),
        ),
        out_specs=P(("region", "tile"), None, None),
        check_vma=False,
    )
```

time: 456 us -> 112 us (0.25)
  other arithmetic: 101 us -> 1.29 us
  matrix products: 86.4 us -> 0 us
  waiting for transfers between devices: 106 us -> 25.6 us
  loops' own time: 54.3 us -> 0 us
  local copies, waits for them, and re-layouts: 52 us -> 8.13 us
  Pallas kernels: 0 us -> 43.3 us
  blocking collectives: 39.7 us -> 0 us
  starting transfers between devices: 0.12 us -> 32.4 us
  between operations: 14.1 us -> 0.89 us
    dot_general x96 -> x0, matrix products: 86.4 us -> none  [render(): jnp.einsum('csi,csj->ij', profile_x, profile_y, precision=lax.Precision.H...]
    add x96 -> x8, other arithmetic: 79.9 us -> 1.29 us  [the longest x4 1.27 us: summed(): return near + jnp.pad(far, ((0, rows - shared_rows), (0, 0), (0, 0)))]
    psum x2 -> x0, waiting for transfers between devices: 64.6 us -> none  [shards(): summed = lax.psum(own_grads, ('epoch', 'band'))]
    another operation x8 -> x0, loops' own time: 54.3 us -> none  [the longest x4 29.1 us: local_gradients(): pieces.append(lax.fori_loop(0, used_slots, grad_slot, empty_grads))]
    pallas_call x0 -> x10, Pallas kernels: none -> 43.3 us  [the longest x4 33 us: tile_gradient(): pl.pallas_call(functools.partial(tile_kernel, layout, tile), grid=(1,), o...]
    reduce_scatter x2 -> x0, waiting for transfers between devices: 41.7 us -> none  [shards(): lax.psum_scatter(dense_grads, 'tile', scatter_dimension=0, tiled=True)]
    all_gather x2 -> x0, blocking collectives: 39.7 us -> none  [shards(): everything = lax.all_gather(current, 'tile', axis=0, tiled=True)]
    slice x129 -> x3, local copies, waits for them, and re-layouts: 40.8 us -> 2.37 us  [the longest x2 1.75 us: spread(): return to_peers([piece] * epochs, [piece[:other_rows]] * epochs)]
  transfers between devices with their start and end apart: 4 -> 33, of which waited for: 4 -> 15; matrix products, arithmetic and copies ran while one was open for 0% -> 3% of each run, Pallas kernels for 0% -> 16%
where the time goes in v1:
time: 112 us
  Pallas kernels  43.3 us (39%)
  starting transfers between devices  32.4 us (29%)
  waiting for transfers between devices  25.6 us (23%)
  local copies, waits for them, and re-layouts  8.13 us (7%)
  other arithmetic  1.29 us (1%)
    pallas_call x4, Pallas kernels, tile_gradient(): pl.pallas_call(functools.partial(tile_kernel, layout, tile), grid=(1,), o...  33 us
    ppermute x12, starting transfers between devices, round_tiles(): lax.ppermute(arrays[k], 'tile', [(i, (i + k) % owners) for i in range(own...  17.4 us
    ppermute x12, waiting for transfers between devices, round_tiles(): lax.ppermute(arrays[k], 'tile', [(i, (i + k) % owners) for i in range(own...  13.4 us
    ppermute x14, waiting for transfers between devices, to_peers(): kept.append(lax.ppermute(other[k], ('epoch', 'band'), pairs))  9.33 us
    ppermute x7, starting transfers between devices, to_peers(): lax.ppermute(same[k], 'epoch', [(i, (i + k) % epochs) for i in range(epoc...  7.7 us
    ppermute x14, starting transfers between devices, to_peers(): kept.append(lax.ppermute(other[k], ('epoch', 'band'), pairs))  7.28 us
    unnamed x59, local copies, waits for them, and re-layouts  5.76 us
    ppermute x7, waiting for transfers between devices, to_peers(): lax.ppermute(same[k], 'epoch', [(i, (i + k) % epochs) for i in range(epoc...  2.84 us
  transfers between devices with their start and end apart: 33, of which 15 were waited for; matrix products, arithmetic and copies ran while one was open for 3% of the time, Pallas kernels for 16%

profile of v1, /device:TPU:0, one launch (start us, length us, event | category | flops | bytes accessed | tf_op | source)
XLA Modules:
  0.0 111.6 jit_solution(13665058072780377858)
XLA Ops:
  0.0 1.6 %pack.1.refs_0_ = f32[12,8,128]{2,1,0:T(8,128)} custom-call(s32[2,8]{1,0:T(2,128)} %lists_ref.5, f32[44,8,128]{2,1,0:T(8,128)} %bitcast.2), custom_call_target="tpu_custom_call" | custom-call | tf_op jit(solution)/shard_map/pack/pallas_call | solution.py:412
  1.6 5.0 %collective-permute-start.2 = (f32[12,8,128]{2,1,0:T(8,128)}, f32[12,8,128]{2,1,0:T(8,128)S(1)}, u32[]{:S(2)}, u32[]{:S(2)}) collective-permute-start(f32[12,8,128]{2,1,0:T(8,128)} %pack.1.refs_0_), channel_id=1, source_target_pairs={{0,12},{4,0},{8,4},{12,8},{1,13},{5,1},{9,5},{13,9},{2,14},{6,2},{... | collective-permute-start | bytes 147464 | tf_op jit(solution)/shard_map/ppermute | solution.py:399
  9.0 2.8 %collective-permute-done.1.refs_2_ = f32[12,8,128]{2,1,0:T(8,128)S(1)} collective-permute-done((f32[12,8,128]{2,1,0:T(8,128)}, f32[12,8,128]{2,1,0:T(8,128)S(1)}, u32[]{:S(2)}, u32[]{:S(2)}) %collective-permute-start.1) | collective-permute-done | bytes 49184 | tf_op jit(solution)/shard_map/ppermute | solution.py:399
  13.4 1.8 %select.5 = (f32[11,16,128]{2,1,0:T(8,128)}, f32[24,64]{1,0:T(8,128)}) custom-call(s32[2,8]{1,0:T(2,128)} %lists_ref.5, f32[12,8,128]{2,1,0:T(8,128)} %pack.1.refs_0_, f32[12,8,128]{2,1,0:T(8,128)} %copy-done.11, f32[12,8,128]{2,1,0:T(8,128)} %copy-done.10, f32[12,8,128]{2,1,0:T(8,128)} %copy-done.9), custom_call_target="tpu_custom_call" | custom-call | tf_op jit(solution)/shard_map/select/pallas_call | solution.py:421
  15.2 1.5 %collective-permute-start.3 = (f32[11,16,128]{2,1,0:T(8,128)}, f32[11,16,128]{2,1,0:T(8,128)S(1)}, u32[]{:S(2)}, u32[]{:S(2)}) collective-permute-start(f32[11,16,128]{2,1,0:T(8,128)} %get-tuple-element.30.refs_0_.slots_ref), channel_id=1, source_target_pairs={{0,2},{2,0},{1,3},{3,1},{4,6},{6,4},{5,7},{7,5},{8,10},{10,8},{9,1... | collective-permute-start | bytes 270344 | tf_op jit(solution)/shard_map/ppermute | solution.py:387
  19.5 1.8 %collective-permute-done.5.refs_3_ = f32[8,16,128]{2,1,0:T(8,128)S(1)} collective-permute-done((f32[8,16,128]{2,1,0:T(8,128)S(1)}, f32[8,16,128]{2,1,0:T(8,128)S(1)}, u32[]{:S(2)}, u32[]{:S(2)}) %collective-permute-start.5) | collective-permute-done | bytes 65568 | tf_op jit(solution)/shard_map/ppermute | solution.py:394
  22.6 7.3 %tile_1.2 = (f32[11,8,128]{2,1,0:T(8,128)}, f32[11,8,128]{2,1,0:T(8,128)}, f32[8,8,128]{2,1,0:T(8,128)}, f32[8,8,128]{2,1,0:T(8,128)}) custom-call(s32[2]{0:T(128)} %counts_ref.7, s32[2,8,2]{2,1,0:T(8,128)} %copy.8.offsets_ref, f32[1,1]{1,0:T(1,128)S(6)} %copy.12.psf_ref, f32[2,1,1,128,128]{4,3,2,1,0:T(8,128)} %data_ref.7, ...), custom_call_target="tpu_custom_call" | custom-call | tf_op jit(solution)/shard_map/tile_1/pallas_call | solution.py:292
  32.1 9.2 %tile_0.2 = (f32[11,8,128]{2,1,0:T(8,128)}, f32[11,8,128]{2,1,0:T(8,128)}, f32[8,8,128]{2,1,0:T(8,128)}, f32[8,8,128]{2,1,0:T(8,128)}) custom-call(s32[2]{0:T(128)} %counts_ref.7, s32[2,8,2]{2,1,0:T(8,128)} %copy.8.offsets_ref, f32[1,1]{1,0:T(1,128)S(6)} %copy.12.psf_ref, f32[2,1,1,128,128]{4,3,2,1,0:T(8,128)} %data_ref.7, ...), custom_call_target="tpu_custom_call" | custom-call | tf_op jit(solution)/shard_map/tile_0/pallas_call | solution.py:292
  43.4 1.4 %collective-permute-done.8 = f32[8,8,128]{2,1,0:T(8,128)S(1)} collective-permute-done((f32[8,8,128]{2,1,0:T(8,128)}, f32[8,8,128]{2,1,0:T(8,128)S(1)}, u32[]{:S(2)}, u32[]{:S(2)}) %collective-permute-start.8) | collective-permute-done | bytes 32800 | tf_op jit(solution)/shard_map/ppermute | solution.py:394
  45.0 3.0 %collective-permute-start.16 = (f32[11,8,128]{2,1,0:T(8,128)S(1)}, f32[11,8,128]{2,1,0:T(8,128)S(1)}, u32[]{:S(2)}, u32[]{:S(2)}) collective-permute-start(f32[11,8,128]{2,1,0:T(8,128)S(1)} %pad_add_fusion.2.refs_4_), channel_id=1, source_target_pairs={{0,8},{4,12},{8,0},{12,4},{1,9},{5,13},{9,1},{13,5},{2,10},{6,14},... | collective-permute-start | bytes 135176 | tf_op jit(solution)/shard_map/ppermute | solution.py:399
  48.0 3.9 %collective-permute-start.11 = (f32[11,8,128]{2,1,0:T(8,128)S(1)}, f32[11,8,128]{2,1,0:T(8,128)S(1)}, u32[]{:S(2)}, u32[]{:S(2)}) collective-permute-start(f32[11,8,128]{2,1,0:T(8,128)S(1)} %pad_add_fusion.3.refs_0_), channel_id=1, source_target_pairs={{0,12},{4,0},{8,4},{12,8},{1,13},{5,1},{9,5},{13,9},{2,14},{6,2},{... | collective-permute-start | bytes 135176 | tf_op jit(solution)/shard_map/ppermute | solution.py:399
  54.3 2.5 %collective-permute-done.10.refs_2_ = f32[11,8,128]{2,1,0:T(8,128)S(1)} collective-permute-done((f32[11,8,128]{2,1,0:T(8,128)S(1)}, f32[11,8,128]{2,1,0:T(8,128)S(1)}, u32[]{:S(2)}, u32[]{:S(2)}) %collective-permute-start.10) | collective-permute-done | bytes 45088 | tf_op jit(solution)/shard_map/ppermute | solution.py:399
  58.4 2.0 %combine.1 = (f32[11,16,128]{2,1,0:T(8,128)}, f32[11,8,128]{2,1,0:T(8,128)}) custom-call(f32[24,64]{1,0:T(8,128)} %get-tuple-element.29.match_ref, f32[11,16,128]{2,1,0:T(8,128)} %get-tuple-element.30.refs_0_.slots_ref, f32[11,8,128]{2,1,0:T(8,128)} %slice.12.own_ref, f32[11,8,128]{2,1,0:T(8,128)} %copy-done.8, f32[11,8,128]{2,1,0:T(8,128)} %copy-done.27, ...), custom_call_target="tpu_custom_call" | custom-call | tf_op jit(solution)/shard_map/combine/pallas_call | solution.py:443
  63.5 3.1 %collective-permute-done.20.refs_3_ = f32[8,16,128]{2,1,0:T(8,128)S(1)} collective-permute-done((f32[8,16,128]{2,1,0:T(8,128)S(1)}, f32[8,16,128]{2,1,0:T(8,128)S(1)}, u32[]{:S(2)}, u32[]{:S(2)}) %collective-permute-start.20) | collective-permute-done | bytes 65568 | tf_op jit(solution)/shard_map/ppermute | solution.py:394
  67.9 7.3 %tile_1.3 = (f32[11,8,128]{2,1,0:T(8,128)}, f32[11,8,128]{2,1,0:T(8,128)}, f32[8,8,128]{2,1,0:T(8,128)}, f32[8,8,128]{2,1,0:T(8,128)}) custom-call(s32[2]{0:T(128)} %counts_ref.7, s32[2,8,2]{2,1,0:T(8,128)} %copy.8.offsets_ref, f32[1,1]{1,0:T(1,128)S(6)} %copy.12.psf_ref, f32[2,1,1,128,128]{4,3,2,1,0:T(8,128)} %data_ref.7, ...), custom_call_target="tpu_custom_call" | custom-call | tf_op jit(solution)/shard_map/tile_1/pallas_call | solution.py:292
  77.4 9.2 %tile_0.3 = (f32[11,8,128]{2,1,0:T(8,128)}, f32[11,8,128]{2,1,0:T(8,128)}, f32[8,8,128]{2,1,0:T(8,128)}, f32[8,8,128]{2,1,0:T(8,128)}) custom-call(s32[2]{0:T(128)} %counts_ref.7, s32[2,8,2]{2,1,0:T(8,128)} %copy.8.offsets_ref, f32[1,1]{1,0:T(1,128)S(6)} %copy.12.psf_ref, f32[2,1,1,128,128]{4,3,2,1,0:T(8,128)} %data_ref.7, ...), custom_call_target="tpu_custom_call" | custom-call | tf_op jit(solution)/shard_map/tile_0/pallas_call | solution.py:292
  88.7 1.4 %collective-permute-done.23 = f32[8,8,128]{2,1,0:T(8,128)S(1)} collective-permute-done((f32[8,8,128]{2,1,0:T(8,128)}, f32[8,8,128]{2,1,0:T(8,128)S(1)}, u32[]{:S(2)}, u32[]{:S(2)}) %collective-permute-start.23) | collective-permute-done | bytes 32800 | tf_op jit(solution)/shard_map/ppermute | solution.py:394
  92.6 1.7 %dense.1 = (f32[11,8,128]{2,1,0:T(8,128)}, f32[11,8,128]{2,1,0:T(8,128)}, f32[11,8,128]{2,1,0:T(8,128)}, f32[11,8,128]{2,1,0:T(8,128)}) custom-call(s32[2,8]{1,0:T(2,128)} %lists_ref.5, f32[11,8,128]{2,1,0:T(8,128)} %pad_add_fusion.1.refs_0_, f32[11,8,128]{2,1,0:T(8,128)} %pad_add_fusion.refs_1_), custom_call_target="tpu_custom_call" | custom-call | tf_op jit(solution)/shard_map/dense/pallas_call | solution.py:452
  95.6 2.6 %collective-permute-start.29 = (f32[11,8,128]{2,1,0:T(8,128)}, f32[11,8,128]{2,1,0:T(8,128)S(1)}, u32[]{:S(2)}, u32[]{:S(2)}) collective-permute-start(f32[11,8,128]{2,1,0:T(8,128)} %get-tuple-element.52), channel_id=1, source_target_pairs={{0,12},{4,0},{8,4},{12,8},{1,13},{5,1},{9,5},{13,9},{2,14},{6,2},{... | collective-permute-start | bytes 135176 | tf_op jit(solution)/shard_map/ppermute | solution.py:399
  98.2 2.5 %collective-permute-done.27.refs_1_ = f32[11,8,128]{2,1,0:T(8,128)S(1)} collective-permute-done((f32[11,8,128]{2,1,0:T(8,128)}, f32[11,8,128]{2,1,0:T(8,128)S(1)}, u32[]{:S(2)}, u32[]{:S(2)}) %collective-permute-start.27) | collective-permute-done | bytes 45088 | tf_op jit(solution)/shard_map/ppermute | solution.py:399
  102.6 1.5 %update.1.refs_0_ = f32[11,8,128]{2,1,0:T(8,128)} custom-call(f32[11,8,128]{2,1,0:T(8,128)} %get-tuple-element.39.own_ref, f32[11,8,128]{2,1,0:T(8,128)} %get-tuple-element.49.refs_0_, f32[11,8,128]{2,1,0:T(8,128)} %copy-done.16, f32[11,8,128]{2,1,0:T(8,128)} %copy-done.17, f32[11,8,128]{2,1,0:T(8,128)} %copy-done.18), custom_call_target="tpu_custom_call" | custom-call | tf_op jit(solution)/shard_map/update/pallas_call | solution.py:461
  106.2 1.5 %collective-permute-done.32.refs_3_ = f32[11,8,128]{2,1,0:T(8,128)S(1)} collective-permute-done((f32[11,8,128]{2,1,0:T(8,128)}, f32[11,8,128]{2,1,0:T(8,128)S(1)}, u32[]{:S(2)}, u32[]{:S(2)}) %collective-permute-start.32) | collective-permute-done | bytes 45088 | tf_op jit(solution)/shard_map/ppermute | solution.py:394
  107.8 1.6 %collective-permute-done.30.refs_1_ = f32[11,8,128]{2,1,0:T(8,128)S(1)} collective-permute-done((f32[11,8,128]{2,1,0:T(8,128)}, f32[11,8,128]{2,1,0:T(8,128)S(1)}, u32[]{:S(2)}, u32[]{:S(2)}) %collective-permute-start.30) | collective-permute-done | bytes 45088 | tf_op jit(solution)/shard_map/ppermute | solution.py:387
  110.0 1.6 %final.1 = f32[44,8,128]{2,1,0:T(8,128)} custom-call(f32[11,8,128]{2,1,0:T(8,128)} %update.1.refs_0_, f32[11,8,128]{2,1,0:T(8,128)} %copy-done.21, f32[11,8,128]{2,1,0:T(8,128)} %copy-done.20, f32[11,8,128]{2,1,0:T(8,128)} %copy-done.19), custom_call_target="tpu_custom_call" | custom-call | tf_op jit(solution)/shard_map/final/pallas_call | solution.py:469
  (122 shorter events, 32.7 us)
Async XLA Ops:
  1.6 7.4 %collective-permute-start.2 = (f32[12,8,128]{2,1,0:T(8,128)}, f32[12,8,128]{2,1,0:T(8,128)S(1)}, u32[]{:S(2)}, u32[]{:S(2)}) collective-permute-start(f32[12,8,128]{2,1,0:T(8,128)} %pack.1.refs_0_), channel_id=1, source_target_pairs={{0,12},{4,0},{8,4},{12,8},{1,13},{5,1},{9,5},{13,9},{2,14},{6,2},{... | collective-permute-start | bytes 147464 | tf_op jit(solution)/shard_map/ppermute | solution.py:399
  6.6 5.2 %collective-permute-start.1 = (f32[12,8,128]{2,1,0:T(8,128)}, f32[12,8,128]{2,1,0:T(8,128)S(1)}, u32[]{:S(2)}, u32[]{:S(2)}) collective-permute-start(f32[12,8,128]{2,1,0:T(8,128)} %pack.1.refs_0_), channel_id=1, source_target_pairs={{0,8},{4,12},{8,0},{12,4},{1,9},{5,13},{9,1},{13,5},{2,10},{6,14},... | collective-permute-start | bytes 147464 | tf_op jit(solution)/shard_map/ppermute | solution.py:399
  6.6 6.1 %collective-permute-start = (f32[12,8,128]{2,1,0:T(8,128)}, f32[12,8,128]{2,1,0:T(8,128)S(1)}, u32[]{:S(2)}, u32[]{:S(2)}) collective-permute-start(f32[12,8,128]{2,1,0:T(8,128)} %pack.1.refs_0_), channel_id=1, source_target_pairs={{0,4},{4,8},{8,12},{12,0},{1,5},{5,9},{9,13},{13,1},{2,6},{6,10},{... | collective-permute-start | bytes 147464 | tf_op jit(solution)/shard_map/ppermute | solution.py:399
  15.2 6.2 %collective-permute-start.3 = (f32[11,16,128]{2,1,0:T(8,128)}, f32[11,16,128]{2,1,0:T(8,128)S(1)}, u32[]{:S(2)}, u32[]{:S(2)}) collective-permute-start(f32[11,16,128]{2,1,0:T(8,128)} %get-tuple-element.30.refs_0_.slots_ref), channel_id=1, source_target_pairs={{0,2},{2,0},{1,3},{3,1},{4,6},{6,4},{5,7},{7,5},{8,10},{10,8},{9,1... | collective-permute-start | bytes 270344 | tf_op jit(solution)/shard_map/ppermute | solution.py:387
  29.9 14.9 %collective-permute-start.12 = (f32[11,8,128]{2,1,0:T(8,128)}, f32[11,8,128]{2,1,0:T(8,128)S(1)}, u32[]{:S(2)}, u32[]{:S(2)}) collective-permute-start(f32[11,8,128]{2,1,0:T(8,128)} %get-tuple-element.36), channel_id=1, source_target_pairs={{0,2},{2,0},{1,3},{3,1},{4,6},{6,4},{5,7},{7,5},{8,10},{10,8},{9,1... | collective-permute-start | bytes 135176 | tf_op jit(solution)/shard_map/ppermute | solution.py:387
  31.0 11.4 %collective-permute-start.13 = (f32[8,8,128]{2,1,0:T(8,128)}, f32[8,8,128]{2,1,0:T(8,128)S(1)}, u32[]{:S(2)}, u32[]{:S(2)}) collective-permute-start(f32[8,8,128]{2,1,0:T(8,128)} %get-tuple-element.37), channel_id=1, source_target_pairs={{0,1},{1,0},{2,3},{3,2},{4,5},{5,4},{6,7},{7,6},{8,9},{9,8},{10,11... | collective-permute-start | bytes 98312 | tf_op jit(solution)/shard_map/ppermute | solution.py:394
  31.0 12.4 %collective-permute-start.14 = (f32[8,8,128]{2,1,0:T(8,128)}, f32[8,8,128]{2,1,0:T(8,128)S(1)}, u32[]{:S(2)}, u32[]{:S(2)}) collective-permute-start(f32[8,8,128]{2,1,0:T(8,128)} %get-tuple-element.38), channel_id=1, source_target_pairs={{0,3},{1,2},{2,1},{3,0},{4,7},{5,6},{6,5},{7,4},{8,11},{9,10},{10,... | collective-permute-start | bytes 98312 | tf_op jit(solution)/shard_map/ppermute | solution.py:394
  42.4 5.5 %collective-permute-start.6 = (f32[11,8,128]{2,1,0:T(8,128)}, f32[11,8,128]{2,1,0:T(8,128)S(1)}, u32[]{:S(2)}, u32[]{:S(2)}) collective-permute-start(f32[11,8,128]{2,1,0:T(8,128)} %get-tuple-element.32), channel_id=1, source_target_pairs={{0,2},{2,0},{1,3},{3,1},{4,6},{6,4},{5,7},{7,5},{8,10},{10,8},{9,1... | collective-permute-start | bytes 135176 | tf_op jit(solution)/shard_map/ppermute | solution.py:387
  44.9 7.0 %collective-permute-start.17 = (f32[11,8,128]{2,1,0:T(8,128)S(1)}, f32[11,8,128]{2,1,0:T(8,128)S(1)}, u32[]{:S(2)}, u32[]{:S(2)}) collective-permute-start(f32[11,8,128]{2,1,0:T(8,128)S(1)} %pad_add_fusion.2.refs_4_), channel_id=1, source_target_pairs={{0,12},{4,0},{8,4},{12,8},{1,13},{5,1},{9,5},{13,9},{2,14},{6,2},{... | collective-permute-start | bytes 135176 | tf_op jit(solution)/shard_map/ppermute | solution.py:399
  45.0 8.2 %collective-permute-start.16 = (f32[11,8,128]{2,1,0:T(8,128)S(1)}, f32[11,8,128]{2,1,0:T(8,128)S(1)}, u32[]{:S(2)}, u32[]{:S(2)}) collective-permute-start(f32[11,8,128]{2,1,0:T(8,128)S(1)} %pad_add_fusion.2.refs_4_), channel_id=1, source_target_pairs={{0,8},{4,12},{8,0},{12,4},{1,9},{5,13},{9,1},{13,5},{2,10},{6,14},... | collective-permute-start | bytes 135176 | tf_op jit(solution)/shard_map/ppermute | solution.py:399
  47.9 6.4 %collective-permute-start.15 = (f32[11,8,128]{2,1,0:T(8,128)S(1)}, f32[11,8,128]{2,1,0:T(8,128)S(1)}, u32[]{:S(2)}, u32[]{:S(2)}) collective-permute-start(f32[11,8,128]{2,1,0:T(8,128)S(1)} %pad_add_fusion.2.refs_4_), channel_id=1, source_target_pairs={{0,4},{4,8},{8,12},{12,0},{1,5},{5,9},{9,13},{13,1},{2,6},{6,10},{... | collective-permute-start | bytes 135176 | tf_op jit(solution)/shard_map/ppermute | solution.py:399
  48.0 6.3 %collective-permute-start.11 = (f32[11,8,128]{2,1,0:T(8,128)S(1)}, f32[11,8,128]{2,1,0:T(8,128)S(1)}, u32[]{:S(2)}, u32[]{:S(2)}) collective-permute-start(f32[11,8,128]{2,1,0:T(8,128)S(1)} %pad_add_fusion.3.refs_0_), channel_id=1, source_target_pairs={{0,12},{4,0},{8,4},{12,8},{1,13},{5,1},{9,5},{13,9},{2,14},{6,2},{... | collective-permute-start | bytes 135176 | tf_op jit(solution)/shard_map/ppermute | solution.py:399
  51.9 4.9 %collective-permute-start.10 = (f32[11,8,128]{2,1,0:T(8,128)S(1)}, f32[11,8,128]{2,1,0:T(8,128)S(1)}, u32[]{:S(2)}, u32[]{:S(2)}) collective-permute-start(f32[11,8,128]{2,1,0:T(8,128)S(1)} %pad_add_fusion.3.refs_0_), channel_id=1, source_target_pairs={{0,8},{4,12},{8,0},{12,4},{1,9},{5,13},{9,1},{13,5},{2,10},{6,14},... | collective-permute-start | bytes 135176 | tf_op jit(solution)/shard_map/ppermute | solution.py:399
  51.9 5.9 %collective-permute-start.9 = (f32[11,8,128]{2,1,0:T(8,128)S(1)}, f32[11,8,128]{2,1,0:T(8,128)S(1)}, u32[]{:S(2)}, u32[]{:S(2)}) collective-permute-start(f32[11,8,128]{2,1,0:T(8,128)S(1)} %pad_add_fusion.3.refs_0_), channel_id=1, source_target_pairs={{0,4},{4,8},{8,12},{12,0},{1,5},{5,9},{9,13},{13,1},{2,6},{6,10},{... | collective-permute-start | bytes 135176 | tf_op jit(solution)/shard_map/ppermute | solution.py:399
  60.4 6.2 %collective-permute-start.18 = (f32[11,16,128]{2,1,0:T(8,128)}, f32[11,16,128]{2,1,0:T(8,128)S(1)}, u32[]{:S(2)}, u32[]{:S(2)}) collective-permute-start(f32[11,16,128]{2,1,0:T(8,128)} %get-tuple-element.40.refs_0_), channel_id=1, source_target_pairs={{0,2},{2,0},{1,3},{3,1},{4,6},{6,4},{5,7},{7,5},{8,10},{10,8},{9,1... | collective-permute-start | bytes 270344 | tf_op jit(solution)/shard_map/ppermute | solution.py:387
  62.4 4.2 %collective-permute-start.19 = (f32[8,16,128]{2,1,0:T(8,128)S(1)}, f32[8,16,128]{2,1,0:T(8,128)S(1)}, u32[]{:S(2)}, u32[]{:S(2)}) collective-permute-start(f32[8,16,128]{2,1,0:T(8,128)S(1)} %slice.11), channel_id=1, source_target_pairs={{0,1},{1,0},{2,3},{3,2},{4,5},{5,4},{6,7},{7,6},{8,9},{9,8},{10,11... | collective-permute-start | bytes 196616 | tf_op jit(solution)/shard_map/ppermute | solution.py:394
  75.2 14.9 %collective-permute-start.24 = (f32[11,8,128]{2,1,0:T(8,128)}, f32[11,8,128]{2,1,0:T(8,128)S(1)}, u32[]{:S(2)}, u32[]{:S(2)}) collective-permute-start(f32[11,8,128]{2,1,0:T(8,128)} %get-tuple-element.46), channel_id=1, source_target_pairs={{0,2},{2,0},{1,3},{3,1},{4,6},{6,4},{5,7},{7,5},{8,10},{10,8},{9,1... | collective-permute-start | bytes 135176 | tf_op jit(solution)/shard_map/ppermute | solution.py:387
  76.3 11.4 %collective-permute-start.25 = (f32[8,8,128]{2,1,0:T(8,128)}, f32[8,8,128]{2,1,0:T(8,128)S(1)}, u32[]{:S(2)}, u32[]{:S(2)}) collective-permute-start(f32[8,8,128]{2,1,0:T(8,128)} %get-tuple-element.47), channel_id=1, source_target_pairs={{0,1},{1,0},{2,3},{3,2},{4,5},{5,4},{6,7},{7,6},{8,9},{9,8},{10,11... | collective-permute-start | bytes 98312 | tf_op jit(solution)/shard_map/ppermute | solution.py:394
  76.3 12.4 %collective-permute-start.26 = (f32[8,8,128]{2,1,0:T(8,128)}, f32[8,8,128]{2,1,0:T(8,128)S(1)}, u32[]{:S(2)}, u32[]{:S(2)}) collective-permute-start(f32[8,8,128]{2,1,0:T(8,128)} %get-tuple-element.48), channel_id=1, source_target_pairs={{0,3},{1,2},{2,1},{3,0},{4,7},{5,6},{6,5},{7,4},{8,11},{9,10},{10,... | collective-permute-start | bytes 98312 | tf_op jit(solution)/shard_map/ppermute | solution.py:394
  87.7 4.3 %collective-permute-start.21 = (f32[11,8,128]{2,1,0:T(8,128)}, f32[11,8,128]{2,1,0:T(8,128)S(1)}, u32[]{:S(2)}, u32[]{:S(2)}) collective-permute-start(f32[11,8,128]{2,1,0:T(8,128)} %get-tuple-element.42), channel_id=1, source_target_pairs={{0,2},{2,0},{1,3},{3,1},{4,6},{6,4},{5,7},{7,5},{8,10},{10,8},{9,1... | collective-permute-start | bytes 135176 | tf_op jit(solution)/shard_map/ppermute | solution.py:387
  94.4 6.3 %collective-permute-start.27 = (f32[11,8,128]{2,1,0:T(8,128)}, f32[11,8,128]{2,1,0:T(8,128)S(1)}, u32[]{:S(2)}, u32[]{:S(2)}) collective-permute-start(f32[11,8,128]{2,1,0:T(8,128)} %get-tuple-element.50), channel_id=1, source_target_pairs={{0,4},{4,8},{8,12},{12,0},{1,5},{5,9},{9,13},{13,1},{2,6},{6,10},{... | collective-permute-start | bytes 135176 | tf_op jit(solution)/shard_map/ppermute | solution.py:399
  95.6 6.3 %collective-permute-start.28 = (f32[11,8,128]{2,1,0:T(8,128)}, f32[11,8,128]{2,1,0:T(8,128)S(1)}, u32[]{:S(2)}, u32[]{:S(2)}) collective-permute-start(f32[11,8,128]{2,1,0:T(8,128)} %get-tuple-element.51), channel_id=1, source_target_pairs={{0,8},{4,12},{8,0},{12,4},{1,9},{5,13},{9,1},{13,5},{2,10},{6,14},... | collective-permute-start | bytes 135176 | tf_op jit(solution)/shard_map/ppermute | solution.py:399
  95.6 6.3 %collective-permute-start.29 = (f32[11,8,128]{2,1,0:T(8,128)}, f32[11,8,128]{2,1,0:T(8,128)S(1)}, u32[]{:S(2)}, u32[]{:S(2)}) collective-permute-start(f32[11,8,128]{2,1,0:T(8,128)} %get-tuple-element.52), channel_id=1, source_target_pairs={{0,12},{4,0},{8,4},{12,8},{1,13},{5,1},{9,5},{13,9},{2,14},{6,2},{... | collective-permute-start | bytes 135176 | tf_op jit(solution)/shard_map/ppermute | solution.py:399
  105.1 4.3 %collective-permute-start.30 = (f32[11,8,128]{2,1,0:T(8,128)}, f32[11,8,128]{2,1,0:T(8,128)S(1)}, u32[]{:S(2)}, u32[]{:S(2)}) collective-permute-start(f32[11,8,128]{2,1,0:T(8,128)} %update.1.refs_0_), channel_id=1, source_target_pairs={{0,2},{2,0},{1,3},{3,1},{4,6},{6,4},{5,7},{7,5},{8,10},{10,8},{9,1... | collective-permute-start | bytes 135176 | tf_op jit(solution)/shard_map/ppermute | solution.py:387
  (38 other events, 83.1 us)

commit v2 on v1

v2 whole, which is shorter than its diff:
```python
import functools
import math

import jax
import jax.numpy as jnp
from jax import lax
from jax.experimental import pallas as pl
from jax.experimental.pallas import tpu as pltpu
from jax.sharding import PartitionSpec as P

ITERS = 2
STEP = 0.005
POSITION_RATE = 1.0 / 64.0
COMPS = 7
BANDS = 2
SHARED = 4 * COMPS
HALF = SHARED // BANDS
LOG2E = math.log2(math.e)
F32 = jnp.float32
BF16 = jnp.bfloat16
MIB = 1024 * 1024


def quarter_layout(epochs):
    shared_rows = -(-HALF // epochs)
    rows = -(-(HALF + COMPS) // epochs)
    pieces, amp = [], 0
    for q in range(epochs):
        piece = [("s", i) for i in range(q * shared_rows, min((q + 1) * shared_rows, HALF))]
        while len(piece) < rows and amp < COMPS:
            piece.append(("a", amp))
            amp += 1
        pieces.append(piece + [None] * (rows - len(piece)))
    return shared_rows, rows, pieces


def row_of(band, entry):
    kind, i = entry
    if kind == "a":
        return 2 + 6 * i + 4 + band, None
    k, c = divmod(HALF * band + i, COMPS)
    return 2 + 6 * c + k, (k if k < 2 else None)


def split3(x):
    hi = x.astype(BF16)
    rest = x - hi.astype(F32)
    mid = rest.astype(BF16)
    low = (rest - mid.astype(F32)).astype(BF16)
    return jnp.concatenate([hi, mid, low], axis=0)


def pick(matrix, rows):
    wide = jnp.concatenate([matrix, matrix, matrix], axis=1).astype(BF16)
    return jnp.dot(wide, split3(rows), preferred_element_type=F32)


def vmem():
    return pl.BlockSpec(memory_space=pltpu.VMEM)


def smem():
    return pl.BlockSpec(memory_space=pltpu.SMEM)


def f32(*shape):
    return jax.ShapeDtypeStruct(shape, F32)


def params(mib=4):
    return pltpu.CompilerParams(vmem_limit_bytes=mib * MIB)


def pack_kernel(layout, spacing, lists_ref, params_ref, out_ref):
    shared_rows, rows, pieces = layout
    band, epoch = lax.axis_index("band"), lax.axis_index("epoch")
    for b in range(BANDS):
        for q in range(len(pieces)):

            @pl.when((band == b) & (epoch == q))
            def _():
                for p, entry in enumerate(pieces[q]):
                    if entry is None:
                        out_ref[p] = jnp.zeros(out_ref.shape[1:], F32)
                        continue
                    row, position = row_of(b, entry)
                    value = params_ref[row]
                    if position is not None:
                        value = spacing * params_ref[position] + value
                    out_ref[p] = value

    tiles, slots = lists_ref.shape
    lane = lax.broadcasted_iota(jnp.int32, (8, 128), 1)
    ids = jnp.zeros((8, 128), jnp.int32)
    for t in range(tiles):
        for s in range(slots):
            ids = jnp.where(lane == t * slots + s, lists_ref[t, s], ids)
    out_ref[rows] = ids.astype(F32)


def select_kernel(layout, lists_ref, *refs):
    shared_rows, rows, pieces = layout
    got, (out_ref, short_ref, match_ref) = refs[:-3], refs[-3:]
    owners = len(got)
    tiles, slots = lists_ref.shape
    blocks = got[0].shape[1]
    wide = tiles * slots
    me = lax.axis_index("tile")

    def slot_ids(shape):
        line = lax.broadcasted_iota(jnp.int32, shape, 0)
        ids = jnp.zeros(shape, jnp.int32)
        for t in range(tiles):
            for s in range(slots):
                ids = jnp.where(line == t * slots + s, lists_ref[t, s], ids)
        return ids

    shape = (wide, owners * blocks)
    lane = lax.broadcasted_iota(jnp.int32, shape, 1)
    held = lax.rem(me - lane // blocks + owners, owners) * blocks + lane % blocks
    choose = (slot_ids(shape) == held).astype(F32)
    for p in range(rows):
        chosen = pick(choose, jnp.concatenate([ref[p] for ref in got], axis=0))
        out_ref[p] = chosen
        if p < shared_rows:
            short_ref[p] = chosen

    shape = (wide + blocks, owners * wide)
    line = lax.broadcasted_iota(jnp.int32, shape, 0)
    own = jnp.where(line < wide, slot_ids(shape), me * blocks + line - wide).astype(F32)
    sent = jnp.concatenate([ref[rows, :1, :wide] for ref in got], axis=1)
    match_ref[...] = (own == sent).astype(F32)


def put_together(layout, band, epoch, ins, half, other, shared, amps):
    shared_rows, rows, pieces = layout
    epochs = len(pieces)
    for k in range(epochs):
        q = lax.rem(epoch - k + epochs, epochs)
        half[q] = ins[k][...]
        other[q] = ins[epochs + k][...]
    for q, piece in enumerate(pieces):
        for p, entry in enumerate(piece):
            if entry is None:
                continue
            kind, i = entry
            if kind == "s":
                shared[band, i] = half[q, p]
                shared[1 - band, i] = other[q, p]
            else:
                amps[i] = half[q, p]


def step_kernel(layout, later, counts_ref, offsets_ref, psf_ref, data_ref, weight_ref, *refs):
    shared_rows, rows, pieces = layout
    epochs = len(pieces)
    taken = 2 * epochs * (2 if later else 1)
    ins, refs = refs[:taken], refs[taken:]
    outs, refs = refs[: 2 * epochs], refs[2 * epochs :]
    shared, amps, derived, prof_x, prof_y, pieces_x, pieces_y, image, sums, half, other = refs[:11]
    band, epoch = lax.axis_index("band"), lax.axis_index("epoch")
    tiles = data_ref.shape[0]
    pixels = data_ref.shape[-1]
    wide = shared.shape[2]
    slots = wide // tiles
    spacing = pixels / 8.0

    put_together(layout, band, epoch, ins[: 2 * epochs], half, other, shared, amps)

    def row(k, c):
        r = k * COMPS + c
        return r // HALF, r % HALF

    if later:
        moved, moved_amps = refs[11:]
        put_together(layout, band, epoch, ins[2 * epochs :], half, other, moved, moved_amps)
        for k in range(4):
            shift = 0.0
            if k < 2:
                shift = functools.reduce(lambda a, b: a + b, [moved[row(k, c)] for c in range(COMPS)])
                shift = shift * (spacing * spacing * POSITION_RATE)
            for c in range(COMPS):
                shared[row(k, c)] = shared[row(k, c)] - STEP * (moved[row(k, c)] + shift)
        for c in range(COMPS):
            amps[c] = amps[c] - STEP * moved_amps[c]

    psf = psf_ref[0, 0]
    line_of = lax.broadcasted_iota(jnp.int32, (wide, 128), 0)
    live = jnp.zeros((wide, 128), jnp.bool_)
    for t in range(tiles):
        live = live | ((line_of >= t * slots) & (line_of < t * slots + counts_ref[t]))
    for c in range(COMPS):
        lw, an = shared[row(2, c)], shared[row(3, c)]
        derived[0, c] = shared[row(0, c)]
        derived[1, c] = shared[row(1, c)]
        derived[2, c] = (-0.5 * LOG2E) / (jnp.exp(2.0 * (lw + an)) + psf * psf)
        derived[3, c] = (-0.5 * LOG2E) / (jnp.exp(2.0 * (lw - an)) + psf * psf)
        derived[4, c] = jnp.where(live, amps[c], 0.0)
    sums[...] = jnp.zeros_like(sums)

    grid = lax.broadcasted_iota(jnp.int32, (pixels, 128), 0).astype(F32)

    def cut(x):
        hi = x.astype(BF16)
        return jnp.concatenate([hi, (x - hi.astype(F32)).astype(BF16)], axis=0)

    def stack(x):
        both = cut(x)
        return jnp.concatenate([both, both], axis=1)

    def total(x):
        return jnp.sum(x, axis=0, keepdims=True)

    def line(index, c, s):
        return derived[index, c, pl.ds(s, 1), :]

    together = 2
    for t in range(tiles):
        trips = (counts_ref[t] + together - 1) // together
        image[...] = jnp.zeros_like(image)

        def render(i, carry):
            for u in range(together):
                s = i * together + u
                g = t * slots + s
                off_x = offsets_ref[t, 0, s].astype(F32)
                off_y = offsets_ref[t, 1, s].astype(F32)
                for c in range(COMPS):
                    d = grid - (line(0, c, g) + off_x)
                    e = jnp.exp2(d * d * line(2, c, g))
                    prof_x[s * COMPS + c] = e
                    pieces_x[s, :, c * 128 : (c + 1) * 128] = cut(e)
                    d = grid - (line(1, c, g) + off_y)
                    e = jnp.exp2(d * d * line(3, c, g))
                    prof_y[s * COMPS + c] = e
                    pieces_y[s, :, c * 128 : (c + 1) * 128] = cut(e * line(4, c, g))
                image[...] += lax.dot_general(
                    pieces_x[s], pieces_y[s], (((1,), (1,)), ((), ())), preferred_element_type=F32
                )
            return carry

        lax.fori_loop(0, trips, render, 0)

        model = (image[:pixels, :pixels] + image[pixels:, pixels:]) + (
            image[:pixels, pixels:] + image[pixels:, :pixels]
        )
        cotangent = weight_ref[t, 0, 0] * (model - data_ref[t, 0, 0])
        left_x, left_y = stack(cotangent), stack(cotangent.T)

        def pull(i, carry):
            for u in range(together):
                s = i * together + u
                g = t * slots + s
                off_x = offsets_ref[t, 0, s].astype(F32)
                off_y = offsets_ref[t, 1, s].astype(F32)
                for first in range(0, COMPS, 2):
                    here = min(2, COMPS - first)
                    span = pl.ds(first * 128, 128 * here)
                    by_x = jnp.dot(left_x, pieces_y[s, :, span], preferred_element_type=F32)
                    by_y = jnp.dot(left_y, pieces_x[s, :, span], preferred_element_type=F32)
                    by_x = by_x[:pixels] + by_x[pixels:]
                    by_y = by_y[:pixels] + by_y[pixels:]
                    for n in range(here):
                        c = first + n
                        d = grid - (line(0, c, g) + off_x)
                        e = prof_x[s * COMPS + c] * by_x[:, n * 128 : (n + 1) * 128]
                        e1 = e * d
                        sums[0, c, pl.ds(g, 1), :] = total(e1)
                        sums[1, c, pl.ds(g, 1), :] = total(e1 * d)
                        d = grid - (line(1, c, g) + off_y)
                        e = prof_y[s * COMPS + c] * by_y[:, n * 128 : (n + 1) * 128]
                        e1 = e * d
                        sums[2, c, pl.ds(g, 1), :] = total(e1)
                        sums[3, c, pl.ds(g, 1), :] = total(e1 * d)
                        sums[4, c, pl.ds(g, 1), :] = total(e)
            return carry

        lax.fori_loop(0, trips, pull, 0)

    def keep(x):
        return jnp.where(live, x, 0.0)

    for c in range(COMPS):
        lw, an = shared[row(2, c)], shared[row(3, c)]
        wide_x, wide_y = jnp.exp(2.0 * (lw + an)), jnp.exp(2.0 * (lw - an))
        inv_x, inv_y = 1.0 / (wide_x + psf * psf), 1.0 / (wide_y + psf * psf)
        amp = amps[c]
        var_x = keep(sums[1, c] * inv_x * inv_x * wide_x)
        var_y = keep(amp * sums[3, c] * inv_y * inv_y * wide_y)
        shared[row(0, c)] = keep(sums[0, c] * inv_x)
        shared[row(1, c)] = keep(amp * sums[2, c] * inv_y)
        shared[row(2, c)] = var_x + var_y
        shared[row(3, c)] = var_x - var_y
        amps[c] = keep(sums[4, c])
    none = jnp.zeros((wide, 128), F32)
    for q, piece in enumerate(pieces):
        for p, entry in enumerate(piece):
            is_shared = entry is not None and entry[0] == "s"
            if is_shared:
                half[q, p] = shared[band, entry[1]]
            else:
                half[q, p] = none if entry is None else amps[entry[1]]
            if p < shared_rows:
                other[q, p] = shared[1 - band, entry[1]] if is_shared else none
    for k in range(epochs):
        outs[k][...] = half[lax.rem(epoch + k, epochs)]
        outs[epochs + k][...] = other[lax.rem(epoch + k, epochs)]


def step_gradient(layout, counts, offsets, psf, data, weight, slot_rows, moved):
    shared_rows, rows, pieces = layout
    epochs = len(pieces)
    later = moved is not None
    tiles, _, slots = offsets.shape
    pixels = data.shape[-1]
    wide = tiles * slots
    shapes = [(rows, wide, 128)] * epochs + [(shared_rows, wide, 128)] * epochs
    ins = slot_rows + (moved or [])
    together = [pltpu.VMEM((BANDS, HALF, wide, 128), F32), pltpu.VMEM((COMPS, wide, 128), F32)]
    return pl.pallas_call(
        functools.partial(step_kernel, layout, later),
        out_shape=[f32(*s) for s in shapes],
        in_specs=[smem()] * 3 + [vmem()] * (2 + len(ins)),
        out_specs=[vmem()] * len(shapes),
        scratch_shapes=together
        + [
            pltpu.VMEM((5, COMPS, wide, 128), F32),
            pltpu.VMEM((slots * COMPS, pixels, 128), F32),
            pltpu.VMEM((slots * COMPS, pixels, 128), F32),
            pltpu.VMEM((slots, 2 * pixels, COMPS * 128), BF16),
            pltpu.VMEM((slots, 2 * pixels, COMPS * 128), BF16),
            pltpu.VMEM((2 * pixels, 2 * pixels), F32),
            pltpu.VMEM((5, COMPS, wide, 128), F32),
            pltpu.VMEM((epochs, rows, wide, 128), F32),
            pltpu.VMEM((epochs, shared_rows, wide, 128), F32),
        ]
        + (together if later else []),
        compiler_params=params(32),
        name="later_step" if later else "first_step",
    )(counts, offsets, psf, data, weight, *ins)


def combine_kernel(layout, match_ref, *refs):
    shared_rows, rows, pieces = layout
    got, (out_ref, short_ref, own_ref) = refs[:-3], refs[-3:]
    wide = out_ref.shape[1]
    match = match_ref[...]
    for p in range(rows):
        both = pick(match, jnp.concatenate([ref[p] for ref in got], axis=0))
        out_ref[p] = both[:wide]
        if p < shared_rows:
            short_ref[p] = both[:wide]
        own_ref[p] = both[wide:]


def dense_kernel(rows, lists_ref, grads, *outs):
    tiles, slots = lists_ref.shape
    owners, blocks = len(outs), outs[0].shape[1]
    shape = (owners * blocks, tiles * slots)
    line = lax.broadcasted_iota(jnp.int32, shape, 0)
    lane = lax.broadcasted_iota(jnp.int32, shape, 1)
    me = lax.axis_index("tile")
    target = lax.rem(me + line // blocks, owners) * blocks + line % blocks
    ids = jnp.zeros(shape, jnp.int32)
    for t in range(tiles):
        for s in range(slots):
            ids = jnp.where(lane == t * slots + s, lists_ref[t, s], ids)
    match = (ids == target).astype(F32)
    for p in range(rows):
        dense = pick(match, grads[p])
        for k, out in enumerate(outs):
            out[p] = dense[k * blocks : (k + 1) * blocks]


def final_kernel(layout, spacing, params_ref, *refs):
    shared_rows, rows, pieces = layout
    epochs = len(pieces)
    ins, (out_ref, held) = refs[: 2 * epochs], refs[2 * epochs :]
    band, epoch = lax.axis_index("band"), lax.axis_index("epoch")
    for k in range(epochs):
        q = lax.rem(epoch - k + epochs, epochs)
        held[band, q] = ins[k][...]
        held[1 - band, q] = ins[epochs + k][...]
    shift = [0.0, 0.0]
    for b in range(BANDS):
        for q, piece in enumerate(pieces):
            for p, entry in enumerate(piece):
                if entry is None:
                    continue
                row, position = row_of(b, entry)
                grad = held[b, q, p]
                out_ref[row] = params_ref[row] - STEP * grad
                if position is not None:
                    shift[position] = shift[position] + grad
    for k in range(2):
        out_ref[k] = params_ref[k] - (STEP * POSITION_RATE * spacing) * shift[k]


def shards(source_params, pixel_data, pixel_weight, psf_width, block_lists, block_counts, block_offsets):
    owners, epochs = lax.axis_size("tile"), lax.axis_size("epoch")
    blocks, param_rows, sources = source_params.shape
    tiles, slots = block_lists.shape
    wide = tiles * slots
    spacing = pixel_data.shape[-1] / 8.0
    layout = quarter_layout(epochs)
    shared_rows, rows, pieces = layout

    def to_peers(same, other):
        kept = [same[0]]
        for k in range(1, epochs):
            kept.append(lax.ppermute(same[k], "epoch", [(i, (i + k) % epochs) for i in range(epochs)]))
        for k in range(epochs):
            pairs = [
                (i * BANDS + b, (i + k) % epochs * BANDS + 1 - b)
                for i in range(epochs)
                for b in range(BANDS)
            ]
            kept.append(lax.ppermute(other[k], ("epoch", "band"), pairs))
        return kept

    def round_tiles(arrays):
        return [arrays[0]] + [
            lax.ppermute(arrays[k], "tile", [(i, (i + k) % owners) for i in range(owners)])
            for k in range(1, owners)
        ]

    def spread(piece, other):
        return to_peers([piece] * epochs, [other] * epochs)

    def summed(parts):
        near = functools.reduce(lambda a, b: a + b, parts[:epochs])
        far = functools.reduce(lambda a, b: a + b, parts[epochs:])
        return near + jnp.pad(far, ((0, rows - shared_rows), (0, 0), (0, 0)))

    by_row = jnp.transpose(source_params, (1, 0, 2))
    offsets = jnp.transpose(block_offsets, (0, 2, 1))
    packed = pl.pallas_call(
        functools.partial(pack_kernel, layout, spacing),
        out_shape=f32(rows + 1, blocks, sources),
        in_specs=[smem(), vmem()],
        out_specs=vmem(),
        compiler_params=params(),
        name="pack",
    )(block_lists, by_row)
    got = round_tiles([packed] * owners)
    slot_piece, slot_short, match = pl.pallas_call(
        functools.partial(select_kernel, layout),
        out_shape=[
            f32(rows, wide, sources),
            f32(shared_rows, wide, sources),
            f32(wide + blocks, owners * wide),
        ],
        in_specs=[smem()] + [vmem()] * owners,
        out_specs=[vmem()] * 3,
        compiler_params=params(),
        name="select",
    )(block_lists, *got)
    slot_rows = spread(slot_piece, slot_short)

    def gradient(moved):
        parts = step_gradient(
            layout, block_counts, offsets, psf_width, pixel_data, pixel_weight, slot_rows, moved
        )
        return summed(to_peers(parts[:epochs], parts[epochs:]))

    got = round_tiles([gradient(None)] * owners)
    slot_piece, slot_short, own_first = pl.pallas_call(
        functools.partial(combine_kernel, layout),
        out_shape=[
            f32(rows, wide, sources),
            f32(shared_rows, wide, sources),
            f32(rows, blocks, sources),
        ],
        in_specs=[vmem()] * (1 + owners),
        out_specs=[vmem()] * 3,
        compiler_params=params(),
        name="combine",
    )(match, *got)

    dense = pl.pallas_call(
        functools.partial(dense_kernel, rows),
        out_shape=[f32(rows, blocks, sources)] * owners,
        in_specs=[smem(), vmem()],
        out_specs=[vmem()] * owners,
        compiler_params=params(),
        name="dense",
    )(block_lists, gradient(spread(slot_piece, slot_short)))
    own = functools.reduce(lambda a, b: a + b, round_tiles(dense), own_first)
    whole = pl.pallas_call(
        functools.partial(final_kernel, layout, spacing),
        out_shape=f32(param_rows, blocks, sources),
        in_specs=[vmem()] * (1 + 2 * epochs),
        out_specs=vmem(),
        scratch_shapes=[pltpu.VMEM((BANDS, epochs, rows, blocks, sources), F32)],
        compiler_params=params(),
        name="final",
    )(by_row, *spread(own, own))
    return jnp.transpose(whole, (1, 0, 2))


def solution(mesh):
    return jax.shard_map(
        shards,
        mesh=mesh,
        in_specs=(
            P(("region", "tile"), None, None),
            P(("region", "tile"), "epoch", "band", None, None),
            P(("region", "tile"), "epoch", "band", None, None),
            P(("region", "epoch"), "band"),
            P(("region", "tile"), None),
            P(("region", "tile")),
            P(("region", "tile"), None, None),
        ),
        out_specs=P(("region", "tile"), None, None),
        check_vma=False,
    )
```

time: 112 us -> 89.4 us (0.80)
  Pallas kernels: 43.3 us -> 19 us
  waiting for transfers between devices: 25.6 us -> 32.2 us
  local copies, waits for them, and re-layouts: 8.13 us -> 1.63 us
  starting transfers between devices: 32.4 us -> 35.6 us
  other arithmetic: 1.29 us -> 0.07 us
    pallas_call x8 -> x5, Pallas kernels: 39.7 us -> 17.4 us  [the longest x2 15.7 us: step_gradient(): pl.pallas_call(functools.partial(step_kernel, layout, later), out_shape=[...]
    ppermute x12 -> x9, starting transfers between devices: 17.4 us -> 24.6 us  [round_tiles(): lax.ppermute(arrays[k], 'tile', [(i, (i + k) % owners) for i in range(own...]
    ppermute x14 -> x10, waiting for transfers between devices: 9.33 us -> 14.1 us  [to_peers(): kept.append(lax.ppermute(other[k], ('epoch', 'band'), pairs))]
    unnamed x59 -> x14, local copies, waits for them, and re-layouts: 5.76 us -> 1.63 us
    ppermute x12 -> x9, waiting for transfers between devices: 13.4 us -> 16.4 us  [round_tiles(): lax.ppermute(arrays[k], 'tile', [(i, (i + k) % owners) for i in range(own...]
    slice x3 -> x0, local copies, waits for them, and re-layouts: 2.37 us -> none  [the longest x2 1.75 us: spread(): return to_peers([piece] * epochs, [piece[:other_rows]] * epochs)]
    ppermute x7 -> x5, starting transfers between devices: 7.7 us -> 5.42 us  [to_peers(): lax.ppermute(same[k], 'epoch', [(i, (i + k) % epochs) for i in range(epoc...]
    ppermute x14 -> x10, starting transfers between devices: 7.28 us -> 5.54 us  [to_peers(): kept.append(lax.ppermute(other[k], ('epoch', 'band'), pairs))]
  transfers between devices with their start and end apart: 33 -> 24, of which waited for: 15 -> 15; matrix products, arithmetic and copies ran while one was open for 3% -> 0% of each run, Pallas kernels for 16% -> 0%
where the time goes in v2:
time: 89.4 us; the launch traced here: 89.2 us
  starting transfers between devices  35.6 us (40%)
  waiting for transfers between devices  32.2 us (36%)
  Pallas kernels  19 us (21%)
  local copies, waits for them, and re-layouts  1.63 us (2%)
    ppermute x9, starting transfers between devices, round_tiles(): lax.ppermute(arrays[k], 'tile', [(i, (i + k) % owners) for i in range(own...  24.6 us
    ppermute x9, waiting for transfers between devices, round_tiles(): lax.ppermute(arrays[k], 'tile', [(i, (i + k) % owners) for i in range(own...  16.4 us
    pallas_call x2, Pallas kernels, step_gradient(): pl.pallas_call(functools.partial(step_kernel, layout, later), out_shape=[...  15.7 us
    ppermute x10, waiting for transfers between devices, to_peers(): kept.append(lax.ppermute(other[k], ('epoch', 'band'), pairs))  14.1 us
    ppermute x10, starting transfers between devices, to_peers(): kept.append(lax.ppermute(other[k], ('epoch', 'band'), pairs))  5.54 us
    ppermute x5, starting transfers between devices, to_peers(): lax.ppermute(same[k], 'epoch', [(i, (i + k) % epochs) for i in range(epoc...  5.42 us
  transfers between devices with their start and end apart: 24, of which 15 were waited for; matrix products, arithmetic and copies ran while one was open for 0% of the time, Pallas kernels for 0%

profile of v2, /device:TPU:0, one launch (start us, length us, event | category | flops | bytes accessed | tf_op | source)
XLA Modules:
  0.0 89.2 jit_solution(10184920614919834830)
XLA Ops:
  2.2 5.1 %collective-permute-start.2 = (f32[12,8,128]{2,1,0:T(8,128)S(1)}, f32[12,8,128]{2,1,0:T(8,128)S(1)}, u32[]{:S(2)}, u32[]{:S(2)}) collective-permute-start(f32[12,8,128]{2,1,0:T(8,128)S(1)} %pack.1.refs_0_), channel_id=1, source_target_pairs={{0,12},{4,0},{8,4},{12,8},{1,13},{5,1},{9,5},{13,9},{2,14},{6,2},{... | collective-permute-start | bytes 147464 | tf_op jit(solution)/shard_map/ppermute | solution.py:423
  7.3 1.0 %collective-permute-start = (f32[12,8,128]{2,1,0:T(8,128)S(1)}, f32[12,8,128]{2,1,0:T(8,128)S(1)}, u32[]{:S(2)}, u32[]{:S(2)}) collective-permute-start(f32[12,8,128]{2,1,0:T(8,128)S(1)} %pack.1.refs_0_), channel_id=1, source_target_pairs={{0,4},{4,8},{8,12},{12,0},{1,5},{5,9},{9,13},{13,1},{2,6},{6,10},{... | collective-permute-start | bytes 147464 | tf_op jit(solution)/shard_map/ppermute | solution.py:423
  8.3 1.0 %collective-permute-done.2.refs_3_ = f32[12,8,128]{2,1,0:T(8,128)S(1)} collective-permute-done((f32[12,8,128]{2,1,0:T(8,128)S(1)}, f32[12,8,128]{2,1,0:T(8,128)S(1)}, u32[]{:S(2)}, u32[]{:S(2)}) %collective-permute-start.2) | collective-permute-done | bytes 49184 | tf_op jit(solution)/shard_map/ppermute | solution.py:423
  9.4 2.9 %collective-permute-done.1.refs_2_ = f32[12,8,128]{2,1,0:T(8,128)S(1)} collective-permute-done((f32[12,8,128]{2,1,0:T(8,128)S(1)}, f32[12,8,128]{2,1,0:T(8,128)S(1)}, u32[]{:S(2)}, u32[]{:S(2)}) %collective-permute-start.1) | collective-permute-done | bytes 49184 | tf_op jit(solution)/shard_map/ppermute | solution.py:423
  14.0 1.5 %collective-permute-start.3 = (f32[11,16,128]{2,1,0:T(8,128)S(1)}, f32[11,16,128]{2,1,0:T(8,128)S(1)}, u32[]{:S(2)}, u32[]{:S(2)}) collective-permute-start(f32[11,16,128]{2,1,0:T(8,128)S(1)} %get-tuple-element.24.refs_0_), channel_id=1, source_target_pairs={{0,2},{2,0},{1,3},{3,1},{4,6},{6,4},{5,7},{7,5},{8,10},{10,8},{9,1... | collective-permute-start | bytes 270344 | tf_op jit(solution)/shard_map/ppermute | solution.py:411
  16.9 2.9 %collective-permute-done.5.refs_3_ = f32[7,16,128]{2,1,0:T(8,128)S(1)} collective-permute-done((f32[7,16,128]{2,1,0:T(8,128)S(1)}, f32[7,16,128]{2,1,0:T(8,128)S(1)}, u32[]{:S(2)}, u32[]{:S(2)}) %collective-permute-start.5) | collective-permute-done | bytes 57376 | tf_op jit(solution)/shard_map/ppermute | solution.py:418
  19.8 7.8 %first_step.1 = (f32[11,16,128]{2,1,0:T(8,128)S(1)}, f32[11,16,128]{2,1,0:T(8,128)S(1)}, f32[7,16,128]{2,1,0:T(8,128)S(1)}, f32[7,16,128]{2,1,0:T(8,128)S(1)}) custom-call(s32[2]{0:T(128)S(1)} %copy-done.6, s32[2,2,8]{2,1,0:T(2,128)S(1)} %bitcast.5, f32[1,1]{1,0:T(1,128)S(6)} %copy.8.psf_ref, f32[2,1,1,128,128]{4,3,2,1,0:T(8,128)S(1)} %copy-done.2, ...), custom_call_target="tpu_custom_call" | custom-call | tf_op jit(solution)/shard_map/first_step/pallas_call | solution.py:320
  28.7 1.1 %collective-permute-start.8 = (f32[7,16,128]{2,1,0:T(8,128)S(1)}, f32[7,16,128]{2,1,0:T(8,128)S(1)}, u32[]{:S(2)}, u32[]{:S(2)}) collective-permute-start(f32[7,16,128]{2,1,0:T(8,128)S(1)} %get-tuple-element.29), channel_id=1, source_target_pairs={{0,3},{1,2},{2,1},{3,0},{4,7},{5,6},{6,5},{7,4},{8,11},{9,10},{10,... | collective-permute-start | bytes 172040 | tf_op jit(solution)/shard_map/ppermute | solution.py:418
  29.8 3.0 %collective-permute-done.8 = f32[7,16,128]{2,1,0:T(8,128)S(1)} collective-permute-done((f32[7,16,128]{2,1,0:T(8,128)S(1)}, f32[7,16,128]{2,1,0:T(8,128)S(1)}, u32[]{:S(2)}, u32[]{:S(2)}) %collective-permute-start.8) | collective-permute-done | bytes 57376 | tf_op jit(solution)/shard_map/ppermute | solution.py:418
  32.9 8.0 %collective-permute-start.11 = (f32[11,16,128]{2,1,0:T(8,128)S(1)}, f32[11,16,128]{2,1,0:T(8,128)S(1)}, u32[]{:S(2)}, u32[]{:S(2)}) collective-permute-start(f32[11,16,128]{2,1,0:T(8,128)S(1)} %pad_add_fusion.1.refs_0_), channel_id=1, source_target_pairs={{0,12},{4,0},{8,4},{12,8},{1,13},{5,1},{9,5},{13,9},{2,14},{6,2},{... | collective-permute-start | bytes 270344 | tf_op jit(solution)/shard_map/ppermute | solution.py:423
  41.6 2.3 %collective-permute-done.11.refs_3_ = f32[11,16,128]{2,1,0:T(8,128)S(1)} collective-permute-done((f32[11,16,128]{2,1,0:T(8,128)S(1)}, f32[11,16,128]{2,1,0:T(8,128)S(1)}, u32[]{:S(2)}, u32[]{:S(2)}) %collective-permute-start.11) | collective-permute-done | bytes 90144 | tf_op jit(solution)/shard_map/ppermute | solution.py:423
  44.0 6.1 %collective-permute-done.10.refs_2_ = f32[11,16,128]{2,1,0:T(8,128)S(1)} collective-permute-done((f32[11,16,128]{2,1,0:T(8,128)S(1)}, f32[11,16,128]{2,1,0:T(8,128)S(1)}, u32[]{:S(2)}, u32[]{:S(2)}) %collective-permute-start.10) | collective-permute-done | bytes 90144 | tf_op jit(solution)/shard_map/ppermute | solution.py:423
  50.4 1.2 %collective-permute-start.12 = (f32[11,16,128]{2,1,0:T(8,128)S(1)}, f32[11,16,128]{2,1,0:T(8,128)S(1)}, u32[]{:S(2)}, u32[]{:S(2)}) collective-permute-start(f32[11,16,128]{2,1,0:T(8,128)S(1)} %get-tuple-element.31.refs_4_), channel_id=1, source_target_pairs={{0,2},{2,0},{1,3},{3,1},{4,6},{6,4},{5,7},{7,5},{8,10},{10,8},{9,1... | collective-permute-start | bytes 270344 | tf_op jit(solution)/shard_map/ppermute | solution.py:411
  52.5 3.2 %collective-permute-done.14.refs_7_ = f32[7,16,128]{2,1,0:T(8,128)S(1)} collective-permute-done((f32[7,16,128]{2,1,0:T(8,128)S(1)}, f32[7,16,128]{2,1,0:T(8,128)S(1)}, u32[]{:S(2)}, u32[]{:S(2)}) %collective-permute-start.14) | collective-permute-done | bytes 57376 | tf_op jit(solution)/shard_map/ppermute | solution.py:418
  55.8 7.9 %later_step.1 = (f32[11,16,128]{2,1,0:T(8,128)S(1)}, f32[11,16,128]{2,1,0:T(8,128)S(1)}, f32[7,16,128]{2,1,0:T(8,128)S(1)}, f32[7,16,128]{2,1,0:T(8,128)S(1)}) custom-call(s32[2]{0:T(128)S(1)} %copy-done.6, s32[2,2,8]{2,1,0:T(2,128)S(1)} %bitcast.6, f32[1,1]{1,0:T(1,128)S(6)} %copy.8.psf_ref, f32[2,1,1,128,128]{4,3,2,1,0:T(8,128)S(1)} %copy-done.2, ...), custom_call_target="tpu_custom_call" | custom-call | tf_op jit(solution)/shard_map/later_step/pallas_call | solution.py:320
  63.7 1.1 %collective-permute-start.15 = (f32[11,16,128]{2,1,0:T(8,128)S(1)}, f32[11,16,128]{2,1,0:T(8,128)S(1)}, u32[]{:S(2)}, u32[]{:S(2)}) collective-permute-start(f32[11,16,128]{2,1,0:T(8,128)S(1)} %get-tuple-element.34), channel_id=1, source_target_pairs={{0,2},{2,0},{1,3},{3,1},{4,6},{6,4},{5,7},{7,5},{8,10},{10,8},{9,1... | collective-permute-start | bytes 270344 | tf_op jit(solution)/shard_map/ppermute | solution.py:411
  66.0 3.1 %collective-permute-done.17 = f32[7,16,128]{2,1,0:T(8,128)S(1)} collective-permute-done((f32[7,16,128]{2,1,0:T(8,128)S(1)}, f32[7,16,128]{2,1,0:T(8,128)S(1)}, u32[]{:S(2)}, u32[]{:S(2)}) %collective-permute-start.17) | collective-permute-done | bytes 57376 | tf_op jit(solution)/shard_map/ppermute | solution.py:418
  69.9 6.7 %collective-permute-start.18 = (f32[11,8,128]{2,1,0:T(8,128)S(1)}, f32[11,8,128]{2,1,0:T(8,128)S(1)}, u32[]{:S(2)}, u32[]{:S(2)}) collective-permute-start(f32[11,8,128]{2,1,0:T(8,128)S(1)} %get-tuple-element.38), channel_id=1, source_target_pairs={{0,4},{4,8},{8,12},{12,0},{1,5},{5,9},{9,13},{13,1},{2,6},{6,10},{... | collective-permute-start | bytes 135176 | tf_op jit(solution)/shard_map/ppermute | solution.py:423
  76.6 2.0 %collective-permute-start.19 = (f32[11,8,128]{2,1,0:T(8,128)S(1)}, f32[11,8,128]{2,1,0:T(8,128)S(1)}, u32[]{:S(2)}, u32[]{:S(2)}) collective-permute-start(f32[11,8,128]{2,1,0:T(8,128)S(1)} %get-tuple-element.39), channel_id=1, source_target_pairs={{0,8},{4,12},{8,0},{12,4},{1,9},{5,13},{9,1},{13,5},{2,10},{6,14},... | collective-permute-start | bytes 135176 | tf_op jit(solution)/shard_map/ppermute | solution.py:423
  78.7 1.1 %collective-permute-start.20 = (f32[11,8,128]{2,1,0:T(8,128)S(1)}, f32[11,8,128]{2,1,0:T(8,128)S(1)}, u32[]{:S(2)}, u32[]{:S(2)}) collective-permute-start(f32[11,8,128]{2,1,0:T(8,128)S(1)} %get-tuple-element.40), channel_id=1, source_target_pairs={{0,12},{4,0},{8,4},{12,8},{1,13},{5,1},{9,5},{13,9},{2,14},{6,2},{... | collective-permute-start | bytes 135176 | tf_op jit(solution)/shard_map/ppermute | solution.py:423
  80.4 2.2 %collective-permute-done.19 = f32[11,8,128]{2,1,0:T(8,128)S(1)} collective-permute-done((f32[11,8,128]{2,1,0:T(8,128)S(1)}, f32[11,8,128]{2,1,0:T(8,128)S(1)}, u32[]{:S(2)}, u32[]{:S(2)}) %collective-permute-start.19) | collective-permute-done | bytes 45088 | tf_op jit(solution)/shard_map/ppermute | solution.py:423
  83.2 1.3 %collective-permute-start.22 = (f32[11,8,128]{2,1,0:T(8,128)S(1)}, f32[11,8,128]{2,1,0:T(8,128)S(1)}, u32[]{:S(2)}, u32[]{:S(2)}) collective-permute-start(f32[11,8,128]{2,1,0:T(8,128)S(1)} %add_add_fusion.refs_0_), channel_id=1, source_target_pairs={{0,1},{1,0},{2,3},{3,2},{4,5},{5,4},{6,7},{7,6},{8,9},{9,8},{10,11... | collective-permute-start | bytes 135176 | tf_op jit(solution)/shard_map/ppermute | solution.py:418
  85.1 1.7 %collective-permute-done.23.refs_3_ = f32[11,8,128]{2,1,0:T(8,128)S(1)} collective-permute-done((f32[11,8,128]{2,1,0:T(8,128)S(1)}, f32[11,8,128]{2,1,0:T(8,128)S(1)}, u32[]{:S(2)}, u32[]{:S(2)}) %collective-permute-start.23) | collective-permute-done | bytes 45088 | tf_op jit(solution)/shard_map/ppermute | solution.py:418
  86.8 1.6 %collective-permute-done.21.refs_1_ = f32[11,8,128]{2,1,0:T(8,128)S(1)} collective-permute-done((f32[11,8,128]{2,1,0:T(8,128)S(1)}, f32[11,8,128]{2,1,0:T(8,128)S(1)}, u32[]{:S(2)}, u32[]{:S(2)}) %collective-permute-start.21) | collective-permute-done | bytes 45088 | tf_op jit(solution)/shard_map/ppermute | solution.py:411
  (50 shorter events, 12.4 us)
Async XLA Ops:
  2.2 7.2 %collective-permute-start.2 = (f32[12,8,128]{2,1,0:T(8,128)S(1)}, f32[12,8,128]{2,1,0:T(8,128)S(1)}, u32[]{:S(2)}, u32[]{:S(2)}) collective-permute-start(f32[12,8,128]{2,1,0:T(8,128)S(1)} %pack.1.refs_0_), channel_id=1, source_target_pairs={{0,12},{4,0},{8,4},{12,8},{1,13},{5,1},{9,5},{13,9},{2,14},{6,2},{... | collective-permute-start | bytes 147464 | tf_op jit(solution)/shard_map/ppermute | solution.py:423
  7.3 5.0 %collective-permute-start.1 = (f32[12,8,128]{2,1,0:T(8,128)S(1)}, f32[12,8,128]{2,1,0:T(8,128)S(1)}, u32[]{:S(2)}, u32[]{:S(2)}) collective-permute-start(f32[12,8,128]{2,1,0:T(8,128)S(1)} %pack.1.refs_0_), channel_id=1, source_target_pairs={{0,8},{4,12},{8,0},{12,4},{1,9},{5,13},{9,1},{13,5},{2,10},{6,14},... | collective-permute-start | bytes 147464 | tf_op jit(solution)/shard_map/ppermute | solution.py:423
  7.3 5.9 %collective-permute-start = (f32[12,8,128]{2,1,0:T(8,128)S(1)}, f32[12,8,128]{2,1,0:T(8,128)S(1)}, u32[]{:S(2)}, u32[]{:S(2)}) collective-permute-start(f32[12,8,128]{2,1,0:T(8,128)S(1)} %pack.1.refs_0_), channel_id=1, source_target_pairs={{0,4},{4,8},{8,12},{12,0},{1,5},{5,9},{9,13},{13,1},{2,6},{6,10},{... | collective-permute-start | bytes 147464 | tf_op jit(solution)/shard_map/ppermute | solution.py:423
  14.0 5.8 %collective-permute-start.3 = (f32[11,16,128]{2,1,0:T(8,128)S(1)}, f32[11,16,128]{2,1,0:T(8,128)S(1)}, u32[]{:S(2)}, u32[]{:S(2)}) collective-permute-start(f32[11,16,128]{2,1,0:T(8,128)S(1)} %get-tuple-element.24.refs_0_), channel_id=1, source_target_pairs={{0,2},{2,0},{1,3},{3,1},{4,6},{6,4},{5,7},{7,5},{8,10},{10,8},{9,1... | collective-permute-start | bytes 270344 | tf_op jit(solution)/shard_map/ppermute | solution.py:411
  15.6 4.2 %collective-permute-start.5 = (f32[7,16,128]{2,1,0:T(8,128)S(1)}, f32[7,16,128]{2,1,0:T(8,128)S(1)}, u32[]{:S(2)}, u32[]{:S(2)}) collective-permute-start(f32[7,16,128]{2,1,0:T(8,128)S(1)} %get-tuple-element.25), channel_id=1, source_target_pairs={{0,3},{1,2},{2,1},{3,0},{4,7},{5,6},{6,5},{7,4},{8,11},{9,10},{10,... | collective-permute-start | bytes 172040 | tf_op jit(solution)/shard_map/ppermute | solution.py:418
  15.6 4.2 %collective-permute-start.4 = (f32[7,16,128]{2,1,0:T(8,128)S(1)}, f32[7,16,128]{2,1,0:T(8,128)S(1)}, u32[]{:S(2)}, u32[]{:S(2)}) collective-permute-start(f32[7,16,128]{2,1,0:T(8,128)S(1)} %get-tuple-element.25), channel_id=1, source_target_pairs={{0,1},{1,0},{2,3},{3,2},{4,5},{5,4},{6,7},{7,6},{8,9},{9,8},{10,11... | collective-permute-start | bytes 172040 | tf_op jit(solution)/shard_map/ppermute | solution.py:418
  27.6 5.3 %collective-permute-start.6 = (f32[11,16,128]{2,1,0:T(8,128)S(1)}, f32[11,16,128]{2,1,0:T(8,128)S(1)}, u32[]{:S(2)}, u32[]{:S(2)}) collective-permute-start(f32[11,16,128]{2,1,0:T(8,128)S(1)} %get-tuple-element.27), channel_id=1, source_target_pairs={{0,2},{2,0},{1,3},{3,1},{4,6},{6,4},{5,7},{7,5},{8,10},{10,8},{9,1... | collective-permute-start | bytes 270344 | tf_op jit(solution)/shard_map/ppermute | solution.py:411
  28.6 1.3 %collective-permute-start.7 = (f32[7,16,128]{2,1,0:T(8,128)S(1)}, f32[7,16,128]{2,1,0:T(8,128)S(1)}, u32[]{:S(2)}, u32[]{:S(2)}) collective-permute-start(f32[7,16,128]{2,1,0:T(8,128)S(1)} %get-tuple-element.28), channel_id=1, source_target_pairs={{0,1},{1,0},{2,3},{3,2},{4,5},{5,4},{6,7},{7,6},{8,9},{9,8},{10,11... | collective-permute-start | bytes 172040 | tf_op jit(solution)/shard_map/ppermute | solution.py:418
  28.7 4.1 %collective-permute-start.8 = (f32[7,16,128]{2,1,0:T(8,128)S(1)}, f32[7,16,128]{2,1,0:T(8,128)S(1)}, u32[]{:S(2)}, u32[]{:S(2)}) collective-permute-start(f32[7,16,128]{2,1,0:T(8,128)S(1)} %get-tuple-element.29), channel_id=1, source_target_pairs={{0,3},{1,2},{2,1},{3,0},{4,7},{5,6},{6,5},{7,4},{8,11},{9,10},{10,... | collective-permute-start | bytes 172040 | tf_op jit(solution)/shard_map/ppermute | solution.py:418
  32.9 11.0 %collective-permute-start.11 = (f32[11,16,128]{2,1,0:T(8,128)S(1)}, f32[11,16,128]{2,1,0:T(8,128)S(1)}, u32[]{:S(2)}, u32[]{:S(2)}) collective-permute-start(f32[11,16,128]{2,1,0:T(8,128)S(1)} %pad_add_fusion.1.refs_0_), channel_id=1, source_target_pairs={{0,12},{4,0},{8,4},{12,8},{1,13},{5,1},{9,5},{13,9},{2,14},{6,2},{... | collective-permute-start | bytes 270344 | tf_op jit(solution)/shard_map/ppermute | solution.py:423
  41.0 9.0 %collective-permute-start.10 = (f32[11,16,128]{2,1,0:T(8,128)S(1)}, f32[11,16,128]{2,1,0:T(8,128)S(1)}, u32[]{:S(2)}, u32[]{:S(2)}) collective-permute-start(f32[11,16,128]{2,1,0:T(8,128)S(1)} %pad_add_fusion.1.refs_0_), channel_id=1, source_target_pairs={{0,8},{4,12},{8,0},{12,4},{1,9},{5,13},{9,1},{13,5},{2,10},{6,14},... | collective-permute-start | bytes 270344 | tf_op jit(solution)/shard_map/ppermute | solution.py:423
  41.0 9.0 %collective-permute-start.9 = (f32[11,16,128]{2,1,0:T(8,128)S(1)}, f32[11,16,128]{2,1,0:T(8,128)S(1)}, u32[]{:S(2)}, u32[]{:S(2)}) collective-permute-start(f32[11,16,128]{2,1,0:T(8,128)S(1)} %pad_add_fusion.1.refs_0_), channel_id=1, source_target_pairs={{0,4},{4,8},{8,12},{12,0},{1,5},{5,9},{9,13},{13,1},{2,6},{6,10},{... | collective-permute-start | bytes 270344 | tf_op jit(solution)/shard_map/ppermute | solution.py:423
  50.4 5.4 %collective-permute-start.12 = (f32[11,16,128]{2,1,0:T(8,128)S(1)}, f32[11,16,128]{2,1,0:T(8,128)S(1)}, u32[]{:S(2)}, u32[]{:S(2)}) collective-permute-start(f32[11,16,128]{2,1,0:T(8,128)S(1)} %get-tuple-element.31.refs_4_), channel_id=1, source_target_pairs={{0,2},{2,0},{1,3},{3,1},{4,6},{6,4},{5,7},{7,5},{8,10},{10,8},{9,1... | collective-permute-start | bytes 270344 | tf_op jit(solution)/shard_map/ppermute | solution.py:411
  51.6 4.2 %collective-permute-start.14 = (f32[7,16,128]{2,1,0:T(8,128)S(1)}, f32[7,16,128]{2,1,0:T(8,128)S(1)}, u32[]{:S(2)}, u32[]{:S(2)}) collective-permute-start(f32[7,16,128]{2,1,0:T(8,128)S(1)} %get-tuple-element.32), channel_id=1, source_target_pairs={{0,3},{1,2},{2,1},{3,0},{4,7},{5,6},{6,5},{7,4},{8,11},{9,10},{10,... | collective-permute-start | bytes 172040 | tf_op jit(solution)/shard_map/ppermute | solution.py:418
  51.8 4.0 %collective-permute-start.13 = (f32[7,16,128]{2,1,0:T(8,128)S(1)}, f32[7,16,128]{2,1,0:T(8,128)S(1)}, u32[]{:S(2)}, u32[]{:S(2)}) collective-permute-start(f32[7,16,128]{2,1,0:T(8,128)S(1)} %get-tuple-element.32), channel_id=1, source_target_pairs={{0,1},{1,0},{2,3},{3,2},{4,5},{5,4},{6,7},{7,6},{8,9},{9,8},{10,11... | collective-permute-start | bytes 172040 | tf_op jit(solution)/shard_map/ppermute | solution.py:418
  63.7 5.4 %collective-permute-start.15 = (f32[11,16,128]{2,1,0:T(8,128)S(1)}, f32[11,16,128]{2,1,0:T(8,128)S(1)}, u32[]{:S(2)}, u32[]{:S(2)}) collective-permute-start(f32[11,16,128]{2,1,0:T(8,128)S(1)} %get-tuple-element.34), channel_id=1, source_target_pairs={{0,2},{2,0},{1,3},{3,1},{4,6},{6,4},{5,7},{7,5},{8,10},{10,8},{9,1... | collective-permute-start | bytes 270344 | tf_op jit(solution)/shard_map/ppermute | solution.py:411
  64.7 1.2 %collective-permute-start.16 = (f32[7,16,128]{2,1,0:T(8,128)S(1)}, f32[7,16,128]{2,1,0:T(8,128)S(1)}, u32[]{:S(2)}, u32[]{:S(2)}) collective-permute-start(f32[7,16,128]{2,1,0:T(8,128)S(1)} %get-tuple-element.35), channel_id=1, source_target_pairs={{0,1},{1,0},{2,3},{3,2},{4,5},{5,4},{6,7},{7,6},{8,9},{9,8},{10,11... | collective-permute-start | bytes 172040 | tf_op jit(solution)/shard_map/ppermute | solution.py:418
  64.9 4.2 %collective-permute-start.17 = (f32[7,16,128]{2,1,0:T(8,128)S(1)}, f32[7,16,128]{2,1,0:T(8,128)S(1)}, u32[]{:S(2)}, u32[]{:S(2)}) collective-permute-start(f32[7,16,128]{2,1,0:T(8,128)S(1)} %get-tuple-element.36), channel_id=1, source_target_pairs={{0,3},{1,2},{2,1},{3,0},{4,7},{5,6},{6,5},{7,4},{8,11},{9,10},{10,... | collective-permute-start | bytes 172040 | tf_op jit(solution)/shard_map/ppermute | solution.py:418
  69.9 10.4 %collective-permute-start.18 = (f32[11,8,128]{2,1,0:T(8,128)S(1)}, f32[11,8,128]{2,1,0:T(8,128)S(1)}, u32[]{:S(2)}, u32[]{:S(2)}) collective-permute-start(f32[11,8,128]{2,1,0:T(8,128)S(1)} %get-tuple-element.38), channel_id=1, source_target_pairs={{0,4},{4,8},{8,12},{12,0},{1,5},{5,9},{9,13},{13,1},{2,6},{6,10},{... | collective-permute-start | bytes 135176 | tf_op jit(solution)/shard_map/ppermute | solution.py:423
  76.6 5.9 %collective-permute-start.19 = (f32[11,8,128]{2,1,0:T(8,128)S(1)}, f32[11,8,128]{2,1,0:T(8,128)S(1)}, u32[]{:S(2)}, u32[]{:S(2)}) collective-permute-start(f32[11,8,128]{2,1,0:T(8,128)S(1)} %get-tuple-element.39), channel_id=1, source_target_pairs={{0,8},{4,12},{8,0},{12,4},{1,9},{5,13},{9,1},{13,5},{2,10},{6,14},... | collective-permute-start | bytes 135176 | tf_op jit(solution)/shard_map/ppermute | solution.py:423
  78.7 4.2 %collective-permute-start.20 = (f32[11,8,128]{2,1,0:T(8,128)S(1)}, f32[11,8,128]{2,1,0:T(8,128)S(1)}, u32[]{:S(2)}, u32[]{:S(2)}) collective-permute-start(f32[11,8,128]{2,1,0:T(8,128)S(1)} %get-tuple-element.40), channel_id=1, source_target_pairs={{0,12},{4,0},{8,4},{12,8},{1,13},{5,1},{9,5},{13,9},{2,14},{6,2},{... | collective-permute-start | bytes 135176 | tf_op jit(solution)/shard_map/ppermute | solution.py:423
  82.9 3.9 %collective-permute-start.23 = (f32[11,8,128]{2,1,0:T(8,128)S(1)}, f32[11,8,128]{2,1,0:T(8,128)S(1)}, u32[]{:S(2)}, u32[]{:S(2)}) collective-permute-start(f32[11,8,128]{2,1,0:T(8,128)S(1)} %add_add_fusion.refs_0_), channel_id=1, source_target_pairs={{0,3},{1,2},{2,1},{3,0},{4,7},{5,6},{6,5},{7,4},{8,11},{9,10},{10,... | collective-permute-start | bytes 135176 | tf_op jit(solution)/shard_map/ppermute | solution.py:418
  83.2 3.7 %collective-permute-start.22 = (f32[11,8,128]{2,1,0:T(8,128)S(1)}, f32[11,8,128]{2,1,0:T(8,128)S(1)}, u32[]{:S(2)}, u32[]{:S(2)}) collective-permute-start(f32[11,8,128]{2,1,0:T(8,128)S(1)} %add_add_fusion.refs_0_), channel_id=1, source_target_pairs={{0,1},{1,0},{2,3},{3,2},{4,5},{5,4},{6,7},{7,6},{8,9},{9,8},{10,11... | collective-permute-start | bytes 135176 | tf_op jit(solution)/shard_map/ppermute | solution.py:418
  84.4 4.0 %collective-permute-start.21 = (f32[11,8,128]{2,1,0:T(8,128)S(1)}, f32[11,8,128]{2,1,0:T(8,128)S(1)}, u32[]{:S(2)}, u32[]{:S(2)}) collective-permute-start(f32[11,8,128]{2,1,0:T(8,128)S(1)} %add_add_fusion.refs_0_), channel_id=1, source_target_pairs={{0,2},{2,0},{1,3},{3,1},{4,6},{6,4},{5,7},{7,5},{8,10},{10,8},{9,1... | collective-permute-start | bytes 135176 | tf_op jit(solution)/shard_map/ppermute | solution.py:411
  (7 other events, 63.9 us)

commit v3 on v2

--- a/solution.py
+++ b/solution.py
@@ -13,6 +13,7 @@
 POSITION_RATE = 1.0 / 64.0
 COMPS = 7
 BANDS = 2
+TOGETHER = 2
 SHARED = 4 * COMPS
 HALF = SHARED // BANDS
 LOG2E = math.log2(math.e)
@@ -100,10 +101,9 @@
 
 def select_kernel(layout, lists_ref, *refs):
     shared_rows, rows, pieces = layout
-    got, (out_ref, short_ref, match_ref) = refs[:-3], refs[-3:]
-    owners = len(got)
+    got_ref, out_ref, short_ref, match_ref = refs
+    owners, _, blocks, _ = got_ref.shape
     tiles, slots = lists_ref.shape
-    blocks = got[0].shape[1]
     wide = tiles * slots
     me = lax.axis_index("tile")
 
@@ -116,11 +116,9 @@
         return ids
 
     shape = (wide, owners * blocks)
-    lane = lax.broadcasted_iota(jnp.int32, shape, 1)
-    held = lax.rem(me - lane // blocks + owners, owners) * blocks + lane % blocks
-    choose = (slot_ids(shape) == held).astype(F32)
+    choose = (slot_ids(shape) == lax.broadcasted_iota(jnp.int32, shape, 1)).astype(F32)
     for p in range(rows):
-        chosen = pick(choose, jnp.concatenate([ref[p] for ref in got], axis=0))
+        chosen = pick(choose, jnp.concatenate([got_ref[k, p] for k in range(owners)], axis=0))
         out_ref[p] = chosen
         if p < shared_rows:
             short_ref[p] = chosen
@@ -128,7 +126,7 @@
     shape = (wide + blocks, owners * wide)
     line = lax.broadcasted_iota(jnp.int32, shape, 0)
     own = jnp.where(line < wide, slot_ids(shape), me * blocks + line - wide).astype(F32)
-    sent = jnp.concatenate([ref[rows, :1, :wide] for ref in got], axis=1)
+    sent = jnp.concatenate([got_ref[k, rows, :1, :wide] for k in range(owners)], axis=1)
     match_ref[...] = (own == sent).astype(F32)
 
 
@@ -205,8 +203,14 @@
         return jnp.concatenate([hi, (x - hi.astype(F32)).astype(BF16)], axis=0)
 
     def stack(x):
-        both = cut(x)
-        return jnp.concatenate([both, both], axis=1)
+        hi = x.astype(BF16)
+        lo = (x - hi.astype(F32)).astype(BF16)
+        turns = [part[r : r + 16] for r in range(0, pixels, 16) for part in (hi, lo)]
+        one = jnp.concatenate(turns, axis=0)
+        return jnp.concatenate([one, one], axis=1)
+
+    def join(x):
+        return jnp.concatenate([x[r : r + 16] + x[r + 16 : r + 32] for r in range(0, 2 * pixels, 32)], axis=0)
 
     def total(x):
         return jnp.sum(x, axis=0, keepdims=True)
@@ -214,29 +218,30 @@
     def line(index, c, s):
         return derived[index, c, pl.ds(s, 1), :]
 
-    together = 2
+    both = TOGETHER * COMPS
     for t in range(tiles):
-        trips = (counts_ref[t] + together - 1) // together
+        trips = (counts_ref[t] + TOGETHER - 1) // TOGETHER
         image[...] = jnp.zeros_like(image)
 
         def render(i, carry):
-            for u in range(together):
-                s = i * together + u
+            for u in range(TOGETHER):
+                s = i * TOGETHER + u
                 g = t * slots + s
                 off_x = offsets_ref[t, 0, s].astype(F32)
                 off_y = offsets_ref[t, 1, s].astype(F32)
                 for c in range(COMPS):
+                    n = u * COMPS + c
                     d = grid - (line(0, c, g) + off_x)
                     e = jnp.exp2(d * d * line(2, c, g))
-                    prof_x[s * COMPS + c] = e
-                    pieces_x[s, :, c * 128 : (c + 1) * 128] = cut(e)
+                    prof_x[i * both + n] = e
+                    pieces_x[i, :, n * 128 : (n + 1) * 128] = cut(e)
                     d = grid - (line(1, c, g) + off_y)
                     e = jnp.exp2(d * d * line(3, c, g))
-                    prof_y[s * COMPS + c] = e
-                    pieces_y[s, :, c * 128 : (c + 1) * 128] = cut(e * line(4, c, g))
-                image[...] += lax.dot_general(
-                    pieces_x[s], pieces_y[s], (((1,), (1,)), ((), ())), preferred_element_type=F32
-                )
+                    prof_y[i * both + n] = e
+                    pieces_y[i, :, n * 128 : (n + 1) * 128] = cut(e * line(4, c, g))
+            image[...] += lax.dot_general(
+                pieces_x[i], pieces_y[i], (((1,), (1,)), ((), ())), preferred_element_type=F32
+            )
             return carry
 
         lax.fori_loop(0, trips, render, 0)
@@ -248,31 +253,26 @@
         left_x, left_y = stack(cotangent), stack(cotangent.T)
 
         def pull(i, carry):
-            for u in range(together):
-                s = i * together + u
-                g = t * slots + s
-                off_x = offsets_ref[t, 0, s].astype(F32)
-                off_y = offsets_ref[t, 1, s].astype(F32)
-                for first in range(0, COMPS, 2):
-                    here = min(2, COMPS - first)
-                    span = pl.ds(first * 128, 128 * here)
-                    by_x = jnp.dot(left_x, pieces_y[s, :, span], preferred_element_type=F32)
-                    by_y = jnp.dot(left_y, pieces_x[s, :, span], preferred_element_type=F32)
-                    by_x = by_x[:pixels] + by_x[pixels:]
-                    by_y = by_y[:pixels] + by_y[pixels:]
-                    for n in range(here):
-                        c = first + n
-                        d = grid - (line(0, c, g) + off_x)
-                        e = prof_x[s * COMPS + c] * by_x[:, n * 128 : (n + 1) * 128]
-                        e1 = e * d
-                        sums[0, c, pl.ds(g, 1), :] = total(e1)
-                        sums[1, c, pl.ds(g, 1), :] = total(e1 * d)
-                        d = grid - (line(1, c, g) + off_y)
-                        e = prof_y[s * COMPS + c] * by_y[:, n * 128 : (n + 1) * 128]
-                        e1 = e * d
-                        sums[2, c, pl.ds(g, 1), :] = total(e1)
-                        sums[3, c, pl.ds(g, 1), :] = total(e1 * d)
-                        sums[4, c, pl.ds(g, 1), :] = total(e)
+            for first in range(0, both, 2):
+                span = pl.ds(first * 128, 256)
+                by_x = join(jnp.dot(left_x, pieces_y[i, :, span], preferred_element_type=F32))
+                by_y = join(jnp.dot(left_y, pieces_x[i, :, span], preferred_element_type=F32))
+                for n in (first, first + 1):
+                    u, c = divmod(n, COMPS)
+                    at = slice((n - first) * 128, (n - first + 1) * 128)
+                    s = i * TOGETHER + u
+                    g = t * slots + s
+                    d = grid - (line(0, c, g) + offsets_ref[t, 0, s].astype(F32))
+                    e = prof_x[i * both + n] * by_x[:, at]
+                    e1 = e * d
+                    sums[0, c, pl.ds(g, 1), :] = total(e1)
+                    sums[1, c, pl.ds(g, 1), :] = total(e1 * d)
+                    d = grid - (line(1, c, g) + offsets_ref[t, 1, s].astype(F32))
+                    e = prof_y[i * both + n] * by_y[:, at]
+                    e1 = e * d
+                    sums[2, c, pl.ds(g, 1), :] = total(e1)
+                    sums[3, c, pl.ds(g, 1), :] = total(e1 * d)
+                    sums[4, c, pl.ds(g, 1), :] = total(e)
             return carry
 
         lax.fori_loop(0, trips, pull, 0)
@@ -327,8 +327,8 @@
             pltpu.VMEM((5, COMPS, wide, 128), F32),
             pltpu.VMEM((slots * COMPS, pixels, 128), F32),
             pltpu.VMEM((slots * COMPS, pixels, 128), F32),
-            pltpu.VMEM((slots, 2 * pixels, COMPS * 128), BF16),
-            pltpu.VMEM((slots, 2 * pixels, COMPS * 128), BF16),
+            pltpu.VMEM((slots // TOGETHER, 2 * pixels, TOGETHER * COMPS * 128), BF16),
+            pltpu.VMEM((slots // TOGETHER, 2 * pixels, TOGETHER * COMPS * 128), BF16),
             pltpu.VMEM((2 * pixels, 2 * pixels), F32),
             pltpu.VMEM((5, COMPS, wide, 128), F32),
             pltpu.VMEM((epochs, rows, wide, 128), F32),
@@ -342,45 +342,37 @@
 
 def combine_kernel(layout, match_ref, *refs):
     shared_rows, rows, pieces = layout
-    got, (out_ref, short_ref, own_ref) = refs[:-3], refs[-3:]
+    got_ref, out_ref, short_ref, own_ref = refs
+    owners = got_ref.shape[0]
     wide = out_ref.shape[1]
     match = match_ref[...]
     for p in range(rows):
-        both = pick(match, jnp.concatenate([ref[p] for ref in got], axis=0))
+        both = pick(match, jnp.concatenate([got_ref[k, p] for k in range(owners)], axis=0))
         out_ref[p] = both[:wide]
         if p < shared_rows:
             short_ref[p] = both[:wide]
         own_ref[p] = both[wide:]
 
 
-def dense_kernel(rows, lists_ref, grads, *outs):
+def dense_kernel(rows, lists_ref, grads, out_ref):
     tiles, slots = lists_ref.shape
-    owners, blocks = len(outs), outs[0].shape[1]
+    owners, _, blocks, _ = out_ref.shape
     shape = (owners * blocks, tiles * slots)
     line = lax.broadcasted_iota(jnp.int32, shape, 0)
     lane = lax.broadcasted_iota(jnp.int32, shape, 1)
-    me = lax.axis_index("tile")
-    target = lax.rem(me + line // blocks, owners) * blocks + line % blocks
     ids = jnp.zeros(shape, jnp.int32)
     for t in range(tiles):
         for s in range(slots):
             ids = jnp.where(lane == t * slots + s, lists_ref[t, s], ids)
-    match = (ids == target).astype(F32)
+    match = (ids == line).astype(F32)
     for p in range(rows):
         dense = pick(match, grads[p])
-        for k, out in enumerate(outs):
-            out[p] = dense[k * blocks : (k + 1) * blocks]
-
-
-def final_kernel(layout, spacing, params_ref, *refs):
-    shared_rows, rows, pieces = layout
-    epochs = len(pieces)
-    ins, (out_ref, held) = refs[: 2 * epochs], refs[2 * epochs :]
-    band, epoch = lax.axis_index("band"), lax.axis_index("epoch")
-    for k in range(epochs):
-        q = lax.rem(epoch - k + epochs, epochs)
-        held[band, q] = ins[k][...]
-        held[1 - band, q] = ins[epochs + k][...]
+        for k in range(owners):
+            out_ref[k, p] = dense[k * blocks : (k + 1) * blocks]
+
+
+def final_kernel(layout, spacing, params_ref, got_ref, out_ref):
+    shared_rows, rows, pieces = layout
     shift = [0.0, 0.0]
     for b in range(BANDS):
         for q, piece in enumerate(pieces):
@@ -388,7 +380,7 @@
                 if entry is None:
                     continue
                 row, position = row_of(b, entry)
-                grad = held[b, q, p]
+                grad = got_ref[q * BANDS + b, p]
                 out_ref[row] = params_ref[row] - STEP * grad
                 if position is not None:
                     shift[position] = shift[position] + grad
@@ -418,11 +410,8 @@
             kept.append(lax.ppermute(other[k], ("epoch", "band"), pairs))
         return kept
 
-    def round_tiles(arrays):
-        return [arrays[0]] + [
-            lax.ppermute(arrays[k], "tile", [(i, (i + k) % owners) for i in range(owners)])
-            for k in range(1, owners)
-        ]
+    def to_all(x, axes, size):
+        return lax.all_to_all(jnp.broadcast_to(x, (size,) + x.shape), axes, 0, 0)
 
     def spread(piece, other):
         return to_peers([piece] * epochs, [other] * epochs)
@@ -442,7 +431,7 @@
         compiler_params=params(),
         name="pack",
     )(block_lists, by_row)
-    got = round_tiles([packed] * owners)
+    got = to_all(packed, "tile", owners)
     slot_piece, slot_short, match = pl.pallas_call(
         functools.partial(select_kernel, layout),
         out_shape=[
@@ -450,11 +439,11 @@
             f32(shared_rows, wide, sources),
             f32(wide + blocks, owners * wide),
         ],
-        in_specs=[smem()] + [vmem()] * owners,
+        in_specs=[smem(), vmem()],
         out_specs=[vmem()] * 3,
         compiler_params=params(),
         name="select",
-    )(block_lists, *got)
+    )(block_lists, got)
     slot_rows = spread(slot_piece, slot_short)
 
     def gradient(moved):
@@ -463,7 +452,7 @@
         )
         return summed(to_peers(parts[:epochs], parts[epochs:]))
 
-    got = round_tiles([gradient(None)] * owners)
+    got = to_all(gradient(None), "tile", owners)
     slot_piece, slot_short, own_first = pl.pallas_call(
         functools.partial(combine_kernel, layout),
         out_shape=[
@@ -471,30 +460,29 @@
             f32(shared_rows, wide, sources),
             f32(rows, blocks, sources),
         ],
-        in_specs=[vmem()] * (1 + owners),
+        in_specs=[vmem()] * 2,
         out_specs=[vmem()] * 3,
         compiler_params=params(),
         name="combine",
-    )(match, *got)
+    )(match, got)
 
     dense = pl.pallas_call(
         functools.partial(dense_kernel, rows),
-        out_shape=[f32(rows, blocks, sources)] * owners,
+        out_shape=f32(owners, rows, blocks, sources),
         in_specs=[smem(), vmem()],
-        out_specs=[vmem()] * owners,
+        out_specs=vmem(),
         compiler_params=params(),
         name="dense",
     )(block_lists, gradient(spread(slot_piece, slot_short)))
-    own = functools.reduce(lambda a, b: a + b, round_tiles(dense), own_first)
+    own = own_first + jnp.sum(lax.all_to_all(dense, "tile", 0, 0), axis=0)
     whole = pl.pallas_call(
         functools.partial(final_kernel, layout, spacing),
         out_shape=f32(param_rows, blocks, sources),
-        in_specs=[vmem()] * (1 + 2 * epochs),
+        in_specs=[vmem()] * 2,
         out_specs=vmem(),
-        scratch_shapes=[pltpu.VMEM((BANDS, epochs, rows, blocks, sources), F32)],
         compiler_params=params(),
         name="final",
-    )(by_row, *spread(own, own))
+    )(by_row, to_all(own, ("epoch", "band"), epochs * BANDS))
     return jnp.transpose(whole, (1, 0, 2))
 
 

time: 89.4 us -> 103 us (1.15)
  blocking collectives: 0 us -> 52.8 us
  starting transfers between devices: 35.6 us -> 8.76 us
  waiting for transfers between devices: 32.2 us -> 12.4 us
  Pallas kernels: 19 us -> 26.3 us
    all_to_all x0 -> x4, blocking collectives: none -> 52.8 us  [the longest x3 39 us: to_all(): return lax.all_to_all(jnp.broadcast_to(x, (size,) + x.shape), axes, 0, 0)]
    ppermute x9 -> x0, starting transfers between devices: 24.6 us -> none  [round_tiles(): lax.ppermute(arrays[k], 'tile', [(i, (i + k) % owners) for i in range(own...]
    ppermute x9 -> x0, waiting for transfers between devices: 16.4 us -> none  [round_tiles(): lax.ppermute(arrays[k], 'tile', [(i, (i + k) % owners) for i in range(own...]
    pallas_call x2, Pallas kernels: 15.7 us -> 23.1 us  [step_gradient(): pl.pallas_call(functools.partial(step_kernel, layout, later), out_shape=[...]
    ppermute x10 -> x8, waiting for transfers between devices: 14.1 us -> 12.4 us  [to_peers(): kept.append(lax.ppermute(other[k], ('epoch', 'band'), pairs))]
    ppermute x5 -> x4, waiting for transfers between devices: 1.75 us -> 0.06 us  [to_peers(): lax.ppermute(same[k], 'epoch', [(i, (i + k) % epochs) for i in range(epoc...]
    ppermute x10 -> x8, starting transfers between devices: 5.54 us -> 3.99 us  [to_peers(): kept.append(lax.ppermute(other[k], ('epoch', 'band'), pairs))]
    ppermute x5 -> x4, starting transfers between devices: 5.42 us -> 4.77 us  [to_peers(): lax.ppermute(same[k], 'epoch', [(i, (i + k) % epochs) for i in range(epoc...]
  transfers between devices with their start and end apart: 24 -> 12, of which waited for: 15 -> 5; matrix products, arithmetic and copies ran while one was open for 0% -> 0% of each run, Pallas kernels for 0% -> 0%
where the time goes in v3:
time: 103 us
  blocking collectives  52.8 us (51%)
  Pallas kernels  26.3 us (26%)
  waiting for transfers between devices  12.4 us (12%)
  starting transfers between devices  8.76 us (9%)
  local copies, waits for them, and re-layouts  1.68 us (2%)
    all_to_all x3, blocking collectives, to_all(): return lax.all_to_all(jnp.broadcast_to(x, (size,) + x.shape), axes, 0, 0)  39 us
    pallas_call x2, Pallas kernels, step_gradient(): pl.pallas_call(functools.partial(step_kernel, layout, later), out_shape=[...  23.1 us
    all_to_all x1, blocking collectives, shards(): own = own_first + jnp.sum(lax.all_to_all(dense, 'tile', 0, 0), axis=0)  13.8 us
    ppermute x8, waiting for transfers between devices, to_peers(): kept.append(lax.ppermute(other[k], ('epoch', 'band'), pairs))  12.4 us
    ppermute x4, starting transfers between devices, to_peers(): lax.ppermute(same[k], 'epoch', [(i, (i + k) % epochs) for i in range(epoc...  4.77 us
    ppermute x8, starting transfers between devices, to_peers(): kept.append(lax.ppermute(other[k], ('epoch', 'band'), pairs))  3.99 us
  transfers between devices with their start and end apart: 12, of which 5 were waited for; matrix products, arithmetic and copies ran while one was open for 0% of the time, Pallas kernels for 0%

profile of v3, /device:TPU:0, one launch (start us, length us, event | category | flops | bytes accessed | tf_op | source)
XLA Modules:
  0.0 102.8 jit_solution(4747662642465407269)
XLA Ops:
  0.0 0.7 copy-done.4
  0.7 0.9 copy-done
  1.6 0.6 pack.1
  2.2 13.7 %all_to_all.20.refs_0_ = f32[4,12,8,128]{3,2,1,0:T(8,128)S(1)} all-to-all(f32[4,12,8,128]{3,2,1,0:T(8,128)S(1)} %broadcast_in_dim.9), channel_id=1, replica_groups=mesh['region'=2,'tile'=4,'epoch'=2,'band'=2] {'tile'}, dimensions={0} | all-to-all | bytes 393216 | tf_op jit(solution)/shard_map/all_to_all | solution.py:414
  16.0 0.8 select.3
  16.8 1.5 %collective-permute-start = (f32[11,16,128]{2,1,0:T(8,128)S(1)}, f32[11,16,128]{2,1,0:T(8,128)S(1)}, u32[]{:S(2)}, u32[]{:S(2)}) collective-permute-start(f32[11,16,128]{2,1,0:T(8,128)S(1)} %get-tuple-element.20.refs_0_), channel_id=1, source_target_pairs={{0,2},{2,0},{1,3},{3,1},{4,6},{6,4},{5,7},{7,5},{8,10},{10,8},{9,1... | collective-permute-start | bytes 270344 | tf_op jit(solution)/shard_map/ppermute | solution.py:403
  18.3 0.6 collective-permute-start.1
  19.6 2.9 %collective-permute-done.2.refs_3_ = f32[7,16,128]{2,1,0:T(8,128)S(1)} collective-permute-done((f32[7,16,128]{2,1,0:T(8,128)S(1)}, f32[7,16,128]{2,1,0:T(8,128)S(1)}, u32[]{:S(2)}, u32[]{:S(2)}) %collective-permute-start.2) | collective-permute-done | bytes 57376 | tf_op jit(solution)/shard_map/ppermute | solution.py:410
  22.6 11.5 %first_step.1 = (f32[11,16,128]{2,1,0:T(8,128)S(1)}, f32[11,16,128]{2,1,0:T(8,128)S(1)}, f32[7,16,128]{2,1,0:T(8,128)S(1)}, f32[7,16,128]{2,1,0:T(8,128)S(1)}) custom-call(s32[2]{0:T(128)S(1)} %copy-done.6, s32[2,2,8]{2,1,0:T(2,128)S(1)} %bitcast.5, f32[1,1]{1,0:T(1,128)S(6)} %copy.8.psf_ref, f32[2,1,1,128,128]{4,3,2,1,0:T(8,128)S(1)} %copy-done.2, ...), custom_call_target="tpu_custom_call" | custom-call | tf_op jit(solution)/shard_map/first_step/pallas_call | solution.py:320
  34.1 0.9 collective-permute-start.3
  35.2 1.1 %collective-permute-start.5 = (f32[7,16,128]{2,1,0:T(8,128)S(1)}, f32[7,16,128]{2,1,0:T(8,128)S(1)}, u32[]{:S(2)}, u32[]{:S(2)}) collective-permute-start(f32[7,16,128]{2,1,0:T(8,128)S(1)} %get-tuple-element.25), channel_id=1, source_target_pairs={{0,3},{1,2},{2,1},{3,0},{4,7},{5,6},{6,5},{7,4},{8,11},{9,10},{10,... | collective-permute-start | bytes 172040 | tf_op jit(solution)/shard_map/ppermute | solution.py:410
  36.3 3.1 %collective-permute-done.5 = f32[7,16,128]{2,1,0:T(8,128)S(1)} collective-permute-done((f32[7,16,128]{2,1,0:T(8,128)S(1)}, f32[7,16,128]{2,1,0:T(8,128)S(1)}, u32[]{:S(2)}, u32[]{:S(2)}) %collective-permute-start.5) | collective-permute-done | bytes 57376 | tf_op jit(solution)/shard_map/ppermute | solution.py:410
  39.4 17.6 %all_to_all.21.refs_0_ = f32[4,11,16,128]{3,2,1,0:T(8,128)S(1)} all-to-all(f32[4,11,16,128]{3,2,1,0:T(8,128)S(1)} %broadcast_in_dim.10), channel_id=1, replica_groups=mesh['region'=2,'tile'=4,'epoch'=2,'band'=2] {'tile'}, dimensions={0} | all-to-all | bytes 720896 | tf_op jit(solution)/shard_map/all_to_all | solution.py:414
  57.4 1.2 %collective-permute-start.6 = (f32[11,16,128]{2,1,0:T(8,128)S(1)}, f32[11,16,128]{2,1,0:T(8,128)S(1)}, u32[]{:S(2)}, u32[]{:S(2)}) collective-permute-start(f32[11,16,128]{2,1,0:T(8,128)S(1)} %get-tuple-element.27.refs_4_), channel_id=1, source_target_pairs={{0,2},{2,0},{1,3},{3,1},{4,6},{6,4},{5,7},{7,5},{8,10},{10,8},{9,1... | collective-permute-start | bytes 270344 | tf_op jit(solution)/shard_map/ppermute | solution.py:403
  58.6 0.9 collective-permute-start.7
  59.6 3.2 %collective-permute-done.8.refs_7_ = f32[7,16,128]{2,1,0:T(8,128)S(1)} collective-permute-done((f32[7,16,128]{2,1,0:T(8,128)S(1)}, f32[7,16,128]{2,1,0:T(8,128)S(1)}, u32[]{:S(2)}, u32[]{:S(2)}) %collective-permute-start.8) | collective-permute-done | bytes 57376 | tf_op jit(solution)/shard_map/ppermute | solution.py:410
  62.8 11.6 %later_step.1 = (f32[11,16,128]{2,1,0:T(8,128)S(1)}, f32[11,16,128]{2,1,0:T(8,128)S(1)}, f32[7,16,128]{2,1,0:T(8,128)S(1)}, f32[7,16,128]{2,1,0:T(8,128)S(1)}) custom-call(s32[2]{0:T(128)S(1)} %copy-done.6, s32[2,2,8]{2,1,0:T(2,128)S(1)} %bitcast.6, f32[1,1]{1,0:T(1,128)S(6)} %copy.8.psf_ref, f32[2,1,1,128,128]{4,3,2,1,0:T(8,128)S(1)} %copy-done.2, ...), custom_call_target="tpu_custom_call" | custom-call | tf_op jit(solution)/shard_map/later_step/pallas_call | solution.py:320
  74.4 1.0 %collective-permute-start.9 = (f32[11,16,128]{2,1,0:T(8,128)S(1)}, f32[11,16,128]{2,1,0:T(8,128)S(1)}, u32[]{:S(2)}, u32[]{:S(2)}) collective-permute-start(f32[11,16,128]{2,1,0:T(8,128)S(1)} %get-tuple-element.30), channel_id=1, source_target_pairs={{0,2},{2,0},{1,3},{3,1},{4,6},{6,4},{5,7},{7,5},{8,10},{10,8},{9,1... | collective-permute-start | bytes 270344 | tf_op jit(solution)/shard_map/ppermute | solution.py:403
  75.6 1.0 collective-permute-start.11
  76.7 3.1 %collective-permute-done.11 = f32[7,16,128]{2,1,0:T(8,128)S(1)} collective-permute-done((f32[7,16,128]{2,1,0:T(8,128)S(1)}, f32[7,16,128]{2,1,0:T(8,128)S(1)}, u32[]{:S(2)}, u32[]{:S(2)}) %collective-permute-start.11) | collective-permute-done | bytes 57376 | tf_op jit(solution)/shard_map/ppermute | solution.py:410
  79.8 0.8 dense.1
  80.6 13.8 %all_to_all.22 = f32[4,11,8,128]{3,2,1,0:T(8,128)S(1)} all-to-all(f32[4,11,8,128]{3,2,1,0:T(8,128)S(1)} %dense.1), channel_id=1, replica_groups=mesh['region'=2,'tile'=4,'epoch'=2,'band'=2] {'tile'}, dimensions={0} | all-to-all | bytes 360448 | tf_op jit(solution)/shard_map/all_to_all | solution.py:477
  94.5 7.7 %all_to_all.23.got_ref = f32[4,11,8,128]{3,2,1,0:T(8,128)S(1)} all-to-all(f32[4,11,8,128]{3,2,1,0:T(8,128)S(1)} %broadcast_in_dim.11), channel_id=1, replica_groups=mesh['region'=2,'tile'=4,'epoch'=2,'band'=2] {'epoch','band'}, dimensions={0} | all-to-all | bytes 360448 | tf_op jit(solution)/shard_map/all_to_all | solution.py:414
  102.1 0.7 final.1
  (34 shorter events, 1.0 us)
Async XLA Ops:
  0.0 0.7 copy-start.4
  0.7 0.9 copy-start
  2.2 20.3 %copy-start.3 = (f32[2,1,1,128,128]{4,3,2,1,0:T(8,128)S(1)}, f32[2,1,1,128,128]{4,3,2,1,0:T(8,128)}, u32[]{:S(2)}) copy-start(f32[2,1,1,128,128]{4,3,2,1,0:T(8,128)} %weight_ref.3) | copy-start | bytes 393220
  16.0 6.6 %copy-start.2 = (f32[2,1,1,128,128]{4,3,2,1,0:T(8,128)S(1)}, f32[2,1,1,128,128]{4,3,2,1,0:T(8,128)}, u32[]{:S(2)}) copy-start(f32[2,1,1,128,128]{4,3,2,1,0:T(8,128)} %data_ref.3) | copy-start | bytes 393220
  16.8 5.7 %collective-permute-start = (f32[11,16,128]{2,1,0:T(8,128)S(1)}, f32[11,16,128]{2,1,0:T(8,128)S(1)}, u32[]{:S(2)}, u32[]{:S(2)}) collective-permute-start(f32[11,16,128]{2,1,0:T(8,128)S(1)} %get-tuple-element.20.refs_0_), channel_id=1, source_target_pairs={{0,2},{2,0},{1,3},{3,1},{4,6},{6,4},{5,7},{7,5},{8,10},{10,8},{9,1... | collective-permute-start | bytes 270344 | tf_op jit(solution)/shard_map/ppermute | solution.py:403
  18.3 4.2 %copy-start.5 = (s32[2,8,2]{1,2,0:T(2,128)S(1)}, s32[2,8,2]{1,2,0:T(2,128)}, u32[]{:S(2)}) copy-start(s32[2,8,2]{1,2,0:T(2,128)} %param.13) | copy-start | bytes 388
  18.3 4.2 %collective-permute-start.2 = (f32[7,16,128]{2,1,0:T(8,128)S(1)}, f32[7,16,128]{2,1,0:T(8,128)S(1)}, u32[]{:S(2)}, u32[]{:S(2)}) collective-permute-start(f32[7,16,128]{2,1,0:T(8,128)S(1)} %get-tuple-element.21), channel_id=1, source_target_pairs={{0,3},{1,2},{2,1},{3,0},{4,7},{5,6},{6,5},{7,4},{8,11},{9,10},{10,... | collective-permute-start | bytes 172040 | tf_op jit(solution)/shard_map/ppermute | solution.py:410
  18.3 4.2 %collective-permute-start.1 = (f32[7,16,128]{2,1,0:T(8,128)S(1)}, f32[7,16,128]{2,1,0:T(8,128)S(1)}, u32[]{:S(2)}, u32[]{:S(2)}) collective-permute-start(f32[7,16,128]{2,1,0:T(8,128)S(1)} %get-tuple-element.21), channel_id=1, source_target_pairs={{0,1},{1,0},{2,3},{3,2},{4,5},{5,4},{6,7},{7,6},{8,9},{9,8},{10,11... | collective-permute-start | bytes 172040 | tf_op jit(solution)/shard_map/ppermute | solution.py:410
  19.6 2.9 %copy-start.6 = (s32[2]{0:T(128)S(1)}, s32[2]{0:T(128)}, u32[]{:S(2)}) copy-start(s32[2]{0:T(128)} %counts_ref.3) | copy-start | bytes 28
  34.1 5.3 %collective-permute-start.3 = (f32[11,16,128]{2,1,0:T(8,128)S(1)}, f32[11,16,128]{2,1,0:T(8,128)S(1)}, u32[]{:S(2)}, u32[]{:S(2)}) collective-permute-start(f32[11,16,128]{2,1,0:T(8,128)S(1)} %get-tuple-element.23), channel_id=1, source_target_pairs={{0,2},{2,0},{1,3},{3,1},{4,6},{6,4},{5,7},{7,5},{8,10},{10,8},{9,1... | collective-permute-start | bytes 270344 | tf_op jit(solution)/shard_map/ppermute | solution.py:403
  35.0 1.3 %collective-permute-start.4 = (f32[7,16,128]{2,1,0:T(8,128)S(1)}, f32[7,16,128]{2,1,0:T(8,128)S(1)}, u32[]{:S(2)}, u32[]{:S(2)}) collective-permute-start(f32[7,16,128]{2,1,0:T(8,128)S(1)} %get-tuple-element.24), channel_id=1, source_target_pairs={{0,1},{1,0},{2,3},{3,2},{4,5},{5,4},{6,7},{7,6},{8,9},{9,8},{10,11... | collective-permute-start | bytes 172040 | tf_op jit(solution)/shard_map/ppermute | solution.py:410
  35.2 4.1 %collective-permute-start.5 = (f32[7,16,128]{2,1,0:T(8,128)S(1)}, f32[7,16,128]{2,1,0:T(8,128)S(1)}, u32[]{:S(2)}, u32[]{:S(2)}) collective-permute-start(f32[7,16,128]{2,1,0:T(8,128)S(1)} %get-tuple-element.25), channel_id=1, source_target_pairs={{0,3},{1,2},{2,1},{3,0},{4,7},{5,6},{6,5},{7,4},{8,11},{9,10},{10,... | collective-permute-start | bytes 172040 | tf_op jit(solution)/shard_map/ppermute | solution.py:410
  57.4 5.4 %collective-permute-start.6 = (f32[11,16,128]{2,1,0:T(8,128)S(1)}, f32[11,16,128]{2,1,0:T(8,128)S(1)}, u32[]{:S(2)}, u32[]{:S(2)}) collective-permute-start(f32[11,16,128]{2,1,0:T(8,128)S(1)} %get-tuple-element.27.refs_4_), channel_id=1, source_target_pairs={{0,2},{2,0},{1,3},{3,1},{4,6},{6,4},{5,7},{7,5},{8,10},{10,8},{9,1... | collective-permute-start | bytes 270344 | tf_op jit(solution)/shard_map/ppermute | solution.py:403
  58.6 4.2 %collective-permute-start.8 = (f32[7,16,128]{2,1,0:T(8,128)S(1)}, f32[7,16,128]{2,1,0:T(8,128)S(1)}, u32[]{:S(2)}, u32[]{:S(2)}) collective-permute-start(f32[7,16,128]{2,1,0:T(8,128)S(1)} %get-tuple-element.28), channel_id=1, source_target_pairs={{0,3},{1,2},{2,1},{3,0},{4,7},{5,6},{6,5},{7,4},{8,11},{9,10},{10,... | collective-permute-start | bytes 172040 | tf_op jit(solution)/shard_map/ppermute | solution.py:410
  58.6 4.2 %collective-permute-start.7 = (f32[7,16,128]{2,1,0:T(8,128)S(1)}, f32[7,16,128]{2,1,0:T(8,128)S(1)}, u32[]{:S(2)}, u32[]{:S(2)}) collective-permute-start(f32[7,16,128]{2,1,0:T(8,128)S(1)} %get-tuple-element.28), channel_id=1, source_target_pairs={{0,1},{1,0},{2,3},{3,2},{4,5},{5,4},{6,7},{7,6},{8,9},{9,8},{10,11... | collective-permute-start | bytes 172040 | tf_op jit(solution)/shard_map/ppermute | solution.py:410
  74.4 5.4 %collective-permute-start.9 = (f32[11,16,128]{2,1,0:T(8,128)S(1)}, f32[11,16,128]{2,1,0:T(8,128)S(1)}, u32[]{:S(2)}, u32[]{:S(2)}) collective-permute-start(f32[11,16,128]{2,1,0:T(8,128)S(1)} %get-tuple-element.30), channel_id=1, source_target_pairs={{0,2},{2,0},{1,3},{3,1},{4,6},{6,4},{5,7},{7,5},{8,10},{10,8},{9,1... | collective-permute-start | bytes 270344 | tf_op jit(solution)/shard_map/ppermute | solution.py:403
  75.5 1.2 %collective-permute-start.10 = (f32[7,16,128]{2,1,0:T(8,128)S(1)}, f32[7,16,128]{2,1,0:T(8,128)S(1)}, u32[]{:S(2)}, u32[]{:S(2)}) collective-permute-start(f32[7,16,128]{2,1,0:T(8,128)S(1)} %get-tuple-element.31), channel_id=1, source_target_pairs={{0,1},{1,0},{2,3},{3,2},{4,5},{5,4},{6,7},{7,6},{8,9},{9,8},{10,11... | collective-permute-start | bytes 172040 | tf_op jit(solution)/shard_map/ppermute | solution.py:410
  75.6 4.2 %collective-permute-start.11 = (f32[7,16,128]{2,1,0:T(8,128)S(1)}, f32[7,16,128]{2,1,0:T(8,128)S(1)}, u32[]{:S(2)}, u32[]{:S(2)}) collective-permute-start(f32[7,16,128]{2,1,0:T(8,128)S(1)} %get-tuple-element.32), channel_id=1, source_target_pairs={{0,3},{1,2},{2,1},{3,0},{4,7},{5,6},{6,5},{7,4},{8,11},{9,10},{10,... | collective-permute-start | bytes 172040 | tf_op jit(solution)/shard_map/ppermute | solution.py:410
  94.5 7.7 %copy-start.1 = (f32[8,44,128]{2,0,1:T(8,128)S(1)}, f32[8,44,128]{2,0,1:T(8,128)}, u32[]{:S(2)}) copy-start(f32[8,44,128]{2,0,1:T(8,128)} %param.7) | copy-start | bytes 540676

commit v4 on v2

--- a/solution.py
+++ b/solution.py
@@ -13,6 +13,7 @@
 POSITION_RATE = 1.0 / 64.0
 COMPS = 7
 BANDS = 2
+TOGETHER = 2
 SHARED = 4 * COMPS
 HALF = SHARED // BANDS
 LOG2E = math.log2(math.e)
@@ -157,7 +158,8 @@
     taken = 2 * epochs * (2 if later else 1)
     ins, refs = refs[:taken], refs[taken:]
     outs, refs = refs[: 2 * epochs], refs[2 * epochs :]
-    shared, amps, derived, prof_x, prof_y, pieces_x, pieces_y, image, sums, half, other = refs[:11]
+    shared, amps, derived, here, prof_x, prof_y, pieces_x, pieces_y, image, sums, here_sums = refs[:11]
+    half, other = refs[11:13]
     band, epoch = lax.axis_index("band"), lax.axis_index("epoch")
     tiles = data_ref.shape[0]
     pixels = data_ref.shape[-1]
@@ -172,7 +174,7 @@
         return r // HALF, r % HALF
 
     if later:
-        moved, moved_amps = refs[11:]
+        moved, moved_amps = refs[13:]
         put_together(layout, band, epoch, ins[2 * epochs :], half, other, moved, moved_amps)
         for k in range(4):
             shift = 0.0
@@ -185,18 +187,24 @@
             amps[c] = amps[c] - STEP * moved_amps[c]
 
     psf = psf_ref[0, 0]
-    line_of = lax.broadcasted_iota(jnp.int32, (wide, 128), 0)
-    live = jnp.zeros((wide, 128), jnp.bool_)
+    line_of = lax.broadcasted_iota(jnp.int32, (slots, 128), 0)
+    live = []
     for t in range(tiles):
-        live = live | ((line_of >= t * slots) & (line_of < t * slots + counts_ref[t]))
-    for c in range(COMPS):
-        lw, an = shared[row(2, c)], shared[row(3, c)]
-        derived[0, c] = shared[row(0, c)]
-        derived[1, c] = shared[row(1, c)]
-        derived[2, c] = (-0.5 * LOG2E) / (jnp.exp(2.0 * (lw + an)) + psf * psf)
-        derived[3, c] = (-0.5 * LOG2E) / (jnp.exp(2.0 * (lw - an)) + psf * psf)
-        derived[4, c] = jnp.where(live, amps[c], 0.0)
-    sums[...] = jnp.zeros_like(sums)
+        live.append(line_of < counts_ref[t])
+        off_x = off_y = jnp.zeros((slots, 128), jnp.int32)
+        for s in range(slots):
+            off_x = jnp.where(line_of == s, offsets_ref[t, 0, s], off_x)
+            off_y = jnp.where(line_of == s, offsets_ref[t, 1, s], off_y)
+        off_x, off_y = off_x.astype(F32), off_y.astype(F32)
+        at = slice(t * slots, (t + 1) * slots)
+        for c in range(COMPS):
+            cx, cy, lw, an = (shared[(*row(k, c), at)] for k in range(4))
+            derived[t, 0, c] = cx + off_x
+            derived[t, 1, c] = cy + off_y
+            derived[t, 2, c] = (-0.5 * LOG2E) / (jnp.exp(2.0 * (lw + an)) + psf * psf)
+            derived[t, 3, c] = (-0.5 * LOG2E) / (jnp.exp(2.0 * (lw - an)) + psf * psf)
+            derived[t, 4, c] = jnp.where(live[t], amps[c, at], 0.0)
+    live = jnp.concatenate(live, axis=0)
 
     grid = lax.broadcasted_iota(jnp.int32, (pixels, 128), 0).astype(F32)
 
@@ -205,41 +213,42 @@
         return jnp.concatenate([hi, (x - hi.astype(F32)).astype(BF16)], axis=0)
 
     def stack(x):
-        both = cut(x)
-        return jnp.concatenate([both, both], axis=1)
+        hi = x.astype(BF16)
+        lo = (x - hi.astype(F32)).astype(BF16)
+        turns = [part[r : r + 16] for r in range(0, pixels, 16) for part in (hi, lo)]
+        one = jnp.concatenate(turns, axis=0)
+        return jnp.concatenate([one, one], axis=1)
+
+    def join(x):
+        return jnp.concatenate([x[r : r + 16] + x[r + 16 : r + 32] for r in range(0, 2 * pixels, 32)], axis=0)
 
     def total(x):
         return jnp.sum(x, axis=0, keepdims=True)
 
-    def line(index, c, s):
-        return derived[index, c, pl.ds(s, 1), :]
-
-    together = 2
-    for t in range(tiles):
-        trips = (counts_ref[t] + together - 1) // together
-        image[...] = jnp.zeros_like(image)
-
-        def render(i, carry):
-            for u in range(together):
-                s = i * together + u
-                g = t * slots + s
-                off_x = offsets_ref[t, 0, s].astype(F32)
-                off_y = offsets_ref[t, 1, s].astype(F32)
-                for c in range(COMPS):
-                    d = grid - (line(0, c, g) + off_x)
-                    e = jnp.exp2(d * d * line(2, c, g))
-                    prof_x[s * COMPS + c] = e
-                    pieces_x[s, :, c * 128 : (c + 1) * 128] = cut(e)
-                    d = grid - (line(1, c, g) + off_y)
-                    e = jnp.exp2(d * d * line(3, c, g))
-                    prof_y[s * COMPS + c] = e
-                    pieces_y[s, :, c * 128 : (c + 1) * 128] = cut(e * line(4, c, g))
-                image[...] += lax.dot_general(
-                    pieces_x[s], pieces_y[s], (((1,), (1,)), ((), ())), preferred_element_type=F32
-                )
-            return carry
-
-        lax.fori_loop(0, trips, render, 0)
+    both = TOGETHER * COMPS
+
+    def tile_body(t, carry):
+        here[...] = derived[t]
+
+        def line(index, c, s):
+            return here[index, c, s : s + 1, :]
+
+        for i in range(slots // TOGETHER):
+            for n in range(both):
+                u, c = divmod(n, COMPS)
+                s = i * TOGETHER + u
+                d = grid - line(0, c, s)
+                e = jnp.exp2(d * d * line(2, c, s))
+                prof_x[i * both + n] = e
+                pieces_x[i, :, n * 128 : (n + 1) * 128] = cut(e)
+                d = grid - line(1, c, s)
+                e = jnp.exp2(d * d * line(3, c, s))
+                prof_y[i * both + n] = e
+                pieces_y[i, :, n * 128 : (n + 1) * 128] = cut(e * line(4, c, s))
+            part = lax.dot_general(
+                pieces_x[i], pieces_y[i], (((1,), (1,)), ((), ())), preferred_element_type=F32
+            )
+            image[...] = part if i == 0 else image[...] + part
 
         model = (image[:pixels, :pixels] + image[pixels:, pixels:]) + (
             image[:pixels, pixels:] + image[pixels:, :pixels]
@@ -247,35 +256,33 @@
         cotangent = weight_ref[t, 0, 0] * (model - data_ref[t, 0, 0])
         left_x, left_y = stack(cotangent), stack(cotangent.T)
 
-        def pull(i, carry):
-            for u in range(together):
-                s = i * together + u
-                g = t * slots + s
-                off_x = offsets_ref[t, 0, s].astype(F32)
-                off_y = offsets_ref[t, 1, s].astype(F32)
-                for first in range(0, COMPS, 2):
-                    here = min(2, COMPS - first)
-                    span = pl.ds(first * 128, 128 * here)
-                    by_x = jnp.dot(left_x, pieces_y[s, :, span], preferred_element_type=F32)
-                    by_y = jnp.dot(left_y, pieces_x[s, :, span], preferred_element_type=F32)
-                    by_x = by_x[:pixels] + by_x[pixels:]
-                    by_y = by_y[:pixels] + by_y[pixels:]
-                    for n in range(here):
-                        c = first + n
-                        d = grid - (line(0, c, g) + off_x)
-                        e = prof_x[s * COMPS + c] * by_x[:, n * 128 : (n + 1) * 128]
-                        e1 = e * d
-                        sums[0, c, pl.ds(g, 1), :] = total(e1)
-                        sums[1, c, pl.ds(g, 1), :] = total(e1 * d)
-                        d = grid - (line(1, c, g) + off_y)
-                        e = prof_y[s * COMPS + c] * by_y[:, n * 128 : (n + 1) * 128]
-                        e1 = e * d
-                        sums[2, c, pl.ds(g, 1), :] = total(e1)
-                        sums[3, c, pl.ds(g, 1), :] = total(e1 * d)
-                        sums[4, c, pl.ds(g, 1), :] = total(e)
-            return carry
-
-        lax.fori_loop(0, trips, pull, 0)
+        for i in range(slots // TOGETHER):
+            for first in range(0, both, 2):
+                span = pl.ds(first * 128, 256)
+                by_x = join(jnp.dot(left_x, pieces_y[i, :, span], preferred_element_type=F32))
+                by_y = join(jnp.dot(left_y, pieces_x[i, :, span], preferred_element_type=F32))
+                for n in (first, first + 1):
+                    u, c = divmod(n, COMPS)
+                    s = i * TOGETHER + u
+                    at = slice((n - first) * 128, (n - first + 1) * 128)
+                    d = grid - line(0, c, s)
+                    e = prof_x[i * both + n] * by_x[:, at]
+                    e1 = e * d
+                    here_sums[0, c, s : s + 1, :] = total(e1)
+                    here_sums[1, c, s : s + 1, :] = total(e1 * d)
+                    d = grid - line(1, c, s)
+                    e = prof_y[i * both + n] * by_y[:, at]
+                    e1 = e * d
+                    here_sums[2, c, s : s + 1, :] = total(e1)
+                    here_sums[3, c, s : s + 1, :] = total(e1 * d)
+                    here_sums[4, c, s : s + 1, :] = total(e)
+        sums[t] = here_sums[...]
+        return carry
+
+    lax.fori_loop(0, tiles, tile_body, 0)
+
+    def sum_of(index, c):
+        return jnp.concatenate([sums[t, index, c] for t in range(tiles)], axis=0)
 
     def keep(x):
         return jnp.where(live, x, 0.0)
@@ -285,13 +292,13 @@
         wide_x, wide_y = jnp.exp(2.0 * (lw + an)), jnp.exp(2.0 * (lw - an))
         inv_x, inv_y = 1.0 / (wide_x + psf * psf), 1.0 / (wide_y + psf * psf)
         amp = amps[c]
-        var_x = keep(sums[1, c] * inv_x * inv_x * wide_x)
-        var_y = keep(amp * sums[3, c] * inv_y * inv_y * wide_y)
-        shared[row(0, c)] = keep(sums[0, c] * inv_x)
-        shared[row(1, c)] = keep(amp * sums[2, c] * inv_y)
+        var_x = keep(sum_of(1, c) * inv_x * (inv_x * wide_x))
+        var_y = keep(amp * sum_of(3, c) * inv_y * (inv_y * wide_y))
+        shared[row(0, c)] = keep(sum_of(0, c) * inv_x)
+        shared[row(1, c)] = keep(amp * sum_of(2, c) * inv_y)
         shared[row(2, c)] = var_x + var_y
         shared[row(3, c)] = var_x - var_y
-        amps[c] = keep(sums[4, c])
+        amps[c] = keep(sum_of(4, c))
     none = jnp.zeros((wide, 128), F32)
     for q, piece in enumerate(pieces):
         for p, entry in enumerate(piece):
@@ -324,13 +331,15 @@
         out_specs=[vmem()] * len(shapes),
         scratch_shapes=together
         + [
-            pltpu.VMEM((5, COMPS, wide, 128), F32),
+            pltpu.VMEM((tiles, 5, COMPS, slots, 128), F32),
+            pltpu.VMEM((5, COMPS, slots, 128), F32),
             pltpu.VMEM((slots * COMPS, pixels, 128), F32),
             pltpu.VMEM((slots * COMPS, pixels, 128), F32),
-            pltpu.VMEM((slots, 2 * pixels, COMPS * 128), BF16),
-            pltpu.VMEM((slots, 2 * pixels, COMPS * 128), BF16),
+            pltpu.VMEM((slots // TOGETHER, 2 * pixels, TOGETHER * COMPS * 128), BF16),
+            pltpu.VMEM((slots // TOGETHER, 2 * pixels, TOGETHER * COMPS * 128), BF16),
             pltpu.VMEM((2 * pixels, 2 * pixels), F32),
-            pltpu.VMEM((5, COMPS, wide, 128), F32),
+            pltpu.VMEM((tiles, 5, COMPS, slots, 128), F32),
+            pltpu.VMEM((5, COMPS, slots, 128), F32),
             pltpu.VMEM((epochs, rows, wide, 128), F32),
             pltpu.VMEM((epochs, shared_rows, wide, 128), F32),
         ]

time: 89.4 us -> 92 us (1.029)
  Pallas kernels: 19 us -> 33.4 us
  starting transfers between devices: 35.6 us -> 25.5 us
  waiting for transfers between devices: 32.2 us -> 30.5 us
    pallas_call x2, Pallas kernels: 15.7 us -> 30.2 us  [step_gradient(): pl.pallas_call(functools.partial(step_kernel, layout, later), out_shape=[...]
    ppermute x9, starting transfers between devices: 24.6 us -> 14.5 us  [round_tiles(): lax.ppermute(arrays[k], 'tile', [(i, (i + k) % owners) for i in range(own...]
    ppermute x9, waiting for transfers between devices: 16.4 us -> 14.8 us  [round_tiles(): lax.ppermute(arrays[k], 'tile', [(i, (i + k) % owners) for i in range(own...]
  transfers between devices with their start and end apart: 24 -> 24, of which waited for: 15 -> 14; matrix products, arithmetic and copies ran while one was open for 0% -> 0% of each run, Pallas kernels for 0% -> 0%
where the time goes in v4:
time: 92 us; the launch traced here: 91.9 us
  Pallas kernels  33.4 us (36%)
  waiting for transfers between devices  30.5 us (33%)
  starting transfers between devices  25.5 us (28%)
  local copies, waits for them, and re-layouts  1.63 us (2%)
    pallas_call x2, Pallas kernels, step_gradient(): pl.pallas_call(functools.partial(step_kernel, layout, later), out_shape=[...  30.2 us
    ppermute x9, waiting for transfers between devices, round_tiles(): lax.ppermute(arrays[k], 'tile', [(i, (i + k) % owners) for i in range(own...  14.8 us
    ppermute x9, starting transfers between devices, round_tiles(): lax.ppermute(arrays[k], 'tile', [(i, (i + k) % owners) for i in range(own...  14.5 us
    ppermute x10, waiting for transfers between devices, to_peers(): kept.append(lax.ppermute(other[k], ('epoch', 'band'), pairs))  14 us
    ppermute x5, starting transfers between devices, to_peers(): lax.ppermute(same[k], 'epoch', [(i, (i + k) % epochs) for i in range(epoc...  5.53 us
    ppermute x10, starting transfers between devices, to_peers(): kept.append(lax.ppermute(other[k], ('epoch', 'band'), pairs))  5.43 us
  transfers between devices with their start and end apart: 24, of which 14 were waited for; matrix products, arithmetic and copies ran while one was open for 0% of the time, Pallas kernels for 0%

profile of v4, /device:TPU:0, one launch (start us, length us, event | category | flops | bytes accessed | tf_op | source)
XLA Modules:
  0.0 91.9 jit_solution(6596325614650868020)
XLA Ops:
  2.2 5.1 %collective-permute-start.2 = (f32[12,8,128]{2,1,0:T(8,128)S(1)}, f32[12,8,128]{2,1,0:T(8,128)S(1)}, u32[]{:S(2)}, u32[]{:S(2)}) collective-permute-start(f32[12,8,128]{2,1,0:T(8,128)S(1)} %pack.1.refs_0_), channel_id=1, source_target_pairs={{0,12},{4,0},{8,4},{12,8},{1,13},{5,1},{9,5},{13,9},{2,14},{6,2},{... | collective-permute-start | bytes 147464 | tf_op jit(solution)/shard_map/ppermute | solution.py:432
  7.3 1.0 %collective-permute-start = (f32[12,8,128]{2,1,0:T(8,128)S(1)}, f32[12,8,128]{2,1,0:T(8,128)S(1)}, u32[]{:S(2)}, u32[]{:S(2)}) collective-permute-start(f32[12,8,128]{2,1,0:T(8,128)S(1)} %pack.1.refs_0_), channel_id=1, source_target_pairs={{0,4},{4,8},{8,12},{12,0},{1,5},{5,9},{9,13},{13,1},{2,6},{6,10},{... | collective-permute-start | bytes 147464 | tf_op jit(solution)/shard_map/ppermute | solution.py:432
  8.3 1.0 %collective-permute-done.2.refs_3_ = f32[12,8,128]{2,1,0:T(8,128)S(1)} collective-permute-done((f32[12,8,128]{2,1,0:T(8,128)S(1)}, f32[12,8,128]{2,1,0:T(8,128)S(1)}, u32[]{:S(2)}, u32[]{:S(2)}) %collective-permute-start.2) | collective-permute-done | bytes 49184 | tf_op jit(solution)/shard_map/ppermute | solution.py:432
  9.4 2.9 %collective-permute-done.1.refs_2_ = f32[12,8,128]{2,1,0:T(8,128)S(1)} collective-permute-done((f32[12,8,128]{2,1,0:T(8,128)S(1)}, f32[12,8,128]{2,1,0:T(8,128)S(1)}, u32[]{:S(2)}, u32[]{:S(2)}) %collective-permute-start.1) | collective-permute-done | bytes 49184 | tf_op jit(solution)/shard_map/ppermute | solution.py:432
  14.0 1.5 %collective-permute-start.3 = (f32[11,16,128]{2,1,0:T(8,128)S(1)}, f32[11,16,128]{2,1,0:T(8,128)S(1)}, u32[]{:S(2)}, u32[]{:S(2)}) collective-permute-start(f32[11,16,128]{2,1,0:T(8,128)S(1)} %get-tuple-element.24.refs_0_), channel_id=1, source_target_pairs={{0,2},{2,0},{1,3},{3,1},{4,6},{6,4},{5,7},{7,5},{8,10},{10,8},{9,1... | collective-permute-start | bytes 270344 | tf_op jit(solution)/shard_map/ppermute | solution.py:420
  16.9 2.9 %collective-permute-done.5.refs_3_ = f32[7,16,128]{2,1,0:T(8,128)S(1)} collective-permute-done((f32[7,16,128]{2,1,0:T(8,128)S(1)}, f32[7,16,128]{2,1,0:T(8,128)S(1)}, u32[]{:S(2)}, u32[]{:S(2)}) %collective-permute-start.5) | collective-permute-done | bytes 57376 | tf_op jit(solution)/shard_map/ppermute | solution.py:427
  19.8 15.0 %first_step.1 = (f32[11,16,128]{2,1,0:T(8,128)S(1)}, f32[11,16,128]{2,1,0:T(8,128)S(1)}, f32[7,16,128]{2,1,0:T(8,128)S(1)}, f32[7,16,128]{2,1,0:T(8,128)S(1)}) custom-call(s32[2]{0:T(128)S(1)} %copy-done.6, s32[2,2,8]{2,1,0:T(2,128)S(1)} %bitcast.5, f32[1,1]{1,0:T(1,128)S(6)} %copy.8.psf_ref, f32[2,1,1,128,128]{4,3,2,1,0:T(8,128)S(1)} %copy-done.2, ...), custom_call_target="tpu_custom_call" | custom-call | tf_op jit(solution)/shard_map/first_step/pallas_call | solution.py:327
  36.0 1.1 %collective-permute-start.8 = (f32[7,16,128]{2,1,0:T(8,128)S(1)}, f32[7,16,128]{2,1,0:T(8,128)S(1)}, u32[]{:S(2)}, u32[]{:S(2)}) collective-permute-start(f32[7,16,128]{2,1,0:T(8,128)S(1)} %get-tuple-element.29), channel_id=1, source_target_pairs={{0,3},{1,2},{2,1},{3,0},{4,7},{5,6},{6,5},{7,4},{8,11},{9,10},{10,... | collective-permute-start | bytes 172040 | tf_op jit(solution)/shard_map/ppermute | solution.py:427
  37.1 3.1 %collective-permute-done.8 = f32[7,16,128]{2,1,0:T(8,128)S(1)} collective-permute-done((f32[7,16,128]{2,1,0:T(8,128)S(1)}, f32[7,16,128]{2,1,0:T(8,128)S(1)}, u32[]{:S(2)}, u32[]{:S(2)}) %collective-permute-start.8) | collective-permute-done | bytes 57376 | tf_op jit(solution)/shard_map/ppermute | solution.py:427
  40.2 1.3 %collective-permute-start.11 = (f32[11,16,128]{2,1,0:T(8,128)S(1)}, f32[11,16,128]{2,1,0:T(8,128)S(1)}, u32[]{:S(2)}, u32[]{:S(2)}) collective-permute-start(f32[11,16,128]{2,1,0:T(8,128)S(1)} %pad_add_fusion.1.refs_0_), channel_id=1, source_target_pairs={{0,12},{4,0},{8,4},{12,8},{1,13},{5,1},{9,5},{13,9},{2,14},{6,2},{... | collective-permute-start | bytes 270344 | tf_op jit(solution)/shard_map/ppermute | solution.py:432
  41.5 1.9 %collective-permute-start.9 = (f32[11,16,128]{2,1,0:T(8,128)S(1)}, f32[11,16,128]{2,1,0:T(8,128)S(1)}, u32[]{:S(2)}, u32[]{:S(2)}) collective-permute-start(f32[11,16,128]{2,1,0:T(8,128)S(1)} %pad_add_fusion.1.refs_0_), channel_id=1, source_target_pairs={{0,4},{4,8},{8,12},{12,0},{1,5},{5,9},{9,13},{13,1},{2,6},{6,10},{... | collective-permute-start | bytes 270344 | tf_op jit(solution)/shard_map/ppermute | solution.py:432
  43.4 1.8 %collective-permute-done.11.refs_3_ = f32[11,16,128]{2,1,0:T(8,128)S(1)} collective-permute-done((f32[11,16,128]{2,1,0:T(8,128)S(1)}, f32[11,16,128]{2,1,0:T(8,128)S(1)}, u32[]{:S(2)}, u32[]{:S(2)}) %collective-permute-start.11) | collective-permute-done | bytes 90144 | tf_op jit(solution)/shard_map/ppermute | solution.py:432
  45.2 5.7 %collective-permute-done.10.refs_2_ = f32[11,16,128]{2,1,0:T(8,128)S(1)} collective-permute-done((f32[11,16,128]{2,1,0:T(8,128)S(1)}, f32[11,16,128]{2,1,0:T(8,128)S(1)}, u32[]{:S(2)}, u32[]{:S(2)}) %collective-permute-start.10) | collective-permute-done | bytes 90144 | tf_op jit(solution)/shard_map/ppermute | solution.py:432
  51.3 1.2 %collective-permute-start.12 = (f32[11,16,128]{2,1,0:T(8,128)S(1)}, f32[11,16,128]{2,1,0:T(8,128)S(1)}, u32[]{:S(2)}, u32[]{:S(2)}) collective-permute-start(f32[11,16,128]{2,1,0:T(8,128)S(1)} %get-tuple-element.31.refs_4_), channel_id=1, source_target_pairs={{0,2},{2,0},{1,3},{3,1},{4,6},{6,4},{5,7},{7,5},{8,10},{10,8},{9,1... | collective-permute-start | bytes 270344 | tf_op jit(solution)/shard_map/ppermute | solution.py:420
  53.5 3.2 %collective-permute-done.14.refs_7_ = f32[7,16,128]{2,1,0:T(8,128)S(1)} collective-permute-done((f32[7,16,128]{2,1,0:T(8,128)S(1)}, f32[7,16,128]{2,1,0:T(8,128)S(1)}, u32[]{:S(2)}, u32[]{:S(2)}) %collective-permute-start.14) | collective-permute-done | bytes 57376 | tf_op jit(solution)/shard_map/ppermute | solution.py:427
  56.7 15.1 %later_step.1 = (f32[11,16,128]{2,1,0:T(8,128)S(1)}, f32[11,16,128]{2,1,0:T(8,128)S(1)}, f32[7,16,128]{2,1,0:T(8,128)S(1)}, f32[7,16,128]{2,1,0:T(8,128)S(1)}) custom-call(s32[2]{0:T(128)S(1)} %copy-done.6, s32[2,2,8]{2,1,0:T(2,128)S(1)} %bitcast.6, f32[1,1]{1,0:T(1,128)S(6)} %copy.8.psf_ref, f32[2,1,1,128,128]{4,3,2,1,0:T(8,128)S(1)} %copy-done.2, ...), custom_call_target="tpu_custom_call" | custom-call | tf_op jit(solution)/shard_map/later_step/pallas_call | solution.py:327
  71.9 1.0 %collective-permute-start.15 = (f32[11,16,128]{2,1,0:T(8,128)S(1)}, f32[11,16,128]{2,1,0:T(8,128)S(1)}, u32[]{:S(2)}, u32[]{:S(2)}) collective-permute-start(f32[11,16,128]{2,1,0:T(8,128)S(1)} %get-tuple-element.34), channel_id=1, source_target_pairs={{0,2},{2,0},{1,3},{3,1},{4,6},{6,4},{5,7},{7,5},{8,10},{10,8},{9,1... | collective-permute-start | bytes 270344 | tf_op jit(solution)/shard_map/ppermute | solution.py:420
  73.1 1.0 %collective-permute-start.17 = (f32[7,16,128]{2,1,0:T(8,128)S(1)}, f32[7,16,128]{2,1,0:T(8,128)S(1)}, u32[]{:S(2)}, u32[]{:S(2)}) collective-permute-start(f32[7,16,128]{2,1,0:T(8,128)S(1)} %get-tuple-element.36), channel_id=1, source_target_pairs={{0,3},{1,2},{2,1},{3,0},{4,7},{5,6},{6,5},{7,4},{8,11},{9,10},{10,... | collective-permute-start | bytes 172040 | tf_op jit(solution)/shard_map/ppermute | solution.py:427
  74.1 3.1 %collective-permute-done.17 = f32[7,16,128]{2,1,0:T(8,128)S(1)} collective-permute-done((f32[7,16,128]{2,1,0:T(8,128)S(1)}, f32[7,16,128]{2,1,0:T(8,128)S(1)}, u32[]{:S(2)}, u32[]{:S(2)}) %collective-permute-start.17) | collective-permute-done | bytes 57376 | tf_op jit(solution)/shard_map/ppermute | solution.py:427
  78.5 2.0 %collective-permute-start.19 = (f32[11,8,128]{2,1,0:T(8,128)S(1)}, f32[11,8,128]{2,1,0:T(8,128)S(1)}, u32[]{:S(2)}, u32[]{:S(2)}) collective-permute-start(f32[11,8,128]{2,1,0:T(8,128)S(1)} %get-tuple-element.39), channel_id=1, source_target_pairs={{0,8},{4,12},{8,0},{12,4},{1,9},{5,13},{9,1},{13,5},{2,10},{6,14},... | collective-permute-start | bytes 135176 | tf_op jit(solution)/shard_map/ppermute | solution.py:432
  80.4 2.8 %collective-permute-start.20 = (f32[11,8,128]{2,1,0:T(8,128)S(1)}, f32[11,8,128]{2,1,0:T(8,128)S(1)}, u32[]{:S(2)}, u32[]{:S(2)}) collective-permute-start(f32[11,8,128]{2,1,0:T(8,128)S(1)} %get-tuple-element.40), channel_id=1, source_target_pairs={{0,12},{4,0},{8,4},{12,8},{1,13},{5,1},{9,5},{13,9},{2,14},{6,2},{... | collective-permute-start | bytes 135176 | tf_op jit(solution)/shard_map/ppermute | solution.py:432
  84.1 1.5 %collective-permute-done.19 = f32[11,8,128]{2,1,0:T(8,128)S(1)} collective-permute-done((f32[11,8,128]{2,1,0:T(8,128)S(1)}, f32[11,8,128]{2,1,0:T(8,128)S(1)}, u32[]{:S(2)}, u32[]{:S(2)}) %collective-permute-start.19) | collective-permute-done | bytes 45088 | tf_op jit(solution)/shard_map/ppermute | solution.py:432
  87.9 1.6 %collective-permute-done.23.refs_3_ = f32[11,8,128]{2,1,0:T(8,128)S(1)} collective-permute-done((f32[11,8,128]{2,1,0:T(8,128)S(1)}, f32[11,8,128]{2,1,0:T(8,128)S(1)}, u32[]{:S(2)}, u32[]{:S(2)}) %collective-permute-start.23) | collective-permute-done | bytes 45088 | tf_op jit(solution)/shard_map/ppermute | solution.py:427
  89.5 1.6 %collective-permute-done.21.refs_1_ = f32[11,8,128]{2,1,0:T(8,128)S(1)} collective-permute-done((f32[11,8,128]{2,1,0:T(8,128)S(1)}, f32[11,8,128]{2,1,0:T(8,128)S(1)}, u32[]{:S(2)}, u32[]{:S(2)}) %collective-permute-start.21) | collective-permute-done | bytes 45088 | tf_op jit(solution)/shard_map/ppermute | solution.py:420
  (50 shorter events, 12.3 us)
Async XLA Ops:
  2.2 7.2 %collective-permute-start.2 = (f32[12,8,128]{2,1,0:T(8,128)S(1)}, f32[12,8,128]{2,1,0:T(8,128)S(1)}, u32[]{:S(2)}, u32[]{:S(2)}) collective-permute-start(f32[12,8,128]{2,1,0:T(8,128)S(1)} %pack.1.refs_0_), channel_id=1, source_target_pairs={{0,12},{4,0},{8,4},{12,8},{1,13},{5,1},{9,5},{13,9},{2,14},{6,2},{... | collective-permute-start | bytes 147464 | tf_op jit(solution)/shard_map/ppermute | solution.py:432
  7.3 5.0 %collective-permute-start.1 = (f32[12,8,128]{2,1,0:T(8,128)S(1)}, f32[12,8,128]{2,1,0:T(8,128)S(1)}, u32[]{:S(2)}, u32[]{:S(2)}) collective-permute-start(f32[12,8,128]{2,1,0:T(8,128)S(1)} %pack.1.refs_0_), channel_id=1, source_target_pairs={{0,8},{4,12},{8,0},{12,4},{1,9},{5,13},{9,1},{13,5},{2,10},{6,14},... | collective-permute-start | bytes 147464 | tf_op jit(solution)/shard_map/ppermute | solution.py:432
  7.3 5.9 %collective-permute-start = (f32[12,8,128]{2,1,0:T(8,128)S(1)}, f32[12,8,128]{2,1,0:T(8,128)S(1)}, u32[]{:S(2)}, u32[]{:S(2)}) collective-permute-start(f32[12,8,128]{2,1,0:T(8,128)S(1)} %pack.1.refs_0_), channel_id=1, source_target_pairs={{0,4},{4,8},{8,12},{12,0},{1,5},{5,9},{9,13},{13,1},{2,6},{6,10},{... | collective-permute-start | bytes 147464 | tf_op jit(solution)/shard_map/ppermute | solution.py:432
  14.0 5.8 %collective-permute-start.3 = (f32[11,16,128]{2,1,0:T(8,128)S(1)}, f32[11,16,128]{2,1,0:T(8,128)S(1)}, u32[]{:S(2)}, u32[]{:S(2)}) collective-permute-start(f32[11,16,128]{2,1,0:T(8,128)S(1)} %get-tuple-element.24.refs_0_), channel_id=1, source_target_pairs={{0,2},{2,0},{1,3},{3,1},{4,6},{6,4},{5,7},{7,5},{8,10},{10,8},{9,1... | collective-permute-start | bytes 270344 | tf_op jit(solution)/shard_map/ppermute | solution.py:420
  15.6 4.2 %collective-permute-start.5 = (f32[7,16,128]{2,1,0:T(8,128)S(1)}, f32[7,16,128]{2,1,0:T(8,128)S(1)}, u32[]{:S(2)}, u32[]{:S(2)}) collective-permute-start(f32[7,16,128]{2,1,0:T(8,128)S(1)} %get-tuple-element.25), channel_id=1, source_target_pairs={{0,3},{1,2},{2,1},{3,0},{4,7},{5,6},{6,5},{7,4},{8,11},{9,10},{10,... | collective-permute-start | bytes 172040 | tf_op jit(solution)/shard_map/ppermute | solution.py:427
  15.6 4.2 %collective-permute-start.4 = (f32[7,16,128]{2,1,0:T(8,128)S(1)}, f32[7,16,128]{2,1,0:T(8,128)S(1)}, u32[]{:S(2)}, u32[]{:S(2)}) collective-permute-start(f32[7,16,128]{2,1,0:T(8,128)S(1)} %get-tuple-element.25), channel_id=1, source_target_pairs={{0,1},{1,0},{2,3},{3,2},{4,5},{5,4},{6,7},{7,6},{8,9},{9,8},{10,11... | collective-permute-start | bytes 172040 | tf_op jit(solution)/shard_map/ppermute | solution.py:427
  34.9 5.3 %collective-permute-start.6 = (f32[11,16,128]{2,1,0:T(8,128)S(1)}, f32[11,16,128]{2,1,0:T(8,128)S(1)}, u32[]{:S(2)}, u32[]{:S(2)}) collective-permute-start(f32[11,16,128]{2,1,0:T(8,128)S(1)} %get-tuple-element.27), channel_id=1, source_target_pairs={{0,2},{2,0},{1,3},{3,1},{4,6},{6,4},{5,7},{7,5},{8,10},{10,8},{9,1... | collective-permute-start | bytes 270344 | tf_op jit(solution)/shard_map/ppermute | solution.py:420
  35.8 1.3 %collective-permute-start.7 = (f32[7,16,128]{2,1,0:T(8,128)S(1)}, f32[7,16,128]{2,1,0:T(8,128)S(1)}, u32[]{:S(2)}, u32[]{:S(2)}) collective-permute-start(f32[7,16,128]{2,1,0:T(8,128)S(1)} %get-tuple-element.28), channel_id=1, source_target_pairs={{0,1},{1,0},{2,3},{3,2},{4,5},{5,4},{6,7},{7,6},{8,9},{9,8},{10,11... | collective-permute-start | bytes 172040 | tf_op jit(solution)/shard_map/ppermute | solution.py:427
  36.0 4.1 %collective-permute-start.8 = (f32[7,16,128]{2,1,0:T(8,128)S(1)}, f32[7,16,128]{2,1,0:T(8,128)S(1)}, u32[]{:S(2)}, u32[]{:S(2)}) collective-permute-start(f32[7,16,128]{2,1,0:T(8,128)S(1)} %get-tuple-element.29), channel_id=1, source_target_pairs={{0,3},{1,2},{2,1},{3,0},{4,7},{5,6},{6,5},{7,4},{8,11},{9,10},{10,... | collective-permute-start | bytes 172040 | tf_op jit(solution)/shard_map/ppermute | solution.py:427
  40.2 5.0 %collective-permute-start.11 = (f32[11,16,128]{2,1,0:T(8,128)S(1)}, f32[11,16,128]{2,1,0:T(8,128)S(1)}, u32[]{:S(2)}, u32[]{:S(2)}) collective-permute-start(f32[11,16,128]{2,1,0:T(8,128)S(1)} %pad_add_fusion.1.refs_0_), channel_id=1, source_target_pairs={{0,12},{4,0},{8,4},{12,8},{1,13},{5,1},{9,5},{13,9},{2,14},{6,2},{... | collective-permute-start | bytes 270344 | tf_op jit(solution)/shard_map/ppermute | solution.py:432
  41.5 9.5 %collective-permute-start.10 = (f32[11,16,128]{2,1,0:T(8,128)S(1)}, f32[11,16,128]{2,1,0:T(8,128)S(1)}, u32[]{:S(2)}, u32[]{:S(2)}) collective-permute-start(f32[11,16,128]{2,1,0:T(8,128)S(1)} %pad_add_fusion.1.refs_0_), channel_id=1, source_target_pairs={{0,8},{4,12},{8,0},{12,4},{1,9},{5,13},{9,1},{13,5},{2,10},{6,14},... | collective-permute-start | bytes 270344 | tf_op jit(solution)/shard_map/ppermute | solution.py:432
  41.5 9.5 %collective-permute-start.9 = (f32[11,16,128]{2,1,0:T(8,128)S(1)}, f32[11,16,128]{2,1,0:T(8,128)S(1)}, u32[]{:S(2)}, u32[]{:S(2)}) collective-permute-start(f32[11,16,128]{2,1,0:T(8,128)S(1)} %pad_add_fusion.1.refs_0_), channel_id=1, source_target_pairs={{0,4},{4,8},{8,12},{12,0},{1,5},{5,9},{9,13},{13,1},{2,6},{6,10},{... | collective-permute-start | bytes 270344 | tf_op jit(solution)/shard_map/ppermute | solution.py:432
  51.3 5.4 %collective-permute-start.12 = (f32[11,16,128]{2,1,0:T(8,128)S(1)}, f32[11,16,128]{2,1,0:T(8,128)S(1)}, u32[]{:S(2)}, u32[]{:S(2)}) collective-permute-start(f32[11,16,128]{2,1,0:T(8,128)S(1)} %get-tuple-element.31.refs_4_), channel_id=1, source_target_pairs={{0,2},{2,0},{1,3},{3,1},{4,6},{6,4},{5,7},{7,5},{8,10},{10,8},{9,1... | collective-permute-start | bytes 270344 | tf_op jit(solution)/shard_map/ppermute | solution.py:420
  52.6 4.2 %collective-permute-start.14 = (f32[7,16,128]{2,1,0:T(8,128)S(1)}, f32[7,16,128]{2,1,0:T(8,128)S(1)}, u32[]{:S(2)}, u32[]{:S(2)}) collective-permute-start(f32[7,16,128]{2,1,0:T(8,128)S(1)} %get-tuple-element.32), channel_id=1, source_target_pairs={{0,3},{1,2},{2,1},{3,0},{4,7},{5,6},{6,5},{7,4},{8,11},{9,10},{10,... | collective-permute-start | bytes 172040 | tf_op jit(solution)/shard_map/ppermute | solution.py:427
  52.6 4.2 %collective-permute-start.13 = (f32[7,16,128]{2,1,0:T(8,128)S(1)}, f32[7,16,128]{2,1,0:T(8,128)S(1)}, u32[]{:S(2)}, u32[]{:S(2)}) collective-permute-start(f32[7,16,128]{2,1,0:T(8,128)S(1)} %get-tuple-element.32), channel_id=1, source_target_pairs={{0,1},{1,0},{2,3},{3,2},{4,5},{5,4},{6,7},{7,6},{8,9},{9,8},{10,11... | collective-permute-start | bytes 172040 | tf_op jit(solution)/shard_map/ppermute | solution.py:427
  71.9 5.4 %collective-permute-start.15 = (f32[11,16,128]{2,1,0:T(8,128)S(1)}, f32[11,16,128]{2,1,0:T(8,128)S(1)}, u32[]{:S(2)}, u32[]{:S(2)}) collective-permute-start(f32[11,16,128]{2,1,0:T(8,128)S(1)} %get-tuple-element.34), channel_id=1, source_target_pairs={{0,2},{2,0},{1,3},{3,1},{4,6},{6,4},{5,7},{7,5},{8,10},{10,8},{9,1... | collective-permute-start | bytes 270344 | tf_op jit(solution)/shard_map/ppermute | solution.py:420
  72.9 1.2 %collective-permute-start.16 = (f32[7,16,128]{2,1,0:T(8,128)S(1)}, f32[7,16,128]{2,1,0:T(8,128)S(1)}, u32[]{:S(2)}, u32[]{:S(2)}) collective-permute-start(f32[7,16,128]{2,1,0:T(8,128)S(1)} %get-tuple-element.35), channel_id=1, source_target_pairs={{0,1},{1,0},{2,3},{3,2},{4,5},{5,4},{6,7},{7,6},{8,9},{9,8},{10,11... | collective-permute-start | bytes 172040 | tf_op jit(solution)/shard_map/ppermute | solution.py:427
  73.1 4.2 %collective-permute-start.17 = (f32[7,16,128]{2,1,0:T(8,128)S(1)}, f32[7,16,128]{2,1,0:T(8,128)S(1)}, u32[]{:S(2)}, u32[]{:S(2)}) collective-permute-start(f32[7,16,128]{2,1,0:T(8,128)S(1)} %get-tuple-element.36), channel_id=1, source_target_pairs={{0,3},{1,2},{2,1},{3,0},{4,7},{5,6},{6,5},{7,4},{8,11},{9,10},{10,... | collective-permute-start | bytes 172040 | tf_op jit(solution)/shard_map/ppermute | solution.py:427
  78.1 6.0 %collective-permute-start.18 = (f32[11,8,128]{2,1,0:T(8,128)S(1)}, f32[11,8,128]{2,1,0:T(8,128)S(1)}, u32[]{:S(2)}, u32[]{:S(2)}) collective-permute-start(f32[11,8,128]{2,1,0:T(8,128)S(1)} %get-tuple-element.38), channel_id=1, source_target_pairs={{0,4},{4,8},{8,12},{12,0},{1,5},{5,9},{9,13},{13,1},{2,6},{6,10},{... | collective-permute-start | bytes 135176 | tf_op jit(solution)/shard_map/ppermute | solution.py:432
  78.5 7.2 %collective-permute-start.19 = (f32[11,8,128]{2,1,0:T(8,128)S(1)}, f32[11,8,128]{2,1,0:T(8,128)S(1)}, u32[]{:S(2)}, u32[]{:S(2)}) collective-permute-start(f32[11,8,128]{2,1,0:T(8,128)S(1)} %get-tuple-element.39), channel_id=1, source_target_pairs={{0,8},{4,12},{8,0},{12,4},{1,9},{5,13},{9,1},{13,5},{2,10},{6,14},... | collective-permute-start | bytes 135176 | tf_op jit(solution)/shard_map/ppermute | solution.py:432
  80.4 5.2 %collective-permute-start.20 = (f32[11,8,128]{2,1,0:T(8,128)S(1)}, f32[11,8,128]{2,1,0:T(8,128)S(1)}, u32[]{:S(2)}, u32[]{:S(2)}) collective-permute-start(f32[11,8,128]{2,1,0:T(8,128)S(1)} %get-tuple-element.40), channel_id=1, source_target_pairs={{0,12},{4,0},{8,4},{12,8},{1,13},{5,1},{9,5},{13,9},{2,14},{6,2},{... | collective-permute-start | bytes 135176 | tf_op jit(solution)/shard_map/ppermute | solution.py:432
  85.7 3.8 %collective-permute-start.23 = (f32[11,8,128]{2,1,0:T(8,128)S(1)}, f32[11,8,128]{2,1,0:T(8,128)S(1)}, u32[]{:S(2)}, u32[]{:S(2)}) collective-permute-start(f32[11,8,128]{2,1,0:T(8,128)S(1)} %add_add_fusion.refs_0_), channel_id=1, source_target_pairs={{0,3},{1,2},{2,1},{3,0},{4,7},{5,6},{6,5},{7,4},{8,11},{9,10},{10,... | collective-permute-start | bytes 135176 | tf_op jit(solution)/shard_map/ppermute | solution.py:427
  86.2 3.3 %collective-permute-start.22 = (f32[11,8,128]{2,1,0:T(8,128)S(1)}, f32[11,8,128]{2,1,0:T(8,128)S(1)}, u32[]{:S(2)}, u32[]{:S(2)}) collective-permute-start(f32[11,8,128]{2,1,0:T(8,128)S(1)} %add_add_fusion.refs_0_), channel_id=1, source_target_pairs={{0,1},{1,0},{2,3},{3,2},{4,5},{5,4},{6,7},{7,6},{8,9},{9,8},{10,11... | collective-permute-start | bytes 135176 | tf_op jit(solution)/shard_map/ppermute | solution.py:427
  87.1 4.0 %collective-permute-start.21 = (f32[11,8,128]{2,1,0:T(8,128)S(1)}, f32[11,8,128]{2,1,0:T(8,128)S(1)}, u32[]{:S(2)}, u32[]{:S(2)}) collective-permute-start(f32[11,8,128]{2,1,0:T(8,128)S(1)} %add_add_fusion.refs_0_), channel_id=1, source_target_pairs={{0,2},{2,0},{1,3},{3,1},{4,6},{6,4},{5,7},{7,5},{8,10},{10,8},{9,1... | collective-permute-start | bytes 135176 | tf_op jit(solution)/shard_map/ppermute | solution.py:420
  (7 other events, 58.4 us)

commit v5 on v2

--- a/solution.py
+++ b/solution.py
@@ -71,24 +71,35 @@
     return pltpu.CompilerParams(vmem_limit_bytes=mib * MIB)
 
 
-def pack_kernel(layout, spacing, lists_ref, params_ref, out_ref):
+def pack_kernel(layout, spacing, lists_hbm, params_hbm, out_ref, lists_ref, positions, fetched, sems):
     shared_rows, rows, pieces = layout
     band, epoch = lax.axis_index("band"), lax.axis_index("epoch")
-    for b in range(BANDS):
-        for q in range(len(pieces)):
-
-            @pl.when((band == b) & (epoch == q))
-            def _():
-                for p, entry in enumerate(pieces[q]):
-                    if entry is None:
-                        out_ref[p] = jnp.zeros(out_ref.shape[1:], F32)
-                        continue
-                    row, position = row_of(b, entry)
-                    value = params_ref[row]
-                    if position is not None:
-                        value = spacing * params_ref[position] + value
-                    out_ref[p] = value
-
+    lists_copy = pltpu.make_async_copy(lists_hbm, lists_ref, sems.at[0])
+    lists_copy.start()
+    positions_copy = pltpu.make_async_copy(params_hbm.at[pl.ds(0, 2)], positions, sems.at[1])
+    positions_copy.start()
+
+    def pick_row(p):
+        row, position = jnp.int32(0), jnp.int32(2)
+        for b in range(BANDS):
+            for q, piece in enumerate(pieces):
+                if piece[p] is None:
+                    continue
+                mine = (band == b) & (epoch == q)
+                its_row, its_position = row_of(b, piece[p])
+                row = jnp.where(mine, its_row, row)
+                if its_position is not None:
+                    position = jnp.where(mine, its_position, position)
+        return row, position
+
+    chosen = [pick_row(p) for p in range(rows)]
+    copies = [
+        pltpu.make_async_copy(params_hbm.at[row], fetched.at[p], sems.at[2 + p])
+        for p, (row, _) in enumerate(chosen)
+    ]
+    for copy in copies:
+        copy.start()
+    lists_copy.wait()
     tiles, slots = lists_ref.shape
     lane = lax.broadcasted_iota(jnp.int32, (8, 128), 1)
     ids = jnp.zeros((8, 128), jnp.int32)
@@ -96,6 +107,11 @@
         for s in range(slots):
             ids = jnp.where(lane == t * slots + s, lists_ref[t, s], ids)
     out_ref[rows] = ids.astype(F32)
+    positions_copy.wait()
+    for p, (copy, (_, position)) in enumerate(zip(copies, chosen)):
+        copy.wait()
+        added = jnp.where(position == 0, positions[0], jnp.where(position == 1, positions[1], 0.0))
+        out_ref[p] = spacing * added + fetched[p]
 
 
 def select_kernel(layout, lists_ref, *refs):
@@ -205,8 +221,12 @@
         return jnp.concatenate([hi, (x - hi.astype(F32)).astype(BF16)], axis=0)
 
     def stack(x):
-        both = cut(x)
-        return jnp.concatenate([both, both], axis=1)
+        hi = x.astype(BF16)
+        return jnp.concatenate([hi, hi], axis=1), (x - hi.astype(F32)).astype(BF16)
+
+    def times(left, right):
+        near = jnp.dot(left[0], right, preferred_element_type=F32)
+        return near + jnp.dot(left[1], right[:pixels], preferred_element_type=F32)
 
     def total(x):
         return jnp.sum(x, axis=0, keepdims=True)
@@ -256,10 +276,8 @@
                 for first in range(0, COMPS, 2):
                     here = min(2, COMPS - first)
                     span = pl.ds(first * 128, 128 * here)
-                    by_x = jnp.dot(left_x, pieces_y[s, :, span], preferred_element_type=F32)
-                    by_y = jnp.dot(left_y, pieces_x[s, :, span], preferred_element_type=F32)
-                    by_x = by_x[:pixels] + by_x[pixels:]
-                    by_y = by_y[:pixels] + by_y[pixels:]
+                    by_x = times(left_x, pieces_y[s, :, span])
+                    by_y = times(left_y, pieces_x[s, :, span])
                     for n in range(here):
                         c = first + n
                         d = grid - (line(0, c, g) + off_x)
@@ -285,8 +303,8 @@
         wide_x, wide_y = jnp.exp(2.0 * (lw + an)), jnp.exp(2.0 * (lw - an))
         inv_x, inv_y = 1.0 / (wide_x + psf * psf), 1.0 / (wide_y + psf * psf)
         amp = amps[c]
-        var_x = keep(sums[1, c] * inv_x * inv_x * wide_x)
-        var_y = keep(amp * sums[3, c] * inv_y * inv_y * wide_y)
+        var_x = keep(sums[1, c] * inv_x * (inv_x * wide_x))
+        var_y = keep(amp * sums[3, c] * inv_y * (inv_y * wide_y))
         shared[row(0, c)] = keep(sums[0, c] * inv_x)
         shared[row(1, c)] = keep(amp * sums[2, c] * inv_y)
         shared[row(2, c)] = var_x + var_y
@@ -437,9 +455,15 @@
     packed = pl.pallas_call(
         functools.partial(pack_kernel, layout, spacing),
         out_shape=f32(rows + 1, blocks, sources),
-        in_specs=[smem(), vmem()],
+        in_specs=[pl.BlockSpec(memory_space=pltpu.HBM)] * 2,
         out_specs=vmem(),
-        compiler_params=params(),
+        scratch_shapes=[
+            pltpu.SMEM((tiles, slots), jnp.int32),
+            pltpu.VMEM((2, blocks, sources), F32),
+            pltpu.VMEM((rows, blocks, sources), F32),
+            pltpu.SemaphoreType.DMA((rows + 2,)),
+        ],
+        compiler_params=params(56),
         name="pack",
     )(block_lists, by_row)
     got = round_tiles([packed] * owners)

time: 89.4 us -> 89.3 us (level)
  Pallas kernels: 19 us -> 26.4 us
  starting transfers between devices: 35.6 us -> 30.7 us
  waiting for transfers between devices: 32.2 us -> 29.6 us
    pallas_call x2, Pallas kernels: 15.7 us -> 22.1 us  [step_gradient(): pl.pallas_call(functools.partial(step_kernel, layout, later), out_shape=[...]
    ppermute x9, starting transfers between devices: 24.6 us -> 19.8 us  [round_tiles(): lax.ppermute(arrays[k], 'tile', [(i, (i + k) % owners) for i in range(own...]
    ppermute x9, waiting for transfers between devices: 16.4 us -> 13.8 us  [round_tiles(): lax.ppermute(arrays[k], 'tile', [(i, (i + k) % owners) for i in range(own...]
    pallas_call x1, Pallas kernels: 0.59 us -> 1.61 us  [shards(): pl.pallas_call(functools.partial(pack_kernel, layout, spacing), out_shape...]
  transfers between devices with their start and end apart: 24 -> 24, of which waited for: 15 -> 12; matrix products, arithmetic and copies ran while one was open for 0% -> 0% of each run, Pallas kernels for 0% -> 0%
where the time goes in v5:
time: 89.3 us; the launch traced here: 88.4 us
  starting transfers between devices  30.7 us (34%)
  waiting for transfers between devices  29.6 us (33%)
  Pallas kernels  26.4 us (30%)
    pallas_call x2, Pallas kernels, step_gradient(): pl.pallas_call(functools.partial(step_kernel, layout, later), out_shape=[...  22.1 us
    ppermute x9, starting transfers between devices, round_tiles(): lax.ppermute(arrays[k], 'tile', [(i, (i + k) % owners) for i in range(own...  19.8 us
    ppermute x10, waiting for transfers between devices, to_peers(): kept.append(lax.ppermute(other[k], ('epoch', 'band'), pairs))  14.1 us
    ppermute x9, waiting for transfers between devices, round_tiles(): lax.ppermute(arrays[k], 'tile', [(i, (i + k) % owners) for i in range(own...  13.8 us
    ppermute x10, starting transfers between devices, to_peers(): kept.append(lax.ppermute(other[k], ('epoch', 'band'), pairs))  5.56 us
    ppermute x5, starting transfers between devices, to_peers(): lax.ppermute(same[k], 'epoch', [(i, (i + k) % epochs) for i in range(epoc...  5.4 us
  transfers between devices with their start and end apart: 24, of which 12 were waited for; matrix products, arithmetic and copies ran while one was open for 0% of the time, Pallas kernels for 0%

profile of v5, /device:TPU:0, one launch (start us, length us, event | category | flops | bytes accessed | tf_op | source)
XLA Modules:
  0.0 88.4 jit_solution(15127561757625726954)
XLA Ops:
  0.0 1.6 %pack.1.refs_0_ = f32[12,8,128]{2,1,0:T(8,128)} custom-call(s32[2,8]{1,0:T(2,128)} %lists_ref.3, f32[44,8,128]{2,1,0:T(8,128)} %bitcast.3), custom_call_target="tpu_custom_call" | custom-call | tf_op jit(solution)/shard_map/pack/pallas_call | solution.py:455
  1.6 5.1 %collective-permute-start.2 = (f32[12,8,128]{2,1,0:T(8,128)}, f32[12,8,128]{2,1,0:T(8,128)S(1)}, u32[]{:S(2)}, u32[]{:S(2)}) collective-permute-start(f32[12,8,128]{2,1,0:T(8,128)} %pack.1.refs_0_), channel_id=1, source_target_pairs={{0,12},{4,0},{8,4},{12,8},{1,13},{5,1},{9,5},{13,9},{2,14},{6,2},{... | collective-permute-start | bytes 147464 | tf_op jit(solution)/shard_map/ppermute | solution.py:441
  6.7 1.0 %collective-permute-start = (f32[12,8,128]{2,1,0:T(8,128)}, f32[12,8,128]{2,1,0:T(8,128)S(1)}, u32[]{:S(2)}, u32[]{:S(2)}) collective-permute-start(f32[12,8,128]{2,1,0:T(8,128)} %pack.1.refs_0_), channel_id=1, source_target_pairs={{0,4},{4,8},{8,12},{12,0},{1,5},{5,9},{9,13},{13,1},{2,6},{6,10},{... | collective-permute-start | bytes 147464 | tf_op jit(solution)/shard_map/ppermute | solution.py:441
  7.8 1.4 %collective-permute-done.2.refs_3_ = f32[12,8,128]{2,1,0:T(8,128)S(1)} collective-permute-done((f32[12,8,128]{2,1,0:T(8,128)}, f32[12,8,128]{2,1,0:T(8,128)S(1)}, u32[]{:S(2)}, u32[]{:S(2)}) %collective-permute-start.2) | collective-permute-done | bytes 49184 | tf_op jit(solution)/shard_map/ppermute | solution.py:441
  9.1 2.8 %collective-permute-done.1.refs_2_ = f32[12,8,128]{2,1,0:T(8,128)S(1)} collective-permute-done((f32[12,8,128]{2,1,0:T(8,128)}, f32[12,8,128]{2,1,0:T(8,128)S(1)}, u32[]{:S(2)}, u32[]{:S(2)}) %collective-permute-start.1) | collective-permute-done | bytes 49184 | tf_op jit(solution)/shard_map/ppermute | solution.py:441
  14.4 1.5 %collective-permute-start.3 = (f32[11,16,128]{2,1,0:T(8,128)S(1)}, f32[11,16,128]{2,1,0:T(8,128)S(1)}, u32[]{:S(2)}, u32[]{:S(2)}) collective-permute-start(f32[11,16,128]{2,1,0:T(8,128)S(1)} %get-tuple-element.24.refs_0_), channel_id=1, source_target_pairs={{0,2},{2,0},{1,3},{3,1},{4,6},{6,4},{5,7},{7,5},{8,10},{10,8},{9,1... | collective-permute-start | bytes 270344 | tf_op jit(solution)/shard_map/ppermute | solution.py:429
  17.3 2.9 %collective-permute-done.5.refs_3_ = f32[7,16,128]{2,1,0:T(8,128)S(1)} collective-permute-done((f32[7,16,128]{2,1,0:T(8,128)S(1)}, f32[7,16,128]{2,1,0:T(8,128)S(1)}, u32[]{:S(2)}, u32[]{:S(2)}) %collective-permute-start.5) | collective-permute-done | bytes 57376 | tf_op jit(solution)/shard_map/ppermute | solution.py:436
  20.2 11.0 %first_step.1 = (f32[11,16,128]{2,1,0:T(8,128)S(1)}, f32[11,16,128]{2,1,0:T(8,128)S(1)}, f32[7,16,128]{2,1,0:T(8,128)S(1)}, f32[7,16,128]{2,1,0:T(8,128)S(1)}) custom-call(s32[2]{0:T(128)S(1)} %copy-done.6, s32[2,2,8]{2,1,0:T(2,128)S(1)} %bitcast.5, f32[1,1]{1,0:T(1,128)S(6)} %copy.8.psf_ref, f32[2,1,1,128,128]{4,3,2,1,0:T(8,128)S(1)} %copy-done.1, ...), custom_call_target="tpu_custom_call" | custom-call | tf_op jit(solution)/shard_map/first_step/pallas_call | solution.py:338
  32.4 1.1 %collective-permute-start.8 = (f32[7,16,128]{2,1,0:T(8,128)S(1)}, f32[7,16,128]{2,1,0:T(8,128)S(1)}, u32[]{:S(2)}, u32[]{:S(2)}) collective-permute-start(f32[7,16,128]{2,1,0:T(8,128)S(1)} %get-tuple-element.29), channel_id=1, source_target_pairs={{0,3},{1,2},{2,1},{3,0},{4,7},{5,6},{6,5},{7,4},{8,11},{9,10},{10,... | collective-permute-start | bytes 172040 | tf_op jit(solution)/shard_map/ppermute | solution.py:436
  33.5 3.0 %collective-permute-done.8 = f32[7,16,128]{2,1,0:T(8,128)S(1)} collective-permute-done((f32[7,16,128]{2,1,0:T(8,128)S(1)}, f32[7,16,128]{2,1,0:T(8,128)S(1)}, u32[]{:S(2)}, u32[]{:S(2)}) %collective-permute-start.8) | collective-permute-done | bytes 57376 | tf_op jit(solution)/shard_map/ppermute | solution.py:436
  36.7 4.5 %collective-permute-start.10 = (f32[11,16,128]{2,1,0:T(8,128)S(1)}, f32[11,16,128]{2,1,0:T(8,128)S(1)}, u32[]{:S(2)}, u32[]{:S(2)}) collective-permute-start(f32[11,16,128]{2,1,0:T(8,128)S(1)} %pad_add_fusion.1.refs_0_), channel_id=1, source_target_pairs={{0,8},{4,12},{8,0},{12,4},{1,9},{5,13},{9,1},{13,5},{2,10},{6,14},... | collective-permute-start | bytes 270344 | tf_op jit(solution)/shard_map/ppermute | solution.py:441
  41.2 1.9 %collective-permute-start.9 = (f32[11,16,128]{2,1,0:T(8,128)S(1)}, f32[11,16,128]{2,1,0:T(8,128)S(1)}, u32[]{:S(2)}, u32[]{:S(2)}) collective-permute-start(f32[11,16,128]{2,1,0:T(8,128)S(1)} %pad_add_fusion.1.refs_0_), channel_id=1, source_target_pairs={{0,4},{4,8},{8,12},{12,0},{1,5},{5,9},{9,13},{13,1},{2,6},{6,10},{... | collective-permute-start | bytes 270344 | tf_op jit(solution)/shard_map/ppermute | solution.py:441
  43.1 7.0 %collective-permute-done.10.refs_2_ = f32[11,16,128]{2,1,0:T(8,128)S(1)} collective-permute-done((f32[11,16,128]{2,1,0:T(8,128)S(1)}, f32[11,16,128]{2,1,0:T(8,128)S(1)}, u32[]{:S(2)}, u32[]{:S(2)}) %collective-permute-start.10) | collective-permute-done | bytes 90144 | tf_op jit(solution)/shard_map/ppermute | solution.py:441
  50.5 1.2 %collective-permute-start.12 = (f32[11,16,128]{2,1,0:T(8,128)S(1)}, f32[11,16,128]{2,1,0:T(8,128)S(1)}, u32[]{:S(2)}, u32[]{:S(2)}) collective-permute-start(f32[11,16,128]{2,1,0:T(8,128)S(1)} %get-tuple-element.31.refs_4_), channel_id=1, source_target_pairs={{0,2},{2,0},{1,3},{3,1},{4,6},{6,4},{5,7},{7,5},{8,10},{10,8},{9,1... | collective-permute-start | bytes 270344 | tf_op jit(solution)/shard_map/ppermute | solution.py:429
  52.7 3.2 %collective-permute-done.14.refs_7_ = f32[7,16,128]{2,1,0:T(8,128)S(1)} collective-permute-done((f32[7,16,128]{2,1,0:T(8,128)S(1)}, f32[7,16,128]{2,1,0:T(8,128)S(1)}, u32[]{:S(2)}, u32[]{:S(2)}) %collective-permute-start.14) | collective-permute-done | bytes 57376 | tf_op jit(solution)/shard_map/ppermute | solution.py:436
  55.9 11.1 %later_step.1 = (f32[11,16,128]{2,1,0:T(8,128)S(1)}, f32[11,16,128]{2,1,0:T(8,128)S(1)}, f32[7,16,128]{2,1,0:T(8,128)S(1)}, f32[7,16,128]{2,1,0:T(8,128)S(1)}) custom-call(s32[2]{0:T(128)S(1)} %copy-done.6, s32[2,2,8]{2,1,0:T(2,128)S(1)} %bitcast.6, f32[1,1]{1,0:T(1,128)S(6)} %copy.8.psf_ref, f32[2,1,1,128,128]{4,3,2,1,0:T(8,128)S(1)} %copy-done.1, ...), custom_call_target="tpu_custom_call" | custom-call | tf_op jit(solution)/shard_map/later_step/pallas_call | solution.py:338
  67.0 1.0 %collective-permute-start.15 = (f32[11,16,128]{2,1,0:T(8,128)S(1)}, f32[11,16,128]{2,1,0:T(8,128)S(1)}, u32[]{:S(2)}, u32[]{:S(2)}) collective-permute-start(f32[11,16,128]{2,1,0:T(8,128)S(1)} %get-tuple-element.34), channel_id=1, source_target_pairs={{0,2},{2,0},{1,3},{3,1},{4,6},{6,4},{5,7},{7,5},{8,10},{10,8},{9,1... | collective-permute-start | bytes 270344 | tf_op jit(solution)/shard_map/ppermute | solution.py:429
  69.3 3.1 %collective-permute-done.17 = f32[7,16,128]{2,1,0:T(8,128)S(1)} collective-permute-done((f32[7,16,128]{2,1,0:T(8,128)S(1)}, f32[7,16,128]{2,1,0:T(8,128)S(1)}, u32[]{:S(2)}, u32[]{:S(2)}) %collective-permute-start.17) | collective-permute-done | bytes 57376 | tf_op jit(solution)/shard_map/ppermute | solution.py:436
  73.3 4.2 %collective-permute-start.19 = (f32[11,8,128]{2,1,0:T(8,128)S(1)}, f32[11,8,128]{2,1,0:T(8,128)S(1)}, u32[]{:S(2)}, u32[]{:S(2)}) collective-permute-start(f32[11,8,128]{2,1,0:T(8,128)S(1)} %get-tuple-element.39), channel_id=1, source_target_pairs={{0,8},{4,12},{8,0},{12,4},{1,9},{5,13},{9,1},{13,5},{2,10},{6,14},... | collective-permute-start | bytes 135176 | tf_op jit(solution)/shard_map/ppermute | solution.py:441
  77.5 2.8 %collective-permute-start.20 = (f32[11,8,128]{2,1,0:T(8,128)S(1)}, f32[11,8,128]{2,1,0:T(8,128)S(1)}, u32[]{:S(2)}, u32[]{:S(2)}) collective-permute-start(f32[11,8,128]{2,1,0:T(8,128)S(1)} %get-tuple-element.40), channel_id=1, source_target_pairs={{0,12},{4,0},{8,4},{12,8},{1,13},{5,1},{9,5},{13,9},{2,14},{6,2},{... | collective-permute-start | bytes 135176 | tf_op jit(solution)/shard_map/ppermute | solution.py:441
  80.4 1.7 %collective-permute-done.20 = f32[11,8,128]{2,1,0:T(8,128)S(1)} collective-permute-done((f32[11,8,128]{2,1,0:T(8,128)S(1)}, f32[11,8,128]{2,1,0:T(8,128)S(1)}, u32[]{:S(2)}, u32[]{:S(2)}) %collective-permute-start.20) | collective-permute-done | bytes 45088 | tf_op jit(solution)/shard_map/ppermute | solution.py:441
  82.2 1.5 %collective-permute-start.22 = (f32[11,8,128]{2,1,0:T(8,128)S(1)}, f32[11,8,128]{2,1,0:T(8,128)S(1)}, u32[]{:S(2)}, u32[]{:S(2)}) collective-permute-start(f32[11,8,128]{2,1,0:T(8,128)S(1)} %add_add_fusion.refs_0_), channel_id=1, source_target_pairs={{0,1},{1,0},{2,3},{3,2},{4,5},{5,4},{6,7},{7,6},{8,9},{9,8},{10,11... | collective-permute-start | bytes 135176 | tf_op jit(solution)/shard_map/ppermute | solution.py:436
  84.3 1.8 %collective-permute-done.23.refs_3_ = f32[11,8,128]{2,1,0:T(8,128)S(1)} collective-permute-done((f32[11,8,128]{2,1,0:T(8,128)S(1)}, f32[11,8,128]{2,1,0:T(8,128)S(1)}, u32[]{:S(2)}, u32[]{:S(2)}) %collective-permute-start.23) | collective-permute-done | bytes 45088 | tf_op jit(solution)/shard_map/ppermute | solution.py:436
  86.1 1.6 %collective-permute-done.21.refs_1_ = f32[11,8,128]{2,1,0:T(8,128)S(1)} collective-permute-done((f32[11,8,128]{2,1,0:T(8,128)S(1)}, f32[11,8,128]{2,1,0:T(8,128)S(1)}, u32[]{:S(2)}, u32[]{:S(2)}) %collective-permute-start.21) | collective-permute-done | bytes 45088 | tf_op jit(solution)/shard_map/ppermute | solution.py:429
  (50 shorter events, 9.3 us)
Async XLA Ops:
  1.6 7.5 %collective-permute-start.2 = (f32[12,8,128]{2,1,0:T(8,128)}, f32[12,8,128]{2,1,0:T(8,128)S(1)}, u32[]{:S(2)}, u32[]{:S(2)}) collective-permute-start(f32[12,8,128]{2,1,0:T(8,128)} %pack.1.refs_0_), channel_id=1, source_target_pairs={{0,12},{4,0},{8,4},{12,8},{1,13},{5,1},{9,5},{13,9},{2,14},{6,2},{... | collective-permute-start | bytes 147464 | tf_op jit(solution)/shard_map/ppermute | solution.py:441
  6.7 5.2 %collective-permute-start.1 = (f32[12,8,128]{2,1,0:T(8,128)}, f32[12,8,128]{2,1,0:T(8,128)S(1)}, u32[]{:S(2)}, u32[]{:S(2)}) collective-permute-start(f32[12,8,128]{2,1,0:T(8,128)} %pack.1.refs_0_), channel_id=1, source_target_pairs={{0,8},{4,12},{8,0},{12,4},{1,9},{5,13},{9,1},{13,5},{2,10},{6,14},... | collective-permute-start | bytes 147464 | tf_op jit(solution)/shard_map/ppermute | solution.py:441
  6.7 6.1 %collective-permute-start = (f32[12,8,128]{2,1,0:T(8,128)}, f32[12,8,128]{2,1,0:T(8,128)S(1)}, u32[]{:S(2)}, u32[]{:S(2)}) collective-permute-start(f32[12,8,128]{2,1,0:T(8,128)} %pack.1.refs_0_), channel_id=1, source_target_pairs={{0,4},{4,8},{8,12},{12,0},{1,5},{5,9},{9,13},{13,1},{2,6},{6,10},{... | collective-permute-start | bytes 147464 | tf_op jit(solution)/shard_map/ppermute | solution.py:441
  14.4 5.8 %collective-permute-start.3 = (f32[11,16,128]{2,1,0:T(8,128)S(1)}, f32[11,16,128]{2,1,0:T(8,128)S(1)}, u32[]{:S(2)}, u32[]{:S(2)}) collective-permute-start(f32[11,16,128]{2,1,0:T(8,128)S(1)} %get-tuple-element.24.refs_0_), channel_id=1, source_target_pairs={{0,2},{2,0},{1,3},{3,1},{4,6},{6,4},{5,7},{7,5},{8,10},{10,8},{9,1... | collective-permute-start | bytes 270344 | tf_op jit(solution)/shard_map/ppermute | solution.py:429
  16.0 4.2 %collective-permute-start.5 = (f32[7,16,128]{2,1,0:T(8,128)S(1)}, f32[7,16,128]{2,1,0:T(8,128)S(1)}, u32[]{:S(2)}, u32[]{:S(2)}) collective-permute-start(f32[7,16,128]{2,1,0:T(8,128)S(1)} %get-tuple-element.25), channel_id=1, source_target_pairs={{0,3},{1,2},{2,1},{3,0},{4,7},{5,6},{6,5},{7,4},{8,11},{9,10},{10,... | collective-permute-start | bytes 172040 | tf_op jit(solution)/shard_map/ppermute | solution.py:436
  16.0 4.2 %collective-permute-start.4 = (f32[7,16,128]{2,1,0:T(8,128)S(1)}, f32[7,16,128]{2,1,0:T(8,128)S(1)}, u32[]{:S(2)}, u32[]{:S(2)}) collective-permute-start(f32[7,16,128]{2,1,0:T(8,128)S(1)} %get-tuple-element.25), channel_id=1, source_target_pairs={{0,1},{1,0},{2,3},{3,2},{4,5},{5,4},{6,7},{7,6},{8,9},{9,8},{10,11... | collective-permute-start | bytes 172040 | tf_op jit(solution)/shard_map/ppermute | solution.py:436
  31.3 5.3 %collective-permute-start.6 = (f32[11,16,128]{2,1,0:T(8,128)S(1)}, f32[11,16,128]{2,1,0:T(8,128)S(1)}, u32[]{:S(2)}, u32[]{:S(2)}) collective-permute-start(f32[11,16,128]{2,1,0:T(8,128)S(1)} %get-tuple-element.27), channel_id=1, source_target_pairs={{0,2},{2,0},{1,3},{3,1},{4,6},{6,4},{5,7},{7,5},{8,10},{10,8},{9,1... | collective-permute-start | bytes 270344 | tf_op jit(solution)/shard_map/ppermute | solution.py:429
  32.2 1.3 %collective-permute-start.7 = (f32[7,16,128]{2,1,0:T(8,128)S(1)}, f32[7,16,128]{2,1,0:T(8,128)S(1)}, u32[]{:S(2)}, u32[]{:S(2)}) collective-permute-start(f32[7,16,128]{2,1,0:T(8,128)S(1)} %get-tuple-element.28), channel_id=1, source_target_pairs={{0,1},{1,0},{2,3},{3,2},{4,5},{5,4},{6,7},{7,6},{8,9},{9,8},{10,11... | collective-permute-start | bytes 172040 | tf_op jit(solution)/shard_map/ppermute | solution.py:436
  32.4 4.1 %collective-permute-start.8 = (f32[7,16,128]{2,1,0:T(8,128)S(1)}, f32[7,16,128]{2,1,0:T(8,128)S(1)}, u32[]{:S(2)}, u32[]{:S(2)}) collective-permute-start(f32[7,16,128]{2,1,0:T(8,128)S(1)} %get-tuple-element.29), channel_id=1, source_target_pairs={{0,3},{1,2},{2,1},{3,0},{4,7},{5,6},{6,5},{7,4},{8,11},{9,10},{10,... | collective-permute-start | bytes 172040 | tf_op jit(solution)/shard_map/ppermute | solution.py:436
  36.6 6.5 %collective-permute-start.11 = (f32[11,16,128]{2,1,0:T(8,128)S(1)}, f32[11,16,128]{2,1,0:T(8,128)S(1)}, u32[]{:S(2)}, u32[]{:S(2)}) collective-permute-start(f32[11,16,128]{2,1,0:T(8,128)S(1)} %pad_add_fusion.1.refs_0_), channel_id=1, source_target_pairs={{0,12},{4,0},{8,4},{12,8},{1,13},{5,1},{9,5},{13,9},{2,14},{6,2},{... | collective-permute-start | bytes 270344 | tf_op jit(solution)/shard_map/ppermute | solution.py:441
  36.7 13.5 %collective-permute-start.10 = (f32[11,16,128]{2,1,0:T(8,128)S(1)}, f32[11,16,128]{2,1,0:T(8,128)S(1)}, u32[]{:S(2)}, u32[]{:S(2)}) collective-permute-start(f32[11,16,128]{2,1,0:T(8,128)S(1)} %pad_add_fusion.1.refs_0_), channel_id=1, source_target_pairs={{0,8},{4,12},{8,0},{12,4},{1,9},{5,13},{9,1},{13,5},{2,10},{6,14},... | collective-permute-start | bytes 270344 | tf_op jit(solution)/shard_map/ppermute | solution.py:441
  41.2 9.0 %collective-permute-start.9 = (f32[11,16,128]{2,1,0:T(8,128)S(1)}, f32[11,16,128]{2,1,0:T(8,128)S(1)}, u32[]{:S(2)}, u32[]{:S(2)}) collective-permute-start(f32[11,16,128]{2,1,0:T(8,128)S(1)} %pad_add_fusion.1.refs_0_), channel_id=1, source_target_pairs={{0,4},{4,8},{8,12},{12,0},{1,5},{5,9},{9,13},{13,1},{2,6},{6,10},{... | collective-permute-start | bytes 270344 | tf_op jit(solution)/shard_map/ppermute | solution.py:441
  50.5 5.4 %collective-permute-start.12 = (f32[11,16,128]{2,1,0:T(8,128)S(1)}, f32[11,16,128]{2,1,0:T(8,128)S(1)}, u32[]{:S(2)}, u32[]{:S(2)}) collective-permute-start(f32[11,16,128]{2,1,0:T(8,128)S(1)} %get-tuple-element.31.refs_4_), channel_id=1, source_target_pairs={{0,2},{2,0},{1,3},{3,1},{4,6},{6,4},{5,7},{7,5},{8,10},{10,8},{9,1... | collective-permute-start | bytes 270344 | tf_op jit(solution)/shard_map/ppermute | solution.py:429
  51.8 4.2 %collective-permute-start.14 = (f32[7,16,128]{2,1,0:T(8,128)S(1)}, f32[7,16,128]{2,1,0:T(8,128)S(1)}, u32[]{:S(2)}, u32[]{:S(2)}) collective-permute-start(f32[7,16,128]{2,1,0:T(8,128)S(1)} %get-tuple-element.32), channel_id=1, source_target_pairs={{0,3},{1,2},{2,1},{3,0},{4,7},{5,6},{6,5},{7,4},{8,11},{9,10},{10,... | collective-permute-start | bytes 172040 | tf_op jit(solution)/shard_map/ppermute | solution.py:436
  51.8 4.1 %collective-permute-start.13 = (f32[7,16,128]{2,1,0:T(8,128)S(1)}, f32[7,16,128]{2,1,0:T(8,128)S(1)}, u32[]{:S(2)}, u32[]{:S(2)}) collective-permute-start(f32[7,16,128]{2,1,0:T(8,128)S(1)} %get-tuple-element.32), channel_id=1, source_target_pairs={{0,1},{1,0},{2,3},{3,2},{4,5},{5,4},{6,7},{7,6},{8,9},{9,8},{10,11... | collective-permute-start | bytes 172040 | tf_op jit(solution)/shard_map/ppermute | solution.py:436
  67.0 5.4 %collective-permute-start.15 = (f32[11,16,128]{2,1,0:T(8,128)S(1)}, f32[11,16,128]{2,1,0:T(8,128)S(1)}, u32[]{:S(2)}, u32[]{:S(2)}) collective-permute-start(f32[11,16,128]{2,1,0:T(8,128)S(1)} %get-tuple-element.34), channel_id=1, source_target_pairs={{0,2},{2,0},{1,3},{3,1},{4,6},{6,4},{5,7},{7,5},{8,10},{10,8},{9,1... | collective-permute-start | bytes 270344 | tf_op jit(solution)/shard_map/ppermute | solution.py:429
  68.1 1.2 %collective-permute-start.16 = (f32[7,16,128]{2,1,0:T(8,128)S(1)}, f32[7,16,128]{2,1,0:T(8,128)S(1)}, u32[]{:S(2)}, u32[]{:S(2)}) collective-permute-start(f32[7,16,128]{2,1,0:T(8,128)S(1)} %get-tuple-element.35), channel_id=1, source_target_pairs={{0,1},{1,0},{2,3},{3,2},{4,5},{5,4},{6,7},{7,6},{8,9},{9,8},{10,11... | collective-permute-start | bytes 172040 | tf_op jit(solution)/shard_map/ppermute | solution.py:436
  68.2 4.1 %collective-permute-start.17 = (f32[7,16,128]{2,1,0:T(8,128)S(1)}, f32[7,16,128]{2,1,0:T(8,128)S(1)}, u32[]{:S(2)}, u32[]{:S(2)}) collective-permute-start(f32[7,16,128]{2,1,0:T(8,128)S(1)} %get-tuple-element.36), channel_id=1, source_target_pairs={{0,3},{1,2},{2,1},{3,0},{4,7},{5,6},{6,5},{7,4},{8,11},{9,10},{10,... | collective-permute-start | bytes 172040 | tf_op jit(solution)/shard_map/ppermute | solution.py:436
  73.2 7.1 %collective-permute-start.18 = (f32[11,8,128]{2,1,0:T(8,128)S(1)}, f32[11,8,128]{2,1,0:T(8,128)S(1)}, u32[]{:S(2)}, u32[]{:S(2)}) collective-permute-start(f32[11,8,128]{2,1,0:T(8,128)S(1)} %get-tuple-element.38), channel_id=1, source_target_pairs={{0,4},{4,8},{8,12},{12,0},{1,5},{5,9},{9,13},{13,1},{2,6},{6,10},{... | collective-permute-start | bytes 135176 | tf_op jit(solution)/shard_map/ppermute | solution.py:441
  73.3 7.1 %collective-permute-start.19 = (f32[11,8,128]{2,1,0:T(8,128)S(1)}, f32[11,8,128]{2,1,0:T(8,128)S(1)}, u32[]{:S(2)}, u32[]{:S(2)}) collective-permute-start(f32[11,8,128]{2,1,0:T(8,128)S(1)} %get-tuple-element.39), channel_id=1, source_target_pairs={{0,8},{4,12},{8,0},{12,4},{1,9},{5,13},{9,1},{13,5},{2,10},{6,14},... | collective-permute-start | bytes 135176 | tf_op jit(solution)/shard_map/ppermute | solution.py:441
  77.5 4.6 %collective-permute-start.20 = (f32[11,8,128]{2,1,0:T(8,128)S(1)}, f32[11,8,128]{2,1,0:T(8,128)S(1)}, u32[]{:S(2)}, u32[]{:S(2)}) collective-permute-start(f32[11,8,128]{2,1,0:T(8,128)S(1)} %get-tuple-element.40), channel_id=1, source_target_pairs={{0,12},{4,0},{8,4},{12,8},{1,13},{5,1},{9,5},{13,9},{2,14},{6,2},{... | collective-permute-start | bytes 135176 | tf_op jit(solution)/shard_map/ppermute | solution.py:441
  82.1 4.0 %collective-permute-start.23 = (f32[11,8,128]{2,1,0:T(8,128)S(1)}, f32[11,8,128]{2,1,0:T(8,128)S(1)}, u32[]{:S(2)}, u32[]{:S(2)}) collective-permute-start(f32[11,8,128]{2,1,0:T(8,128)S(1)} %add_add_fusion.refs_0_), channel_id=1, source_target_pairs={{0,3},{1,2},{2,1},{3,0},{4,7},{5,6},{6,5},{7,4},{8,11},{9,10},{10,... | collective-permute-start | bytes 135176 | tf_op jit(solution)/shard_map/ppermute | solution.py:436
  82.2 3.9 %collective-permute-start.22 = (f32[11,8,128]{2,1,0:T(8,128)S(1)}, f32[11,8,128]{2,1,0:T(8,128)S(1)}, u32[]{:S(2)}, u32[]{:S(2)}) collective-permute-start(f32[11,8,128]{2,1,0:T(8,128)S(1)} %add_add_fusion.refs_0_), channel_id=1, source_target_pairs={{0,1},{1,0},{2,3},{3,2},{4,5},{5,4},{6,7},{7,6},{8,9},{9,8},{10,11... | collective-permute-start | bytes 135176 | tf_op jit(solution)/shard_map/ppermute | solution.py:436
  83.7 4.0 %collective-permute-start.21 = (f32[11,8,128]{2,1,0:T(8,128)S(1)}, f32[11,8,128]{2,1,0:T(8,128)S(1)}, u32[]{:S(2)}, u32[]{:S(2)}) collective-permute-start(f32[11,8,128]{2,1,0:T(8,128)S(1)} %add_add_fusion.refs_0_), channel_id=1, source_target_pairs={{0,2},{2,0},{1,3},{3,1},{4,6},{6,4},{5,7},{7,5},{8,10},{10,8},{9,1... | collective-permute-start | bytes 135176 | tf_op jit(solution)/shard_map/ppermute | solution.py:429
  (7 other events, 74.9 us)

commit v6 on v2

--- a/solution.py
+++ b/solution.py
@@ -157,7 +157,7 @@
     taken = 2 * epochs * (2 if later else 1)
     ins, refs = refs[:taken], refs[taken:]
     outs, refs = refs[: 2 * epochs], refs[2 * epochs :]
-    shared, amps, derived, prof_x, prof_y, pieces_x, pieces_y, image, sums, half, other = refs[:11]
+    shared, amps, derived, pieces_x, pieces_y, image, sums, half, other = refs[:9]
     band, epoch = lax.axis_index("band"), lax.axis_index("epoch")
     tiles = data_ref.shape[0]
     pixels = data_ref.shape[-1]
@@ -172,7 +172,7 @@
         return r // HALF, r % HALF
 
     if later:
-        moved, moved_amps = refs[11:]
+        moved, moved_amps = refs[9:]
         put_together(layout, band, epoch, ins[2 * epochs :], half, other, moved, moved_amps)
         for k in range(4):
             shift = 0.0
@@ -205,8 +205,12 @@
         return jnp.concatenate([hi, (x - hi.astype(F32)).astype(BF16)], axis=0)
 
     def stack(x):
-        both = cut(x)
-        return jnp.concatenate([both, both], axis=1)
+        hi = x.astype(BF16)
+        return jnp.concatenate([hi, hi], axis=1), (x - hi.astype(F32)).astype(BF16)
+
+    def times(left, right):
+        near = jnp.dot(left[0], right, preferred_element_type=F32)
+        return near + jnp.dot(left[1], right[:pixels], preferred_element_type=F32)
 
     def total(x):
         return jnp.sum(x, axis=0, keepdims=True)
@@ -228,11 +232,9 @@
                 for c in range(COMPS):
                     d = grid - (line(0, c, g) + off_x)
                     e = jnp.exp2(d * d * line(2, c, g))
-                    prof_x[s * COMPS + c] = e
                     pieces_x[s, :, c * 128 : (c + 1) * 128] = cut(e)
                     d = grid - (line(1, c, g) + off_y)
                     e = jnp.exp2(d * d * line(3, c, g))
-                    prof_y[s * COMPS + c] = e
                     pieces_y[s, :, c * 128 : (c + 1) * 128] = cut(e * line(4, c, g))
                 image[...] += lax.dot_general(
                     pieces_x[s], pieces_y[s], (((1,), (1,)), ((), ())), preferred_element_type=F32
@@ -256,19 +258,17 @@
                 for first in range(0, COMPS, 2):
                     here = min(2, COMPS - first)
                     span = pl.ds(first * 128, 128 * here)
-                    by_x = jnp.dot(left_x, pieces_y[s, :, span], preferred_element_type=F32)
-                    by_y = jnp.dot(left_y, pieces_x[s, :, span], preferred_element_type=F32)
-                    by_x = by_x[:pixels] + by_x[pixels:]
-                    by_y = by_y[:pixels] + by_y[pixels:]
+                    by_x = times(left_x, pieces_y[s, :, span])
+                    by_y = times(left_y, pieces_x[s, :, span])
                     for n in range(here):
                         c = first + n
                         d = grid - (line(0, c, g) + off_x)
-                        e = prof_x[s * COMPS + c] * by_x[:, n * 128 : (n + 1) * 128]
+                        e = jnp.exp2(d * d * line(2, c, g)) * by_x[:, n * 128 : (n + 1) * 128]
                         e1 = e * d
                         sums[0, c, pl.ds(g, 1), :] = total(e1)
                         sums[1, c, pl.ds(g, 1), :] = total(e1 * d)
                         d = grid - (line(1, c, g) + off_y)
-                        e = prof_y[s * COMPS + c] * by_y[:, n * 128 : (n + 1) * 128]
+                        e = jnp.exp2(d * d * line(3, c, g)) * by_y[:, n * 128 : (n + 1) * 128]
                         e1 = e * d
                         sums[2, c, pl.ds(g, 1), :] = total(e1)
                         sums[3, c, pl.ds(g, 1), :] = total(e1 * d)
@@ -285,8 +285,8 @@
         wide_x, wide_y = jnp.exp(2.0 * (lw + an)), jnp.exp(2.0 * (lw - an))
         inv_x, inv_y = 1.0 / (wide_x + psf * psf), 1.0 / (wide_y + psf * psf)
         amp = amps[c]
-        var_x = keep(sums[1, c] * inv_x * inv_x * wide_x)
-        var_y = keep(amp * sums[3, c] * inv_y * inv_y * wide_y)
+        var_x = keep(sums[1, c] * inv_x * (inv_x * wide_x))
+        var_y = keep(amp * sums[3, c] * inv_y * (inv_y * wide_y))
         shared[row(0, c)] = keep(sums[0, c] * inv_x)
         shared[row(1, c)] = keep(amp * sums[2, c] * inv_y)
         shared[row(2, c)] = var_x + var_y
@@ -325,8 +325,6 @@
         scratch_shapes=together
         + [
             pltpu.VMEM((5, COMPS, wide, 128), F32),
-            pltpu.VMEM((slots * COMPS, pixels, 128), F32),
-            pltpu.VMEM((slots * COMPS, pixels, 128), F32),
             pltpu.VMEM((slots, 2 * pixels, COMPS * 128), BF16),
             pltpu.VMEM((slots, 2 * pixels, COMPS * 128), BF16),
             pltpu.VMEM((2 * pixels, 2 * pixels), F32),

time: 89.4 us -> 91.3 us (1.021)
  Pallas kernels: 19 us -> 26.6 us
  starting transfers between devices: 35.6 us -> 28.1 us
  waiting for transfers between devices: 32.2 us -> 33.3 us
    pallas_call x2, Pallas kernels: 15.7 us -> 23.3 us  [step_gradient(): pl.pallas_call(functools.partial(step_kernel, layout, later), out_shape=[...]
    ppermute x9, starting transfers between devices: 24.6 us -> 17.1 us  [round_tiles(): lax.ppermute(arrays[k], 'tile', [(i, (i + k) % owners) for i in range(own...]
    ppermute x9, waiting for transfers between devices: 16.4 us -> 17.6 us  [round_tiles(): lax.ppermute(arrays[k], 'tile', [(i, (i + k) % owners) for i in range(own...]
where the time goes in v6:
time: 91.3 us; the launch traced here: 90.4 us
  waiting for transfers between devices  33.3 us (36%)
  starting transfers between devices  28.1 us (31%)
  Pallas kernels  26.6 us (29%)
  local copies, waits for them, and re-layouts  1.63 us (2%)
    pallas_call x2, Pallas kernels, step_gradient(): pl.pallas_call(functools.partial(step_kernel, layout, later), out_shape=[...  23.3 us
    ppermute x9, waiting for transfers between devices, round_tiles(): lax.ppermute(arrays[k], 'tile', [(i, (i + k) % owners) for i in range(own...  17.6 us
    ppermute x9, starting transfers between devices, round_tiles(): lax.ppermute(arrays[k], 'tile', [(i, (i + k) % owners) for i in range(own...  17.1 us
    ppermute x10, waiting for transfers between devices, to_peers(): kept.append(lax.ppermute(other[k], ('epoch', 'band'), pairs))  14.1 us
    ppermute x5, starting transfers between devices, to_peers(): lax.ppermute(same[k], 'epoch', [(i, (i + k) % epochs) for i in range(epoc...  5.55 us
    ppermute x10, starting transfers between devices, to_peers(): kept.append(lax.ppermute(other[k], ('epoch', 'band'), pairs))  5.42 us
  transfers between devices with their start and end apart: 24, of which 15 were waited for; matrix products, arithmetic and copies ran while one was open for 0% of the time, Pallas kernels for 0%

profile of v6, /device:TPU:0, one launch (start us, length us, event | category | flops | bytes accessed | tf_op | source)
XLA Modules:
  0.0 90.4 jit_solution(9531911297581685615)
XLA Ops:
  2.2 5.1 %collective-permute-start.2 = (f32[12,8,128]{2,1,0:T(8,128)S(1)}, f32[12,8,128]{2,1,0:T(8,128)S(1)}, u32[]{:S(2)}, u32[]{:S(2)}) collective-permute-start(f32[12,8,128]{2,1,0:T(8,128)S(1)} %pack.1.refs_0_), channel_id=1, source_target_pairs={{0,12},{4,0},{8,4},{12,8},{1,13},{5,1},{9,5},{13,9},{2,14},{6,2},{... | collective-permute-start | bytes 147464 | tf_op jit(solution)/shard_map/ppermute | solution.py:421
  7.3 1.0 %collective-permute-start = (f32[12,8,128]{2,1,0:T(8,128)S(1)}, f32[12,8,128]{2,1,0:T(8,128)S(1)}, u32[]{:S(2)}, u32[]{:S(2)}) collective-permute-start(f32[12,8,128]{2,1,0:T(8,128)S(1)} %pack.1.refs_0_), channel_id=1, source_target_pairs={{0,4},{4,8},{8,12},{12,0},{1,5},{5,9},{9,13},{13,1},{2,6},{6,10},{... | collective-permute-start | bytes 147464 | tf_op jit(solution)/shard_map/ppermute | solution.py:421
  8.3 1.0 %collective-permute-done.2.refs_3_ = f32[12,8,128]{2,1,0:T(8,128)S(1)} collective-permute-done((f32[12,8,128]{2,1,0:T(8,128)S(1)}, f32[12,8,128]{2,1,0:T(8,128)S(1)}, u32[]{:S(2)}, u32[]{:S(2)}) %collective-permute-start.2) | collective-permute-done | bytes 49184 | tf_op jit(solution)/shard_map/ppermute | solution.py:421
  9.4 2.9 %collective-permute-done.1.refs_2_ = f32[12,8,128]{2,1,0:T(8,128)S(1)} collective-permute-done((f32[12,8,128]{2,1,0:T(8,128)S(1)}, f32[12,8,128]{2,1,0:T(8,128)S(1)}, u32[]{:S(2)}, u32[]{:S(2)}) %collective-permute-start.1) | collective-permute-done | bytes 49184 | tf_op jit(solution)/shard_map/ppermute | solution.py:421
  14.0 1.5 %collective-permute-start.3 = (f32[11,16,128]{2,1,0:T(8,128)S(1)}, f32[11,16,128]{2,1,0:T(8,128)S(1)}, u32[]{:S(2)}, u32[]{:S(2)}) collective-permute-start(f32[11,16,128]{2,1,0:T(8,128)S(1)} %get-tuple-element.24.refs_0_), channel_id=1, source_target_pairs={{0,2},{2,0},{1,3},{3,1},{4,6},{6,4},{5,7},{7,5},{8,10},{10,8},{9,1... | collective-permute-start | bytes 270344 | tf_op jit(solution)/shard_map/ppermute | solution.py:409
  16.9 2.9 %collective-permute-done.5.refs_3_ = f32[7,16,128]{2,1,0:T(8,128)S(1)} collective-permute-done((f32[7,16,128]{2,1,0:T(8,128)S(1)}, f32[7,16,128]{2,1,0:T(8,128)S(1)}, u32[]{:S(2)}, u32[]{:S(2)}) %collective-permute-start.5) | collective-permute-done | bytes 57376 | tf_op jit(solution)/shard_map/ppermute | solution.py:416
  19.8 11.6 %first_step.1 = (f32[11,16,128]{2,1,0:T(8,128)S(1)}, f32[11,16,128]{2,1,0:T(8,128)S(1)}, f32[7,16,128]{2,1,0:T(8,128)S(1)}, f32[7,16,128]{2,1,0:T(8,128)S(1)}) custom-call(s32[2]{0:T(128)S(1)} %copy-done.6, s32[2,2,8]{2,1,0:T(2,128)S(1)} %bitcast.5, f32[1,1]{1,0:T(1,128)S(6)} %copy.8.psf_ref, f32[2,1,1,128,128]{4,3,2,1,0:T(8,128)S(1)} %copy-done.2, ...), custom_call_target="tpu_custom_call" | custom-call | tf_op jit(solution)/shard_map/first_step/pallas_call | solution.py:320
  31.4 0.9 %collective-permute-start.6 = (f32[11,16,128]{2,1,0:T(8,128)S(1)}, f32[11,16,128]{2,1,0:T(8,128)S(1)}, u32[]{:S(2)}, u32[]{:S(2)}) collective-permute-start(f32[11,16,128]{2,1,0:T(8,128)S(1)} %get-tuple-element.27), channel_id=1, source_target_pairs={{0,2},{2,0},{1,3},{3,1},{4,6},{6,4},{5,7},{7,5},{8,10},{10,8},{9,1... | collective-permute-start | bytes 270344 | tf_op jit(solution)/shard_map/ppermute | solution.py:409
  32.5 1.1 %collective-permute-start.8 = (f32[7,16,128]{2,1,0:T(8,128)S(1)}, f32[7,16,128]{2,1,0:T(8,128)S(1)}, u32[]{:S(2)}, u32[]{:S(2)}) collective-permute-start(f32[7,16,128]{2,1,0:T(8,128)S(1)} %get-tuple-element.29), channel_id=1, source_target_pairs={{0,3},{1,2},{2,1},{3,0},{4,7},{5,6},{6,5},{7,4},{8,11},{9,10},{10,... | collective-permute-start | bytes 172040 | tf_op jit(solution)/shard_map/ppermute | solution.py:416
  33.6 3.0 %collective-permute-done.8 = f32[7,16,128]{2,1,0:T(8,128)S(1)} collective-permute-done((f32[7,16,128]{2,1,0:T(8,128)S(1)}, f32[7,16,128]{2,1,0:T(8,128)S(1)}, u32[]{:S(2)}, u32[]{:S(2)}) %collective-permute-start.8) | collective-permute-done | bytes 57376 | tf_op jit(solution)/shard_map/ppermute | solution.py:416
  36.8 4.8 %collective-permute-start.11 = (f32[11,16,128]{2,1,0:T(8,128)S(1)}, f32[11,16,128]{2,1,0:T(8,128)S(1)}, u32[]{:S(2)}, u32[]{:S(2)}) collective-permute-start(f32[11,16,128]{2,1,0:T(8,128)S(1)} %pad_add_fusion.1.refs_0_), channel_id=1, source_target_pairs={{0,12},{4,0},{8,4},{12,8},{1,13},{5,1},{9,5},{13,9},{2,14},{6,2},{... | collective-permute-start | bytes 270344 | tf_op jit(solution)/shard_map/ppermute | solution.py:421
  42.2 2.3 %collective-permute-done.11.refs_3_ = f32[11,16,128]{2,1,0:T(8,128)S(1)} collective-permute-done((f32[11,16,128]{2,1,0:T(8,128)S(1)}, f32[11,16,128]{2,1,0:T(8,128)S(1)}, u32[]{:S(2)}, u32[]{:S(2)}) %collective-permute-start.11) | collective-permute-done | bytes 90144 | tf_op jit(solution)/shard_map/ppermute | solution.py:421
  44.5 6.1 %collective-permute-done.10.refs_2_ = f32[11,16,128]{2,1,0:T(8,128)S(1)} collective-permute-done((f32[11,16,128]{2,1,0:T(8,128)S(1)}, f32[11,16,128]{2,1,0:T(8,128)S(1)}, u32[]{:S(2)}, u32[]{:S(2)}) %collective-permute-start.10) | collective-permute-done | bytes 90144 | tf_op jit(solution)/shard_map/ppermute | solution.py:421
  51.0 1.2 %collective-permute-start.12 = (f32[11,16,128]{2,1,0:T(8,128)S(1)}, f32[11,16,128]{2,1,0:T(8,128)S(1)}, u32[]{:S(2)}, u32[]{:S(2)}) collective-permute-start(f32[11,16,128]{2,1,0:T(8,128)S(1)} %get-tuple-element.31.refs_4_), channel_id=1, source_target_pairs={{0,2},{2,0},{1,3},{3,1},{4,6},{6,4},{5,7},{7,5},{8,10},{10,8},{9,1... | collective-permute-start | bytes 270344 | tf_op jit(solution)/shard_map/ppermute | solution.py:409
  53.1 3.2 %collective-permute-done.14.refs_7_ = f32[7,16,128]{2,1,0:T(8,128)S(1)} collective-permute-done((f32[7,16,128]{2,1,0:T(8,128)S(1)}, f32[7,16,128]{2,1,0:T(8,128)S(1)}, u32[]{:S(2)}, u32[]{:S(2)}) %collective-permute-start.14) | collective-permute-done | bytes 57376 | tf_op jit(solution)/shard_map/ppermute | solution.py:416
  56.4 11.7 %later_step.1 = (f32[11,16,128]{2,1,0:T(8,128)S(1)}, f32[11,16,128]{2,1,0:T(8,128)S(1)}, f32[7,16,128]{2,1,0:T(8,128)S(1)}, f32[7,16,128]{2,1,0:T(8,128)S(1)}) custom-call(s32[2]{0:T(128)S(1)} %copy-done.6, s32[2,2,8]{2,1,0:T(2,128)S(1)} %bitcast.6, f32[1,1]{1,0:T(1,128)S(6)} %copy.8.psf_ref, f32[2,1,1,128,128]{4,3,2,1,0:T(8,128)S(1)} %copy-done.2, ...), custom_call_target="tpu_custom_call" | custom-call | tf_op jit(solution)/shard_map/later_step/pallas_call | solution.py:320
  68.1 1.1 %collective-permute-start.15 = (f32[11,16,128]{2,1,0:T(8,128)S(1)}, f32[11,16,128]{2,1,0:T(8,128)S(1)}, u32[]{:S(2)}, u32[]{:S(2)}) collective-permute-start(f32[11,16,128]{2,1,0:T(8,128)S(1)} %get-tuple-element.34), channel_id=1, source_target_pairs={{0,2},{2,0},{1,3},{3,1},{4,6},{6,4},{5,7},{7,5},{8,10},{10,8},{9,1... | collective-permute-start | bytes 270344 | tf_op jit(solution)/shard_map/ppermute | solution.py:409
  69.3 1.0 %collective-permute-start.17 = (f32[7,16,128]{2,1,0:T(8,128)S(1)}, f32[7,16,128]{2,1,0:T(8,128)S(1)}, u32[]{:S(2)}, u32[]{:S(2)}) collective-permute-start(f32[7,16,128]{2,1,0:T(8,128)S(1)} %get-tuple-element.36), channel_id=1, source_target_pairs={{0,3},{1,2},{2,1},{3,0},{4,7},{5,6},{6,5},{7,4},{8,11},{9,10},{10,... | collective-permute-start | bytes 172040 | tf_op jit(solution)/shard_map/ppermute | solution.py:416
  70.4 3.1 %collective-permute-done.17 = f32[7,16,128]{2,1,0:T(8,128)S(1)} collective-permute-done((f32[7,16,128]{2,1,0:T(8,128)S(1)}, f32[7,16,128]{2,1,0:T(8,128)S(1)}, u32[]{:S(2)}, u32[]{:S(2)}) %collective-permute-start.17) | collective-permute-done | bytes 57376 | tf_op jit(solution)/shard_map/ppermute | solution.py:416
  74.4 5.5 %collective-permute-start.19 = (f32[11,8,128]{2,1,0:T(8,128)S(1)}, f32[11,8,128]{2,1,0:T(8,128)S(1)}, u32[]{:S(2)}, u32[]{:S(2)}) collective-permute-start(f32[11,8,128]{2,1,0:T(8,128)S(1)} %get-tuple-element.39), channel_id=1, source_target_pairs={{0,8},{4,12},{8,0},{12,4},{1,9},{5,13},{9,1},{13,5},{2,10},{6,14},... | collective-permute-start | bytes 135176 | tf_op jit(solution)/shard_map/ppermute | solution.py:421
  79.9 2.0 %collective-permute-done.18 = f32[11,8,128]{2,1,0:T(8,128)S(1)} collective-permute-done((f32[11,8,128]{2,1,0:T(8,128)S(1)}, f32[11,8,128]{2,1,0:T(8,128)S(1)}, u32[]{:S(2)}, u32[]{:S(2)}) %collective-permute-start.18) | collective-permute-done | bytes 45088 | tf_op jit(solution)/shard_map/ppermute | solution.py:421
  81.9 1.7 %collective-permute-done.19 = f32[11,8,128]{2,1,0:T(8,128)S(1)} collective-permute-done((f32[11,8,128]{2,1,0:T(8,128)S(1)}, f32[11,8,128]{2,1,0:T(8,128)S(1)}, u32[]{:S(2)}, u32[]{:S(2)}) %collective-permute-start.19) | collective-permute-done | bytes 45088 | tf_op jit(solution)/shard_map/ppermute | solution.py:421
  86.4 1.7 %collective-permute-done.23.refs_3_ = f32[11,8,128]{2,1,0:T(8,128)S(1)} collective-permute-done((f32[11,8,128]{2,1,0:T(8,128)S(1)}, f32[11,8,128]{2,1,0:T(8,128)S(1)}, u32[]{:S(2)}, u32[]{:S(2)}) %collective-permute-start.23) | collective-permute-done | bytes 45088 | tf_op jit(solution)/shard_map/ppermute | solution.py:416
  88.1 1.6 %collective-permute-done.21.refs_1_ = f32[11,8,128]{2,1,0:T(8,128)S(1)} collective-permute-done((f32[11,8,128]{2,1,0:T(8,128)S(1)}, f32[11,8,128]{2,1,0:T(8,128)S(1)}, u32[]{:S(2)}, u32[]{:S(2)}) %collective-permute-start.21) | collective-permute-done | bytes 45088 | tf_op jit(solution)/shard_map/ppermute | solution.py:409
  (50 shorter events, 11.5 us)
Async XLA Ops:
  2.2 7.2 %collective-permute-start.2 = (f32[12,8,128]{2,1,0:T(8,128)S(1)}, f32[12,8,128]{2,1,0:T(8,128)S(1)}, u32[]{:S(2)}, u32[]{:S(2)}) collective-permute-start(f32[12,8,128]{2,1,0:T(8,128)S(1)} %pack.1.refs_0_), channel_id=1, source_target_pairs={{0,12},{4,0},{8,4},{12,8},{1,13},{5,1},{9,5},{13,9},{2,14},{6,2},{... | collective-permute-start | bytes 147464 | tf_op jit(solution)/shard_map/ppermute | solution.py:421
  7.3 5.0 %collective-permute-start.1 = (f32[12,8,128]{2,1,0:T(8,128)S(1)}, f32[12,8,128]{2,1,0:T(8,128)S(1)}, u32[]{:S(2)}, u32[]{:S(2)}) collective-permute-start(f32[12,8,128]{2,1,0:T(8,128)S(1)} %pack.1.refs_0_), channel_id=1, source_target_pairs={{0,8},{4,12},{8,0},{12,4},{1,9},{5,13},{9,1},{13,5},{2,10},{6,14},... | collective-permute-start | bytes 147464 | tf_op jit(solution)/shard_map/ppermute | solution.py:421
  7.3 5.9 %collective-permute-start = (f32[12,8,128]{2,1,0:T(8,128)S(1)}, f32[12,8,128]{2,1,0:T(8,128)S(1)}, u32[]{:S(2)}, u32[]{:S(2)}) collective-permute-start(f32[12,8,128]{2,1,0:T(8,128)S(1)} %pack.1.refs_0_), channel_id=1, source_target_pairs={{0,4},{4,8},{8,12},{12,0},{1,5},{5,9},{9,13},{13,1},{2,6},{6,10},{... | collective-permute-start | bytes 147464 | tf_op jit(solution)/shard_map/ppermute | solution.py:421
  14.0 5.8 %collective-permute-start.3 = (f32[11,16,128]{2,1,0:T(8,128)S(1)}, f32[11,16,128]{2,1,0:T(8,128)S(1)}, u32[]{:S(2)}, u32[]{:S(2)}) collective-permute-start(f32[11,16,128]{2,1,0:T(8,128)S(1)} %get-tuple-element.24.refs_0_), channel_id=1, source_target_pairs={{0,2},{2,0},{1,3},{3,1},{4,6},{6,4},{5,7},{7,5},{8,10},{10,8},{9,1... | collective-permute-start | bytes 270344 | tf_op jit(solution)/shard_map/ppermute | solution.py:409
  15.6 4.2 %collective-permute-start.5 = (f32[7,16,128]{2,1,0:T(8,128)S(1)}, f32[7,16,128]{2,1,0:T(8,128)S(1)}, u32[]{:S(2)}, u32[]{:S(2)}) collective-permute-start(f32[7,16,128]{2,1,0:T(8,128)S(1)} %get-tuple-element.25), channel_id=1, source_target_pairs={{0,3},{1,2},{2,1},{3,0},{4,7},{5,6},{6,5},{7,4},{8,11},{9,10},{10,... | collective-permute-start | bytes 172040 | tf_op jit(solution)/shard_map/ppermute | solution.py:416
  15.6 4.2 %collective-permute-start.4 = (f32[7,16,128]{2,1,0:T(8,128)S(1)}, f32[7,16,128]{2,1,0:T(8,128)S(1)}, u32[]{:S(2)}, u32[]{:S(2)}) collective-permute-start(f32[7,16,128]{2,1,0:T(8,128)S(1)} %get-tuple-element.25), channel_id=1, source_target_pairs={{0,1},{1,0},{2,3},{3,2},{4,5},{5,4},{6,7},{7,6},{8,9},{9,8},{10,11... | collective-permute-start | bytes 172040 | tf_op jit(solution)/shard_map/ppermute | solution.py:416
  31.4 5.3 %collective-permute-start.6 = (f32[11,16,128]{2,1,0:T(8,128)S(1)}, f32[11,16,128]{2,1,0:T(8,128)S(1)}, u32[]{:S(2)}, u32[]{:S(2)}) collective-permute-start(f32[11,16,128]{2,1,0:T(8,128)S(1)} %get-tuple-element.27), channel_id=1, source_target_pairs={{0,2},{2,0},{1,3},{3,1},{4,6},{6,4},{5,7},{7,5},{8,10},{10,8},{9,1... | collective-permute-start | bytes 270344 | tf_op jit(solution)/shard_map/ppermute | solution.py:409
  32.4 1.3 %collective-permute-start.7 = (f32[7,16,128]{2,1,0:T(8,128)S(1)}, f32[7,16,128]{2,1,0:T(8,128)S(1)}, u32[]{:S(2)}, u32[]{:S(2)}) collective-permute-start(f32[7,16,128]{2,1,0:T(8,128)S(1)} %get-tuple-element.28), channel_id=1, source_target_pairs={{0,1},{1,0},{2,3},{3,2},{4,5},{5,4},{6,7},{7,6},{8,9},{9,8},{10,11... | collective-permute-start | bytes 172040 | tf_op jit(solution)/shard_map/ppermute | solution.py:416
  32.5 4.1 %collective-permute-start.8 = (f32[7,16,128]{2,1,0:T(8,128)S(1)}, f32[7,16,128]{2,1,0:T(8,128)S(1)}, u32[]{:S(2)}, u32[]{:S(2)}) collective-permute-start(f32[7,16,128]{2,1,0:T(8,128)S(1)} %get-tuple-element.29), channel_id=1, source_target_pairs={{0,3},{1,2},{2,1},{3,0},{4,7},{5,6},{6,5},{7,4},{8,11},{9,10},{10,... | collective-permute-start | bytes 172040 | tf_op jit(solution)/shard_map/ppermute | solution.py:416
  36.8 7.8 %collective-permute-start.11 = (f32[11,16,128]{2,1,0:T(8,128)S(1)}, f32[11,16,128]{2,1,0:T(8,128)S(1)}, u32[]{:S(2)}, u32[]{:S(2)}) collective-permute-start(f32[11,16,128]{2,1,0:T(8,128)S(1)} %pad_add_fusion.1.refs_0_), channel_id=1, source_target_pairs={{0,12},{4,0},{8,4},{12,8},{1,13},{5,1},{9,5},{13,9},{2,14},{6,2},{... | collective-permute-start | bytes 270344 | tf_op jit(solution)/shard_map/ppermute | solution.py:421
  41.6 9.0 %collective-permute-start.10 = (f32[11,16,128]{2,1,0:T(8,128)S(1)}, f32[11,16,128]{2,1,0:T(8,128)S(1)}, u32[]{:S(2)}, u32[]{:S(2)}) collective-permute-start(f32[11,16,128]{2,1,0:T(8,128)S(1)} %pad_add_fusion.1.refs_0_), channel_id=1, source_target_pairs={{0,8},{4,12},{8,0},{12,4},{1,9},{5,13},{9,1},{13,5},{2,10},{6,14},... | collective-permute-start | bytes 270344 | tf_op jit(solution)/shard_map/ppermute | solution.py:421
  41.6 9.0 %collective-permute-start.9 = (f32[11,16,128]{2,1,0:T(8,128)S(1)}, f32[11,16,128]{2,1,0:T(8,128)S(1)}, u32[]{:S(2)}, u32[]{:S(2)}) collective-permute-start(f32[11,16,128]{2,1,0:T(8,128)S(1)} %pad_add_fusion.1.refs_0_), channel_id=1, source_target_pairs={{0,4},{4,8},{8,12},{12,0},{1,5},{5,9},{9,13},{13,1},{2,6},{6,10},{... | collective-permute-start | bytes 270344 | tf_op jit(solution)/shard_map/ppermute | solution.py:421
  51.0 5.4 %collective-permute-start.12 = (f32[11,16,128]{2,1,0:T(8,128)S(1)}, f32[11,16,128]{2,1,0:T(8,128)S(1)}, u32[]{:S(2)}, u32[]{:S(2)}) collective-permute-start(f32[11,16,128]{2,1,0:T(8,128)S(1)} %get-tuple-element.31.refs_4_), channel_id=1, source_target_pairs={{0,2},{2,0},{1,3},{3,1},{4,6},{6,4},{5,7},{7,5},{8,10},{10,8},{9,1... | collective-permute-start | bytes 270344 | tf_op jit(solution)/shard_map/ppermute | solution.py:409
  52.2 4.2 %collective-permute-start.14 = (f32[7,16,128]{2,1,0:T(8,128)S(1)}, f32[7,16,128]{2,1,0:T(8,128)S(1)}, u32[]{:S(2)}, u32[]{:S(2)}) collective-permute-start(f32[7,16,128]{2,1,0:T(8,128)S(1)} %get-tuple-element.32), channel_id=1, source_target_pairs={{0,3},{1,2},{2,1},{3,0},{4,7},{5,6},{6,5},{7,4},{8,11},{9,10},{10,... | collective-permute-start | bytes 172040 | tf_op jit(solution)/shard_map/ppermute | solution.py:416
  52.4 4.0 %collective-permute-start.13 = (f32[7,16,128]{2,1,0:T(8,128)S(1)}, f32[7,16,128]{2,1,0:T(8,128)S(1)}, u32[]{:S(2)}, u32[]{:S(2)}) collective-permute-start(f32[7,16,128]{2,1,0:T(8,128)S(1)} %get-tuple-element.32), channel_id=1, source_target_pairs={{0,1},{1,0},{2,3},{3,2},{4,5},{5,4},{6,7},{7,6},{8,9},{9,8},{10,11... | collective-permute-start | bytes 172040 | tf_op jit(solution)/shard_map/ppermute | solution.py:416
  68.1 5.4 %collective-permute-start.15 = (f32[11,16,128]{2,1,0:T(8,128)S(1)}, f32[11,16,128]{2,1,0:T(8,128)S(1)}, u32[]{:S(2)}, u32[]{:S(2)}) collective-permute-start(f32[11,16,128]{2,1,0:T(8,128)S(1)} %get-tuple-element.34), channel_id=1, source_target_pairs={{0,2},{2,0},{1,3},{3,1},{4,6},{6,4},{5,7},{7,5},{8,10},{10,8},{9,1... | collective-permute-start | bytes 270344 | tf_op jit(solution)/shard_map/ppermute | solution.py:409
  69.1 1.2 %collective-permute-start.16 = (f32[7,16,128]{2,1,0:T(8,128)S(1)}, f32[7,16,128]{2,1,0:T(8,128)S(1)}, u32[]{:S(2)}, u32[]{:S(2)}) collective-permute-start(f32[7,16,128]{2,1,0:T(8,128)S(1)} %get-tuple-element.35), channel_id=1, source_target_pairs={{0,1},{1,0},{2,3},{3,2},{4,5},{5,4},{6,7},{7,6},{8,9},{9,8},{10,11... | collective-permute-start | bytes 172040 | tf_op jit(solution)/shard_map/ppermute | solution.py:416
  69.3 4.2 %collective-permute-start.17 = (f32[7,16,128]{2,1,0:T(8,128)S(1)}, f32[7,16,128]{2,1,0:T(8,128)S(1)}, u32[]{:S(2)}, u32[]{:S(2)}) collective-permute-start(f32[7,16,128]{2,1,0:T(8,128)S(1)} %get-tuple-element.36), channel_id=1, source_target_pairs={{0,3},{1,2},{2,1},{3,0},{4,7},{5,6},{6,5},{7,4},{8,11},{9,10},{10,... | collective-permute-start | bytes 172040 | tf_op jit(solution)/shard_map/ppermute | solution.py:416
  74.3 7.6 %collective-permute-start.18 = (f32[11,8,128]{2,1,0:T(8,128)S(1)}, f32[11,8,128]{2,1,0:T(8,128)S(1)}, u32[]{:S(2)}, u32[]{:S(2)}) collective-permute-start(f32[11,8,128]{2,1,0:T(8,128)S(1)} %get-tuple-element.38), channel_id=1, source_target_pairs={{0,4},{4,8},{8,12},{12,0},{1,5},{5,9},{9,13},{13,1},{2,6},{6,10},{... | collective-permute-start | bytes 135176 | tf_op jit(solution)/shard_map/ppermute | solution.py:421
  74.4 9.2 %collective-permute-start.19 = (f32[11,8,128]{2,1,0:T(8,128)S(1)}, f32[11,8,128]{2,1,0:T(8,128)S(1)}, u32[]{:S(2)}, u32[]{:S(2)}) collective-permute-start(f32[11,8,128]{2,1,0:T(8,128)S(1)} %get-tuple-element.39), channel_id=1, source_target_pairs={{0,8},{4,12},{8,0},{12,4},{1,9},{5,13},{9,1},{13,5},{2,10},{6,14},... | collective-permute-start | bytes 135176 | tf_op jit(solution)/shard_map/ppermute | solution.py:421
  79.8 4.3 %collective-permute-start.20 = (f32[11,8,128]{2,1,0:T(8,128)S(1)}, f32[11,8,128]{2,1,0:T(8,128)S(1)}, u32[]{:S(2)}, u32[]{:S(2)}) collective-permute-start(f32[11,8,128]{2,1,0:T(8,128)S(1)} %get-tuple-element.40), channel_id=1, source_target_pairs={{0,12},{4,0},{8,4},{12,8},{1,13},{5,1},{9,5},{13,9},{2,14},{6,2},{... | collective-permute-start | bytes 135176 | tf_op jit(solution)/shard_map/ppermute | solution.py:421
  84.2 3.9 %collective-permute-start.23 = (f32[11,8,128]{2,1,0:T(8,128)S(1)}, f32[11,8,128]{2,1,0:T(8,128)S(1)}, u32[]{:S(2)}, u32[]{:S(2)}) collective-permute-start(f32[11,8,128]{2,1,0:T(8,128)S(1)} %add_add_fusion.refs_0_), channel_id=1, source_target_pairs={{0,3},{1,2},{2,1},{3,0},{4,7},{5,6},{6,5},{7,4},{8,11},{9,10},{10,... | collective-permute-start | bytes 135176 | tf_op jit(solution)/shard_map/ppermute | solution.py:416
  84.8 3.3 %collective-permute-start.22 = (f32[11,8,128]{2,1,0:T(8,128)S(1)}, f32[11,8,128]{2,1,0:T(8,128)S(1)}, u32[]{:S(2)}, u32[]{:S(2)}) collective-permute-start(f32[11,8,128]{2,1,0:T(8,128)S(1)} %add_add_fusion.refs_0_), channel_id=1, source_target_pairs={{0,1},{1,0},{2,3},{3,2},{4,5},{5,4},{6,7},{7,6},{8,9},{9,8},{10,11... | collective-permute-start | bytes 135176 | tf_op jit(solution)/shard_map/ppermute | solution.py:416
  85.6 4.0 %collective-permute-start.21 = (f32[11,8,128]{2,1,0:T(8,128)S(1)}, f32[11,8,128]{2,1,0:T(8,128)S(1)}, u32[]{:S(2)}, u32[]{:S(2)}) collective-permute-start(f32[11,8,128]{2,1,0:T(8,128)S(1)} %add_add_fusion.refs_0_), channel_id=1, source_target_pairs={{0,2},{2,0},{1,3},{3,1},{4,6},{6,4},{5,7},{7,5},{8,10},{10,8},{9,1... | collective-permute-start | bytes 135176 | tf_op jit(solution)/shard_map/ppermute | solution.py:409
  (7 other events, 60.7 us)

commit v7 on v6

--- a/solution.py
+++ b/solution.py
@@ -151,58 +151,93 @@
                 amps[i] = half[q, p]
 
 
-def step_kernel(layout, later, counts_ref, offsets_ref, psf_ref, data_ref, weight_ref, *refs):
+def row_at(k, c):
+    r = k * COMPS + c
+    return r // HALF, r % HALF
+
+
+def cut(x):
+    hi = x.astype(BF16)
+    return jnp.concatenate([hi, (x - hi.astype(F32)).astype(BF16)], axis=0)
+
+
+def render_kernel(layout, later, counts_ref, offsets_ref, psf_ref, data_ref, weight_ref, *refs):
     shared_rows, rows, pieces = layout
     epochs = len(pieces)
     taken = 2 * epochs * (2 if later else 1)
     ins, refs = refs[:taken], refs[taken:]
-    outs, refs = refs[: 2 * epochs], refs[2 * epochs :]
-    shared, amps, derived, pieces_x, pieces_y, image, sums, half, other = refs[:9]
+    tiles = data_ref.shape[0]
+    cotangents, shared, amps, derived = refs[:4]
+    pieces_x, pieces_y, refs = refs[4 : 4 + tiles], refs[4 + tiles : 4 + 2 * tiles], refs[4 + 2 * tiles :]
+    image, half, other = refs[:3]
     band, epoch = lax.axis_index("band"), lax.axis_index("epoch")
-    tiles = data_ref.shape[0]
     pixels = data_ref.shape[-1]
     wide = shared.shape[2]
     slots = wide // tiles
     spacing = pixels / 8.0
 
     put_together(layout, band, epoch, ins[: 2 * epochs], half, other, shared, amps)
-
-    def row(k, c):
-        r = k * COMPS + c
-        return r // HALF, r % HALF
-
     if later:
-        moved, moved_amps = refs[9:]
+        moved, moved_amps = refs[3:]
         put_together(layout, band, epoch, ins[2 * epochs :], half, other, moved, moved_amps)
         for k in range(4):
             shift = 0.0
             if k < 2:
-                shift = functools.reduce(lambda a, b: a + b, [moved[row(k, c)] for c in range(COMPS)])
+                shift = functools.reduce(lambda a, b: a + b, [moved[row_at(k, c)] for c in range(COMPS)])
                 shift = shift * (spacing * spacing * POSITION_RATE)
             for c in range(COMPS):
-                shared[row(k, c)] = shared[row(k, c)] - STEP * (moved[row(k, c)] + shift)
+                shared[row_at(k, c)] = shared[row_at(k, c)] - STEP * (moved[row_at(k, c)] + shift)
         for c in range(COMPS):
             amps[c] = amps[c] - STEP * moved_amps[c]
 
     psf = psf_ref[0, 0]
-    line_of = lax.broadcasted_iota(jnp.int32, (wide, 128), 0)
-    live = jnp.zeros((wide, 128), jnp.bool_)
-    for t in range(tiles):
-        live = live | ((line_of >= t * slots) & (line_of < t * slots + counts_ref[t]))
     for c in range(COMPS):
-        lw, an = shared[row(2, c)], shared[row(3, c)]
-        derived[0, c] = shared[row(0, c)]
-        derived[1, c] = shared[row(1, c)]
+        lw, an = shared[row_at(2, c)], shared[row_at(3, c)]
+        derived[0, c] = shared[row_at(0, c)]
+        derived[1, c] = shared[row_at(1, c)]
         derived[2, c] = (-0.5 * LOG2E) / (jnp.exp(2.0 * (lw + an)) + psf * psf)
         derived[3, c] = (-0.5 * LOG2E) / (jnp.exp(2.0 * (lw - an)) + psf * psf)
-        derived[4, c] = jnp.where(live, amps[c], 0.0)
-    sums[...] = jnp.zeros_like(sums)
 
     grid = lax.broadcasted_iota(jnp.int32, (pixels, 128), 0).astype(F32)
 
-    def cut(x):
-        hi = x.astype(BF16)
-        return jnp.concatenate([hi, (x - hi.astype(F32)).astype(BF16)], axis=0)
+    for t in range(tiles):
+        image[...] = jnp.zeros_like(image)
+
+        def render(s, carry):
+            g = t * slots + s
+            off_x = offsets_ref[t, 0, s].astype(F32)
+            off_y = offsets_ref[t, 1, s].astype(F32)
+            for c in range(COMPS):
+                d = grid - (derived[0, c, pl.ds(g, 1), :] + off_x)
+                e = jnp.exp2(d * d * derived[2, c, pl.ds(g, 1), :])
+                pieces_x[t][s, :, c * 128 : (c + 1) * 128] = cut(e)
+                d = grid - (derived[1, c, pl.ds(g, 1), :] + off_y)
+                e = jnp.exp2(d * d * derived[3, c, pl.ds(g, 1), :])
+                pieces_y[t][s, :, c * 128 : (c + 1) * 128] = cut(e * amps[c, pl.ds(g, 1), :])
+            image[...] += lax.dot_general(
+                pieces_x[t][s], pieces_y[t][s], (((1,), (1,)), ((), ())), preferred_element_type=F32
+            )
+            return carry
+
+        lax.fori_loop(0, counts_ref[t], render, 0)
+
+        model = (image[:pixels, :pixels] + image[pixels:, pixels:]) + (
+            image[:pixels, pixels:] + image[pixels:, :pixels]
+        )
+        cotangents[t] = weight_ref[t, 0, 0] * (model - data_ref[t, 0, 0])
+
+
+def pull_kernel(layout, tile, counts_ref, offsets_ref, psf_ref, *refs):
+    shared_rows, rows, pieces = layout
+    epochs = len(pieces)
+    (cotangents, shared, amps, derived, pieces_x, pieces_y), refs = refs[:6], refs[6:]
+    outs, (sums, half, other, grads) = refs[: 2 * epochs], refs[2 * epochs :]
+    band, epoch = lax.axis_index("band"), lax.axis_index("epoch")
+    pixels = cotangents.shape[-1]
+    slots = sums.shape[2]
+    used = counts_ref[tile]
+    cotangent = cotangents[tile]
+    grid = lax.broadcasted_iota(jnp.int32, (pixels, 128), 0).astype(F32)
 
     def stack(x):
         hi = x.astype(BF16)
@@ -215,127 +250,111 @@
     def total(x):
         return jnp.sum(x, axis=0, keepdims=True)
 
-    def line(index, c, s):
-        return derived[index, c, pl.ds(s, 1), :]
-
-    together = 2
-    for t in range(tiles):
-        trips = (counts_ref[t] + together - 1) // together
-        image[...] = jnp.zeros_like(image)
-
-        def render(i, carry):
-            for u in range(together):
-                s = i * together + u
-                g = t * slots + s
-                off_x = offsets_ref[t, 0, s].astype(F32)
-                off_y = offsets_ref[t, 1, s].astype(F32)
-                for c in range(COMPS):
-                    d = grid - (line(0, c, g) + off_x)
-                    e = jnp.exp2(d * d * line(2, c, g))
-                    pieces_x[s, :, c * 128 : (c + 1) * 128] = cut(e)
-                    d = grid - (line(1, c, g) + off_y)
-                    e = jnp.exp2(d * d * line(3, c, g))
-                    pieces_y[s, :, c * 128 : (c + 1) * 128] = cut(e * line(4, c, g))
-                image[...] += lax.dot_general(
-                    pieces_x[s], pieces_y[s], (((1,), (1,)), ((), ())), preferred_element_type=F32
-                )
-            return carry
-
-        lax.fori_loop(0, trips, render, 0)
-
-        model = (image[:pixels, :pixels] + image[pixels:, pixels:]) + (
-            image[:pixels, pixels:] + image[pixels:, :pixels]
-        )
-        cotangent = weight_ref[t, 0, 0] * (model - data_ref[t, 0, 0])
-        left_x, left_y = stack(cotangent), stack(cotangent.T)
-
-        def pull(i, carry):
-            for u in range(together):
-                s = i * together + u
-                g = t * slots + s
-                off_x = offsets_ref[t, 0, s].astype(F32)
-                off_y = offsets_ref[t, 1, s].astype(F32)
-                for first in range(0, COMPS, 2):
-                    here = min(2, COMPS - first)
-                    span = pl.ds(first * 128, 128 * here)
-                    by_x = times(left_x, pieces_y[s, :, span])
-                    by_y = times(left_y, pieces_x[s, :, span])
-                    for n in range(here):
-                        c = first + n
-                        d = grid - (line(0, c, g) + off_x)
-                        e = jnp.exp2(d * d * line(2, c, g)) * by_x[:, n * 128 : (n + 1) * 128]
-                        e1 = e * d
-                        sums[0, c, pl.ds(g, 1), :] = total(e1)
-                        sums[1, c, pl.ds(g, 1), :] = total(e1 * d)
-                        d = grid - (line(1, c, g) + off_y)
-                        e = jnp.exp2(d * d * line(3, c, g)) * by_y[:, n * 128 : (n + 1) * 128]
-                        e1 = e * d
-                        sums[2, c, pl.ds(g, 1), :] = total(e1)
-                        sums[3, c, pl.ds(g, 1), :] = total(e1 * d)
-                        sums[4, c, pl.ds(g, 1), :] = total(e)
-            return carry
-
-        lax.fori_loop(0, trips, pull, 0)
+    left_x, left_y = stack(cotangent), stack(cotangent.T)
+    sums[...] = jnp.zeros_like(sums)
+
+    def pull(s, carry):
+        g = tile * slots + s
+        off_x = offsets_ref[tile, 0, s].astype(F32)
+        off_y = offsets_ref[tile, 1, s].astype(F32)
+        for first in range(0, COMPS, 2):
+            here = min(2, COMPS - first)
+            span = pl.ds(first * 128, 128 * here)
+            by_x = times(left_x, pieces_y[s, :, span])
+            by_y = times(left_y, pieces_x[s, :, span])
+            for n in range(here):
+                c = first + n
+                d = grid - (derived[0, c, pl.ds(g, 1), :] + off_x)
+                e = jnp.exp2(d * d * derived[2, c, pl.ds(g, 1), :]) * by_x[:, n * 128 : (n + 1) * 128]
+                e1 = e * d
+                sums[0, c, pl.ds(s, 1), :] = total(e1)
+                sums[1, c, pl.ds(s, 1), :] = total(e1 * d)
+                d = grid - (derived[1, c, pl.ds(g, 1), :] + off_y)
+                e = jnp.exp2(d * d * derived[3, c, pl.ds(g, 1), :]) * by_y[:, n * 128 : (n + 1) * 128]
+                e1 = e * d
+                sums[2, c, pl.ds(s, 1), :] = total(e1)
+                sums[3, c, pl.ds(s, 1), :] = total(e1 * d)
+                sums[4, c, pl.ds(s, 1), :] = total(e)
+        return carry
+
+    lax.fori_loop(0, used, pull, 0)
+
+    live = lax.broadcasted_iota(jnp.int32, (slots, 128), 0) < used
+    psf = psf_ref[0, 0]
+    at = slice(tile * slots, (tile + 1) * slots)
 
     def keep(x):
         return jnp.where(live, x, 0.0)
 
     for c in range(COMPS):
-        lw, an = shared[row(2, c)], shared[row(3, c)]
+        lw, an = shared[(*row_at(2, c), at)], shared[(*row_at(3, c), at)]
         wide_x, wide_y = jnp.exp(2.0 * (lw + an)), jnp.exp(2.0 * (lw - an))
         inv_x, inv_y = 1.0 / (wide_x + psf * psf), 1.0 / (wide_y + psf * psf)
-        amp = amps[c]
+        amp = amps[c, at]
         var_x = keep(sums[1, c] * inv_x * (inv_x * wide_x))
         var_y = keep(amp * sums[3, c] * inv_y * (inv_y * wide_y))
-        shared[row(0, c)] = keep(sums[0, c] * inv_x)
-        shared[row(1, c)] = keep(amp * sums[2, c] * inv_y)
-        shared[row(2, c)] = var_x + var_y
-        shared[row(3, c)] = var_x - var_y
-        amps[c] = keep(sums[4, c])
-    none = jnp.zeros((wide, 128), F32)
+        grads[row_at(0, c)] = keep(sums[0, c] * inv_x)
+        grads[row_at(1, c)] = keep(amp * sums[2, c] * inv_y)
+        grads[row_at(2, c)] = var_x + var_y
+        grads[row_at(3, c)] = var_x - var_y
+    none = jnp.zeros((slots, 128), F32)
     for q, piece in enumerate(pieces):
         for p, entry in enumerate(piece):
             is_shared = entry is not None and entry[0] == "s"
             if is_shared:
-                half[q, p] = shared[band, entry[1]]
+                half[q, p] = grads[band, entry[1]]
             else:
-                half[q, p] = none if entry is None else amps[entry[1]]
+                half[q, p] = none if entry is None else keep(sums[4, entry[1]])
             if p < shared_rows:
-                other[q, p] = shared[1 - band, entry[1]] if is_shared else none
+                other[q, p] = grads[1 - band, entry[1]] if is_shared else none
     for k in range(epochs):
         outs[k][...] = half[lax.rem(epoch + k, epochs)]
         outs[epochs + k][...] = other[lax.rem(epoch + k, epochs)]
 
 
-def step_gradient(layout, counts, offsets, psf, data, weight, slot_rows, moved):
+def step_gradients(layout, counts, offsets, psf, data, weight, slot_rows, moved):
     shared_rows, rows, pieces = layout
     epochs = len(pieces)
     later = moved is not None
     tiles, _, slots = offsets.shape
     pixels = data.shape[-1]
     wide = tiles * slots
-    shapes = [(rows, wide, 128)] * epochs + [(shared_rows, wide, 128)] * epochs
     ins = slot_rows + (moved or [])
-    together = [pltpu.VMEM((BANDS, HALF, wide, 128), F32), pltpu.VMEM((COMPS, wide, 128), F32)]
-    return pl.pallas_call(
-        functools.partial(step_kernel, layout, later),
-        out_shape=[f32(*s) for s in shapes],
+    shared, amps = (BANDS, HALF, wide, 128), (COMPS, wide, 128)
+    kept = jax.ShapeDtypeStruct((slots, 2 * pixels, COMPS * 128), BF16)
+    cotangents, *rest = pl.pallas_call(
+        functools.partial(render_kernel, layout, later),
+        out_shape=[f32(tiles, pixels, pixels), f32(*shared), f32(*amps), f32(4, *amps)] + [kept] * (2 * tiles),
         in_specs=[smem()] * 3 + [vmem()] * (2 + len(ins)),
-        out_specs=[vmem()] * len(shapes),
-        scratch_shapes=together
-        + [
-            pltpu.VMEM((5, COMPS, wide, 128), F32),
-            pltpu.VMEM((slots, 2 * pixels, COMPS * 128), BF16),
-            pltpu.VMEM((slots, 2 * pixels, COMPS * 128), BF16),
+        out_specs=[vmem()] * (4 + 2 * tiles),
+        scratch_shapes=[
             pltpu.VMEM((2 * pixels, 2 * pixels), F32),
-            pltpu.VMEM((5, COMPS, wide, 128), F32),
             pltpu.VMEM((epochs, rows, wide, 128), F32),
             pltpu.VMEM((epochs, shared_rows, wide, 128), F32),
         ]
-        + (together if later else []),
-        compiler_params=params(32),
-        name="later_step" if later else "first_step",
+        + ([pltpu.VMEM(shared, F32), pltpu.VMEM(amps, F32)] if later else []),
+        compiler_params=params(20),
+        name="later_render" if later else "first_render",
     )(counts, offsets, psf, data, weight, *ins)
+    tables, kept_x, kept_y = rest[:3], rest[3 : 3 + tiles], rest[3 + tiles :]
+    shapes = [(rows, slots, 128)] * epochs + [(shared_rows, slots, 128)] * epochs
+    return [
+        pl.pallas_call(
+            functools.partial(pull_kernel, layout, t),
+            out_shape=[f32(*s) for s in shapes],
+            in_specs=[smem()] * 3 + [vmem()] * 6,
+            out_specs=[vmem()] * len(shapes),
+            scratch_shapes=[
+                pltpu.VMEM((5, COMPS, slots, 128), F32),
+                pltpu.VMEM((epochs, rows, slots, 128), F32),
+                pltpu.VMEM((epochs, shared_rows, slots, 128), F32),
+                pltpu.VMEM((BANDS, HALF, slots, 128), F32),
+            ],
+            compiler_params=params(12),
+            name=f"pull_{t}",
+        )(counts, offsets, psf, cotangents, *tables, kept_x[t], kept_y[t])
+        for t in range(tiles)
+    ]
 
 
 def combine_kernel(layout, match_ref, *refs):
@@ -456,10 +475,12 @@
     slot_rows = spread(slot_piece, slot_short)
 
     def gradient(moved):
-        parts = step_gradient(
+        sums = []
+        for parts in step_gradients(
             layout, block_counts, offsets, psf_width, pixel_data, pixel_weight, slot_rows, moved
-        )
-        return summed(to_peers(parts[:epochs], parts[epochs:]))
+        ):
+            sums.append(summed(to_peers(parts[:epochs], parts[epochs:])))
+        return jnp.concatenate(sums, axis=1)
 
     got = round_tiles([gradient(None)] * owners)
     slot_piece, slot_short, own_first = pl.pallas_call(

time: 91.3 us -> 103 us (1.13)
  Pallas kernels: 26.6 us -> 34.5 us
  starting transfers between devices: 28.1 us -> 32.5 us
  local copies, waits for them, and re-layouts: 1.63 us -> 4.75 us
  waiting for transfers between devices: 33.3 us -> 30.3 us
    pallas_call x2 -> x6, Pallas kernels: 23.3 us -> 31.2 us  [the longest x4 15.9 us: step_gradients(): pl.pallas_call(functools.partial(pull_kernel, layout, t), out_shape=[f32(...]
    ppermute x10 -> x14, waiting for transfers between devices: 14.1 us -> 9.68 us  [to_peers(): kept.append(lax.ppermute(other[k], ('epoch', 'band'), pairs))]
    ppermute x5 -> x7, waiting for transfers between devices: 1.65 us -> 5.1 us  [to_peers(): lax.ppermute(same[k], 'epoch', [(i, (i + k) % epochs) for i in range(epoc...]
    unnamed x14 -> x16, local copies, waits for them, and re-layouts: 1.63 us -> 4.75 us
    ppermute x10 -> x14, starting transfers between devices: 5.42 us -> 7.69 us  [to_peers(): kept.append(lax.ppermute(other[k], ('epoch', 'band'), pairs))]
    ppermute x5 -> x7, starting transfers between devices: 5.55 us -> 7.68 us  [to_peers(): lax.ppermute(same[k], 'epoch', [(i, (i + k) % epochs) for i in range(epoc...]
    ppermute x9, waiting for transfers between devices: 17.6 us -> 15.6 us  [round_tiles(): lax.ppermute(arrays[k], 'tile', [(i, (i + k) % owners) for i in range(own...]
  transfers between devices with their start and end apart: 24 -> 30, of which waited for: 15 -> 16; matrix products, arithmetic and copies ran while one was open for 0% -> 0% of each run, Pallas kernels for 0% -> 9%
where the time goes in v7:
time: 103 us
  Pallas kernels  34.5 us (33%)
  starting transfers between devices  32.5 us (32%)
  waiting for transfers between devices  30.3 us (29%)
  local copies, waits for them, and re-layouts  4.75 us (5%)
    ppermute x9, starting transfers between devices, round_tiles(): lax.ppermute(arrays[k], 'tile', [(i, (i + k) % owners) for i in range(own...  17.1 us
    pallas_call x4, Pallas kernels, step_gradients(): pl.pallas_call(functools.partial(pull_kernel, layout, t), out_shape=[f32(...  15.9 us
    ppermute x9, waiting for transfers between devices, round_tiles(): lax.ppermute(arrays[k], 'tile', [(i, (i + k) % owners) for i in range(own...  15.6 us
    pallas_call x2, Pallas kernels, step_gradients(): pl.pallas_call(functools.partial(render_kernel, layout, later), out_shape...  15.3 us
    ppermute x14, waiting for transfers between devices, to_peers(): kept.append(lax.ppermute(other[k], ('epoch', 'band'), pairs))  9.68 us
    ppermute x14, starting transfers between devices, to_peers(): kept.append(lax.ppermute(other[k], ('epoch', 'band'), pairs))  7.69 us
    ppermute x7, starting transfers between devices, to_peers(): lax.ppermute(same[k], 'epoch', [(i, (i + k) % epochs) for i in range(epoc...  7.68 us
    ppermute x7, waiting for transfers between devices, to_peers(): lax.ppermute(same[k], 'epoch', [(i, (i + k) % epochs) for i in range(epoc...  5.1 us
  transfers between devices with their start and end apart: 30, of which 16 were waited for; matrix products, arithmetic and copies ran while one was open for 0% of the time, Pallas kernels for 9%

profile of v7, /device:TPU:0, one launch (start us, length us, event | category | flops | bytes accessed | tf_op | source)
XLA Modules:
  0.0 103.0 jit_solution(4278013411482599745)
XLA Ops:
  2.2 5.1 %collective-permute-start.2 = (f32[12,8,128]{2,1,0:T(8,128)S(1)}, f32[12,8,128]{2,1,0:T(8,128)S(1)}, u32[]{:S(2)}, u32[]{:S(2)}) collective-permute-start(f32[12,8,128]{2,1,0:T(8,128)S(1)} %pack.1.refs_0_), channel_id=1, source_target_pairs={{0,12},{4,0},{8,4},{12,8},{1,13},{5,1},{9,5},{13,9},{2,14},{6,2},{... | collective-permute-start | bytes 147464 | tf_op jit(solution)/shard_map/ppermute | solution.py:440
  9.4 2.9 %collective-permute-done.1.refs_2_ = f32[12,8,128]{2,1,0:T(8,128)S(1)} collective-permute-done((f32[12,8,128]{2,1,0:T(8,128)S(1)}, f32[12,8,128]{2,1,0:T(8,128)S(1)}, u32[]{:S(2)}, u32[]{:S(2)}) %collective-permute-start.1) | collective-permute-done | bytes 49184 | tf_op jit(solution)/shard_map/ppermute | solution.py:440
  14.0 1.5 %collective-permute-start.3 = (f32[11,16,128]{2,1,0:T(8,128)S(1)}, f32[11,16,128]{2,1,0:T(8,128)S(1)}, u32[]{:S(2)}, u32[]{:S(2)}) collective-permute-start(f32[11,16,128]{2,1,0:T(8,128)S(1)} %get-tuple-element.48.refs_0_), channel_id=1, source_target_pairs={{0,2},{2,0},{1,3},{3,1},{4,6},{6,4},{5,7},{7,5},{8,10},{10,8},{9,1... | collective-permute-start | bytes 270344 | tf_op jit(solution)/shard_map/ppermute | solution.py:428
  16.9 2.9 %collective-permute-done.5.refs_3_ = f32[7,16,128]{2,1,0:T(8,128)S(1)} collective-permute-done((f32[7,16,128]{2,1,0:T(8,128)S(1)}, f32[7,16,128]{2,1,0:T(8,128)S(1)}, u32[]{:S(2)}, u32[]{:S(2)}) %collective-permute-start.5) | collective-permute-done | bytes 57376 | tf_op jit(solution)/shard_map/ppermute | solution.py:435
  22.9 7.6 %first_render.1 = (f32[2,128,128]{2,1,0:T(8,128)S(1)}, f32[2,14,16,128]{3,2,1,0:T(8,128)S(1)}, f32[7,16,128]{2,1,0:T(8,128)S(1)}, f32[4,7,16,128]{3,2,1,0:T(8,12...) custom-call(s32[2]{0:T(128)S(1)} %copy-done.5, ...), custom_call_target="tpu_custom_call" | custom-call | tf_op jit(solution)/shard_map/first_render/pallas_call | solution.py:325
  30.5 3.2 %pull_0.2 = (f32[11,8,128]{2,1,0:T(8,128)S(1)}, f32[11,8,128]{2,1,0:T(8,128)S(1)}, f32[7,8,128]{2,1,0:T(8,128)S(1)}, f32[7,8,128]{2,1,0:T(8,128)S(1)}) custom-call(s32[2]{0:T(128)S(1)} %copy-done.5, s32[2,2,8]{2,1,0:T(2,128)S(1)} %bitcast.6, f32[1,1]{1,0:T(1,128)S(6)} %copy.8.psf_ref, f32[2,128,128]{2,1,0:T(8,128)S(1)} %get-tuple-element.50.refs_0_, ...), custom_call_target="tpu_custom_call" | custom-call | tf_op jit(solution)/shard_map/pull_0/pallas_call | solution.py:342
  36.0 4.7 %pull_1.2 = (f32[11,8,128]{2,1,0:T(8,128)S(1)}, f32[11,8,128]{2,1,0:T(8,128)S(1)}, f32[7,8,128]{2,1,0:T(8,128)S(1)}, f32[7,8,128]{2,1,0:T(8,128)S(1)}) custom-call(s32[2]{0:T(128)S(1)} %copy-done.5, s32[2,2,8]{2,1,0:T(2,128)S(1)} %bitcast.7, f32[1,1]{1,0:T(1,128)S(6)} %copy.8.psf_ref, f32[2,128,128]{2,1,0:T(8,128)S(1)} %get-tuple-element.50.refs_0_, ...), custom_call_target="tpu_custom_call" | custom-call | tf_op jit(solution)/shard_map/pull_1/pallas_call | solution.py:342
  42.9 1.2 %collective-permute-done.11 = f32[7,8,128]{2,1,0:T(8,128)S(1)} collective-permute-done((f32[7,8,128]{2,1,0:T(8,128)S(1)}, f32[7,8,128]{2,1,0:T(8,128)S(1)}, u32[]{:S(2)}, u32[]{:S(2)}) %collective-permute-start.11) | collective-permute-done | bytes 28704 | tf_op jit(solution)/shard_map/ppermute | solution.py:435
  44.1 1.7 %collective-permute-done.9 = f32[11,8,128]{2,1,0:T(8,128)S(1)} collective-permute-done((f32[11,8,128]{2,1,0:T(8,128)S(1)}, f32[11,8,128]{2,1,0:T(8,128)S(1)}, u32[]{:S(2)}, u32[]{:S(2)}) %collective-permute-start.9) | collective-permute-done | bytes 45088 | tf_op jit(solution)/shard_map/ppermute | solution.py:428
  45.8 4.4 %collective-permute-start.14 = (f32[11,16,128]{2,1,0:T(8,128)S(1)}, f32[11,16,128]{2,1,0:T(8,128)S(1)}, u32[]{:S(2)}, u32[]{:S(2)}) collective-permute-start(f32[11,16,128]{2,1,0:T(8,128)S(1)} %pad_maximum_fusion.refs_0_), channel_id=1, source_target_pairs={{0,12},{4,0},{8,4},{12,8},{1,13},{5,1},{9,5},{13,9},{2,14},{6,2},{... | collective-permute-start | bytes 270344 | tf_op jit(solution)/shard_map/ppermute | solution.py:440
  50.8 2.4 %collective-permute-done.14.refs_3_ = f32[11,16,128]{2,1,0:T(8,128)S(1)} collective-permute-done((f32[11,16,128]{2,1,0:T(8,128)S(1)}, f32[11,16,128]{2,1,0:T(8,128)S(1)}, u32[]{:S(2)}, u32[]{:S(2)}) %collective-permute-start.14) | collective-permute-done | bytes 90144 | tf_op jit(solution)/shard_map/ppermute | solution.py:440
  53.3 4.2 %collective-permute-done.13.refs_2_ = f32[11,16,128]{2,1,0:T(8,128)S(1)} collective-permute-done((f32[11,16,128]{2,1,0:T(8,128)S(1)}, f32[11,16,128]{2,1,0:T(8,128)S(1)}, u32[]{:S(2)}, u32[]{:S(2)}) %collective-permute-start.13) | collective-permute-done | bytes 90144 | tf_op jit(solution)/shard_map/ppermute | solution.py:440
  58.7 1.3 %collective-permute-start.16 = (f32[7,16,128]{2,1,0:T(8,128)S(1)}, f32[7,16,128]{2,1,0:T(8,128)S(1)}, u32[]{:S(2)}, u32[]{:S(2)}) collective-permute-start(f32[7,16,128]{2,1,0:T(8,128)S(1)} %get-tuple-element.68), channel_id=1, source_target_pairs={{0,1},{1,0},{2,3},{3,2},{4,5},{5,4},{6,7},{7,6},{8,9},{9,8},{10,11... | collective-permute-start | bytes 172040 | tf_op jit(solution)/shard_map/ppermute | solution.py:435
  60.0 3.0 %collective-permute-done.17.refs_7_ = f32[7,16,128]{2,1,0:T(8,128)S(1)} collective-permute-done((f32[7,16,128]{2,1,0:T(8,128)S(1)}, f32[7,16,128]{2,1,0:T(8,128)S(1)}, u32[]{:S(2)}, u32[]{:S(2)}) %collective-permute-start.17) | collective-permute-done | bytes 57376 | tf_op jit(solution)/shard_map/ppermute | solution.py:435
  63.0 7.7 %later_render.1 = (f32[2,128,128]{2,1,0:T(8,128)S(1)}, f32[2,14,16,128]{3,2,1,0:T(8,128)S(1)}, f32[7,16,128]{2,1,0:T(8,128)S(1)}, f32[4,7,16,128]{3,2,1,0:T(8,12...) custom-call(s32[2]{0:T(128)S(1)} %copy-done.5, ...), custom_call_target="tpu_custom_call" | custom-call | tf_op jit(solution)/shard_map/later_render/pallas_call | solution.py:325
  70.7 3.2 %pull_0.3 = (f32[11,8,128]{2,1,0:T(8,128)S(1)}, f32[11,8,128]{2,1,0:T(8,128)S(1)}, f32[7,8,128]{2,1,0:T(8,128)S(1)}, f32[7,8,128]{2,1,0:T(8,128)S(1)}) custom-call(s32[2]{0:T(128)S(1)} %copy-done.5, s32[2,2,8]{2,1,0:T(2,128)S(1)} %bitcast.9, f32[1,1]{1,0:T(1,128)S(6)} %copy.8.psf_ref, f32[2,128,128]{2,1,0:T(8,128)S(1)} %get-tuple-element.69.refs_0_, ...), custom_call_target="tpu_custom_call" | custom-call | tf_op jit(solution)/shard_map/pull_0/pallas_call | solution.py:342
  76.2 4.7 %pull_1.3 = (f32[11,8,128]{2,1,0:T(8,128)S(1)}, f32[11,8,128]{2,1,0:T(8,128)S(1)}, f32[7,8,128]{2,1,0:T(8,128)S(1)}, f32[7,8,128]{2,1,0:T(8,128)S(1)}) custom-call(s32[2]{0:T(128)S(1)} %copy-done.5, s32[2,2,8]{2,1,0:T(2,128)S(1)} %bitcast.10, f32[1,1]{1,0:T(1,128)S(6)} %copy.8.psf_ref, f32[2,128,128]{2,1,0:T(8,128)S(1)} %get-tuple-element.69.refs_0_, ...), custom_call_target="tpu_custom_call" | custom-call | tf_op jit(solution)/shard_map/pull_1/pallas_call | solution.py:342
  83.1 1.3 %collective-permute-done.23 = f32[7,8,128]{2,1,0:T(8,128)S(1)} collective-permute-done((f32[7,8,128]{2,1,0:T(8,128)S(1)}, f32[7,8,128]{2,1,0:T(8,128)S(1)}, u32[]{:S(2)}, u32[]{:S(2)}) %collective-permute-start.23) | collective-permute-done | bytes 28704 | tf_op jit(solution)/shard_map/ppermute | solution.py:435
  84.4 1.7 %collective-permute-done.21 = f32[11,8,128]{2,1,0:T(8,128)S(1)} collective-permute-done((f32[11,8,128]{2,1,0:T(8,128)S(1)}, f32[11,8,128]{2,1,0:T(8,128)S(1)}, u32[]{:S(2)}, u32[]{:S(2)}) %collective-permute-start.21) | collective-permute-done | bytes 45088 | tf_op jit(solution)/shard_map/ppermute | solution.py:428
  87.1 5.9 %collective-permute-start.25 = (f32[11,8,128]{2,1,0:T(8,128)S(1)}, f32[11,8,128]{2,1,0:T(8,128)S(1)}, u32[]{:S(2)}, u32[]{:S(2)}) collective-permute-start(f32[11,8,128]{2,1,0:T(8,128)S(1)} %get-tuple-element.87), channel_id=1, source_target_pairs={{0,8},{4,12},{8,0},{12,4},{1,9},{5,13},{9,1},{13,5},{2,10},{6,14},... | collective-permute-start | bytes 135176 | tf_op jit(solution)/shard_map/ppermute | solution.py:440
  93.0 1.9 %collective-permute-done.24 = f32[11,8,128]{2,1,0:T(8,128)S(1)} collective-permute-done((f32[11,8,128]{2,1,0:T(8,128)S(1)}, f32[11,8,128]{2,1,0:T(8,128)S(1)}, u32[]{:S(2)}, u32[]{:S(2)}) %collective-permute-start.24) | collective-permute-done | bytes 45088 | tf_op jit(solution)/shard_map/ppermute | solution.py:440
  95.8 1.2 %collective-permute-done.26 = f32[11,8,128]{2,1,0:T(8,128)S(1)} collective-permute-done((f32[11,8,128]{2,1,0:T(8,128)S(1)}, f32[11,8,128]{2,1,0:T(8,128)S(1)}, u32[]{:S(2)}, u32[]{:S(2)}) %collective-permute-start.26) | collective-permute-done | bytes 45088 | tf_op jit(solution)/shard_map/ppermute | solution.py:440
  99.3 1.3 %collective-permute-done.29.refs_3_ = f32[11,8,128]{2,1,0:T(8,128)S(1)} collective-permute-done((f32[11,8,128]{2,1,0:T(8,128)S(1)}, f32[11,8,128]{2,1,0:T(8,128)S(1)}, u32[]{:S(2)}, u32[]{:S(2)}) %collective-permute-start.29) | collective-permute-done | bytes 45088 | tf_op jit(solution)/shard_map/ppermute | solution.py:435
  100.6 1.6 %collective-permute-done.27.refs_1_ = f32[11,8,128]{2,1,0:T(8,128)S(1)} collective-permute-done((f32[11,8,128]{2,1,0:T(8,128)S(1)}, f32[11,8,128]{2,1,0:T(8,128)S(1)}, u32[]{:S(2)}, u32[]{:S(2)}) %collective-permute-start.27) | collective-permute-done | bytes 45088 | tf_op jit(solution)/shard_map/ppermute | solution.py:428
  (74 shorter events, 25.3 us)
Async XLA Ops:
  2.2 7.2 %collective-permute-start.2 = (f32[12,8,128]{2,1,0:T(8,128)S(1)}, f32[12,8,128]{2,1,0:T(8,128)S(1)}, u32[]{:S(2)}, u32[]{:S(2)}) collective-permute-start(f32[12,8,128]{2,1,0:T(8,128)S(1)} %pack.1.refs_0_), channel_id=1, source_target_pairs={{0,12},{4,0},{8,4},{12,8},{1,13},{5,1},{9,5},{13,9},{2,14},{6,2},{... | collective-permute-start | bytes 147464 | tf_op jit(solution)/shard_map/ppermute | solution.py:440
  7.3 5.0 %collective-permute-start.1 = (f32[12,8,128]{2,1,0:T(8,128)S(1)}, f32[12,8,128]{2,1,0:T(8,128)S(1)}, u32[]{:S(2)}, u32[]{:S(2)}) collective-permute-start(f32[12,8,128]{2,1,0:T(8,128)S(1)} %pack.1.refs_0_), channel_id=1, source_target_pairs={{0,8},{4,12},{8,0},{12,4},{1,9},{5,13},{9,1},{13,5},{2,10},{6,14},... | collective-permute-start | bytes 147464 | tf_op jit(solution)/shard_map/ppermute | solution.py:440
  7.3 5.9 %collective-permute-start = (f32[12,8,128]{2,1,0:T(8,128)S(1)}, f32[12,8,128]{2,1,0:T(8,128)S(1)}, u32[]{:S(2)}, u32[]{:S(2)}) collective-permute-start(f32[12,8,128]{2,1,0:T(8,128)S(1)} %pack.1.refs_0_), channel_id=1, source_target_pairs={{0,4},{4,8},{8,12},{12,0},{1,5},{5,9},{9,13},{13,1},{2,6},{6,10},{... | collective-permute-start | bytes 147464 | tf_op jit(solution)/shard_map/ppermute | solution.py:440
  14.0 5.7 %collective-permute-start.3 = (f32[11,16,128]{2,1,0:T(8,128)S(1)}, f32[11,16,128]{2,1,0:T(8,128)S(1)}, u32[]{:S(2)}, u32[]{:S(2)}) collective-permute-start(f32[11,16,128]{2,1,0:T(8,128)S(1)} %get-tuple-element.48.refs_0_), channel_id=1, source_target_pairs={{0,2},{2,0},{1,3},{3,1},{4,6},{6,4},{5,7},{7,5},{8,10},{10,8},{9,1... | collective-permute-start | bytes 270344 | tf_op jit(solution)/shard_map/ppermute | solution.py:428
  15.5 4.2 %collective-permute-start.5 = (f32[7,16,128]{2,1,0:T(8,128)S(1)}, f32[7,16,128]{2,1,0:T(8,128)S(1)}, u32[]{:S(2)}, u32[]{:S(2)}) collective-permute-start(f32[7,16,128]{2,1,0:T(8,128)S(1)} %get-tuple-element.49), channel_id=1, source_target_pairs={{0,3},{1,2},{2,1},{3,0},{4,7},{5,6},{6,5},{7,4},{8,11},{9,10},{10,... | collective-permute-start | bytes 172040 | tf_op jit(solution)/shard_map/ppermute | solution.py:435
  15.6 4.2 %collective-permute-start.4 = (f32[7,16,128]{2,1,0:T(8,128)S(1)}, f32[7,16,128]{2,1,0:T(8,128)S(1)}, u32[]{:S(2)}, u32[]{:S(2)}) collective-permute-start(f32[7,16,128]{2,1,0:T(8,128)S(1)} %get-tuple-element.49), channel_id=1, source_target_pairs={{0,1},{1,0},{2,3},{3,2},{4,5},{5,4},{6,7},{7,6},{8,9},{9,8},{10,11... | collective-permute-start | bytes 172040 | tf_op jit(solution)/shard_map/ppermute | solution.py:435
  33.7 10.4 %collective-permute-start.6 = (f32[11,8,128]{2,1,0:T(8,128)S(1)}, f32[11,8,128]{2,1,0:T(8,128)S(1)}, u32[]{:S(2)}, u32[]{:S(2)}) collective-permute-start(f32[11,8,128]{2,1,0:T(8,128)S(1)} %get-tuple-element.57), channel_id=1, source_target_pairs={{0,2},{2,0},{1,3},{3,1},{4,6},{6,4},{5,7},{7,5},{8,10},{10,8},{9,1... | collective-permute-start | bytes 135176 | tf_op jit(solution)/shard_map/ppermute | solution.py:428
  34.7 7.0 %collective-permute-start.7 = (f32[7,8,128]{2,1,0:T(8,128)S(1)}, f32[7,8,128]{2,1,0:T(8,128)S(1)}, u32[]{:S(2)}, u32[]{:S(2)}) collective-permute-start(f32[7,8,128]{2,1,0:T(8,128)S(1)} %get-tuple-element.58), channel_id=1, source_target_pairs={{0,1},{1,0},{2,3},{3,2},{4,5},{5,4},{6,7},{7,6},{8,9},{9,8},{10,11... | collective-permute-start | bytes 86024 | tf_op jit(solution)/shard_map/ppermute | solution.py:435
  34.9 8.0 %collective-permute-start.8 = (f32[7,8,128]{2,1,0:T(8,128)S(1)}, f32[7,8,128]{2,1,0:T(8,128)S(1)}, u32[]{:S(2)}, u32[]{:S(2)}) collective-permute-start(f32[7,8,128]{2,1,0:T(8,128)S(1)} %get-tuple-element.59), channel_id=1, source_target_pairs={{0,3},{1,2},{2,1},{3,0},{4,7},{5,6},{6,5},{7,4},{8,11},{9,10},{10,... | collective-permute-start | bytes 86024 | tf_op jit(solution)/shard_map/ppermute | solution.py:435
  41.8 4.0 %collective-permute-start.9 = (f32[11,8,128]{2,1,0:T(8,128)S(1)}, f32[11,8,128]{2,1,0:T(8,128)S(1)}, u32[]{:S(2)}, u32[]{:S(2)}) collective-permute-start(f32[11,8,128]{2,1,0:T(8,128)S(1)} %get-tuple-element.63), channel_id=1, source_target_pairs={{0,2},{2,0},{1,3},{3,1},{4,6},{6,4},{5,7},{7,5},{8,10},{10,8},{9,1... | collective-permute-start | bytes 135176 | tf_op jit(solution)/shard_map/ppermute | solution.py:428
  45.8 7.4 %collective-permute-start.14 = (f32[11,16,128]{2,1,0:T(8,128)S(1)}, f32[11,16,128]{2,1,0:T(8,128)S(1)}, u32[]{:S(2)}, u32[]{:S(2)}) collective-permute-start(f32[11,16,128]{2,1,0:T(8,128)S(1)} %pad_maximum_fusion.refs_0_), channel_id=1, source_target_pairs={{0,12},{4,0},{8,4},{12,8},{1,13},{5,1},{9,5},{13,9},{2,14},{6,2},{... | collective-permute-start | bytes 270344 | tf_op jit(solution)/shard_map/ppermute | solution.py:440
  50.2 7.3 %collective-permute-start.13 = (f32[11,16,128]{2,1,0:T(8,128)S(1)}, f32[11,16,128]{2,1,0:T(8,128)S(1)}, u32[]{:S(2)}, u32[]{:S(2)}) collective-permute-start(f32[11,16,128]{2,1,0:T(8,128)S(1)} %pad_maximum_fusion.refs_0_), channel_id=1, source_target_pairs={{0,8},{4,12},{8,0},{12,4},{1,9},{5,13},{9,1},{13,5},{2,10},{6,14},... | collective-permute-start | bytes 270344 | tf_op jit(solution)/shard_map/ppermute | solution.py:440
  50.2 7.3 %collective-permute-start.12 = (f32[11,16,128]{2,1,0:T(8,128)S(1)}, f32[11,16,128]{2,1,0:T(8,128)S(1)}, u32[]{:S(2)}, u32[]{:S(2)}) collective-permute-start(f32[11,16,128]{2,1,0:T(8,128)S(1)} %pad_maximum_fusion.refs_0_), channel_id=1, source_target_pairs={{0,4},{4,8},{8,12},{12,0},{1,5},{5,9},{9,13},{13,1},{2,6},{6,10},{... | collective-permute-start | bytes 270344 | tf_op jit(solution)/shard_map/ppermute | solution.py:440
  57.8 5.2 %collective-permute-start.15 = (f32[11,16,128]{2,1,0:T(8,128)S(1)}, f32[11,16,128]{2,1,0:T(8,128)S(1)}, u32[]{:S(2)}, u32[]{:S(2)}) collective-permute-start(f32[11,16,128]{2,1,0:T(8,128)S(1)} %get-tuple-element.67.refs_4_), channel_id=1, source_target_pairs={{0,2},{2,0},{1,3},{3,1},{4,6},{6,4},{5,7},{7,5},{8,10},{10,8},{9,1... | collective-permute-start | bytes 270344 | tf_op jit(solution)/shard_map/ppermute | solution.py:428
  58.7 4.2 %collective-permute-start.17 = (f32[7,16,128]{2,1,0:T(8,128)S(1)}, f32[7,16,128]{2,1,0:T(8,128)S(1)}, u32[]{:S(2)}, u32[]{:S(2)}) collective-permute-start(f32[7,16,128]{2,1,0:T(8,128)S(1)} %get-tuple-element.68), channel_id=1, source_target_pairs={{0,3},{1,2},{2,1},{3,0},{4,7},{5,6},{6,5},{7,4},{8,11},{9,10},{10,... | collective-permute-start | bytes 172040 | tf_op jit(solution)/shard_map/ppermute | solution.py:435
  58.7 4.2 %collective-permute-start.16 = (f32[7,16,128]{2,1,0:T(8,128)S(1)}, f32[7,16,128]{2,1,0:T(8,128)S(1)}, u32[]{:S(2)}, u32[]{:S(2)}) collective-permute-start(f32[7,16,128]{2,1,0:T(8,128)S(1)} %get-tuple-element.68), channel_id=1, source_target_pairs={{0,1},{1,0},{2,3},{3,2},{4,5},{5,4},{6,7},{7,6},{8,9},{9,8},{10,11... | collective-permute-start | bytes 172040 | tf_op jit(solution)/shard_map/ppermute | solution.py:435
  73.9 10.5 %collective-permute-start.18 = (f32[11,8,128]{2,1,0:T(8,128)S(1)}, f32[11,8,128]{2,1,0:T(8,128)S(1)}, u32[]{:S(2)}, u32[]{:S(2)}) collective-permute-start(f32[11,8,128]{2,1,0:T(8,128)S(1)} %get-tuple-element.76), channel_id=1, source_target_pairs={{0,2},{2,0},{1,3},{3,1},{4,6},{6,4},{5,7},{7,5},{8,10},{10,8},{9,1... | collective-permute-start | bytes 135176 | tf_op jit(solution)/shard_map/ppermute | solution.py:428
  75.1 7.1 %collective-permute-start.19 = (f32[7,8,128]{2,1,0:T(8,128)S(1)}, f32[7,8,128]{2,1,0:T(8,128)S(1)}, u32[]{:S(2)}, u32[]{:S(2)}) collective-permute-start(f32[7,8,128]{2,1,0:T(8,128)S(1)} %get-tuple-element.77), channel_id=1, source_target_pairs={{0,1},{1,0},{2,3},{3,2},{4,5},{5,4},{6,7},{7,6},{8,9},{9,8},{10,11... | collective-permute-start | bytes 86024 | tf_op jit(solution)/shard_map/ppermute | solution.py:435
  75.1 8.0 %collective-permute-start.20 = (f32[7,8,128]{2,1,0:T(8,128)S(1)}, f32[7,8,128]{2,1,0:T(8,128)S(1)}, u32[]{:S(2)}, u32[]{:S(2)}) collective-permute-start(f32[7,8,128]{2,1,0:T(8,128)S(1)} %get-tuple-element.78), channel_id=1, source_target_pairs={{0,3},{1,2},{2,1},{3,0},{4,7},{5,6},{6,5},{7,4},{8,11},{9,10},{10,... | collective-permute-start | bytes 86024 | tf_op jit(solution)/shard_map/ppermute | solution.py:435
  82.1 4.0 %collective-permute-start.21 = (f32[11,8,128]{2,1,0:T(8,128)S(1)}, f32[11,8,128]{2,1,0:T(8,128)S(1)}, u32[]{:S(2)}, u32[]{:S(2)}) collective-permute-start(f32[11,8,128]{2,1,0:T(8,128)S(1)} %get-tuple-element.82), channel_id=1, source_target_pairs={{0,2},{2,0},{1,3},{3,1},{4,6},{6,4},{5,7},{7,5},{8,10},{10,8},{9,1... | collective-permute-start | bytes 135176 | tf_op jit(solution)/shard_map/ppermute | solution.py:428
  87.0 7.9 %collective-permute-start.24 = (f32[11,8,128]{2,1,0:T(8,128)S(1)}, f32[11,8,128]{2,1,0:T(8,128)S(1)}, u32[]{:S(2)}, u32[]{:S(2)}) collective-permute-start(f32[11,8,128]{2,1,0:T(8,128)S(1)} %get-tuple-element.86), channel_id=1, source_target_pairs={{0,4},{4,8},{8,12},{12,0},{1,5},{5,9},{9,13},{13,1},{2,6},{6,10},{... | collective-permute-start | bytes 135176 | tf_op jit(solution)/shard_map/ppermute | solution.py:440
  87.1 8.7 %collective-permute-start.25 = (f32[11,8,128]{2,1,0:T(8,128)S(1)}, f32[11,8,128]{2,1,0:T(8,128)S(1)}, u32[]{:S(2)}, u32[]{:S(2)}) collective-permute-start(f32[11,8,128]{2,1,0:T(8,128)S(1)} %get-tuple-element.87), channel_id=1, source_target_pairs={{0,8},{4,12},{8,0},{12,4},{1,9},{5,13},{9,1},{13,5},{2,10},{6,14},... | collective-permute-start | bytes 135176 | tf_op jit(solution)/shard_map/ppermute | solution.py:440
  93.0 4.0 %collective-permute-start.26 = (f32[11,8,128]{2,1,0:T(8,128)S(1)}, f32[11,8,128]{2,1,0:T(8,128)S(1)}, u32[]{:S(2)}, u32[]{:S(2)}) collective-permute-start(f32[11,8,128]{2,1,0:T(8,128)S(1)} %get-tuple-element.88), channel_id=1, source_target_pairs={{0,12},{4,0},{8,4},{12,8},{1,13},{5,1},{9,5},{13,9},{2,14},{6,2},{... | collective-permute-start | bytes 135176 | tf_op jit(solution)/shard_map/ppermute | solution.py:440
  98.2 4.0 %collective-permute-start.27 = (f32[11,8,128]{2,1,0:T(8,128)S(1)}, f32[11,8,128]{2,1,0:T(8,128)S(1)}, u32[]{:S(2)}, u32[]{:S(2)}) collective-permute-start(f32[11,8,128]{2,1,0:T(8,128)S(1)} %add_add_fusion.refs_0_), channel_id=1, source_target_pairs={{0,2},{2,0},{1,3},{3,1},{4,6},{6,4},{5,7},{7,5},{8,10},{10,8},{9,1... | collective-permute-start | bytes 135176 | tf_op jit(solution)/shard_map/ppermute | solution.py:428
  (14 other events, 59.0 us)

commit v8 on v6

--- a/solution.py
+++ b/solution.py
@@ -15,6 +15,8 @@
 BANDS = 2
 SHARED = 4 * COMPS
 HALF = SHARED // BANDS
+SPLIT_UNIT = 49152.0
+SPLIT_SCALE = 65536.0
 LOG2E = math.log2(math.e)
 F32 = jnp.float32
 BF16 = jnp.bfloat16
@@ -157,7 +159,7 @@
     taken = 2 * epochs * (2 if later else 1)
     ins, refs = refs[:taken], refs[taken:]
     outs, refs = refs[: 2 * epochs], refs[2 * epochs :]
-    shared, amps, derived, pieces_x, pieces_y, image, sums, half, other = refs[:9]
+    shared, amps, derived, prof_y, pieces_x, pieces_y, image, sums, half, other = refs[:10]
     band, epoch = lax.axis_index("band"), lax.axis_index("epoch")
     tiles = data_ref.shape[0]
     pixels = data_ref.shape[-1]
@@ -172,7 +174,7 @@
         return r // HALF, r % HALF
 
     if later:
-        moved, moved_amps = refs[9:]
+        moved, moved_amps = refs[10:]
         put_together(layout, band, epoch, ins[2 * epochs :], half, other, moved, moved_amps)
         for k in range(4):
             shift = 0.0
@@ -196,17 +198,18 @@
         derived[2, c] = (-0.5 * LOG2E) / (jnp.exp(2.0 * (lw + an)) + psf * psf)
         derived[3, c] = (-0.5 * LOG2E) / (jnp.exp(2.0 * (lw - an)) + psf * psf)
         derived[4, c] = jnp.where(live, amps[c], 0.0)
+        derived[5, c] = derived[4, c] * SPLIT_SCALE
     sums[...] = jnp.zeros_like(sums)
 
     grid = lax.broadcasted_iota(jnp.int32, (pixels, 128), 0).astype(F32)
 
-    def cut(x):
-        hi = x.astype(BF16)
-        return jnp.concatenate([hi, (x - hi.astype(F32)).astype(BF16)], axis=0)
+    def cut(x, large):
+        hi = (x + large) - large
+        return jnp.concatenate([hi, x - hi], axis=0)
 
     def stack(x):
-        hi = x.astype(BF16)
-        return jnp.concatenate([hi, hi], axis=1), (x - hi.astype(F32)).astype(BF16)
+        hi = x.astype(BF16).astype(F32)
+        return jnp.concatenate([hi, hi], axis=1), x - hi
 
     def times(left, right):
         near = jnp.dot(left[0], right, preferred_element_type=F32)
@@ -232,10 +235,11 @@
                 for c in range(COMPS):
                     d = grid - (line(0, c, g) + off_x)
                     e = jnp.exp2(d * d * line(2, c, g))
-                    pieces_x[s, :, c * 128 : (c + 1) * 128] = cut(e)
+                    pieces_x[s, :, c * 128 : (c + 1) * 128] = cut(e, SPLIT_UNIT)
                     d = grid - (line(1, c, g) + off_y)
                     e = jnp.exp2(d * d * line(3, c, g))
-                    pieces_y[s, :, c * 128 : (c + 1) * 128] = cut(e * line(4, c, g))
+                    prof_y[s * COMPS + c] = e
+                    pieces_y[s, :, c * 128 : (c + 1) * 128] = cut(e * line(4, c, g), line(5, c, g))
                 image[...] += lax.dot_general(
                     pieces_x[s], pieces_y[s], (((1,), (1,)), ((), ())), preferred_element_type=F32
                 )
@@ -263,12 +267,14 @@
                     for n in range(here):
                         c = first + n
                         d = grid - (line(0, c, g) + off_x)
-                        e = jnp.exp2(d * d * line(2, c, g)) * by_x[:, n * 128 : (n + 1) * 128]
+                        at = slice(c * 128, (c + 1) * 128)
+                        e = pieces_x[s, :pixels, at] + pieces_x[s, pixels:, at]
+                        e = e * by_x[:, n * 128 : (n + 1) * 128]
                         e1 = e * d
                         sums[0, c, pl.ds(g, 1), :] = total(e1)
                         sums[1, c, pl.ds(g, 1), :] = total(e1 * d)
                         d = grid - (line(1, c, g) + off_y)
-                        e = jnp.exp2(d * d * line(3, c, g)) * by_y[:, n * 128 : (n + 1) * 128]
+                        e = prof_y[s * COMPS + c] * by_y[:, n * 128 : (n + 1) * 128]
                         e1 = e * d
                         sums[2, c, pl.ds(g, 1), :] = total(e1)
                         sums[3, c, pl.ds(g, 1), :] = total(e1 * d)
@@ -324,16 +330,17 @@
         out_specs=[vmem()] * len(shapes),
         scratch_shapes=together
         + [
-            pltpu.VMEM((5, COMPS, wide, 128), F32),
-            pltpu.VMEM((slots, 2 * pixels, COMPS * 128), BF16),
-            pltpu.VMEM((slots, 2 * pixels, COMPS * 128), BF16),
+            pltpu.VMEM((6, COMPS, wide, 128), F32),
+            pltpu.VMEM((slots * COMPS, pixels, 128), F32),
+            pltpu.VMEM((slots, 2 * pixels, COMPS * 128), F32),
+            pltpu.VMEM((slots, 2 * pixels, COMPS * 128), F32),
             pltpu.VMEM((2 * pixels, 2 * pixels), F32),
             pltpu.VMEM((5, COMPS, wide, 128), F32),
             pltpu.VMEM((epochs, rows, wide, 128), F32),
             pltpu.VMEM((epochs, shared_rows, wide, 128), F32),
         ]
         + (together if later else []),
-        compiler_params=params(32),
+        compiler_params=params(40),
         name="later_step" if later else "first_step",
     )(counts, offsets, psf, data, weight, *ins)
 

time: 91.3 us -> 88.2 us (0.966)
  starting transfers between devices: 28.1 us -> 24.7 us
  Pallas kernels: 26.6 us -> 27.8 us
    ppermute x9, starting transfers between devices: 17.1 us -> 13.7 us  [round_tiles(): lax.ppermute(arrays[k], 'tile', [(i, (i + k) % owners) for i in range(own...]
    pallas_call x2, Pallas kernels: 23.3 us -> 24.6 us  [step_gradient(): pl.pallas_call(functools.partial(step_kernel, layout, later), out_shape=[...]
  transfers between devices with their start and end apart: 24 -> 24, of which waited for: 15 -> 14; matrix products, arithmetic and copies ran while one was open for 0% -> 0% of each run, Pallas kernels for 0% -> 0%
where the time goes in v8:
time: 88.2 us; the launch traced here: 87.4 us
  waiting for transfers between devices  32.4 us (37%)
  Pallas kernels  27.8 us (32%)
  starting transfers between devices  24.7 us (28%)
  local copies, waits for them, and re-layouts  1.63 us (2%)
    pallas_call x2, Pallas kernels, step_gradient(): pl.pallas_call(functools.partial(step_kernel, layout, later), out_shape=[...  24.6 us
    ppermute x9, waiting for transfers between devices, round_tiles(): lax.ppermute(arrays[k], 'tile', [(i, (i + k) % owners) for i in range(own...  16.8 us
    ppermute x10, waiting for transfers between devices, to_peers(): kept.append(lax.ppermute(other[k], ('epoch', 'band'), pairs))  14.1 us
    ppermute x9, starting transfers between devices, round_tiles(): lax.ppermute(arrays[k], 'tile', [(i, (i + k) % owners) for i in range(own...  13.7 us
    ppermute x5, starting transfers between devices, to_peers(): lax.ppermute(same[k], 'epoch', [(i, (i + k) % epochs) for i in range(epoc...  5.6 us
    ppermute x10, starting transfers between devices, to_peers(): kept.append(lax.ppermute(other[k], ('epoch', 'band'), pairs))  5.39 us
  transfers between devices with their start and end apart: 24, of which 14 were waited for; matrix products, arithmetic and copies ran while one was open for 0% of the time, Pallas kernels for 0%

profile of v8, /device:TPU:0, one launch (start us, length us, event | category | flops | bytes accessed | tf_op | source)
XLA Modules:
  0.0 87.4 jit_solution(16342764217998696246)
XLA Ops:
  2.2 5.1 %collective-permute-start.2 = (f32[12,8,128]{2,1,0:T(8,128)S(1)}, f32[12,8,128]{2,1,0:T(8,128)S(1)}, u32[]{:S(2)}, u32[]{:S(2)}) collective-permute-start(f32[12,8,128]{2,1,0:T(8,128)S(1)} %pack.1.refs_0_), channel_id=1, source_target_pairs={{0,12},{4,0},{8,4},{12,8},{1,13},{5,1},{9,5},{13,9},{2,14},{6,2},{... | collective-permute-start | bytes 147464 | tf_op jit(solution)/shard_map/ppermute | solution.py:428
  7.3 1.0 %collective-permute-start = (f32[12,8,128]{2,1,0:T(8,128)S(1)}, f32[12,8,128]{2,1,0:T(8,128)S(1)}, u32[]{:S(2)}, u32[]{:S(2)}) collective-permute-start(f32[12,8,128]{2,1,0:T(8,128)S(1)} %pack.1.refs_0_), channel_id=1, source_target_pairs={{0,4},{4,8},{8,12},{12,0},{1,5},{5,9},{9,13},{13,1},{2,6},{6,10},{... | collective-permute-start | bytes 147464 | tf_op jit(solution)/shard_map/ppermute | solution.py:428
  8.3 1.0 %collective-permute-done.2.refs_3_ = f32[12,8,128]{2,1,0:T(8,128)S(1)} collective-permute-done((f32[12,8,128]{2,1,0:T(8,128)S(1)}, f32[12,8,128]{2,1,0:T(8,128)S(1)}, u32[]{:S(2)}, u32[]{:S(2)}) %collective-permute-start.2) | collective-permute-done | bytes 49184 | tf_op jit(solution)/shard_map/ppermute | solution.py:428
  9.4 2.9 %collective-permute-done.1.refs_2_ = f32[12,8,128]{2,1,0:T(8,128)S(1)} collective-permute-done((f32[12,8,128]{2,1,0:T(8,128)S(1)}, f32[12,8,128]{2,1,0:T(8,128)S(1)}, u32[]{:S(2)}, u32[]{:S(2)}) %collective-permute-start.1) | collective-permute-done | bytes 49184 | tf_op jit(solution)/shard_map/ppermute | solution.py:428
  14.0 1.5 %collective-permute-start.3 = (f32[11,16,128]{2,1,0:T(8,128)S(1)}, f32[11,16,128]{2,1,0:T(8,128)S(1)}, u32[]{:S(2)}, u32[]{:S(2)}) collective-permute-start(f32[11,16,128]{2,1,0:T(8,128)S(1)} %get-tuple-element.24.refs_0_), channel_id=1, source_target_pairs={{0,2},{2,0},{1,3},{3,1},{4,6},{6,4},{5,7},{7,5},{8,10},{10,8},{9,1... | collective-permute-start | bytes 270344 | tf_op jit(solution)/shard_map/ppermute | solution.py:416
  16.9 2.9 %collective-permute-done.5.refs_3_ = f32[7,16,128]{2,1,0:T(8,128)S(1)} collective-permute-done((f32[7,16,128]{2,1,0:T(8,128)S(1)}, f32[7,16,128]{2,1,0:T(8,128)S(1)}, u32[]{:S(2)}, u32[]{:S(2)}) %collective-permute-start.5) | collective-permute-done | bytes 57376 | tf_op jit(solution)/shard_map/ppermute | solution.py:423
  19.8 12.2 %first_step.1 = (f32[11,16,128]{2,1,0:T(8,128)S(1)}, f32[11,16,128]{2,1,0:T(8,128)S(1)}, f32[7,16,128]{2,1,0:T(8,128)S(1)}, f32[7,16,128]{2,1,0:T(8,128)S(1)}) custom-call(s32[2]{0:T(128)S(1)} %copy-done.6, s32[2,2,8]{2,1,0:T(2,128)S(1)} %bitcast.5, f32[1,1]{1,0:T(1,128)S(6)} %copy.8.psf_ref, f32[2,1,1,128,128]{4,3,2,1,0:T(8,128)S(1)} %copy-done.2, ...), custom_call_target="tpu_custom_call" | custom-call | tf_op jit(solution)/shard_map/first_step/pallas_call | solution.py:326
  33.2 1.1 %collective-permute-start.8 = (f32[7,16,128]{2,1,0:T(8,128)S(1)}, f32[7,16,128]{2,1,0:T(8,128)S(1)}, u32[]{:S(2)}, u32[]{:S(2)}) collective-permute-start(f32[7,16,128]{2,1,0:T(8,128)S(1)} %get-tuple-element.29), channel_id=1, source_target_pairs={{0,3},{1,2},{2,1},{3,0},{4,7},{5,6},{6,5},{7,4},{8,11},{9,10},{10,... | collective-permute-start | bytes 172040 | tf_op jit(solution)/shard_map/ppermute | solution.py:423
  34.3 3.1 %collective-permute-done.8 = f32[7,16,128]{2,1,0:T(8,128)S(1)} collective-permute-done((f32[7,16,128]{2,1,0:T(8,128)S(1)}, f32[7,16,128]{2,1,0:T(8,128)S(1)}, u32[]{:S(2)}, u32[]{:S(2)}) %collective-permute-start.8) | collective-permute-done | bytes 57376 | tf_op jit(solution)/shard_map/ppermute | solution.py:423
  37.4 1.3 %collective-permute-start.11 = (f32[11,16,128]{2,1,0:T(8,128)S(1)}, f32[11,16,128]{2,1,0:T(8,128)S(1)}, u32[]{:S(2)}, u32[]{:S(2)}) collective-permute-start(f32[11,16,128]{2,1,0:T(8,128)S(1)} %pad_add_fusion.1.refs_0_), channel_id=1, source_target_pairs={{0,12},{4,0},{8,4},{12,8},{1,13},{5,1},{9,5},{13,9},{2,14},{6,2},{... | collective-permute-start | bytes 270344 | tf_op jit(solution)/shard_map/ppermute | solution.py:428
  38.7 1.5 %collective-permute-start.10 = (f32[11,16,128]{2,1,0:T(8,128)S(1)}, f32[11,16,128]{2,1,0:T(8,128)S(1)}, u32[]{:S(2)}, u32[]{:S(2)}) collective-permute-start(f32[11,16,128]{2,1,0:T(8,128)S(1)} %pad_add_fusion.1.refs_0_), channel_id=1, source_target_pairs={{0,8},{4,12},{8,0},{12,4},{1,9},{5,13},{9,1},{13,5},{2,10},{6,14},... | collective-permute-start | bytes 270344 | tf_op jit(solution)/shard_map/ppermute | solution.py:428
  40.6 1.8 %collective-permute-done.11.refs_3_ = f32[11,16,128]{2,1,0:T(8,128)S(1)} collective-permute-done((f32[11,16,128]{2,1,0:T(8,128)S(1)}, f32[11,16,128]{2,1,0:T(8,128)S(1)}, u32[]{:S(2)}, u32[]{:S(2)}) %collective-permute-start.11) | collective-permute-done | bytes 90144 | tf_op jit(solution)/shard_map/ppermute | solution.py:428
  42.4 6.5 %collective-permute-done.10.refs_2_ = f32[11,16,128]{2,1,0:T(8,128)S(1)} collective-permute-done((f32[11,16,128]{2,1,0:T(8,128)S(1)}, f32[11,16,128]{2,1,0:T(8,128)S(1)}, u32[]{:S(2)}, u32[]{:S(2)}) %collective-permute-start.10) | collective-permute-done | bytes 90144 | tf_op jit(solution)/shard_map/ppermute | solution.py:428
  49.3 1.2 %collective-permute-start.12 = (f32[11,16,128]{2,1,0:T(8,128)S(1)}, f32[11,16,128]{2,1,0:T(8,128)S(1)}, u32[]{:S(2)}, u32[]{:S(2)}) collective-permute-start(f32[11,16,128]{2,1,0:T(8,128)S(1)} %get-tuple-element.31.refs_4_), channel_id=1, source_target_pairs={{0,2},{2,0},{1,3},{3,1},{4,6},{6,4},{5,7},{7,5},{8,10},{10,8},{9,1... | collective-permute-start | bytes 270344 | tf_op jit(solution)/shard_map/ppermute | solution.py:416
  51.5 3.2 %collective-permute-done.14.refs_7_ = f32[7,16,128]{2,1,0:T(8,128)S(1)} collective-permute-done((f32[7,16,128]{2,1,0:T(8,128)S(1)}, f32[7,16,128]{2,1,0:T(8,128)S(1)}, u32[]{:S(2)}, u32[]{:S(2)}) %collective-permute-start.14) | collective-permute-done | bytes 57376 | tf_op jit(solution)/shard_map/ppermute | solution.py:423
  54.7 12.3 %later_step.1 = (f32[11,16,128]{2,1,0:T(8,128)S(1)}, f32[11,16,128]{2,1,0:T(8,128)S(1)}, f32[7,16,128]{2,1,0:T(8,128)S(1)}, f32[7,16,128]{2,1,0:T(8,128)S(1)}) custom-call(s32[2]{0:T(128)S(1)} %copy-done.6, s32[2,2,8]{2,1,0:T(2,128)S(1)} %bitcast.6, f32[1,1]{1,0:T(1,128)S(6)} %copy.8.psf_ref, f32[2,1,1,128,128]{4,3,2,1,0:T(8,128)S(1)} %copy-done.2, ...), custom_call_target="tpu_custom_call" | custom-call | tf_op jit(solution)/shard_map/later_step/pallas_call | solution.py:326
  67.1 1.0 %collective-permute-start.15 = (f32[11,16,128]{2,1,0:T(8,128)S(1)}, f32[11,16,128]{2,1,0:T(8,128)S(1)}, u32[]{:S(2)}, u32[]{:S(2)}) collective-permute-start(f32[11,16,128]{2,1,0:T(8,128)S(1)} %get-tuple-element.34), channel_id=1, source_target_pairs={{0,2},{2,0},{1,3},{3,1},{4,6},{6,4},{5,7},{7,5},{8,10},{10,8},{9,1... | collective-permute-start | bytes 270344 | tf_op jit(solution)/shard_map/ppermute | solution.py:416
  69.3 3.1 %collective-permute-done.17 = f32[7,16,128]{2,1,0:T(8,128)S(1)} collective-permute-done((f32[7,16,128]{2,1,0:T(8,128)S(1)}, f32[7,16,128]{2,1,0:T(8,128)S(1)}, u32[]{:S(2)}, u32[]{:S(2)}) %collective-permute-start.17) | collective-permute-done | bytes 57376 | tf_op jit(solution)/shard_map/ppermute | solution.py:423
  73.3 1.1 %collective-permute-start.18 = (f32[11,8,128]{2,1,0:T(8,128)S(1)}, f32[11,8,128]{2,1,0:T(8,128)S(1)}, u32[]{:S(2)}, u32[]{:S(2)}) collective-permute-start(f32[11,8,128]{2,1,0:T(8,128)S(1)} %get-tuple-element.38), channel_id=1, source_target_pairs={{0,4},{4,8},{8,12},{12,0},{1,5},{5,9},{9,13},{13,1},{2,6},{6,10},{... | collective-permute-start | bytes 135176 | tf_op jit(solution)/shard_map/ppermute | solution.py:428
  74.8 2.8 %collective-permute-start.20 = (f32[11,8,128]{2,1,0:T(8,128)S(1)}, f32[11,8,128]{2,1,0:T(8,128)S(1)}, u32[]{:S(2)}, u32[]{:S(2)}) collective-permute-start(f32[11,8,128]{2,1,0:T(8,128)S(1)} %get-tuple-element.40), channel_id=1, source_target_pairs={{0,12},{4,0},{8,4},{12,8},{1,13},{5,1},{9,5},{13,9},{2,14},{6,2},{... | collective-permute-start | bytes 135176 | tf_op jit(solution)/shard_map/ppermute | solution.py:428
  77.7 2.0 %collective-permute-done.18 = f32[11,8,128]{2,1,0:T(8,128)S(1)} collective-permute-done((f32[11,8,128]{2,1,0:T(8,128)S(1)}, f32[11,8,128]{2,1,0:T(8,128)S(1)}, u32[]{:S(2)}, u32[]{:S(2)}) %collective-permute-start.18) | collective-permute-done | bytes 45088 | tf_op jit(solution)/shard_map/ppermute | solution.py:428
  79.7 1.5 %collective-permute-done.19 = f32[11,8,128]{2,1,0:T(8,128)S(1)} collective-permute-done((f32[11,8,128]{2,1,0:T(8,128)S(1)}, f32[11,8,128]{2,1,0:T(8,128)S(1)}, u32[]{:S(2)}, u32[]{:S(2)}) %collective-permute-start.19) | collective-permute-done | bytes 45088 | tf_op jit(solution)/shard_map/ppermute | solution.py:428
  83.4 1.7 %collective-permute-done.23.refs_3_ = f32[11,8,128]{2,1,0:T(8,128)S(1)} collective-permute-done((f32[11,8,128]{2,1,0:T(8,128)S(1)}, f32[11,8,128]{2,1,0:T(8,128)S(1)}, u32[]{:S(2)}, u32[]{:S(2)}) %collective-permute-start.23) | collective-permute-done | bytes 45088 | tf_op jit(solution)/shard_map/ppermute | solution.py:423
  85.2 1.5 %collective-permute-done.21.refs_1_ = f32[11,8,128]{2,1,0:T(8,128)S(1)} collective-permute-done((f32[11,8,128]{2,1,0:T(8,128)S(1)}, f32[11,8,128]{2,1,0:T(8,128)S(1)}, u32[]{:S(2)}, u32[]{:S(2)}) %collective-permute-start.21) | collective-permute-done | bytes 45088 | tf_op jit(solution)/shard_map/ppermute | solution.py:416
  (50 shorter events, 12.9 us)
Async XLA Ops:
  2.2 7.2 %collective-permute-start.2 = (f32[12,8,128]{2,1,0:T(8,128)S(1)}, f32[12,8,128]{2,1,0:T(8,128)S(1)}, u32[]{:S(2)}, u32[]{:S(2)}) collective-permute-start(f32[12,8,128]{2,1,0:T(8,128)S(1)} %pack.1.refs_0_), channel_id=1, source_target_pairs={{0,12},{4,0},{8,4},{12,8},{1,13},{5,1},{9,5},{13,9},{2,14},{6,2},{... | collective-permute-start | bytes 147464 | tf_op jit(solution)/shard_map/ppermute | solution.py:428
  7.3 5.0 %collective-permute-start.1 = (f32[12,8,128]{2,1,0:T(8,128)S(1)}, f32[12,8,128]{2,1,0:T(8,128)S(1)}, u32[]{:S(2)}, u32[]{:S(2)}) collective-permute-start(f32[12,8,128]{2,1,0:T(8,128)S(1)} %pack.1.refs_0_), channel_id=1, source_target_pairs={{0,8},{4,12},{8,0},{12,4},{1,9},{5,13},{9,1},{13,5},{2,10},{6,14},... | collective-permute-start | bytes 147464 | tf_op jit(solution)/shard_map/ppermute | solution.py:428
  7.3 5.9 %collective-permute-start = (f32[12,8,128]{2,1,0:T(8,128)S(1)}, f32[12,8,128]{2,1,0:T(8,128)S(1)}, u32[]{:S(2)}, u32[]{:S(2)}) collective-permute-start(f32[12,8,128]{2,1,0:T(8,128)S(1)} %pack.1.refs_0_), channel_id=1, source_target_pairs={{0,4},{4,8},{8,12},{12,0},{1,5},{5,9},{9,13},{13,1},{2,6},{6,10},{... | collective-permute-start | bytes 147464 | tf_op jit(solution)/shard_map/ppermute | solution.py:428
  14.0 5.8 %collective-permute-start.3 = (f32[11,16,128]{2,1,0:T(8,128)S(1)}, f32[11,16,128]{2,1,0:T(8,128)S(1)}, u32[]{:S(2)}, u32[]{:S(2)}) collective-permute-start(f32[11,16,128]{2,1,0:T(8,128)S(1)} %get-tuple-element.24.refs_0_), channel_id=1, source_target_pairs={{0,2},{2,0},{1,3},{3,1},{4,6},{6,4},{5,7},{7,5},{8,10},{10,8},{9,1... | collective-permute-start | bytes 270344 | tf_op jit(solution)/shard_map/ppermute | solution.py:416
  15.6 4.2 %collective-permute-start.5 = (f32[7,16,128]{2,1,0:T(8,128)S(1)}, f32[7,16,128]{2,1,0:T(8,128)S(1)}, u32[]{:S(2)}, u32[]{:S(2)}) collective-permute-start(f32[7,16,128]{2,1,0:T(8,128)S(1)} %get-tuple-element.25), channel_id=1, source_target_pairs={{0,3},{1,2},{2,1},{3,0},{4,7},{5,6},{6,5},{7,4},{8,11},{9,10},{10,... | collective-permute-start | bytes 172040 | tf_op jit(solution)/shard_map/ppermute | solution.py:423
  15.6 4.2 %collective-permute-start.4 = (f32[7,16,128]{2,1,0:T(8,128)S(1)}, f32[7,16,128]{2,1,0:T(8,128)S(1)}, u32[]{:S(2)}, u32[]{:S(2)}) collective-permute-start(f32[7,16,128]{2,1,0:T(8,128)S(1)} %get-tuple-element.25), channel_id=1, source_target_pairs={{0,1},{1,0},{2,3},{3,2},{4,5},{5,4},{6,7},{7,6},{8,9},{9,8},{10,11... | collective-permute-start | bytes 172040 | tf_op jit(solution)/shard_map/ppermute | solution.py:423
  32.1 5.3 %collective-permute-start.6 = (f32[11,16,128]{2,1,0:T(8,128)S(1)}, f32[11,16,128]{2,1,0:T(8,128)S(1)}, u32[]{:S(2)}, u32[]{:S(2)}) collective-permute-start(f32[11,16,128]{2,1,0:T(8,128)S(1)} %get-tuple-element.27), channel_id=1, source_target_pairs={{0,2},{2,0},{1,3},{3,1},{4,6},{6,4},{5,7},{7,5},{8,10},{10,8},{9,1... | collective-permute-start | bytes 270344 | tf_op jit(solution)/shard_map/ppermute | solution.py:416
  33.0 1.3 %collective-permute-start.7 = (f32[7,16,128]{2,1,0:T(8,128)S(1)}, f32[7,16,128]{2,1,0:T(8,128)S(1)}, u32[]{:S(2)}, u32[]{:S(2)}) collective-permute-start(f32[7,16,128]{2,1,0:T(8,128)S(1)} %get-tuple-element.28), channel_id=1, source_target_pairs={{0,1},{1,0},{2,3},{3,2},{4,5},{5,4},{6,7},{7,6},{8,9},{9,8},{10,11... | collective-permute-start | bytes 172040 | tf_op jit(solution)/shard_map/ppermute | solution.py:423
  33.2 4.1 %collective-permute-start.8 = (f32[7,16,128]{2,1,0:T(8,128)S(1)}, f32[7,16,128]{2,1,0:T(8,128)S(1)}, u32[]{:S(2)}, u32[]{:S(2)}) collective-permute-start(f32[7,16,128]{2,1,0:T(8,128)S(1)} %get-tuple-element.29), channel_id=1, source_target_pairs={{0,3},{1,2},{2,1},{3,0},{4,7},{5,6},{6,5},{7,4},{8,11},{9,10},{10,... | collective-permute-start | bytes 172040 | tf_op jit(solution)/shard_map/ppermute | solution.py:423
  37.4 5.0 %collective-permute-start.11 = (f32[11,16,128]{2,1,0:T(8,128)S(1)}, f32[11,16,128]{2,1,0:T(8,128)S(1)}, u32[]{:S(2)}, u32[]{:S(2)}) collective-permute-start(f32[11,16,128]{2,1,0:T(8,128)S(1)} %pad_add_fusion.1.refs_0_), channel_id=1, source_target_pairs={{0,12},{4,0},{8,4},{12,8},{1,13},{5,1},{9,5},{13,9},{2,14},{6,2},{... | collective-permute-start | bytes 270344 | tf_op jit(solution)/shard_map/ppermute | solution.py:428
  38.7 10.3 %collective-permute-start.10 = (f32[11,16,128]{2,1,0:T(8,128)S(1)}, f32[11,16,128]{2,1,0:T(8,128)S(1)}, u32[]{:S(2)}, u32[]{:S(2)}) collective-permute-start(f32[11,16,128]{2,1,0:T(8,128)S(1)} %pad_add_fusion.1.refs_0_), channel_id=1, source_target_pairs={{0,8},{4,12},{8,0},{12,4},{1,9},{5,13},{9,1},{13,5},{2,10},{6,14},... | collective-permute-start | bytes 270344 | tf_op jit(solution)/shard_map/ppermute | solution.py:428
  40.2 8.8 %collective-permute-start.9 = (f32[11,16,128]{2,1,0:T(8,128)S(1)}, f32[11,16,128]{2,1,0:T(8,128)S(1)}, u32[]{:S(2)}, u32[]{:S(2)}) collective-permute-start(f32[11,16,128]{2,1,0:T(8,128)S(1)} %pad_add_fusion.1.refs_0_), channel_id=1, source_target_pairs={{0,4},{4,8},{8,12},{12,0},{1,5},{5,9},{9,13},{13,1},{2,6},{6,10},{... | collective-permute-start | bytes 270344 | tf_op jit(solution)/shard_map/ppermute | solution.py:428
  49.3 5.4 %collective-permute-start.12 = (f32[11,16,128]{2,1,0:T(8,128)S(1)}, f32[11,16,128]{2,1,0:T(8,128)S(1)}, u32[]{:S(2)}, u32[]{:S(2)}) collective-permute-start(f32[11,16,128]{2,1,0:T(8,128)S(1)} %get-tuple-element.31.refs_4_), channel_id=1, source_target_pairs={{0,2},{2,0},{1,3},{3,1},{4,6},{6,4},{5,7},{7,5},{8,10},{10,8},{9,1... | collective-permute-start | bytes 270344 | tf_op jit(solution)/shard_map/ppermute | solution.py:416
  50.6 4.2 %collective-permute-start.14 = (f32[7,16,128]{2,1,0:T(8,128)S(1)}, f32[7,16,128]{2,1,0:T(8,128)S(1)}, u32[]{:S(2)}, u32[]{:S(2)}) collective-permute-start(f32[7,16,128]{2,1,0:T(8,128)S(1)} %get-tuple-element.32), channel_id=1, source_target_pairs={{0,3},{1,2},{2,1},{3,0},{4,7},{5,6},{6,5},{7,4},{8,11},{9,10},{10,... | collective-permute-start | bytes 172040 | tf_op jit(solution)/shard_map/ppermute | solution.py:423
  50.6 4.2 %collective-permute-start.13 = (f32[7,16,128]{2,1,0:T(8,128)S(1)}, f32[7,16,128]{2,1,0:T(8,128)S(1)}, u32[]{:S(2)}, u32[]{:S(2)}) collective-permute-start(f32[7,16,128]{2,1,0:T(8,128)S(1)} %get-tuple-element.32), channel_id=1, source_target_pairs={{0,1},{1,0},{2,3},{3,2},{4,5},{5,4},{6,7},{7,6},{8,9},{9,8},{10,11... | collective-permute-start | bytes 172040 | tf_op jit(solution)/shard_map/ppermute | solution.py:423
  67.1 5.4 %collective-permute-start.15 = (f32[11,16,128]{2,1,0:T(8,128)S(1)}, f32[11,16,128]{2,1,0:T(8,128)S(1)}, u32[]{:S(2)}, u32[]{:S(2)}) collective-permute-start(f32[11,16,128]{2,1,0:T(8,128)S(1)} %get-tuple-element.34), channel_id=1, source_target_pairs={{0,2},{2,0},{1,3},{3,1},{4,6},{6,4},{5,7},{7,5},{8,10},{10,8},{9,1... | collective-permute-start | bytes 270344 | tf_op jit(solution)/shard_map/ppermute | solution.py:416
  68.1 1.2 %collective-permute-start.16 = (f32[7,16,128]{2,1,0:T(8,128)S(1)}, f32[7,16,128]{2,1,0:T(8,128)S(1)}, u32[]{:S(2)}, u32[]{:S(2)}) collective-permute-start(f32[7,16,128]{2,1,0:T(8,128)S(1)} %get-tuple-element.35), channel_id=1, source_target_pairs={{0,1},{1,0},{2,3},{3,2},{4,5},{5,4},{6,7},{7,6},{8,9},{9,8},{10,11... | collective-permute-start | bytes 172040 | tf_op jit(solution)/shard_map/ppermute | solution.py:423
  68.3 4.2 %collective-permute-start.17 = (f32[7,16,128]{2,1,0:T(8,128)S(1)}, f32[7,16,128]{2,1,0:T(8,128)S(1)}, u32[]{:S(2)}, u32[]{:S(2)}) collective-permute-start(f32[7,16,128]{2,1,0:T(8,128)S(1)} %get-tuple-element.36), channel_id=1, source_target_pairs={{0,3},{1,2},{2,1},{3,0},{4,7},{5,6},{6,5},{7,4},{8,11},{9,10},{10,... | collective-permute-start | bytes 172040 | tf_op jit(solution)/shard_map/ppermute | solution.py:423
  73.3 6.4 %collective-permute-start.18 = (f32[11,8,128]{2,1,0:T(8,128)S(1)}, f32[11,8,128]{2,1,0:T(8,128)S(1)}, u32[]{:S(2)}, u32[]{:S(2)}) collective-permute-start(f32[11,8,128]{2,1,0:T(8,128)S(1)} %get-tuple-element.38), channel_id=1, source_target_pairs={{0,4},{4,8},{8,12},{12,0},{1,5},{5,9},{9,13},{13,1},{2,6},{6,10},{... | collective-permute-start | bytes 135176 | tf_op jit(solution)/shard_map/ppermute | solution.py:428
  74.5 6.7 %collective-permute-start.19 = (f32[11,8,128]{2,1,0:T(8,128)S(1)}, f32[11,8,128]{2,1,0:T(8,128)S(1)}, u32[]{:S(2)}, u32[]{:S(2)}) collective-permute-start(f32[11,8,128]{2,1,0:T(8,128)S(1)} %get-tuple-element.39), channel_id=1, source_target_pairs={{0,8},{4,12},{8,0},{12,4},{1,9},{5,13},{9,1},{13,5},{2,10},{6,14},... | collective-permute-start | bytes 135176 | tf_op jit(solution)/shard_map/ppermute | solution.py:428
  74.8 6.4 %collective-permute-start.20 = (f32[11,8,128]{2,1,0:T(8,128)S(1)}, f32[11,8,128]{2,1,0:T(8,128)S(1)}, u32[]{:S(2)}, u32[]{:S(2)}) collective-permute-start(f32[11,8,128]{2,1,0:T(8,128)S(1)} %get-tuple-element.40), channel_id=1, source_target_pairs={{0,12},{4,0},{8,4},{12,8},{1,13},{5,1},{9,5},{13,9},{2,14},{6,2},{... | collective-permute-start | bytes 135176 | tf_op jit(solution)/shard_map/ppermute | solution.py:428
  81.2 4.0 %collective-permute-start.23 = (f32[11,8,128]{2,1,0:T(8,128)S(1)}, f32[11,8,128]{2,1,0:T(8,128)S(1)}, u32[]{:S(2)}, u32[]{:S(2)}) collective-permute-start(f32[11,8,128]{2,1,0:T(8,128)S(1)} %add_add_fusion.refs_0_), channel_id=1, source_target_pairs={{0,3},{1,2},{2,1},{3,0},{4,7},{5,6},{6,5},{7,4},{8,11},{9,10},{10,... | collective-permute-start | bytes 135176 | tf_op jit(solution)/shard_map/ppermute | solution.py:423
  81.9 3.3 %collective-permute-start.22 = (f32[11,8,128]{2,1,0:T(8,128)S(1)}, f32[11,8,128]{2,1,0:T(8,128)S(1)}, u32[]{:S(2)}, u32[]{:S(2)}) collective-permute-start(f32[11,8,128]{2,1,0:T(8,128)S(1)} %add_add_fusion.refs_0_), channel_id=1, source_target_pairs={{0,1},{1,0},{2,3},{3,2},{4,5},{5,4},{6,7},{7,6},{8,9},{9,8},{10,11... | collective-permute-start | bytes 135176 | tf_op jit(solution)/shard_map/ppermute | solution.py:423
  82.6 4.0 %collective-permute-start.21 = (f32[11,8,128]{2,1,0:T(8,128)S(1)}, f32[11,8,128]{2,1,0:T(8,128)S(1)}, u32[]{:S(2)}, u32[]{:S(2)}) collective-permute-start(f32[11,8,128]{2,1,0:T(8,128)S(1)} %add_add_fusion.refs_0_), channel_id=1, source_target_pairs={{0,2},{2,0},{1,3},{3,1},{4,6},{6,4},{5,7},{7,5},{8,10},{10,8},{9,1... | collective-permute-start | bytes 135176 | tf_op jit(solution)/shard_map/ppermute | solution.py:416
  (7 other events, 58.7 us)

commit v9 on v8

--- a/solution.py
+++ b/solution.py
@@ -159,7 +159,8 @@
     taken = 2 * epochs * (2 if later else 1)
     ins, refs = refs[:taken], refs[taken:]
     outs, refs = refs[: 2 * epochs], refs[2 * epochs :]
-    shared, amps, derived, prof_y, pieces_x, pieces_y, image, sums, half, other = refs[:10]
+    shared, amps, derived, image, sums, half, other = refs[:7]
+    prof_y, pieces_x, pieces_y, by_x, by_y = (refs[7 + 2 * n : 9 + 2 * n] for n in range(5))
     band, epoch = lax.axis_index("band"), lax.axis_index("epoch")
     tiles = data_ref.shape[0]
     pixels = data_ref.shape[-1]
@@ -174,7 +175,7 @@
         return r // HALF, r % HALF
 
     if later:
-        moved, moved_amps = refs[10:]
+        moved, moved_amps = refs[17:]
         put_together(layout, band, epoch, ins[2 * epochs :], half, other, moved, moved_amps)
         for k in range(4):
             shift = 0.0
@@ -218,31 +219,42 @@
     def total(x):
         return jnp.sum(x, axis=0, keepdims=True)
 
-    def line(index, c, s):
-        return derived[index, c, pl.ds(s, 1), :]
-
-    together = 2
+    def line(index, c, g):
+        return derived[index, c, pl.ds(g, 1), :]
+
+    def place(t, s):
+        s = jnp.minimum(s, slots - 1)
+        return t * slots + s, offsets_ref[t, 0, s].astype(F32), offsets_ref[t, 1, s].astype(F32)
+
+    spans = [(first, min(2, COMPS - first)) for first in range(0, COMPS, 2)]
+
     for t in range(tiles):
-        trips = (counts_ref[t] + together - 1) // together
+        trips = (counts_ref[t] + 1) // 2
+
+        def profiles(i, u):
+            at = i + u // 2
+            g, off_x, off_y = place(t, 2 * i + u)
+            for c in range(COMPS):
+                d = grid - (line(0, c, g) + off_x)
+                e = jnp.exp2(d * d * line(2, c, g))
+                pieces_x[u % 2][at, :, c * 128 : (c + 1) * 128] = cut(e, SPLIT_UNIT)
+                d = grid - (line(1, c, g) + off_y)
+                e = jnp.exp2(d * d * line(3, c, g))
+                prof_y[u % 2][at, :, c * 128 : (c + 1) * 128] = e
+                pieces_y[u % 2][at, :, c * 128 : (c + 1) * 128] = cut(e * line(4, c, g), line(5, c, g))
+
+        def add_image(i, u):
+            image[...] += lax.dot_general(
+                pieces_x[u][i], pieces_y[u][i], (((1,), (1,)), ((), ())), preferred_element_type=F32
+            )
+
         image[...] = jnp.zeros_like(image)
+        profiles(0, 0)
 
         def render(i, carry):
-            for u in range(together):
-                s = i * together + u
-                g = t * slots + s
-                off_x = offsets_ref[t, 0, s].astype(F32)
-                off_y = offsets_ref[t, 1, s].astype(F32)
-                for c in range(COMPS):
-                    d = grid - (line(0, c, g) + off_x)
-                    e = jnp.exp2(d * d * line(2, c, g))
-                    pieces_x[s, :, c * 128 : (c + 1) * 128] = cut(e, SPLIT_UNIT)
-                    d = grid - (line(1, c, g) + off_y)
-                    e = jnp.exp2(d * d * line(3, c, g))
-                    prof_y[s * COMPS + c] = e
-                    pieces_y[s, :, c * 128 : (c + 1) * 128] = cut(e * line(4, c, g), line(5, c, g))
-                image[...] += lax.dot_general(
-                    pieces_x[s], pieces_y[s], (((1,), (1,)), ((), ())), preferred_element_type=F32
-                )
+            for u in range(2):
+                add_image(i, u)
+                profiles(i, u + 1)
             return carry
 
         lax.fori_loop(0, trips, render, 0)
@@ -253,32 +265,37 @@
         cotangent = weight_ref[t, 0, 0] * (model - data_ref[t, 0, 0])
         left_x, left_y = stack(cotangent), stack(cotangent.T)
 
+        def products(i, u, first, here):
+            at = i + u // 2
+            span = slice(first * 128, (first + here) * 128)
+            by_x[u % 2][:, span] = times(left_x, pieces_y[u % 2][at, :, span])
+            by_y[u % 2][:, span] = times(left_y, pieces_x[u % 2][at, :, span])
+
+        def reduce(i, u, first, here):
+            g, off_x, off_y = place(t, 2 * i + u)
+            for c in range(first, first + here):
+                at = slice(c * 128, (c + 1) * 128)
+                d = grid - (line(0, c, g) + off_x)
+                e = pieces_x[u][i, :pixels, at] + pieces_x[u][i, pixels:, at]
+                e = e * by_x[u][:, at]
+                e1 = e * d
+                sums[0, c, pl.ds(g, 1), :] = total(e1)
+                sums[1, c, pl.ds(g, 1), :] = total(e1 * d)
+                d = grid - (line(1, c, g) + off_y)
+                e = prof_y[u][i, :, at] * by_y[u][:, at]
+                e1 = e * d
+                sums[2, c, pl.ds(g, 1), :] = total(e1)
+                sums[3, c, pl.ds(g, 1), :] = total(e1 * d)
+                sums[4, c, pl.ds(g, 1), :] = total(e)
+
+        for span in spans:
+            products(0, 0, *span)
+
         def pull(i, carry):
-            for u in range(together):
-                s = i * together + u
-                g = t * slots + s
-                off_x = offsets_ref[t, 0, s].astype(F32)
-                off_y = offsets_ref[t, 1, s].astype(F32)
-                for first in range(0, COMPS, 2):
-                    here = min(2, COMPS - first)
-                    span = pl.ds(first * 128, 128 * here)
-                    by_x = times(left_x, pieces_y[s, :, span])
-                    by_y = times(left_y, pieces_x[s, :, span])
-                    for n in range(here):
-                        c = first + n
-                        d = grid - (line(0, c, g) + off_x)
-                        at = slice(c * 128, (c + 1) * 128)
-                        e = pieces_x[s, :pixels, at] + pieces_x[s, pixels:, at]
-                        e = e * by_x[:, n * 128 : (n + 1) * 128]
-                        e1 = e * d
-                        sums[0, c, pl.ds(g, 1), :] = total(e1)
-                        sums[1, c, pl.ds(g, 1), :] = total(e1 * d)
-                        d = grid - (line(1, c, g) + off_y)
-                        e = prof_y[s * COMPS + c] * by_y[:, n * 128 : (n + 1) * 128]
-                        e1 = e * d
-                        sums[2, c, pl.ds(g, 1), :] = total(e1)
-                        sums[3, c, pl.ds(g, 1), :] = total(e1 * d)
-                        sums[4, c, pl.ds(g, 1), :] = total(e)
+            for u in range(2):
+                for span in spans:
+                    products(i, u + 1, *span)
+                    reduce(i, u, *span)
             return carry
 
         lax.fori_loop(0, trips, pull, 0)
@@ -331,14 +348,14 @@
         scratch_shapes=together
         + [
             pltpu.VMEM((6, COMPS, wide, 128), F32),
-            pltpu.VMEM((slots * COMPS, pixels, 128), F32),
-            pltpu.VMEM((slots, 2 * pixels, COMPS * 128), F32),
-            pltpu.VMEM((slots, 2 * pixels, COMPS * 128), F32),
             pltpu.VMEM((2 * pixels, 2 * pixels), F32),
             pltpu.VMEM((5, COMPS, wide, 128), F32),
             pltpu.VMEM((epochs, rows, wide, 128), F32),
             pltpu.VMEM((epochs, shared_rows, wide, 128), F32),
         ]
+        + [pltpu.VMEM((slots // 2 + 1 - u, pixels, COMPS * 128), F32) for u in range(2)]
+        + [pltpu.VMEM((slots // 2 + 1 - u, 2 * pixels, COMPS * 128), F32) for u in (0, 1, 0, 1)]
+        + [pltpu.VMEM((pixels, COMPS * 128), F32)] * 4
         + (together if later else []),
         compiler_params=params(40),
         name="later_step" if later else "first_step",

time: 88.2 us -> 89.6 us (1.016); the launches traced: 87.4 us -> 90.7 us
  Pallas kernels: 27.8 us -> 32.2 us
  waiting for transfers between devices: 32.4 us -> 30.5 us
    pallas_call x2, Pallas kernels: 24.6 us -> 29 us  [step_gradient(): pl.pallas_call(functools.partial(step_kernel, layout, later), out_shape=[...]
    ppermute x9, waiting for transfers between devices: 16.8 us -> 14.7 us  [round_tiles(): lax.ppermute(arrays[k], 'tile', [(i, (i + k) % owners) for i in range(own...]
where the time goes in v9:
time: 89.6 us; the launch traced here: 90.7 us
  Pallas kernels  32.2 us (36%)
  waiting for transfers between devices  30.5 us (34%)
  starting transfers between devices  25.5 us (28%)
  local copies, waits for them, and re-layouts  1.63 us (2%)
    pallas_call x2, Pallas kernels, step_gradient(): pl.pallas_call(functools.partial(step_kernel, layout, later), out_shape=[...  29 us
    ppermute x9, waiting for transfers between devices, round_tiles(): lax.ppermute(arrays[k], 'tile', [(i, (i + k) % owners) for i in range(own...  14.7 us
    ppermute x9, starting transfers between devices, round_tiles(): lax.ppermute(arrays[k], 'tile', [(i, (i + k) % owners) for i in range(own...  14.5 us
    ppermute x10, waiting for transfers between devices, to_peers(): kept.append(lax.ppermute(other[k], ('epoch', 'band'), pairs))  14.1 us
    ppermute x5, starting transfers between devices, to_peers(): lax.ppermute(same[k], 'epoch', [(i, (i + k) % epochs) for i in range(epoc...  5.48 us
    ppermute x10, starting transfers between devices, to_peers(): kept.append(lax.ppermute(other[k], ('epoch', 'band'), pairs))  5.48 us
  transfers between devices with their start and end apart: 24, of which 14 were waited for; matrix products, arithmetic and copies ran while one was open for 0% of the time, Pallas kernels for 0%

profile of v9, /device:TPU:0, one launch (start us, length us, event | category | flops | bytes accessed | tf_op | source)
XLA Modules:
  0.0 90.7 jit_solution(5340738752603678698)
XLA Ops:
  2.2 5.1 %collective-permute-start.2 = (f32[12,8,128]{2,1,0:T(8,128)S(1)}, f32[12,8,128]{2,1,0:T(8,128)S(1)}, u32[]{:S(2)}, u32[]{:S(2)}) collective-permute-start(f32[12,8,128]{2,1,0:T(8,128)S(1)} %pack.1.refs_0_), channel_id=1, source_target_pairs={{0,12},{4,0},{8,4},{12,8},{1,13},{5,1},{9,5},{13,9},{2,14},{6,2},{... | collective-permute-start | bytes 147464 | tf_op jit(solution)/shard_map/ppermute | solution.py:445
  7.3 1.0 %collective-permute-start = (f32[12,8,128]{2,1,0:T(8,128)S(1)}, f32[12,8,128]{2,1,0:T(8,128)S(1)}, u32[]{:S(2)}, u32[]{:S(2)}) collective-permute-start(f32[12,8,128]{2,1,0:T(8,128)S(1)} %pack.1.refs_0_), channel_id=1, source_target_pairs={{0,4},{4,8},{8,12},{12,0},{1,5},{5,9},{9,13},{13,1},{2,6},{6,10},{... | collective-permute-start | bytes 147464 | tf_op jit(solution)/shard_map/ppermute | solution.py:445
  8.3 1.0 %collective-permute-done.2.refs_3_ = f32[12,8,128]{2,1,0:T(8,128)S(1)} collective-permute-done((f32[12,8,128]{2,1,0:T(8,128)S(1)}, f32[12,8,128]{2,1,0:T(8,128)S(1)}, u32[]{:S(2)}, u32[]{:S(2)}) %collective-permute-start.2) | collective-permute-done | bytes 49184 | tf_op jit(solution)/shard_map/ppermute | solution.py:445
  9.4 2.9 %collective-permute-done.1.refs_2_ = f32[12,8,128]{2,1,0:T(8,128)S(1)} collective-permute-done((f32[12,8,128]{2,1,0:T(8,128)S(1)}, f32[12,8,128]{2,1,0:T(8,128)S(1)}, u32[]{:S(2)}, u32[]{:S(2)}) %collective-permute-start.1) | collective-permute-done | bytes 49184 | tf_op jit(solution)/shard_map/ppermute | solution.py:445
  14.0 1.5 %collective-permute-start.3 = (f32[11,16,128]{2,1,0:T(8,128)S(1)}, f32[11,16,128]{2,1,0:T(8,128)S(1)}, u32[]{:S(2)}, u32[]{:S(2)}) collective-permute-start(f32[11,16,128]{2,1,0:T(8,128)S(1)} %get-tuple-element.24.refs_0_), channel_id=1, source_target_pairs={{0,2},{2,0},{1,3},{3,1},{4,6},{6,4},{5,7},{7,5},{8,10},{10,8},{9,1... | collective-permute-start | bytes 270344 | tf_op jit(solution)/shard_map/ppermute | solution.py:433
  16.9 2.9 %collective-permute-done.5.refs_3_ = f32[7,16,128]{2,1,0:T(8,128)S(1)} collective-permute-done((f32[7,16,128]{2,1,0:T(8,128)S(1)}, f32[7,16,128]{2,1,0:T(8,128)S(1)}, u32[]{:S(2)}, u32[]{:S(2)}) %collective-permute-start.5) | collective-permute-done | bytes 57376 | tf_op jit(solution)/shard_map/ppermute | solution.py:440
  19.8 14.5 %first_step.1 = (f32[11,16,128]{2,1,0:T(8,128)S(1)}, f32[11,16,128]{2,1,0:T(8,128)S(1)}, f32[7,16,128]{2,1,0:T(8,128)S(1)}, f32[7,16,128]{2,1,0:T(8,128)S(1)}) custom-call(s32[2]{0:T(128)S(1)} %copy-done.6, s32[2,2,8]{2,1,0:T(2,128)S(1)} %bitcast.5, f32[1,1]{1,0:T(1,128)S(6)} %copy.8.psf_ref, f32[2,1,1,128,128]{4,3,2,1,0:T(8,128)S(1)} %copy-done.2, ...), custom_call_target="tpu_custom_call" | custom-call | tf_op jit(solution)/shard_map/first_step/pallas_call | solution.py:343
  35.4 1.1 %collective-permute-start.8 = (f32[7,16,128]{2,1,0:T(8,128)S(1)}, f32[7,16,128]{2,1,0:T(8,128)S(1)}, u32[]{:S(2)}, u32[]{:S(2)}) collective-permute-start(f32[7,16,128]{2,1,0:T(8,128)S(1)} %get-tuple-element.29), channel_id=1, source_target_pairs={{0,3},{1,2},{2,1},{3,0},{4,7},{5,6},{6,5},{7,4},{8,11},{9,10},{10,... | collective-permute-start | bytes 172040 | tf_op jit(solution)/shard_map/ppermute | solution.py:440
  36.5 3.1 %collective-permute-done.8 = f32[7,16,128]{2,1,0:T(8,128)S(1)} collective-permute-done((f32[7,16,128]{2,1,0:T(8,128)S(1)}, f32[7,16,128]{2,1,0:T(8,128)S(1)}, u32[]{:S(2)}, u32[]{:S(2)}) %collective-permute-start.8) | collective-permute-done | bytes 57376 | tf_op jit(solution)/shard_map/ppermute | solution.py:440
  39.6 1.2 %collective-permute-start.11 = (f32[11,16,128]{2,1,0:T(8,128)S(1)}, f32[11,16,128]{2,1,0:T(8,128)S(1)}, u32[]{:S(2)}, u32[]{:S(2)}) collective-permute-start(f32[11,16,128]{2,1,0:T(8,128)S(1)} %pad_add_fusion.1.refs_0_), channel_id=1, source_target_pairs={{0,12},{4,0},{8,4},{12,8},{1,13},{5,1},{9,5},{13,9},{2,14},{6,2},{... | collective-permute-start | bytes 270344 | tf_op jit(solution)/shard_map/ppermute | solution.py:445
  40.9 1.9 %collective-permute-start.9 = (f32[11,16,128]{2,1,0:T(8,128)S(1)}, f32[11,16,128]{2,1,0:T(8,128)S(1)}, u32[]{:S(2)}, u32[]{:S(2)}) collective-permute-start(f32[11,16,128]{2,1,0:T(8,128)S(1)} %pad_add_fusion.1.refs_0_), channel_id=1, source_target_pairs={{0,4},{4,8},{8,12},{12,0},{1,5},{5,9},{9,13},{13,1},{2,6},{6,10},{... | collective-permute-start | bytes 270344 | tf_op jit(solution)/shard_map/ppermute | solution.py:445
  42.8 2.3 %collective-permute-done.11.refs_3_ = f32[11,16,128]{2,1,0:T(8,128)S(1)} collective-permute-done((f32[11,16,128]{2,1,0:T(8,128)S(1)}, f32[11,16,128]{2,1,0:T(8,128)S(1)}, u32[]{:S(2)}, u32[]{:S(2)}) %collective-permute-start.11) | collective-permute-done | bytes 90144 | tf_op jit(solution)/shard_map/ppermute | solution.py:445
  45.1 5.3 %collective-permute-done.10.refs_2_ = f32[11,16,128]{2,1,0:T(8,128)S(1)} collective-permute-done((f32[11,16,128]{2,1,0:T(8,128)S(1)}, f32[11,16,128]{2,1,0:T(8,128)S(1)}, u32[]{:S(2)}, u32[]{:S(2)}) %collective-permute-start.10) | collective-permute-done | bytes 90144 | tf_op jit(solution)/shard_map/ppermute | solution.py:445
  50.7 1.2 %collective-permute-start.12 = (f32[11,16,128]{2,1,0:T(8,128)S(1)}, f32[11,16,128]{2,1,0:T(8,128)S(1)}, u32[]{:S(2)}, u32[]{:S(2)}) collective-permute-start(f32[11,16,128]{2,1,0:T(8,128)S(1)} %get-tuple-element.31.refs_4_), channel_id=1, source_target_pairs={{0,2},{2,0},{1,3},{3,1},{4,6},{6,4},{5,7},{7,5},{8,10},{10,8},{9,1... | collective-permute-start | bytes 270344 | tf_op jit(solution)/shard_map/ppermute | solution.py:433
  52.9 3.2 %collective-permute-done.14.refs_7_ = f32[7,16,128]{2,1,0:T(8,128)S(1)} collective-permute-done((f32[7,16,128]{2,1,0:T(8,128)S(1)}, f32[7,16,128]{2,1,0:T(8,128)S(1)}, u32[]{:S(2)}, u32[]{:S(2)}) %collective-permute-start.14) | collective-permute-done | bytes 57376 | tf_op jit(solution)/shard_map/ppermute | solution.py:440
  56.1 14.5 %later_step.1 = (f32[11,16,128]{2,1,0:T(8,128)S(1)}, f32[11,16,128]{2,1,0:T(8,128)S(1)}, f32[7,16,128]{2,1,0:T(8,128)S(1)}, f32[7,16,128]{2,1,0:T(8,128)S(1)}) custom-call(s32[2]{0:T(128)S(1)} %copy-done.6, s32[2,2,8]{2,1,0:T(2,128)S(1)} %bitcast.6, f32[1,1]{1,0:T(1,128)S(6)} %copy.8.psf_ref, f32[2,1,1,128,128]{4,3,2,1,0:T(8,128)S(1)} %copy-done.2, ...), custom_call_target="tpu_custom_call" | custom-call | tf_op jit(solution)/shard_map/later_step/pallas_call | solution.py:343
  70.6 1.1 %collective-permute-start.15 = (f32[11,16,128]{2,1,0:T(8,128)S(1)}, f32[11,16,128]{2,1,0:T(8,128)S(1)}, u32[]{:S(2)}, u32[]{:S(2)}) collective-permute-start(f32[11,16,128]{2,1,0:T(8,128)S(1)} %get-tuple-element.34), channel_id=1, source_target_pairs={{0,2},{2,0},{1,3},{3,1},{4,6},{6,4},{5,7},{7,5},{8,10},{10,8},{9,1... | collective-permute-start | bytes 270344 | tf_op jit(solution)/shard_map/ppermute | solution.py:433
  71.9 1.0 %collective-permute-start.17 = (f32[7,16,128]{2,1,0:T(8,128)S(1)}, f32[7,16,128]{2,1,0:T(8,128)S(1)}, u32[]{:S(2)}, u32[]{:S(2)}) collective-permute-start(f32[7,16,128]{2,1,0:T(8,128)S(1)} %get-tuple-element.36), channel_id=1, source_target_pairs={{0,3},{1,2},{2,1},{3,0},{4,7},{5,6},{6,5},{7,4},{8,11},{9,10},{10,... | collective-permute-start | bytes 172040 | tf_op jit(solution)/shard_map/ppermute | solution.py:440
  73.0 3.1 %collective-permute-done.17 = f32[7,16,128]{2,1,0:T(8,128)S(1)} collective-permute-done((f32[7,16,128]{2,1,0:T(8,128)S(1)}, f32[7,16,128]{2,1,0:T(8,128)S(1)}, u32[]{:S(2)}, u32[]{:S(2)}) %collective-permute-start.17) | collective-permute-done | bytes 57376 | tf_op jit(solution)/shard_map/ppermute | solution.py:440
  77.2 2.0 %collective-permute-start.19 = (f32[11,8,128]{2,1,0:T(8,128)S(1)}, f32[11,8,128]{2,1,0:T(8,128)S(1)}, u32[]{:S(2)}, u32[]{:S(2)}) collective-permute-start(f32[11,8,128]{2,1,0:T(8,128)S(1)} %get-tuple-element.39), channel_id=1, source_target_pairs={{0,8},{4,12},{8,0},{12,4},{1,9},{5,13},{9,1},{13,5},{2,10},{6,14},... | collective-permute-start | bytes 135176 | tf_op jit(solution)/shard_map/ppermute | solution.py:445
  79.3 2.8 %collective-permute-start.20 = (f32[11,8,128]{2,1,0:T(8,128)S(1)}, f32[11,8,128]{2,1,0:T(8,128)S(1)}, u32[]{:S(2)}, u32[]{:S(2)}) collective-permute-start(f32[11,8,128]{2,1,0:T(8,128)S(1)} %get-tuple-element.40), channel_id=1, source_target_pairs={{0,12},{4,0},{8,4},{12,8},{1,13},{5,1},{9,5},{13,9},{2,14},{6,2},{... | collective-permute-start | bytes 135176 | tf_op jit(solution)/shard_map/ppermute | solution.py:445
  82.9 1.5 %collective-permute-done.19 = f32[11,8,128]{2,1,0:T(8,128)S(1)} collective-permute-done((f32[11,8,128]{2,1,0:T(8,128)S(1)}, f32[11,8,128]{2,1,0:T(8,128)S(1)}, u32[]{:S(2)}, u32[]{:S(2)}) %collective-permute-start.19) | collective-permute-done | bytes 45088 | tf_op jit(solution)/shard_map/ppermute | solution.py:445
  86.6 1.7 %collective-permute-done.23.refs_3_ = f32[11,8,128]{2,1,0:T(8,128)S(1)} collective-permute-done((f32[11,8,128]{2,1,0:T(8,128)S(1)}, f32[11,8,128]{2,1,0:T(8,128)S(1)}, u32[]{:S(2)}, u32[]{:S(2)}) %collective-permute-start.23) | collective-permute-done | bytes 45088 | tf_op jit(solution)/shard_map/ppermute | solution.py:440
  88.3 1.6 %collective-permute-done.21.refs_1_ = f32[11,8,128]{2,1,0:T(8,128)S(1)} collective-permute-done((f32[11,8,128]{2,1,0:T(8,128)S(1)}, f32[11,8,128]{2,1,0:T(8,128)S(1)}, u32[]{:S(2)}, u32[]{:S(2)}) %collective-permute-start.21) | collective-permute-done | bytes 45088 | tf_op jit(solution)/shard_map/ppermute | solution.py:433
  (50 shorter events, 12.3 us)
Async XLA Ops:
  2.2 7.2 %collective-permute-start.2 = (f32[12,8,128]{2,1,0:T(8,128)S(1)}, f32[12,8,128]{2,1,0:T(8,128)S(1)}, u32[]{:S(2)}, u32[]{:S(2)}) collective-permute-start(f32[12,8,128]{2,1,0:T(8,128)S(1)} %pack.1.refs_0_), channel_id=1, source_target_pairs={{0,12},{4,0},{8,4},{12,8},{1,13},{5,1},{9,5},{13,9},{2,14},{6,2},{... | collective-permute-start | bytes 147464 | tf_op jit(solution)/shard_map/ppermute | solution.py:445
  7.3 5.0 %collective-permute-start.1 = (f32[12,8,128]{2,1,0:T(8,128)S(1)}, f32[12,8,128]{2,1,0:T(8,128)S(1)}, u32[]{:S(2)}, u32[]{:S(2)}) collective-permute-start(f32[12,8,128]{2,1,0:T(8,128)S(1)} %pack.1.refs_0_), channel_id=1, source_target_pairs={{0,8},{4,12},{8,0},{12,4},{1,9},{5,13},{9,1},{13,5},{2,10},{6,14},... | collective-permute-start | bytes 147464 | tf_op jit(solution)/shard_map/ppermute | solution.py:445
  7.3 5.9 %collective-permute-start = (f32[12,8,128]{2,1,0:T(8,128)S(1)}, f32[12,8,128]{2,1,0:T(8,128)S(1)}, u32[]{:S(2)}, u32[]{:S(2)}) collective-permute-start(f32[12,8,128]{2,1,0:T(8,128)S(1)} %pack.1.refs_0_), channel_id=1, source_target_pairs={{0,4},{4,8},{8,12},{12,0},{1,5},{5,9},{9,13},{13,1},{2,6},{6,10},{... | collective-permute-start | bytes 147464 | tf_op jit(solution)/shard_map/ppermute | solution.py:445
  14.0 5.8 %collective-permute-start.3 = (f32[11,16,128]{2,1,0:T(8,128)S(1)}, f32[11,16,128]{2,1,0:T(8,128)S(1)}, u32[]{:S(2)}, u32[]{:S(2)}) collective-permute-start(f32[11,16,128]{2,1,0:T(8,128)S(1)} %get-tuple-element.24.refs_0_), channel_id=1, source_target_pairs={{0,2},{2,0},{1,3},{3,1},{4,6},{6,4},{5,7},{7,5},{8,10},{10,8},{9,1... | collective-permute-start | bytes 270344 | tf_op jit(solution)/shard_map/ppermute | solution.py:433
  15.6 4.2 %collective-permute-start.5 = (f32[7,16,128]{2,1,0:T(8,128)S(1)}, f32[7,16,128]{2,1,0:T(8,128)S(1)}, u32[]{:S(2)}, u32[]{:S(2)}) collective-permute-start(f32[7,16,128]{2,1,0:T(8,128)S(1)} %get-tuple-element.25), channel_id=1, source_target_pairs={{0,3},{1,2},{2,1},{3,0},{4,7},{5,6},{6,5},{7,4},{8,11},{9,10},{10,... | collective-permute-start | bytes 172040 | tf_op jit(solution)/shard_map/ppermute | solution.py:440
  15.6 4.2 %collective-permute-start.4 = (f32[7,16,128]{2,1,0:T(8,128)S(1)}, f32[7,16,128]{2,1,0:T(8,128)S(1)}, u32[]{:S(2)}, u32[]{:S(2)}) collective-permute-start(f32[7,16,128]{2,1,0:T(8,128)S(1)} %get-tuple-element.25), channel_id=1, source_target_pairs={{0,1},{1,0},{2,3},{3,2},{4,5},{5,4},{6,7},{7,6},{8,9},{9,8},{10,11... | collective-permute-start | bytes 172040 | tf_op jit(solution)/shard_map/ppermute | solution.py:440
  34.3 5.3 %collective-permute-start.6 = (f32[11,16,128]{2,1,0:T(8,128)S(1)}, f32[11,16,128]{2,1,0:T(8,128)S(1)}, u32[]{:S(2)}, u32[]{:S(2)}) collective-permute-start(f32[11,16,128]{2,1,0:T(8,128)S(1)} %get-tuple-element.27), channel_id=1, source_target_pairs={{0,2},{2,0},{1,3},{3,1},{4,6},{6,4},{5,7},{7,5},{8,10},{10,8},{9,1... | collective-permute-start | bytes 270344 | tf_op jit(solution)/shard_map/ppermute | solution.py:433
  35.2 1.3 %collective-permute-start.7 = (f32[7,16,128]{2,1,0:T(8,128)S(1)}, f32[7,16,128]{2,1,0:T(8,128)S(1)}, u32[]{:S(2)}, u32[]{:S(2)}) collective-permute-start(f32[7,16,128]{2,1,0:T(8,128)S(1)} %get-tuple-element.28), channel_id=1, source_target_pairs={{0,1},{1,0},{2,3},{3,2},{4,5},{5,4},{6,7},{7,6},{8,9},{9,8},{10,11... | collective-permute-start | bytes 172040 | tf_op jit(solution)/shard_map/ppermute | solution.py:440
  35.4 4.1 %collective-permute-start.8 = (f32[7,16,128]{2,1,0:T(8,128)S(1)}, f32[7,16,128]{2,1,0:T(8,128)S(1)}, u32[]{:S(2)}, u32[]{:S(2)}) collective-permute-start(f32[7,16,128]{2,1,0:T(8,128)S(1)} %get-tuple-element.29), channel_id=1, source_target_pairs={{0,3},{1,2},{2,1},{3,0},{4,7},{5,6},{6,5},{7,4},{8,11},{9,10},{10,... | collective-permute-start | bytes 172040 | tf_op jit(solution)/shard_map/ppermute | solution.py:440
  39.6 5.4 %collective-permute-start.11 = (f32[11,16,128]{2,1,0:T(8,128)S(1)}, f32[11,16,128]{2,1,0:T(8,128)S(1)}, u32[]{:S(2)}, u32[]{:S(2)}) collective-permute-start(f32[11,16,128]{2,1,0:T(8,128)S(1)} %pad_add_fusion.1.refs_0_), channel_id=1, source_target_pairs={{0,12},{4,0},{8,4},{12,8},{1,13},{5,1},{9,5},{13,9},{2,14},{6,2},{... | collective-permute-start | bytes 270344 | tf_op jit(solution)/shard_map/ppermute | solution.py:445
  40.9 9.5 %collective-permute-start.10 = (f32[11,16,128]{2,1,0:T(8,128)S(1)}, f32[11,16,128]{2,1,0:T(8,128)S(1)}, u32[]{:S(2)}, u32[]{:S(2)}) collective-permute-start(f32[11,16,128]{2,1,0:T(8,128)S(1)} %pad_add_fusion.1.refs_0_), channel_id=1, source_target_pairs={{0,8},{4,12},{8,0},{12,4},{1,9},{5,13},{9,1},{13,5},{2,10},{6,14},... | collective-permute-start | bytes 270344 | tf_op jit(solution)/shard_map/ppermute | solution.py:445
  40.9 9.5 %collective-permute-start.9 = (f32[11,16,128]{2,1,0:T(8,128)S(1)}, f32[11,16,128]{2,1,0:T(8,128)S(1)}, u32[]{:S(2)}, u32[]{:S(2)}) collective-permute-start(f32[11,16,128]{2,1,0:T(8,128)S(1)} %pad_add_fusion.1.refs_0_), channel_id=1, source_target_pairs={{0,4},{4,8},{8,12},{12,0},{1,5},{5,9},{9,13},{13,1},{2,6},{6,10},{... | collective-permute-start | bytes 270344 | tf_op jit(solution)/shard_map/ppermute | solution.py:445
  50.7 5.4 %collective-permute-start.12 = (f32[11,16,128]{2,1,0:T(8,128)S(1)}, f32[11,16,128]{2,1,0:T(8,128)S(1)}, u32[]{:S(2)}, u32[]{:S(2)}) collective-permute-start(f32[11,16,128]{2,1,0:T(8,128)S(1)} %get-tuple-element.31.refs_4_), channel_id=1, source_target_pairs={{0,2},{2,0},{1,3},{3,1},{4,6},{6,4},{5,7},{7,5},{8,10},{10,8},{9,1... | collective-permute-start | bytes 270344 | tf_op jit(solution)/shard_map/ppermute | solution.py:433
  51.9 4.2 %collective-permute-start.14 = (f32[7,16,128]{2,1,0:T(8,128)S(1)}, f32[7,16,128]{2,1,0:T(8,128)S(1)}, u32[]{:S(2)}, u32[]{:S(2)}) collective-permute-start(f32[7,16,128]{2,1,0:T(8,128)S(1)} %get-tuple-element.32), channel_id=1, source_target_pairs={{0,3},{1,2},{2,1},{3,0},{4,7},{5,6},{6,5},{7,4},{8,11},{9,10},{10,... | collective-permute-start | bytes 172040 | tf_op jit(solution)/shard_map/ppermute | solution.py:440
  52.0 4.2 %collective-permute-start.13 = (f32[7,16,128]{2,1,0:T(8,128)S(1)}, f32[7,16,128]{2,1,0:T(8,128)S(1)}, u32[]{:S(2)}, u32[]{:S(2)}) collective-permute-start(f32[7,16,128]{2,1,0:T(8,128)S(1)} %get-tuple-element.32), channel_id=1, source_target_pairs={{0,1},{1,0},{2,3},{3,2},{4,5},{5,4},{6,7},{7,6},{8,9},{9,8},{10,11... | collective-permute-start | bytes 172040 | tf_op jit(solution)/shard_map/ppermute | solution.py:440
  70.6 5.4 %collective-permute-start.15 = (f32[11,16,128]{2,1,0:T(8,128)S(1)}, f32[11,16,128]{2,1,0:T(8,128)S(1)}, u32[]{:S(2)}, u32[]{:S(2)}) collective-permute-start(f32[11,16,128]{2,1,0:T(8,128)S(1)} %get-tuple-element.34), channel_id=1, source_target_pairs={{0,2},{2,0},{1,3},{3,1},{4,6},{6,4},{5,7},{7,5},{8,10},{10,8},{9,1... | collective-permute-start | bytes 270344 | tf_op jit(solution)/shard_map/ppermute | solution.py:433
  71.7 1.2 %collective-permute-start.16 = (f32[7,16,128]{2,1,0:T(8,128)S(1)}, f32[7,16,128]{2,1,0:T(8,128)S(1)}, u32[]{:S(2)}, u32[]{:S(2)}) collective-permute-start(f32[7,16,128]{2,1,0:T(8,128)S(1)} %get-tuple-element.35), channel_id=1, source_target_pairs={{0,1},{1,0},{2,3},{3,2},{4,5},{5,4},{6,7},{7,6},{8,9},{9,8},{10,11... | collective-permute-start | bytes 172040 | tf_op jit(solution)/shard_map/ppermute | solution.py:440
  71.9 4.2 %collective-permute-start.17 = (f32[7,16,128]{2,1,0:T(8,128)S(1)}, f32[7,16,128]{2,1,0:T(8,128)S(1)}, u32[]{:S(2)}, u32[]{:S(2)}) collective-permute-start(f32[7,16,128]{2,1,0:T(8,128)S(1)} %get-tuple-element.36), channel_id=1, source_target_pairs={{0,3},{1,2},{2,1},{3,0},{4,7},{5,6},{6,5},{7,4},{8,11},{9,10},{10,... | collective-permute-start | bytes 172040 | tf_op jit(solution)/shard_map/ppermute | solution.py:440
  76.9 6.0 %collective-permute-start.18 = (f32[11,8,128]{2,1,0:T(8,128)S(1)}, f32[11,8,128]{2,1,0:T(8,128)S(1)}, u32[]{:S(2)}, u32[]{:S(2)}) collective-permute-start(f32[11,8,128]{2,1,0:T(8,128)S(1)} %get-tuple-element.38), channel_id=1, source_target_pairs={{0,4},{4,8},{8,12},{12,0},{1,5},{5,9},{9,13},{13,1},{2,6},{6,10},{... | collective-permute-start | bytes 135176 | tf_op jit(solution)/shard_map/ppermute | solution.py:445
  77.2 7.2 %collective-permute-start.19 = (f32[11,8,128]{2,1,0:T(8,128)S(1)}, f32[11,8,128]{2,1,0:T(8,128)S(1)}, u32[]{:S(2)}, u32[]{:S(2)}) collective-permute-start(f32[11,8,128]{2,1,0:T(8,128)S(1)} %get-tuple-element.39), channel_id=1, source_target_pairs={{0,8},{4,12},{8,0},{12,4},{1,9},{5,13},{9,1},{13,5},{2,10},{6,14},... | collective-permute-start | bytes 135176 | tf_op jit(solution)/shard_map/ppermute | solution.py:445
  79.3 5.1 %collective-permute-start.20 = (f32[11,8,128]{2,1,0:T(8,128)S(1)}, f32[11,8,128]{2,1,0:T(8,128)S(1)}, u32[]{:S(2)}, u32[]{:S(2)}) collective-permute-start(f32[11,8,128]{2,1,0:T(8,128)S(1)} %get-tuple-element.40), channel_id=1, source_target_pairs={{0,12},{4,0},{8,4},{12,8},{1,13},{5,1},{9,5},{13,9},{2,14},{6,2},{... | collective-permute-start | bytes 135176 | tf_op jit(solution)/shard_map/ppermute | solution.py:445
  84.4 3.9 %collective-permute-start.23 = (f32[11,8,128]{2,1,0:T(8,128)S(1)}, f32[11,8,128]{2,1,0:T(8,128)S(1)}, u32[]{:S(2)}, u32[]{:S(2)}) collective-permute-start(f32[11,8,128]{2,1,0:T(8,128)S(1)} %add_add_fusion.refs_0_), channel_id=1, source_target_pairs={{0,3},{1,2},{2,1},{3,0},{4,7},{5,6},{6,5},{7,4},{8,11},{9,10},{10,... | collective-permute-start | bytes 135176 | tf_op jit(solution)/shard_map/ppermute | solution.py:440
  85.1 3.3 %collective-permute-start.22 = (f32[11,8,128]{2,1,0:T(8,128)S(1)}, f32[11,8,128]{2,1,0:T(8,128)S(1)}, u32[]{:S(2)}, u32[]{:S(2)}) collective-permute-start(f32[11,8,128]{2,1,0:T(8,128)S(1)} %add_add_fusion.refs_0_), channel_id=1, source_target_pairs={{0,1},{1,0},{2,3},{3,2},{4,5},{5,4},{6,7},{7,6},{8,9},{9,8},{10,11... | collective-permute-start | bytes 135176 | tf_op jit(solution)/shard_map/ppermute | solution.py:440
  85.9 4.0 %collective-permute-start.21 = (f32[11,8,128]{2,1,0:T(8,128)S(1)}, f32[11,8,128]{2,1,0:T(8,128)S(1)}, u32[]{:S(2)}, u32[]{:S(2)}) collective-permute-start(f32[11,8,128]{2,1,0:T(8,128)S(1)} %add_add_fusion.refs_0_), channel_id=1, source_target_pairs={{0,2},{2,0},{1,3},{3,1},{4,6},{6,4},{5,7},{7,5},{8,10},{10,8},{9,1... | collective-permute-start | bytes 135176 | tf_op jit(solution)/shard_map/ppermute | solution.py:433
  (7 other events, 58.4 us)

commit v10 on v8

--- a/solution.py
+++ b/solution.py
@@ -160,6 +160,7 @@
     ins, refs = refs[:taken], refs[taken:]
     outs, refs = refs[: 2 * epochs], refs[2 * epochs :]
     shared, amps, derived, prof_y, pieces_x, pieces_y, image, sums, half, other = refs[:10]
+    right = refs[10:12]
     band, epoch = lax.axis_index("band"), lax.axis_index("epoch")
     tiles = data_ref.shape[0]
     pixels = data_ref.shape[-1]
@@ -174,7 +175,7 @@
         return r // HALF, r % HALF
 
     if later:
-        moved, moved_amps = refs[10:]
+        moved, moved_amps = refs[12:]
         put_together(layout, band, epoch, ins[2 * epochs :], half, other, moved, moved_amps)
         for k in range(4):
             shift = 0.0
@@ -239,10 +240,12 @@
                     d = grid - (line(1, c, g) + off_y)
                     e = jnp.exp2(d * d * line(3, c, g))
                     prof_y[s * COMPS + c] = e
-                    pieces_y[s, :, c * 128 : (c + 1) * 128] = cut(e * line(4, c, g), line(5, c, g))
-                image[...] += lax.dot_general(
-                    pieces_x[s], pieces_y[s], (((1,), (1,)), ((), ())), preferred_element_type=F32
-                )
+                    e = e * line(4, c, g)
+                    pieces_y[s, :, c * 128 : (c + 1) * 128] = cut(e, line(5, c, g))
+                    turned = e.T
+                    hi = turned.astype(BF16).astype(F32)
+                    right[u][c * 128 : (c + 1) * 128] = jnp.concatenate([hi, turned - hi], axis=1)
+                image[...] += jnp.dot(pieces_x[s], right[u][...], preferred_element_type=F32)
             return carry
 
         lax.fori_loop(0, trips, render, 0)
@@ -339,6 +342,7 @@
             pltpu.VMEM((epochs, rows, wide, 128), F32),
             pltpu.VMEM((epochs, shared_rows, wide, 128), F32),
         ]
+        + [pltpu.VMEM((COMPS * 128, 2 * pixels), F32)] * 2
         + (together if later else []),
         compiler_params=params(40),
         name="later_step" if later else "first_step",

time: 88.2 us -> 89.1 us (1.010)
  starting transfers between devices: 24.7 us -> 35.5 us
  Pallas kernels: 27.8 us -> 18.8 us
    ppermute x9, starting transfers between devices: 13.7 us -> 24.5 us  [round_tiles(): lax.ppermute(arrays[k], 'tile', [(i, (i + k) % owners) for i in range(own...]
    pallas_call x2, Pallas kernels: 24.6 us -> 15.5 us  [step_gradient(): pl.pallas_call(functools.partial(step_kernel, layout, later), out_shape=[...]
  transfers between devices with their start and end apart: 24 -> 24, of which waited for: 14 -> 15; matrix products, arithmetic and copies ran while one was open for 0% -> 0% of each run, Pallas kernels for 0% -> 0%
where the time goes in v10:
time: 89.1 us; the launch traced here: 88.9 us
  starting transfers between devices  35.5 us (40%)
  waiting for transfers between devices  32.1 us (36%)
  Pallas kernels  18.8 us (21%)
  local copies, waits for them, and re-layouts  1.63 us (2%)
    ppermute x9, starting transfers between devices, round_tiles(): lax.ppermute(arrays[k], 'tile', [(i, (i + k) % owners) for i in range(own...  24.5 us
    ppermute x9, waiting for transfers between devices, round_tiles(): lax.ppermute(arrays[k], 'tile', [(i, (i + k) % owners) for i in range(own...  16.2 us
    pallas_call x2, Pallas kernels, step_gradient(): pl.pallas_call(functools.partial(step_kernel, layout, later), out_shape=[...  15.5 us
    ppermute x10, waiting for transfers between devices, to_peers(): kept.append(lax.ppermute(other[k], ('epoch', 'band'), pairs))  14.1 us
    ppermute x10, starting transfers between devices, to_peers(): kept.append(lax.ppermute(other[k], ('epoch', 'band'), pairs))  5.53 us
    ppermute x5, starting transfers between devices, to_peers(): lax.ppermute(same[k], 'epoch', [(i, (i + k) % epochs) for i in range(epoc...  5.43 us
  transfers between devices with their start and end apart: 24, of which 15 were waited for; matrix products, arithmetic and copies ran while one was open for 0% of the time, Pallas kernels for 0%

profile of v10, /device:TPU:0, one launch (start us, length us, event | category | flops | bytes accessed | tf_op | source)
XLA Modules:
  0.0 88.9 jit_solution(11633183613148069296)
XLA Ops:
  2.2 5.1 %collective-permute-start.2 = (f32[12,8,128]{2,1,0:T(8,128)S(1)}, f32[12,8,128]{2,1,0:T(8,128)S(1)}, u32[]{:S(2)}, u32[]{:S(2)}) collective-permute-start(f32[12,8,128]{2,1,0:T(8,128)S(1)} %pack.1.refs_0_), channel_id=1, source_target_pairs={{0,12},{4,0},{8,4},{12,8},{1,13},{5,1},{9,5},{13,9},{2,14},{6,2},{... | collective-permute-start | bytes 147464 | tf_op jit(solution)/shard_map/ppermute | solution.py:432
  7.3 1.0 %collective-permute-start = (f32[12,8,128]{2,1,0:T(8,128)S(1)}, f32[12,8,128]{2,1,0:T(8,128)S(1)}, u32[]{:S(2)}, u32[]{:S(2)}) collective-permute-start(f32[12,8,128]{2,1,0:T(8,128)S(1)} %pack.1.refs_0_), channel_id=1, source_target_pairs={{0,4},{4,8},{8,12},{12,0},{1,5},{5,9},{9,13},{13,1},{2,6},{6,10},{... | collective-permute-start | bytes 147464 | tf_op jit(solution)/shard_map/ppermute | solution.py:432
  8.3 1.0 %collective-permute-done.2.refs_3_ = f32[12,8,128]{2,1,0:T(8,128)S(1)} collective-permute-done((f32[12,8,128]{2,1,0:T(8,128)S(1)}, f32[12,8,128]{2,1,0:T(8,128)S(1)}, u32[]{:S(2)}, u32[]{:S(2)}) %collective-permute-start.2) | collective-permute-done | bytes 49184 | tf_op jit(solution)/shard_map/ppermute | solution.py:432
  9.4 2.9 %collective-permute-done.1.refs_2_ = f32[12,8,128]{2,1,0:T(8,128)S(1)} collective-permute-done((f32[12,8,128]{2,1,0:T(8,128)S(1)}, f32[12,8,128]{2,1,0:T(8,128)S(1)}, u32[]{:S(2)}, u32[]{:S(2)}) %collective-permute-start.1) | collective-permute-done | bytes 49184 | tf_op jit(solution)/shard_map/ppermute | solution.py:432
  14.0 1.5 %collective-permute-start.3 = (f32[11,16,128]{2,1,0:T(8,128)S(1)}, f32[11,16,128]{2,1,0:T(8,128)S(1)}, u32[]{:S(2)}, u32[]{:S(2)}) collective-permute-start(f32[11,16,128]{2,1,0:T(8,128)S(1)} %get-tuple-element.24.refs_0_), channel_id=1, source_target_pairs={{0,2},{2,0},{1,3},{3,1},{4,6},{6,4},{5,7},{7,5},{8,10},{10,8},{9,1... | collective-permute-start | bytes 270344 | tf_op jit(solution)/shard_map/ppermute | solution.py:420
  16.9 2.9 %collective-permute-done.5.refs_3_ = f32[7,16,128]{2,1,0:T(8,128)S(1)} collective-permute-done((f32[7,16,128]{2,1,0:T(8,128)S(1)}, f32[7,16,128]{2,1,0:T(8,128)S(1)}, u32[]{:S(2)}, u32[]{:S(2)}) %collective-permute-start.5) | collective-permute-done | bytes 57376 | tf_op jit(solution)/shard_map/ppermute | solution.py:427
  19.8 7.7 %first_step.1 = (f32[11,16,128]{2,1,0:T(8,128)S(1)}, f32[11,16,128]{2,1,0:T(8,128)S(1)}, f32[7,16,128]{2,1,0:T(8,128)S(1)}, f32[7,16,128]{2,1,0:T(8,128)S(1)}) custom-call(s32[2]{0:T(128)S(1)} %copy-done.6, s32[2,2,8]{2,1,0:T(2,128)S(1)} %bitcast.5, f32[1,1]{1,0:T(1,128)S(6)} %copy.8.psf_ref, f32[2,1,1,128,128]{4,3,2,1,0:T(8,128)S(1)} %copy-done.2, ...), custom_call_target="tpu_custom_call" | custom-call | tf_op jit(solution)/shard_map/first_step/pallas_call | solution.py:329
  28.7 1.1 %collective-permute-start.8 = (f32[7,16,128]{2,1,0:T(8,128)S(1)}, f32[7,16,128]{2,1,0:T(8,128)S(1)}, u32[]{:S(2)}, u32[]{:S(2)}) collective-permute-start(f32[7,16,128]{2,1,0:T(8,128)S(1)} %get-tuple-element.29), channel_id=1, source_target_pairs={{0,3},{1,2},{2,1},{3,0},{4,7},{5,6},{6,5},{7,4},{8,11},{9,10},{10,... | collective-permute-start | bytes 172040 | tf_op jit(solution)/shard_map/ppermute | solution.py:427
  29.8 3.0 %collective-permute-done.8 = f32[7,16,128]{2,1,0:T(8,128)S(1)} collective-permute-done((f32[7,16,128]{2,1,0:T(8,128)S(1)}, f32[7,16,128]{2,1,0:T(8,128)S(1)}, u32[]{:S(2)}, u32[]{:S(2)}) %collective-permute-start.8) | collective-permute-done | bytes 57376 | tf_op jit(solution)/shard_map/ppermute | solution.py:427
  32.9 8.0 %collective-permute-start.11 = (f32[11,16,128]{2,1,0:T(8,128)S(1)}, f32[11,16,128]{2,1,0:T(8,128)S(1)}, u32[]{:S(2)}, u32[]{:S(2)}) collective-permute-start(f32[11,16,128]{2,1,0:T(8,128)S(1)} %pad_add_fusion.1.refs_0_), channel_id=1, source_target_pairs={{0,12},{4,0},{8,4},{12,8},{1,13},{5,1},{9,5},{13,9},{2,14},{6,2},{... | collective-permute-start | bytes 270344 | tf_op jit(solution)/shard_map/ppermute | solution.py:432
  41.5 2.3 %collective-permute-done.11.refs_3_ = f32[11,16,128]{2,1,0:T(8,128)S(1)} collective-permute-done((f32[11,16,128]{2,1,0:T(8,128)S(1)}, f32[11,16,128]{2,1,0:T(8,128)S(1)}, u32[]{:S(2)}, u32[]{:S(2)}) %collective-permute-start.11) | collective-permute-done | bytes 90144 | tf_op jit(solution)/shard_map/ppermute | solution.py:432
  43.8 6.1 %collective-permute-done.10.refs_2_ = f32[11,16,128]{2,1,0:T(8,128)S(1)} collective-permute-done((f32[11,16,128]{2,1,0:T(8,128)S(1)}, f32[11,16,128]{2,1,0:T(8,128)S(1)}, u32[]{:S(2)}, u32[]{:S(2)}) %collective-permute-start.10) | collective-permute-done | bytes 90144 | tf_op jit(solution)/shard_map/ppermute | solution.py:432
  50.3 1.2 %collective-permute-start.12 = (f32[11,16,128]{2,1,0:T(8,128)S(1)}, f32[11,16,128]{2,1,0:T(8,128)S(1)}, u32[]{:S(2)}, u32[]{:S(2)}) collective-permute-start(f32[11,16,128]{2,1,0:T(8,128)S(1)} %get-tuple-element.31.refs_4_), channel_id=1, source_target_pairs={{0,2},{2,0},{1,3},{3,1},{4,6},{6,4},{5,7},{7,5},{8,10},{10,8},{9,1... | collective-permute-start | bytes 270344 | tf_op jit(solution)/shard_map/ppermute | solution.py:420
  52.4 3.2 %collective-permute-done.14.refs_7_ = f32[7,16,128]{2,1,0:T(8,128)S(1)} collective-permute-done((f32[7,16,128]{2,1,0:T(8,128)S(1)}, f32[7,16,128]{2,1,0:T(8,128)S(1)}, u32[]{:S(2)}, u32[]{:S(2)}) %collective-permute-start.14) | collective-permute-done | bytes 57376 | tf_op jit(solution)/shard_map/ppermute | solution.py:427
  55.7 7.8 %later_step.1 = (f32[11,16,128]{2,1,0:T(8,128)S(1)}, f32[11,16,128]{2,1,0:T(8,128)S(1)}, f32[7,16,128]{2,1,0:T(8,128)S(1)}, f32[7,16,128]{2,1,0:T(8,128)S(1)}) custom-call(s32[2]{0:T(128)S(1)} %copy-done.6, s32[2,2,8]{2,1,0:T(2,128)S(1)} %bitcast.6, f32[1,1]{1,0:T(1,128)S(6)} %copy.8.psf_ref, f32[2,1,1,128,128]{4,3,2,1,0:T(8,128)S(1)} %copy-done.2, ...), custom_call_target="tpu_custom_call" | custom-call | tf_op jit(solution)/shard_map/later_step/pallas_call | solution.py:329
  63.5 1.1 %collective-permute-start.15 = (f32[11,16,128]{2,1,0:T(8,128)S(1)}, f32[11,16,128]{2,1,0:T(8,128)S(1)}, u32[]{:S(2)}, u32[]{:S(2)}) collective-permute-start(f32[11,16,128]{2,1,0:T(8,128)S(1)} %get-tuple-element.34), channel_id=1, source_target_pairs={{0,2},{2,0},{1,3},{3,1},{4,6},{6,4},{5,7},{7,5},{8,10},{10,8},{9,1... | collective-permute-start | bytes 270344 | tf_op jit(solution)/shard_map/ppermute | solution.py:420
  65.8 3.1 %collective-permute-done.17 = f32[7,16,128]{2,1,0:T(8,128)S(1)} collective-permute-done((f32[7,16,128]{2,1,0:T(8,128)S(1)}, f32[7,16,128]{2,1,0:T(8,128)S(1)}, u32[]{:S(2)}, u32[]{:S(2)}) %collective-permute-start.17) | collective-permute-done | bytes 57376 | tf_op jit(solution)/shard_map/ppermute | solution.py:427
  69.7 4.9 %collective-permute-start.18 = (f32[11,8,128]{2,1,0:T(8,128)S(1)}, f32[11,8,128]{2,1,0:T(8,128)S(1)}, u32[]{:S(2)}, u32[]{:S(2)}) collective-permute-start(f32[11,8,128]{2,1,0:T(8,128)S(1)} %get-tuple-element.38), channel_id=1, source_target_pairs={{0,4},{4,8},{8,12},{12,0},{1,5},{5,9},{9,13},{13,1},{2,6},{6,10},{... | collective-permute-start | bytes 135176 | tf_op jit(solution)/shard_map/ppermute | solution.py:432
  74.7 3.7 %collective-permute-start.19 = (f32[11,8,128]{2,1,0:T(8,128)S(1)}, f32[11,8,128]{2,1,0:T(8,128)S(1)}, u32[]{:S(2)}, u32[]{:S(2)}) collective-permute-start(f32[11,8,128]{2,1,0:T(8,128)S(1)} %get-tuple-element.39), channel_id=1, source_target_pairs={{0,8},{4,12},{8,0},{12,4},{1,9},{5,13},{9,1},{13,5},{2,10},{6,14},... | collective-permute-start | bytes 135176 | tf_op jit(solution)/shard_map/ppermute | solution.py:432
  78.4 1.1 %collective-permute-start.20 = (f32[11,8,128]{2,1,0:T(8,128)S(1)}, f32[11,8,128]{2,1,0:T(8,128)S(1)}, u32[]{:S(2)}, u32[]{:S(2)}) collective-permute-start(f32[11,8,128]{2,1,0:T(8,128)S(1)} %get-tuple-element.40), channel_id=1, source_target_pairs={{0,12},{4,0},{8,4},{12,8},{1,13},{5,1},{9,5},{13,9},{2,14},{6,2},{... | collective-permute-start | bytes 135176 | tf_op jit(solution)/shard_map/ppermute | solution.py:432
  80.2 1.9 %collective-permute-done.19 = f32[11,8,128]{2,1,0:T(8,128)S(1)} collective-permute-done((f32[11,8,128]{2,1,0:T(8,128)S(1)}, f32[11,8,128]{2,1,0:T(8,128)S(1)}, u32[]{:S(2)}, u32[]{:S(2)}) %collective-permute-start.19) | collective-permute-done | bytes 45088 | tf_op jit(solution)/shard_map/ppermute | solution.py:432
  83.0 1.0 %collective-permute-start.22 = (f32[11,8,128]{2,1,0:T(8,128)S(1)}, f32[11,8,128]{2,1,0:T(8,128)S(1)}, u32[]{:S(2)}, u32[]{:S(2)}) collective-permute-start(f32[11,8,128]{2,1,0:T(8,128)S(1)} %add_add_fusion.refs_0_), channel_id=1, source_target_pairs={{0,1},{1,0},{2,3},{3,2},{4,5},{5,4},{6,7},{7,6},{8,9},{9,8},{10,11... | collective-permute-start | bytes 135176 | tf_op jit(solution)/shard_map/ppermute | solution.py:427
  84.7 1.7 %collective-permute-done.23.refs_3_ = f32[11,8,128]{2,1,0:T(8,128)S(1)} collective-permute-done((f32[11,8,128]{2,1,0:T(8,128)S(1)}, f32[11,8,128]{2,1,0:T(8,128)S(1)}, u32[]{:S(2)}, u32[]{:S(2)}) %collective-permute-start.23) | collective-permute-done | bytes 45088 | tf_op jit(solution)/shard_map/ppermute | solution.py:427
  86.5 1.6 %collective-permute-done.21.refs_1_ = f32[11,8,128]{2,1,0:T(8,128)S(1)} collective-permute-done((f32[11,8,128]{2,1,0:T(8,128)S(1)}, f32[11,8,128]{2,1,0:T(8,128)S(1)}, u32[]{:S(2)}, u32[]{:S(2)}) %collective-permute-start.21) | collective-permute-done | bytes 45088 | tf_op jit(solution)/shard_map/ppermute | solution.py:420
  (50 shorter events, 12.8 us)
Async XLA Ops:
  2.2 7.2 %collective-permute-start.2 = (f32[12,8,128]{2,1,0:T(8,128)S(1)}, f32[12,8,128]{2,1,0:T(8,128)S(1)}, u32[]{:S(2)}, u32[]{:S(2)}) collective-permute-start(f32[12,8,128]{2,1,0:T(8,128)S(1)} %pack.1.refs_0_), channel_id=1, source_target_pairs={{0,12},{4,0},{8,4},{12,8},{1,13},{5,1},{9,5},{13,9},{2,14},{6,2},{... | collective-permute-start | bytes 147464 | tf_op jit(solution)/shard_map/ppermute | solution.py:432
  7.3 5.0 %collective-permute-start.1 = (f32[12,8,128]{2,1,0:T(8,128)S(1)}, f32[12,8,128]{2,1,0:T(8,128)S(1)}, u32[]{:S(2)}, u32[]{:S(2)}) collective-permute-start(f32[12,8,128]{2,1,0:T(8,128)S(1)} %pack.1.refs_0_), channel_id=1, source_target_pairs={{0,8},{4,12},{8,0},{12,4},{1,9},{5,13},{9,1},{13,5},{2,10},{6,14},... | collective-permute-start | bytes 147464 | tf_op jit(solution)/shard_map/ppermute | solution.py:432
  7.3 5.9 %collective-permute-start = (f32[12,8,128]{2,1,0:T(8,128)S(1)}, f32[12,8,128]{2,1,0:T(8,128)S(1)}, u32[]{:S(2)}, u32[]{:S(2)}) collective-permute-start(f32[12,8,128]{2,1,0:T(8,128)S(1)} %pack.1.refs_0_), channel_id=1, source_target_pairs={{0,4},{4,8},{8,12},{12,0},{1,5},{5,9},{9,13},{13,1},{2,6},{6,10},{... | collective-permute-start | bytes 147464 | tf_op jit(solution)/shard_map/ppermute | solution.py:432
  14.0 5.8 %collective-permute-start.3 = (f32[11,16,128]{2,1,0:T(8,128)S(1)}, f32[11,16,128]{2,1,0:T(8,128)S(1)}, u32[]{:S(2)}, u32[]{:S(2)}) collective-permute-start(f32[11,16,128]{2,1,0:T(8,128)S(1)} %get-tuple-element.24.refs_0_), channel_id=1, source_target_pairs={{0,2},{2,0},{1,3},{3,1},{4,6},{6,4},{5,7},{7,5},{8,10},{10,8},{9,1... | collective-permute-start | bytes 270344 | tf_op jit(solution)/shard_map/ppermute | solution.py:420
  15.6 4.2 %collective-permute-start.5 = (f32[7,16,128]{2,1,0:T(8,128)S(1)}, f32[7,16,128]{2,1,0:T(8,128)S(1)}, u32[]{:S(2)}, u32[]{:S(2)}) collective-permute-start(f32[7,16,128]{2,1,0:T(8,128)S(1)} %get-tuple-element.25), channel_id=1, source_target_pairs={{0,3},{1,2},{2,1},{3,0},{4,7},{5,6},{6,5},{7,4},{8,11},{9,10},{10,... | collective-permute-start | bytes 172040 | tf_op jit(solution)/shard_map/ppermute | solution.py:427
  15.6 4.2 %collective-permute-start.4 = (f32[7,16,128]{2,1,0:T(8,128)S(1)}, f32[7,16,128]{2,1,0:T(8,128)S(1)}, u32[]{:S(2)}, u32[]{:S(2)}) collective-permute-start(f32[7,16,128]{2,1,0:T(8,128)S(1)} %get-tuple-element.25), channel_id=1, source_target_pairs={{0,1},{1,0},{2,3},{3,2},{4,5},{5,4},{6,7},{7,6},{8,9},{9,8},{10,11... | collective-permute-start | bytes 172040 | tf_op jit(solution)/shard_map/ppermute | solution.py:427
  27.5 5.3 %collective-permute-start.6 = (f32[11,16,128]{2,1,0:T(8,128)S(1)}, f32[11,16,128]{2,1,0:T(8,128)S(1)}, u32[]{:S(2)}, u32[]{:S(2)}) collective-permute-start(f32[11,16,128]{2,1,0:T(8,128)S(1)} %get-tuple-element.27), channel_id=1, source_target_pairs={{0,2},{2,0},{1,3},{3,1},{4,6},{6,4},{5,7},{7,5},{8,10},{10,8},{9,1... | collective-permute-start | bytes 270344 | tf_op jit(solution)/shard_map/ppermute | solution.py:420
  28.5 1.3 %collective-permute-start.7 = (f32[7,16,128]{2,1,0:T(8,128)S(1)}, f32[7,16,128]{2,1,0:T(8,128)S(1)}, u32[]{:S(2)}, u32[]{:S(2)}) collective-permute-start(f32[7,16,128]{2,1,0:T(8,128)S(1)} %get-tuple-element.28), channel_id=1, source_target_pairs={{0,1},{1,0},{2,3},{3,2},{4,5},{5,4},{6,7},{7,6},{8,9},{9,8},{10,11... | collective-permute-start | bytes 172040 | tf_op jit(solution)/shard_map/ppermute | solution.py:427
  28.7 4.1 %collective-permute-start.8 = (f32[7,16,128]{2,1,0:T(8,128)S(1)}, f32[7,16,128]{2,1,0:T(8,128)S(1)}, u32[]{:S(2)}, u32[]{:S(2)}) collective-permute-start(f32[7,16,128]{2,1,0:T(8,128)S(1)} %get-tuple-element.29), channel_id=1, source_target_pairs={{0,3},{1,2},{2,1},{3,0},{4,7},{5,6},{6,5},{7,4},{8,11},{9,10},{10,... | collective-permute-start | bytes 172040 | tf_op jit(solution)/shard_map/ppermute | solution.py:427
  32.9 11.0 %collective-permute-start.11 = (f32[11,16,128]{2,1,0:T(8,128)S(1)}, f32[11,16,128]{2,1,0:T(8,128)S(1)}, u32[]{:S(2)}, u32[]{:S(2)}) collective-permute-start(f32[11,16,128]{2,1,0:T(8,128)S(1)} %pad_add_fusion.1.refs_0_), channel_id=1, source_target_pairs={{0,12},{4,0},{8,4},{12,8},{1,13},{5,1},{9,5},{13,9},{2,14},{6,2},{... | collective-permute-start | bytes 270344 | tf_op jit(solution)/shard_map/ppermute | solution.py:432
  40.9 9.0 %collective-permute-start.10 = (f32[11,16,128]{2,1,0:T(8,128)S(1)}, f32[11,16,128]{2,1,0:T(8,128)S(1)}, u32[]{:S(2)}, u32[]{:S(2)}) collective-permute-start(f32[11,16,128]{2,1,0:T(8,128)S(1)} %pad_add_fusion.1.refs_0_), channel_id=1, source_target_pairs={{0,8},{4,12},{8,0},{12,4},{1,9},{5,13},{9,1},{13,5},{2,10},{6,14},... | collective-permute-start | bytes 270344 | tf_op jit(solution)/shard_map/ppermute | solution.py:432
  40.9 9.0 %collective-permute-start.9 = (f32[11,16,128]{2,1,0:T(8,128)S(1)}, f32[11,16,128]{2,1,0:T(8,128)S(1)}, u32[]{:S(2)}, u32[]{:S(2)}) collective-permute-start(f32[11,16,128]{2,1,0:T(8,128)S(1)} %pad_add_fusion.1.refs_0_), channel_id=1, source_target_pairs={{0,4},{4,8},{8,12},{12,0},{1,5},{5,9},{9,13},{13,1},{2,6},{6,10},{... | collective-permute-start | bytes 270344 | tf_op jit(solution)/shard_map/ppermute | solution.py:432
  50.3 5.4 %collective-permute-start.12 = (f32[11,16,128]{2,1,0:T(8,128)S(1)}, f32[11,16,128]{2,1,0:T(8,128)S(1)}, u32[]{:S(2)}, u32[]{:S(2)}) collective-permute-start(f32[11,16,128]{2,1,0:T(8,128)S(1)} %get-tuple-element.31.refs_4_), channel_id=1, source_target_pairs={{0,2},{2,0},{1,3},{3,1},{4,6},{6,4},{5,7},{7,5},{8,10},{10,8},{9,1... | collective-permute-start | bytes 270344 | tf_op jit(solution)/shard_map/ppermute | solution.py:420
  51.5 4.2 %collective-permute-start.14 = (f32[7,16,128]{2,1,0:T(8,128)S(1)}, f32[7,16,128]{2,1,0:T(8,128)S(1)}, u32[]{:S(2)}, u32[]{:S(2)}) collective-permute-start(f32[7,16,128]{2,1,0:T(8,128)S(1)} %get-tuple-element.32), channel_id=1, source_target_pairs={{0,3},{1,2},{2,1},{3,0},{4,7},{5,6},{6,5},{7,4},{8,11},{9,10},{10,... | collective-permute-start | bytes 172040 | tf_op jit(solution)/shard_map/ppermute | solution.py:427
  51.7 4.0 %collective-permute-start.13 = (f32[7,16,128]{2,1,0:T(8,128)S(1)}, f32[7,16,128]{2,1,0:T(8,128)S(1)}, u32[]{:S(2)}, u32[]{:S(2)}) collective-permute-start(f32[7,16,128]{2,1,0:T(8,128)S(1)} %get-tuple-element.32), channel_id=1, source_target_pairs={{0,1},{1,0},{2,3},{3,2},{4,5},{5,4},{6,7},{7,6},{8,9},{9,8},{10,11... | collective-permute-start | bytes 172040 | tf_op jit(solution)/shard_map/ppermute | solution.py:427
  63.5 5.4 %collective-permute-start.15 = (f32[11,16,128]{2,1,0:T(8,128)S(1)}, f32[11,16,128]{2,1,0:T(8,128)S(1)}, u32[]{:S(2)}, u32[]{:S(2)}) collective-permute-start(f32[11,16,128]{2,1,0:T(8,128)S(1)} %get-tuple-element.34), channel_id=1, source_target_pairs={{0,2},{2,0},{1,3},{3,1},{4,6},{6,4},{5,7},{7,5},{8,10},{10,8},{9,1... | collective-permute-start | bytes 270344 | tf_op jit(solution)/shard_map/ppermute | solution.py:420
  64.5 1.2 %collective-permute-start.16 = (f32[7,16,128]{2,1,0:T(8,128)S(1)}, f32[7,16,128]{2,1,0:T(8,128)S(1)}, u32[]{:S(2)}, u32[]{:S(2)}) collective-permute-start(f32[7,16,128]{2,1,0:T(8,128)S(1)} %get-tuple-element.35), channel_id=1, source_target_pairs={{0,1},{1,0},{2,3},{3,2},{4,5},{5,4},{6,7},{7,6},{8,9},{9,8},{10,11... | collective-permute-start | bytes 172040 | tf_op jit(solution)/shard_map/ppermute | solution.py:427
  64.7 4.2 %collective-permute-start.17 = (f32[7,16,128]{2,1,0:T(8,128)S(1)}, f32[7,16,128]{2,1,0:T(8,128)S(1)}, u32[]{:S(2)}, u32[]{:S(2)}) collective-permute-start(f32[7,16,128]{2,1,0:T(8,128)S(1)} %get-tuple-element.36), channel_id=1, source_target_pairs={{0,3},{1,2},{2,1},{3,0},{4,7},{5,6},{6,5},{7,4},{8,11},{9,10},{10,... | collective-permute-start | bytes 172040 | tf_op jit(solution)/shard_map/ppermute | solution.py:427
  69.7 10.4 %collective-permute-start.18 = (f32[11,8,128]{2,1,0:T(8,128)S(1)}, f32[11,8,128]{2,1,0:T(8,128)S(1)}, u32[]{:S(2)}, u32[]{:S(2)}) collective-permute-start(f32[11,8,128]{2,1,0:T(8,128)S(1)} %get-tuple-element.38), channel_id=1, source_target_pairs={{0,4},{4,8},{8,12},{12,0},{1,5},{5,9},{9,13},{13,1},{2,6},{6,10},{... | collective-permute-start | bytes 135176 | tf_op jit(solution)/shard_map/ppermute | solution.py:432
  74.7 7.4 %collective-permute-start.19 = (f32[11,8,128]{2,1,0:T(8,128)S(1)}, f32[11,8,128]{2,1,0:T(8,128)S(1)}, u32[]{:S(2)}, u32[]{:S(2)}) collective-permute-start(f32[11,8,128]{2,1,0:T(8,128)S(1)} %get-tuple-element.39), channel_id=1, source_target_pairs={{0,8},{4,12},{8,0},{12,4},{1,9},{5,13},{9,1},{13,5},{2,10},{6,14},... | collective-permute-start | bytes 135176 | tf_op jit(solution)/shard_map/ppermute | solution.py:432
  78.4 4.1 %collective-permute-start.20 = (f32[11,8,128]{2,1,0:T(8,128)S(1)}, f32[11,8,128]{2,1,0:T(8,128)S(1)}, u32[]{:S(2)}, u32[]{:S(2)}) collective-permute-start(f32[11,8,128]{2,1,0:T(8,128)S(1)} %get-tuple-element.40), channel_id=1, source_target_pairs={{0,12},{4,0},{8,4},{12,8},{1,13},{5,1},{9,5},{13,9},{2,14},{6,2},{... | collective-permute-start | bytes 135176 | tf_op jit(solution)/shard_map/ppermute | solution.py:432
  82.5 4.0 %collective-permute-start.23 = (f32[11,8,128]{2,1,0:T(8,128)S(1)}, f32[11,8,128]{2,1,0:T(8,128)S(1)}, u32[]{:S(2)}, u32[]{:S(2)}) collective-permute-start(f32[11,8,128]{2,1,0:T(8,128)S(1)} %add_add_fusion.refs_0_), channel_id=1, source_target_pairs={{0,3},{1,2},{2,1},{3,0},{4,7},{5,6},{6,5},{7,4},{8,11},{9,10},{10,... | collective-permute-start | bytes 135176 | tf_op jit(solution)/shard_map/ppermute | solution.py:427
  83.0 3.4 %collective-permute-start.22 = (f32[11,8,128]{2,1,0:T(8,128)S(1)}, f32[11,8,128]{2,1,0:T(8,128)S(1)}, u32[]{:S(2)}, u32[]{:S(2)}) collective-permute-start(f32[11,8,128]{2,1,0:T(8,128)S(1)} %add_add_fusion.refs_0_), channel_id=1, source_target_pairs={{0,1},{1,0},{2,3},{3,2},{4,5},{5,4},{6,7},{7,6},{8,9},{9,8},{10,11... | collective-permute-start | bytes 135176 | tf_op jit(solution)/shard_map/ppermute | solution.py:427
  84.1 4.0 %collective-permute-start.21 = (f32[11,8,128]{2,1,0:T(8,128)S(1)}, f32[11,8,128]{2,1,0:T(8,128)S(1)}, u32[]{:S(2)}, u32[]{:S(2)}) collective-permute-start(f32[11,8,128]{2,1,0:T(8,128)S(1)} %add_add_fusion.refs_0_), channel_id=1, source_target_pairs={{0,2},{2,0},{1,3},{3,1},{4,6},{6,4},{5,7},{7,5},{8,10},{10,8},{9,1... | collective-permute-start | bytes 135176 | tf_op jit(solution)/shard_map/ppermute | solution.py:420
  (7 other events, 63.7 us)

commit v11 on v8

--- a/solution.py
+++ b/solution.py
@@ -100,38 +100,32 @@
     out_ref[rows] = ids.astype(F32)
 
 
-def select_kernel(layout, lists_ref, *refs):
-    shared_rows, rows, pieces = layout
-    got, (out_ref, short_ref, match_ref) = refs[:-3], refs[-3:]
+def select_kernel(layout, wide, *refs):
+    shared_rows, rows, pieces = layout
+    got, (out_ref, short_ref, match_ref, place_ref) = refs[:-4], refs[-4:]
     owners = len(got)
-    tiles, slots = lists_ref.shape
     blocks = got[0].shape[1]
-    wide = tiles * slots
     me = lax.axis_index("tile")
-
-    def slot_ids(shape):
-        line = lax.broadcasted_iota(jnp.int32, shape, 0)
-        ids = jnp.zeros(shape, jnp.int32)
-        for t in range(tiles):
-            for s in range(slots):
-                ids = jnp.where(line == t * slots + s, lists_ref[t, s], ids)
-        return ids
+    own_line = got[0][rows, :1, :]
+    own_column = jnp.broadcast_to(own_line, (128, 128)).T[:wide]
 
     shape = (wide, owners * blocks)
     lane = lax.broadcasted_iota(jnp.int32, shape, 1)
     held = lax.rem(me - lane // blocks + owners, owners) * blocks + lane % blocks
-    choose = (slot_ids(shape) == held).astype(F32)
+    choose = (own_column[:, : owners * blocks] == held.astype(F32)).astype(F32)
     for p in range(rows):
         chosen = pick(choose, jnp.concatenate([ref[p] for ref in got], axis=0))
         out_ref[p] = chosen
         if p < shared_rows:
             short_ref[p] = chosen
 
-    shape = (wide + blocks, owners * wide)
-    line = lax.broadcasted_iota(jnp.int32, shape, 0)
-    own = jnp.where(line < wide, slot_ids(shape), me * blocks + line - wide).astype(F32)
-    sent = jnp.concatenate([ref[rows, :1, :wide] for ref in got], axis=1)
-    match_ref[...] = (own == sent).astype(F32)
+    lists = jnp.concatenate([ref[rows, :1, :wide] for ref in got], axis=1)
+    match_ref[:wide] = (own_column[:, :1] == lists).astype(F32)
+    own_blocks = me * blocks + lax.broadcasted_iota(jnp.int32, (blocks, owners * wide), 0)
+    match_ref[wide:] = (own_blocks.astype(F32) == lists).astype(F32)
+    line = lax.broadcasted_iota(jnp.int32, (owners * blocks, wide), 0)
+    target = lax.rem(me + line // blocks, owners) * blocks + line % blocks
+    place_ref[...] = (own_line[:, :wide] == target.astype(F32)).astype(F32)
 
 
 def put_together(layout, band, epoch, ins, half, other, shared, amps):
@@ -159,7 +153,7 @@
     taken = 2 * epochs * (2 if later else 1)
     ins, refs = refs[:taken], refs[taken:]
     outs, refs = refs[: 2 * epochs], refs[2 * epochs :]
-    shared, amps, derived, prof_y, pieces_x, pieces_y, image, sums, half, other = refs[:10]
+    shared, amps, derived, prof_x, prof_y, pieces_x, pieces_y, image, sums, half, other = refs[:11]
     band, epoch = lax.axis_index("band"), lax.axis_index("epoch")
     tiles = data_ref.shape[0]
     pixels = data_ref.shape[-1]
@@ -174,7 +168,7 @@
         return r // HALF, r % HALF
 
     if later:
-        moved, moved_amps = refs[10:]
+        moved, moved_amps = refs[11:]
         put_together(layout, band, epoch, ins[2 * epochs :], half, other, moved, moved_amps)
         for k in range(4):
             shift = 0.0
@@ -191,10 +185,17 @@
     live = jnp.zeros((wide, 128), jnp.bool_)
     for t in range(tiles):
         live = live | ((line_of >= t * slots) & (line_of < t * slots + counts_ref[t]))
+    off_x = off_y = jnp.zeros((wide, 128), jnp.int32)
+    for t in range(tiles):
+        for s in range(slots):
+            at = line_of == t * slots + s
+            off_x = jnp.where(at, offsets_ref[t, 0, s], off_x)
+            off_y = jnp.where(at, offsets_ref[t, 1, s], off_y)
+    off_x, off_y = off_x.astype(F32), off_y.astype(F32)
     for c in range(COMPS):
         lw, an = shared[row(2, c)], shared[row(3, c)]
-        derived[0, c] = shared[row(0, c)]
-        derived[1, c] = shared[row(1, c)]
+        derived[0, c] = shared[row(0, c)] + off_x
+        derived[1, c] = shared[row(1, c)] + off_y
         derived[2, c] = (-0.5 * LOG2E) / (jnp.exp(2.0 * (lw + an)) + psf * psf)
         derived[3, c] = (-0.5 * LOG2E) / (jnp.exp(2.0 * (lw - an)) + psf * psf)
         derived[4, c] = jnp.where(live, amps[c], 0.0)
@@ -209,14 +210,32 @@
 
     def stack(x):
         hi = x.astype(BF16).astype(F32)
-        return jnp.concatenate([hi, hi], axis=1), x - hi
+        return jnp.concatenate([hi, hi, x - hi], axis=1)
 
     def times(left, right):
-        near = jnp.dot(left[0], right, preferred_element_type=F32)
-        return near + jnp.dot(left[1], right[:pixels], preferred_element_type=F32)
-
-    def total(x):
-        return jnp.sum(x, axis=0, keepdims=True)
+        return jnp.dot(left, jnp.concatenate([right, right[:pixels]], axis=0), preferred_element_type=F32)
+
+    middle = pixels // 2
+    inner = lax.broadcasted_iota(jnp.int32, (8, 128), 0).astype(F32)
+
+    def running(groups):
+        sum_0 = sum_1 = sum_2 = groups[0]
+        for group in groups[1:]:
+            sum_0 = sum_0 + group
+            sum_1 = sum_1 + sum_0
+            sum_2 = sum_2 + sum_1
+        return sum_0, sum_1, sum_2
+
+    def moments(x):
+        groups = [x[r : r + 8] for r in range(0, pixels, 8)]
+        high = running(groups[len(groups) // 2 :][::-1])
+        low = running(groups[: len(groups) // 2])
+        m0 = high[0] + low[0]
+        m1 = high[1] - high[0] - low[1]
+        m2 = 2.0 * (high[2] + low[2]) - 2.0 * high[1] - (high[1] - high[0]) - low[1]
+        first = inner * m0 + 8.0 * m1
+        second = inner * (first + 8.0 * m1) + 64.0 * m2
+        return [jnp.sum(m, axis=0, keepdims=True) for m in (m0, first, second)]
 
     def line(index, c, s):
         return derived[index, c, pl.ds(s, 1), :]
@@ -230,13 +249,12 @@
             for u in range(together):
                 s = i * together + u
                 g = t * slots + s
-                off_x = offsets_ref[t, 0, s].astype(F32)
-                off_y = offsets_ref[t, 1, s].astype(F32)
                 for c in range(COMPS):
-                    d = grid - (line(0, c, g) + off_x)
+                    d = grid - line(0, c, g)
                     e = jnp.exp2(d * d * line(2, c, g))
+                    prof_x[s * COMPS + c] = e
                     pieces_x[s, :, c * 128 : (c + 1) * 128] = cut(e, SPLIT_UNIT)
-                    d = grid - (line(1, c, g) + off_y)
+                    d = grid - line(1, c, g)
                     e = jnp.exp2(d * d * line(3, c, g))
                     prof_y[s * COMPS + c] = e
                     pieces_y[s, :, c * 128 : (c + 1) * 128] = cut(e * line(4, c, g), line(5, c, g))
@@ -257,8 +275,6 @@
             for u in range(together):
                 s = i * together + u
                 g = t * slots + s
-                off_x = offsets_ref[t, 0, s].astype(F32)
-                off_y = offsets_ref[t, 1, s].astype(F32)
                 for first in range(0, COMPS, 2):
                     here = min(2, COMPS - first)
                     span = pl.ds(first * 128, 128 * here)
@@ -266,19 +282,11 @@
                     by_y = times(left_y, pieces_x[s, :, span])
                     for n in range(here):
                         c = first + n
-                        d = grid - (line(0, c, g) + off_x)
-                        at = slice(c * 128, (c + 1) * 128)
-                        e = pieces_x[s, :pixels, at] + pieces_x[s, pixels:, at]
-                        e = e * by_x[:, n * 128 : (n + 1) * 128]
-                        e1 = e * d
-                        sums[0, c, pl.ds(g, 1), :] = total(e1)
-                        sums[1, c, pl.ds(g, 1), :] = total(e1 * d)
-                        d = grid - (line(1, c, g) + off_y)
-                        e = prof_y[s * COMPS + c] * by_y[:, n * 128 : (n + 1) * 128]
-                        e1 = e * d
-                        sums[2, c, pl.ds(g, 1), :] = total(e1)
-                        sums[3, c, pl.ds(g, 1), :] = total(e1 * d)
-                        sums[4, c, pl.ds(g, 1), :] = total(e)
+                        at = slice(n * 128, (n + 1) * 128)
+                        for k, value in enumerate(moments(prof_x[s * COMPS + c] * by_x[:, at])):
+                            sums[k, c, pl.ds(g, 1), :] = value
+                        for k, value in enumerate(moments(prof_y[s * COMPS + c] * by_y[:, at])):
+                            sums[3 + k, c, pl.ds(g, 1), :] = value
             return carry
 
         lax.fori_loop(0, trips, pull, 0)
@@ -291,13 +299,18 @@
         wide_x, wide_y = jnp.exp(2.0 * (lw + an)), jnp.exp(2.0 * (lw - an))
         inv_x, inv_y = 1.0 / (wide_x + psf * psf), 1.0 / (wide_y + psf * psf)
         amp = amps[c]
-        var_x = keep(sums[1, c] * inv_x * (inv_x * wide_x))
-        var_y = keep(amp * sums[3, c] * inv_y * (inv_y * wide_y))
-        shared[row(0, c)] = keep(sums[0, c] * inv_x)
-        shared[row(1, c)] = keep(amp * sums[2, c] * inv_y)
+        shift_x, shift_y = middle - derived[0, c], middle - derived[1, c]
+        first_x = sums[1, c] + shift_x * sums[0, c]
+        first_y = sums[4, c] + shift_y * sums[3, c]
+        second_x = sums[2, c] + shift_x * (sums[1, c] + first_x)
+        second_y = sums[5, c] + shift_y * (sums[4, c] + first_y)
+        var_x = keep(second_x * inv_x * (inv_x * wide_x))
+        var_y = keep(amp * second_y * inv_y * (inv_y * wide_y))
+        shared[row(0, c)] = keep(first_x * inv_x)
+        shared[row(1, c)] = keep(amp * first_y * inv_y)
         shared[row(2, c)] = var_x + var_y
         shared[row(3, c)] = var_x - var_y
-        amps[c] = keep(sums[4, c])
+        amps[c] = keep(sums[3, c])
     none = jnp.zeros((wide, 128), F32)
     for q, piece in enumerate(pieces):
         for p, entry in enumerate(piece):
@@ -332,10 +345,11 @@
         + [
             pltpu.VMEM((6, COMPS, wide, 128), F32),
             pltpu.VMEM((slots * COMPS, pixels, 128), F32),
+            pltpu.VMEM((slots * COMPS, pixels, 128), F32),
             pltpu.VMEM((slots, 2 * pixels, COMPS * 128), F32),
             pltpu.VMEM((slots, 2 * pixels, COMPS * 128), F32),
             pltpu.VMEM((2 * pixels, 2 * pixels), F32),
-            pltpu.VMEM((5, COMPS, wide, 128), F32),
+            pltpu.VMEM((6, COMPS, wide, 128), F32),
             pltpu.VMEM((epochs, rows, wide, 128), F32),
             pltpu.VMEM((epochs, shared_rows, wide, 128), F32),
         ]
@@ -358,21 +372,11 @@
         own_ref[p] = both[wide:]
 
 
-def dense_kernel(rows, lists_ref, grads, *outs):
-    tiles, slots = lists_ref.shape
-    owners, blocks = len(outs), outs[0].shape[1]
-    shape = (owners * blocks, tiles * slots)
-    line = lax.broadcasted_iota(jnp.int32, shape, 0)
-    lane = lax.broadcasted_iota(jnp.int32, shape, 1)
-    me = lax.axis_index("tile")
-    target = lax.rem(me + line // blocks, owners) * blocks + line % blocks
-    ids = jnp.zeros(shape, jnp.int32)
-    for t in range(tiles):
-        for s in range(slots):
-            ids = jnp.where(lane == t * slots + s, lists_ref[t, s], ids)
-    match = (ids == target).astype(F32)
+def dense_kernel(rows, place_ref, grads, *outs):
+    blocks = outs[0].shape[1]
+    place = place_ref[...]
     for p in range(rows):
-        dense = pick(match, grads[p])
+        dense = pick(place, grads[p])
         for k, out in enumerate(outs):
             out[p] = dense[k * blocks : (k + 1) * blocks]
 
@@ -448,18 +452,19 @@
         name="pack",
     )(block_lists, by_row)
     got = round_tiles([packed] * owners)
-    slot_piece, slot_short, match = pl.pallas_call(
-        functools.partial(select_kernel, layout),
+    slot_piece, slot_short, match, place = pl.pallas_call(
+        functools.partial(select_kernel, layout, wide),
         out_shape=[
             f32(rows, wide, sources),
             f32(shared_rows, wide, sources),
             f32(wide + blocks, owners * wide),
+            f32(owners * blocks, wide),
         ],
-        in_specs=[smem()] + [vmem()] * owners,
-        out_specs=[vmem()] * 3,
+        in_specs=[vmem()] * owners,
+        out_specs=[vmem()] * 4,
         compiler_params=params(),
         name="select",
-    )(block_lists, *got)
+    )(*got)
     slot_rows = spread(slot_piece, slot_short)
 
     def gradient(moved):
@@ -485,11 +490,11 @@
     dense = pl.pallas_call(
         functools.partial(dense_kernel, rows),
         out_shape=[f32(rows, blocks, sources)] * owners,
-        in_specs=[smem(), vmem()],
+        in_specs=[vmem()] * 2,
         out_specs=[vmem()] * owners,
         compiler_params=params(),
         name="dense",
-    )(block_lists, gradient(spread(slot_piece, slot_short)))
+    )(place, gradient(spread(slot_piece, slot_short)))
     own = functools.reduce(lambda a, b: a + b, round_tiles(dense), own_first)
     whole = pl.pallas_call(
         functools.partial(final_kernel, layout, spacing),

time: 88.2 us -> 86.7 us (0.983)
  waiting for transfers between devices: 32.4 us -> 30 us
  Pallas kernels: 27.8 us -> 28.7 us
    ppermute x9, waiting for transfers between devices: 16.8 us -> 14.1 us  [round_tiles(): lax.ppermute(arrays[k], 'tile', [(i, (i + k) % owners) for i in range(own...]
    pallas_call x2, Pallas kernels: 24.6 us -> 26.5 us  [step_gradient(): pl.pallas_call(functools.partial(step_kernel, layout, later), out_shape=[...]
  transfers between devices with their start and end apart: 24 -> 24, of which waited for: 14 -> 15; matrix products, arithmetic and copies ran while one was open for 0% -> 0% of each run, Pallas kernels for 0% -> 0%
where the time goes in v11:
time: 86.7 us; the launch traced here: 86.2 us
  waiting for transfers between devices  30 us (35%)
  Pallas kernels  28.7 us (33%)
  starting transfers between devices  25.1 us (29%)
  local copies, waits for them, and re-layouts  1.63 us (2%)
    pallas_call x2, Pallas kernels, step_gradient(): pl.pallas_call(functools.partial(step_kernel, layout, later), out_shape=[...  26.5 us
    ppermute x9, starting transfers between devices, round_tiles(): lax.ppermute(arrays[k], 'tile', [(i, (i + k) % owners) for i in range(own...  14.1 us
    ppermute x9, waiting for transfers between devices, round_tiles(): lax.ppermute(arrays[k], 'tile', [(i, (i + k) % owners) for i in range(own...  14.1 us
    ppermute x10, waiting for transfers between devices, to_peers(): kept.append(lax.ppermute(other[k], ('epoch', 'band'), pairs))  14.1 us
    ppermute x10, starting transfers between devices, to_peers(): kept.append(lax.ppermute(other[k], ('epoch', 'band'), pairs))  5.64 us
    ppermute x5, starting transfers between devices, to_peers(): lax.ppermute(same[k], 'epoch', [(i, (i + k) % epochs) for i in range(epoc...  5.32 us
    ppermute x5, waiting for transfers between devices, to_peers(): lax.ppermute(same[k], 'epoch', [(i, (i + k) % epochs) for i in range(epoc...  1.86 us
  transfers between devices with their start and end apart: 24, of which 15 were waited for; matrix products, arithmetic and copies ran while one was open for 0% of the time, Pallas kernels for 0%

profile of v11, /device:TPU:0, one launch (start us, length us, event | category | flops | bytes accessed | tf_op | source)
XLA Modules:
  0.0 86.2 jit_solution(11314239271534140716)
XLA Ops:
  2.2 5.1 %collective-permute-start.2 = (f32[12,8,128]{2,1,0:T(8,128)S(1)}, f32[12,8,128]{2,1,0:T(8,128)S(1)}, u32[]{:S(2)}, u32[]{:S(2)}) collective-permute-start(f32[12,8,128]{2,1,0:T(8,128)S(1)} %pack.1.refs_0_), channel_id=1, source_target_pairs={{0,12},{4,0},{8,4},{12,8},{1,13},{5,1},{9,5},{13,9},{2,14},{6,2},{... | collective-permute-start | bytes 147464 | tf_op jit(solution)/shard_map/ppermute | solution.py:432
  7.3 1.0 %collective-permute-start = (f32[12,8,128]{2,1,0:T(8,128)S(1)}, f32[12,8,128]{2,1,0:T(8,128)S(1)}, u32[]{:S(2)}, u32[]{:S(2)}) collective-permute-start(f32[12,8,128]{2,1,0:T(8,128)S(1)} %pack.1.refs_0_), channel_id=1, source_target_pairs={{0,4},{4,8},{8,12},{12,0},{1,5},{5,9},{9,13},{13,1},{2,6},{6,10},{... | collective-permute-start | bytes 147464 | tf_op jit(solution)/shard_map/ppermute | solution.py:432
  8.3 1.0 %collective-permute-done.2.refs_3_ = f32[12,8,128]{2,1,0:T(8,128)S(1)} collective-permute-done((f32[12,8,128]{2,1,0:T(8,128)S(1)}, f32[12,8,128]{2,1,0:T(8,128)S(1)}, u32[]{:S(2)}, u32[]{:S(2)}) %collective-permute-start.2) | collective-permute-done | bytes 49184 | tf_op jit(solution)/shard_map/ppermute | solution.py:432
  9.4 2.9 %collective-permute-done.1.refs_2_ = f32[12,8,128]{2,1,0:T(8,128)S(1)} collective-permute-done((f32[12,8,128]{2,1,0:T(8,128)S(1)}, f32[12,8,128]{2,1,0:T(8,128)S(1)}, u32[]{:S(2)}, u32[]{:S(2)}) %collective-permute-start.1) | collective-permute-done | bytes 49184 | tf_op jit(solution)/shard_map/ppermute | solution.py:432
  13.5 1.5 %collective-permute-start.3 = (f32[11,16,128]{2,1,0:T(8,128)S(1)}, f32[11,16,128]{2,1,0:T(8,128)S(1)}, u32[]{:S(2)}, u32[]{:S(2)}) collective-permute-start(f32[11,16,128]{2,1,0:T(8,128)S(1)} %get-tuple-element.25.refs_0_), channel_id=1, source_target_pairs={{0,2},{2,0},{1,3},{3,1},{4,6},{6,4},{5,7},{7,5},{8,10},{10,8},{9,1... | collective-permute-start | bytes 270344 | tf_op jit(solution)/shard_map/ppermute | solution.py:420
  16.4 2.9 %collective-permute-done.5.refs_3_ = f32[7,16,128]{2,1,0:T(8,128)S(1)} collective-permute-done((f32[7,16,128]{2,1,0:T(8,128)S(1)}, f32[7,16,128]{2,1,0:T(8,128)S(1)}, u32[]{:S(2)}, u32[]{:S(2)}) %collective-permute-start.5) | collective-permute-done | bytes 57376 | tf_op jit(solution)/shard_map/ppermute | solution.py:427
  19.3 13.2 %first_step.1 = (f32[11,16,128]{2,1,0:T(8,128)S(1)}, f32[11,16,128]{2,1,0:T(8,128)S(1)}, f32[7,16,128]{2,1,0:T(8,128)S(1)}, f32[7,16,128]{2,1,0:T(8,128)S(1)}) custom-call(s32[2]{0:T(128)S(1)} %copy-done.5, s32[2,2,8]{2,1,0:T(2,128)S(1)} %bitcast.5, f32[1,1]{1,0:T(1,128)S(6)} %copy.8.psf_ref, f32[2,1,1,128,128]{4,3,2,1,0:T(8,128)S(1)} %copy-done.2, ...), custom_call_target="tpu_custom_call" | custom-call | tf_op jit(solution)/shard_map/first_step/pallas_call | solution.py:339
  33.6 1.1 %collective-permute-start.8 = (f32[7,16,128]{2,1,0:T(8,128)S(1)}, f32[7,16,128]{2,1,0:T(8,128)S(1)}, u32[]{:S(2)}, u32[]{:S(2)}) collective-permute-start(f32[7,16,128]{2,1,0:T(8,128)S(1)} %get-tuple-element.30), channel_id=1, source_target_pairs={{0,3},{1,2},{2,1},{3,0},{4,7},{5,6},{6,5},{7,4},{8,11},{9,10},{10,... | collective-permute-start | bytes 172040 | tf_op jit(solution)/shard_map/ppermute | solution.py:427
  34.7 3.1 %collective-permute-done.8 = f32[7,16,128]{2,1,0:T(8,128)S(1)} collective-permute-done((f32[7,16,128]{2,1,0:T(8,128)S(1)}, f32[7,16,128]{2,1,0:T(8,128)S(1)}, u32[]{:S(2)}, u32[]{:S(2)}) %collective-permute-start.8) | collective-permute-done | bytes 57376 | tf_op jit(solution)/shard_map/ppermute | solution.py:427
  37.9 1.2 %collective-permute-start.10 = (f32[11,16,128]{2,1,0:T(8,128)S(1)}, f32[11,16,128]{2,1,0:T(8,128)S(1)}, u32[]{:S(2)}, u32[]{:S(2)}) collective-permute-start(f32[11,16,128]{2,1,0:T(8,128)S(1)} %pad_add_fusion.1.refs_0_), channel_id=1, source_target_pairs={{0,8},{4,12},{8,0},{12,4},{1,9},{5,13},{9,1},{13,5},{2,10},{6,14},... | collective-permute-start | bytes 270344 | tf_op jit(solution)/shard_map/ppermute | solution.py:432
  39.1 1.9 %collective-permute-start.9 = (f32[11,16,128]{2,1,0:T(8,128)S(1)}, f32[11,16,128]{2,1,0:T(8,128)S(1)}, u32[]{:S(2)}, u32[]{:S(2)}) collective-permute-start(f32[11,16,128]{2,1,0:T(8,128)S(1)} %pad_add_fusion.1.refs_0_), channel_id=1, source_target_pairs={{0,4},{4,8},{8,12},{12,0},{1,5},{5,9},{9,13},{13,1},{2,6},{6,10},{... | collective-permute-start | bytes 270344 | tf_op jit(solution)/shard_map/ppermute | solution.py:432
  41.0 3.1 %collective-permute-done.11.refs_3_ = f32[11,16,128]{2,1,0:T(8,128)S(1)} collective-permute-done((f32[11,16,128]{2,1,0:T(8,128)S(1)}, f32[11,16,128]{2,1,0:T(8,128)S(1)}, u32[]{:S(2)}, u32[]{:S(2)}) %collective-permute-start.11) | collective-permute-done | bytes 90144 | tf_op jit(solution)/shard_map/ppermute | solution.py:432
  44.1 3.9 %collective-permute-done.10.refs_2_ = f32[11,16,128]{2,1,0:T(8,128)S(1)} collective-permute-done((f32[11,16,128]{2,1,0:T(8,128)S(1)}, f32[11,16,128]{2,1,0:T(8,128)S(1)}, u32[]{:S(2)}, u32[]{:S(2)}) %collective-permute-start.10) | collective-permute-done | bytes 90144 | tf_op jit(solution)/shard_map/ppermute | solution.py:432
  48.4 1.3 %collective-permute-start.12 = (f32[11,16,128]{2,1,0:T(8,128)S(1)}, f32[11,16,128]{2,1,0:T(8,128)S(1)}, u32[]{:S(2)}, u32[]{:S(2)}) collective-permute-start(f32[11,16,128]{2,1,0:T(8,128)S(1)} %get-tuple-element.33.refs_4_), channel_id=1, source_target_pairs={{0,2},{2,0},{1,3},{3,1},{4,6},{6,4},{5,7},{7,5},{8,10},{10,8},{9,1... | collective-permute-start | bytes 270344 | tf_op jit(solution)/shard_map/ppermute | solution.py:420
  50.6 3.3 %collective-permute-done.14.refs_7_ = f32[7,16,128]{2,1,0:T(8,128)S(1)} collective-permute-done((f32[7,16,128]{2,1,0:T(8,128)S(1)}, f32[7,16,128]{2,1,0:T(8,128)S(1)}, u32[]{:S(2)}, u32[]{:S(2)}) %collective-permute-start.14) | collective-permute-done | bytes 57376 | tf_op jit(solution)/shard_map/ppermute | solution.py:427
  53.8 13.3 %later_step.1 = (f32[11,16,128]{2,1,0:T(8,128)S(1)}, f32[11,16,128]{2,1,0:T(8,128)S(1)}, f32[7,16,128]{2,1,0:T(8,128)S(1)}, f32[7,16,128]{2,1,0:T(8,128)S(1)}) custom-call(s32[2]{0:T(128)S(1)} %copy-done.5, s32[2,2,8]{2,1,0:T(2,128)S(1)} %bitcast.6, f32[1,1]{1,0:T(1,128)S(6)} %copy.8.psf_ref, f32[2,1,1,128,128]{4,3,2,1,0:T(8,128)S(1)} %copy-done.2, ...), custom_call_target="tpu_custom_call" | custom-call | tf_op jit(solution)/shard_map/later_step/pallas_call | solution.py:339
  67.1 1.0 %collective-permute-start.15 = (f32[11,16,128]{2,1,0:T(8,128)S(1)}, f32[11,16,128]{2,1,0:T(8,128)S(1)}, u32[]{:S(2)}, u32[]{:S(2)}) collective-permute-start(f32[11,16,128]{2,1,0:T(8,128)S(1)} %get-tuple-element.36), channel_id=1, source_target_pairs={{0,2},{2,0},{1,3},{3,1},{4,6},{6,4},{5,7},{7,5},{8,10},{10,8},{9,1... | collective-permute-start | bytes 270344 | tf_op jit(solution)/shard_map/ppermute | solution.py:420
  68.3 1.0 %collective-permute-start.17 = (f32[7,16,128]{2,1,0:T(8,128)S(1)}, f32[7,16,128]{2,1,0:T(8,128)S(1)}, u32[]{:S(2)}, u32[]{:S(2)}) collective-permute-start(f32[7,16,128]{2,1,0:T(8,128)S(1)} %get-tuple-element.38), channel_id=1, source_target_pairs={{0,3},{1,2},{2,1},{3,0},{4,7},{5,6},{6,5},{7,4},{8,11},{9,10},{10,... | collective-permute-start | bytes 172040 | tf_op jit(solution)/shard_map/ppermute | solution.py:427
  69.4 3.1 %collective-permute-done.17 = f32[7,16,128]{2,1,0:T(8,128)S(1)} collective-permute-done((f32[7,16,128]{2,1,0:T(8,128)S(1)}, f32[7,16,128]{2,1,0:T(8,128)S(1)}, u32[]{:S(2)}, u32[]{:S(2)}) %collective-permute-start.17) | collective-permute-done | bytes 57376 | tf_op jit(solution)/shard_map/ppermute | solution.py:427
  72.8 1.9 %collective-permute-start.19 = (f32[11,8,128]{2,1,0:T(8,128)S(1)}, f32[11,8,128]{2,1,0:T(8,128)S(1)}, u32[]{:S(2)}, u32[]{:S(2)}) collective-permute-start(f32[11,8,128]{2,1,0:T(8,128)S(1)} %get-tuple-element.41), channel_id=1, source_target_pairs={{0,8},{4,12},{8,0},{12,4},{1,9},{5,13},{9,1},{13,5},{2,10},{6,14},... | collective-permute-start | bytes 135176 | tf_op jit(solution)/shard_map/ppermute | solution.py:432
  74.7 2.8 %collective-permute-start.20 = (f32[11,8,128]{2,1,0:T(8,128)S(1)}, f32[11,8,128]{2,1,0:T(8,128)S(1)}, u32[]{:S(2)}, u32[]{:S(2)}) collective-permute-start(f32[11,8,128]{2,1,0:T(8,128)S(1)} %get-tuple-element.42), channel_id=1, source_target_pairs={{0,12},{4,0},{8,4},{12,8},{1,13},{5,1},{9,5},{13,9},{2,14},{6,2},{... | collective-permute-start | bytes 135176 | tf_op jit(solution)/shard_map/ppermute | solution.py:432
  77.5 1.5 %collective-permute-done.18 = f32[11,8,128]{2,1,0:T(8,128)S(1)} collective-permute-done((f32[11,8,128]{2,1,0:T(8,128)S(1)}, f32[11,8,128]{2,1,0:T(8,128)S(1)}, u32[]{:S(2)}, u32[]{:S(2)}) %collective-permute-start.18) | collective-permute-done | bytes 45088 | tf_op jit(solution)/shard_map/ppermute | solution.py:432
  82.0 1.7 %collective-permute-done.23.refs_3_ = f32[11,8,128]{2,1,0:T(8,128)S(1)} collective-permute-done((f32[11,8,128]{2,1,0:T(8,128)S(1)}, f32[11,8,128]{2,1,0:T(8,128)S(1)}, u32[]{:S(2)}, u32[]{:S(2)}) %collective-permute-start.23) | collective-permute-done | bytes 45088 | tf_op jit(solution)/shard_map/ppermute | solution.py:427
  83.7 1.8 %collective-permute-done.21.refs_1_ = f32[11,8,128]{2,1,0:T(8,128)S(1)} collective-permute-done((f32[11,8,128]{2,1,0:T(8,128)S(1)}, f32[11,8,128]{2,1,0:T(8,128)S(1)}, u32[]{:S(2)}, u32[]{:S(2)}) %collective-permute-start.21) | collective-permute-done | bytes 45088 | tf_op jit(solution)/shard_map/ppermute | solution.py:420
  (50 shorter events, 10.8 us)
Async XLA Ops:
  2.2 7.2 %collective-permute-start.2 = (f32[12,8,128]{2,1,0:T(8,128)S(1)}, f32[12,8,128]{2,1,0:T(8,128)S(1)}, u32[]{:S(2)}, u32[]{:S(2)}) collective-permute-start(f32[12,8,128]{2,1,0:T(8,128)S(1)} %pack.1.refs_0_), channel_id=1, source_target_pairs={{0,12},{4,0},{8,4},{12,8},{1,13},{5,1},{9,5},{13,9},{2,14},{6,2},{... | collective-permute-start | bytes 147464 | tf_op jit(solution)/shard_map/ppermute | solution.py:432
  7.3 5.0 %collective-permute-start.1 = (f32[12,8,128]{2,1,0:T(8,128)S(1)}, f32[12,8,128]{2,1,0:T(8,128)S(1)}, u32[]{:S(2)}, u32[]{:S(2)}) collective-permute-start(f32[12,8,128]{2,1,0:T(8,128)S(1)} %pack.1.refs_0_), channel_id=1, source_target_pairs={{0,8},{4,12},{8,0},{12,4},{1,9},{5,13},{9,1},{13,5},{2,10},{6,14},... | collective-permute-start | bytes 147464 | tf_op jit(solution)/shard_map/ppermute | solution.py:432
  7.3 5.9 %collective-permute-start = (f32[12,8,128]{2,1,0:T(8,128)S(1)}, f32[12,8,128]{2,1,0:T(8,128)S(1)}, u32[]{:S(2)}, u32[]{:S(2)}) collective-permute-start(f32[12,8,128]{2,1,0:T(8,128)S(1)} %pack.1.refs_0_), channel_id=1, source_target_pairs={{0,4},{4,8},{8,12},{12,0},{1,5},{5,9},{9,13},{13,1},{2,6},{6,10},{... | collective-permute-start | bytes 147464 | tf_op jit(solution)/shard_map/ppermute | solution.py:432
  13.5 5.7 %collective-permute-start.3 = (f32[11,16,128]{2,1,0:T(8,128)S(1)}, f32[11,16,128]{2,1,0:T(8,128)S(1)}, u32[]{:S(2)}, u32[]{:S(2)}) collective-permute-start(f32[11,16,128]{2,1,0:T(8,128)S(1)} %get-tuple-element.25.refs_0_), channel_id=1, source_target_pairs={{0,2},{2,0},{1,3},{3,1},{4,6},{6,4},{5,7},{7,5},{8,10},{10,8},{9,1... | collective-permute-start | bytes 270344 | tf_op jit(solution)/shard_map/ppermute | solution.py:420
  15.1 4.2 %collective-permute-start.5 = (f32[7,16,128]{2,1,0:T(8,128)S(1)}, f32[7,16,128]{2,1,0:T(8,128)S(1)}, u32[]{:S(2)}, u32[]{:S(2)}) collective-permute-start(f32[7,16,128]{2,1,0:T(8,128)S(1)} %get-tuple-element.26), channel_id=1, source_target_pairs={{0,3},{1,2},{2,1},{3,0},{4,7},{5,6},{6,5},{7,4},{8,11},{9,10},{10,... | collective-permute-start | bytes 172040 | tf_op jit(solution)/shard_map/ppermute | solution.py:427
  15.1 4.2 %collective-permute-start.4 = (f32[7,16,128]{2,1,0:T(8,128)S(1)}, f32[7,16,128]{2,1,0:T(8,128)S(1)}, u32[]{:S(2)}, u32[]{:S(2)}) collective-permute-start(f32[7,16,128]{2,1,0:T(8,128)S(1)} %get-tuple-element.26), channel_id=1, source_target_pairs={{0,1},{1,0},{2,3},{3,2},{4,5},{5,4},{6,7},{7,6},{8,9},{9,8},{10,11... | collective-permute-start | bytes 172040 | tf_op jit(solution)/shard_map/ppermute | solution.py:427
  32.5 5.3 %collective-permute-start.6 = (f32[11,16,128]{2,1,0:T(8,128)S(1)}, f32[11,16,128]{2,1,0:T(8,128)S(1)}, u32[]{:S(2)}, u32[]{:S(2)}) collective-permute-start(f32[11,16,128]{2,1,0:T(8,128)S(1)} %get-tuple-element.28), channel_id=1, source_target_pairs={{0,2},{2,0},{1,3},{3,1},{4,6},{6,4},{5,7},{7,5},{8,10},{10,8},{9,1... | collective-permute-start | bytes 270344 | tf_op jit(solution)/shard_map/ppermute | solution.py:420
  33.4 1.3 %collective-permute-start.7 = (f32[7,16,128]{2,1,0:T(8,128)S(1)}, f32[7,16,128]{2,1,0:T(8,128)S(1)}, u32[]{:S(2)}, u32[]{:S(2)}) collective-permute-start(f32[7,16,128]{2,1,0:T(8,128)S(1)} %get-tuple-element.29), channel_id=1, source_target_pairs={{0,1},{1,0},{2,3},{3,2},{4,5},{5,4},{6,7},{7,6},{8,9},{9,8},{10,11... | collective-permute-start | bytes 172040 | tf_op jit(solution)/shard_map/ppermute | solution.py:427
  33.6 4.1 %collective-permute-start.8 = (f32[7,16,128]{2,1,0:T(8,128)S(1)}, f32[7,16,128]{2,1,0:T(8,128)S(1)}, u32[]{:S(2)}, u32[]{:S(2)}) collective-permute-start(f32[7,16,128]{2,1,0:T(8,128)S(1)} %get-tuple-element.30), channel_id=1, source_target_pairs={{0,3},{1,2},{2,1},{3,0},{4,7},{5,6},{6,5},{7,4},{8,11},{9,10},{10,... | collective-permute-start | bytes 172040 | tf_op jit(solution)/shard_map/ppermute | solution.py:427
  37.8 6.3 %collective-permute-start.11 = (f32[11,16,128]{2,1,0:T(8,128)S(1)}, f32[11,16,128]{2,1,0:T(8,128)S(1)}, u32[]{:S(2)}, u32[]{:S(2)}) collective-permute-start(f32[11,16,128]{2,1,0:T(8,128)S(1)} %pad_add_fusion.1.refs_0_), channel_id=1, source_target_pairs={{0,12},{4,0},{8,4},{12,8},{1,13},{5,1},{9,5},{13,9},{2,14},{6,2},{... | collective-permute-start | bytes 270344 | tf_op jit(solution)/shard_map/ppermute | solution.py:432
  37.9 10.2 %collective-permute-start.10 = (f32[11,16,128]{2,1,0:T(8,128)S(1)}, f32[11,16,128]{2,1,0:T(8,128)S(1)}, u32[]{:S(2)}, u32[]{:S(2)}) collective-permute-start(f32[11,16,128]{2,1,0:T(8,128)S(1)} %pad_add_fusion.1.refs_0_), channel_id=1, source_target_pairs={{0,8},{4,12},{8,0},{12,4},{1,9},{5,13},{9,1},{13,5},{2,10},{6,14},... | collective-permute-start | bytes 270344 | tf_op jit(solution)/shard_map/ppermute | solution.py:432
  39.1 9.0 %collective-permute-start.9 = (f32[11,16,128]{2,1,0:T(8,128)S(1)}, f32[11,16,128]{2,1,0:T(8,128)S(1)}, u32[]{:S(2)}, u32[]{:S(2)}) collective-permute-start(f32[11,16,128]{2,1,0:T(8,128)S(1)} %pad_add_fusion.1.refs_0_), channel_id=1, source_target_pairs={{0,4},{4,8},{8,12},{12,0},{1,5},{5,9},{9,13},{13,1},{2,6},{6,10},{... | collective-permute-start | bytes 270344 | tf_op jit(solution)/shard_map/ppermute | solution.py:432
  48.4 5.4 %collective-permute-start.12 = (f32[11,16,128]{2,1,0:T(8,128)S(1)}, f32[11,16,128]{2,1,0:T(8,128)S(1)}, u32[]{:S(2)}, u32[]{:S(2)}) collective-permute-start(f32[11,16,128]{2,1,0:T(8,128)S(1)} %get-tuple-element.33.refs_4_), channel_id=1, source_target_pairs={{0,2},{2,0},{1,3},{3,1},{4,6},{6,4},{5,7},{7,5},{8,10},{10,8},{9,1... | collective-permute-start | bytes 270344 | tf_op jit(solution)/shard_map/ppermute | solution.py:420
  49.7 4.2 %collective-permute-start.14 = (f32[7,16,128]{2,1,0:T(8,128)S(1)}, f32[7,16,128]{2,1,0:T(8,128)S(1)}, u32[]{:S(2)}, u32[]{:S(2)}) collective-permute-start(f32[7,16,128]{2,1,0:T(8,128)S(1)} %get-tuple-element.34), channel_id=1, source_target_pairs={{0,3},{1,2},{2,1},{3,0},{4,7},{5,6},{6,5},{7,4},{8,11},{9,10},{10,... | collective-permute-start | bytes 172040 | tf_op jit(solution)/shard_map/ppermute | solution.py:427
  49.7 4.2 %collective-permute-start.13 = (f32[7,16,128]{2,1,0:T(8,128)S(1)}, f32[7,16,128]{2,1,0:T(8,128)S(1)}, u32[]{:S(2)}, u32[]{:S(2)}) collective-permute-start(f32[7,16,128]{2,1,0:T(8,128)S(1)} %get-tuple-element.34), channel_id=1, source_target_pairs={{0,1},{1,0},{2,3},{3,2},{4,5},{5,4},{6,7},{7,6},{8,9},{9,8},{10,11... | collective-permute-start | bytes 172040 | tf_op jit(solution)/shard_map/ppermute | solution.py:427
  67.1 5.4 %collective-permute-start.15 = (f32[11,16,128]{2,1,0:T(8,128)S(1)}, f32[11,16,128]{2,1,0:T(8,128)S(1)}, u32[]{:S(2)}, u32[]{:S(2)}) collective-permute-start(f32[11,16,128]{2,1,0:T(8,128)S(1)} %get-tuple-element.36), channel_id=1, source_target_pairs={{0,2},{2,0},{1,3},{3,1},{4,6},{6,4},{5,7},{7,5},{8,10},{10,8},{9,1... | collective-permute-start | bytes 270344 | tf_op jit(solution)/shard_map/ppermute | solution.py:420
  68.1 1.2 %collective-permute-start.16 = (f32[7,16,128]{2,1,0:T(8,128)S(1)}, f32[7,16,128]{2,1,0:T(8,128)S(1)}, u32[]{:S(2)}, u32[]{:S(2)}) collective-permute-start(f32[7,16,128]{2,1,0:T(8,128)S(1)} %get-tuple-element.37), channel_id=1, source_target_pairs={{0,1},{1,0},{2,3},{3,2},{4,5},{5,4},{6,7},{7,6},{8,9},{9,8},{10,11... | collective-permute-start | bytes 172040 | tf_op jit(solution)/shard_map/ppermute | solution.py:427
  68.3 4.2 %collective-permute-start.17 = (f32[7,16,128]{2,1,0:T(8,128)S(1)}, f32[7,16,128]{2,1,0:T(8,128)S(1)}, u32[]{:S(2)}, u32[]{:S(2)}) collective-permute-start(f32[7,16,128]{2,1,0:T(8,128)S(1)} %get-tuple-element.38), channel_id=1, source_target_pairs={{0,3},{1,2},{2,1},{3,0},{4,7},{5,6},{6,5},{7,4},{8,11},{9,10},{10,... | collective-permute-start | bytes 172040 | tf_op jit(solution)/shard_map/ppermute | solution.py:427
  72.7 6.3 %collective-permute-start.18 = (f32[11,8,128]{2,1,0:T(8,128)S(1)}, f32[11,8,128]{2,1,0:T(8,128)S(1)}, u32[]{:S(2)}, u32[]{:S(2)}) collective-permute-start(f32[11,8,128]{2,1,0:T(8,128)S(1)} %get-tuple-element.40), channel_id=1, source_target_pairs={{0,4},{4,8},{8,12},{12,0},{1,5},{5,9},{9,13},{13,1},{2,6},{6,10},{... | collective-permute-start | bytes 135176 | tf_op jit(solution)/shard_map/ppermute | solution.py:432
  72.8 6.7 %collective-permute-start.19 = (f32[11,8,128]{2,1,0:T(8,128)S(1)}, f32[11,8,128]{2,1,0:T(8,128)S(1)}, u32[]{:S(2)}, u32[]{:S(2)}) collective-permute-start(f32[11,8,128]{2,1,0:T(8,128)S(1)} %get-tuple-element.41), channel_id=1, source_target_pairs={{0,8},{4,12},{8,0},{12,4},{1,9},{5,13},{9,1},{13,5},{2,10},{6,14},... | collective-permute-start | bytes 135176 | tf_op jit(solution)/shard_map/ppermute | solution.py:432
  74.7 5.1 %collective-permute-start.20 = (f32[11,8,128]{2,1,0:T(8,128)S(1)}, f32[11,8,128]{2,1,0:T(8,128)S(1)}, u32[]{:S(2)}, u32[]{:S(2)}) collective-permute-start(f32[11,8,128]{2,1,0:T(8,128)S(1)} %get-tuple-element.42), channel_id=1, source_target_pairs={{0,12},{4,0},{8,4},{12,8},{1,13},{5,1},{9,5},{13,9},{2,14},{6,2},{... | collective-permute-start | bytes 135176 | tf_op jit(solution)/shard_map/ppermute | solution.py:432
  79.8 3.9 %collective-permute-start.23 = (f32[11,8,128]{2,1,0:T(8,128)S(1)}, f32[11,8,128]{2,1,0:T(8,128)S(1)}, u32[]{:S(2)}, u32[]{:S(2)}) collective-permute-start(f32[11,8,128]{2,1,0:T(8,128)S(1)} %add_add_fusion.refs_0_), channel_id=1, source_target_pairs={{0,3},{1,2},{2,1},{3,0},{4,7},{5,6},{6,5},{7,4},{8,11},{9,10},{10,... | collective-permute-start | bytes 135176 | tf_op jit(solution)/shard_map/ppermute | solution.py:427
  80.5 3.2 %collective-permute-start.22 = (f32[11,8,128]{2,1,0:T(8,128)S(1)}, f32[11,8,128]{2,1,0:T(8,128)S(1)}, u32[]{:S(2)}, u32[]{:S(2)}) collective-permute-start(f32[11,8,128]{2,1,0:T(8,128)S(1)} %add_add_fusion.refs_0_), channel_id=1, source_target_pairs={{0,1},{1,0},{2,3},{3,2},{4,5},{5,4},{6,7},{7,6},{8,9},{9,8},{10,11... | collective-permute-start | bytes 135176 | tf_op jit(solution)/shard_map/ppermute | solution.py:427
  81.4 4.0 %collective-permute-start.21 = (f32[11,8,128]{2,1,0:T(8,128)S(1)}, f32[11,8,128]{2,1,0:T(8,128)S(1)}, u32[]{:S(2)}, u32[]{:S(2)}) collective-permute-start(f32[11,8,128]{2,1,0:T(8,128)S(1)} %add_add_fusion.refs_0_), channel_id=1, source_target_pairs={{0,2},{2,0},{1,3},{3,1},{4,6},{6,4},{5,7},{7,5},{8,10},{10,8},{9,1... | collective-permute-start | bytes 135176 | tf_op jit(solution)/shard_map/ppermute | solution.py:420
  (7 other events, 56.5 us)

commit v12 on v11

--- a/solution.py
+++ b/solution.py
@@ -20,6 +20,7 @@
 LOG2E = math.log2(math.e)
 F32 = jnp.float32
 BF16 = jnp.bfloat16
+BLOCK = 32
 MIB = 1024 * 1024
 
 
@@ -202,11 +203,7 @@
         derived[5, c] = derived[4, c] * SPLIT_SCALE
     sums[...] = jnp.zeros_like(sums)
 
-    grid = lax.broadcasted_iota(jnp.int32, (pixels, 128), 0).astype(F32)
-
-    def cut(x, large):
-        hi = (x + large) - large
-        return jnp.concatenate([hi, x - hi], axis=0)
+    first_rows = lax.broadcasted_iota(jnp.int32, (BLOCK, 128), 0).astype(F32)
 
     def stack(x):
         hi = x.astype(BF16).astype(F32)
@@ -250,14 +247,24 @@
                 s = i * together + u
                 g = t * slots + s
                 for c in range(COMPS):
-                    d = grid - line(0, c, g)
-                    e = jnp.exp2(d * d * line(2, c, g))
-                    prof_x[s * COMPS + c] = e
-                    pieces_x[s, :, c * 128 : (c + 1) * 128] = cut(e, SPLIT_UNIT)
-                    d = grid - line(1, c, g)
-                    e = jnp.exp2(d * d * line(3, c, g))
-                    prof_y[s * COMPS + c] = e
-                    pieces_y[s, :, c * 128 : (c + 1) * 128] = cut(e * line(4, c, g), line(5, c, g))
+                    at = slice(c * 128, (c + 1) * 128)
+                    centre_x, centre_y = line(0, c, g), line(1, c, g)
+                    scale_x, scale_y = line(2, c, g), line(3, c, g)
+                    amp, large = line(4, c, g), line(5, c, g)
+                    for r in range(0, pixels, BLOCK):
+                        d = (first_rows - centre_x) + F32(r)
+                        e = jnp.exp2(d * d * scale_x)
+                        prof_x[s * COMPS + c, r : r + BLOCK] = e
+                        hi = (e + SPLIT_UNIT) - SPLIT_UNIT
+                        pieces_x[s, r : r + BLOCK, at] = hi
+                        pieces_x[s, pixels + r : pixels + r + BLOCK, at] = e - hi
+                        d = (first_rows - centre_y) + F32(r)
+                        e = jnp.exp2(d * d * scale_y)
+                        prof_y[s * COMPS + c, r : r + BLOCK] = e
+                        e = e * amp
+                        hi = (e + large) - large
+                        pieces_y[s, r : r + BLOCK, at] = hi
+                        pieces_y[s, pixels + r : pixels + r + BLOCK, at] = e - hi
                 image[...] += lax.dot_general(
                     pieces_x[s], pieces_y[s], (((1,), (1,)), ((), ())), preferred_element_type=F32
                 )
@@ -278,15 +285,16 @@
                 for first in range(0, COMPS, 2):
                     here = min(2, COMPS - first)
                     span = pl.ds(first * 128, 128 * here)
-                    by_x = times(left_x, pieces_y[s, :, span])
-                    by_y = times(left_y, pieces_x[s, :, span])
-                    for n in range(here):
-                        c = first + n
-                        at = slice(n * 128, (n + 1) * 128)
-                        for k, value in enumerate(moments(prof_x[s * COMPS + c] * by_x[:, at])):
-                            sums[k, c, pl.ds(g, 1), :] = value
-                        for k, value in enumerate(moments(prof_y[s * COMPS + c] * by_y[:, at])):
-                            sums[3 + k, c, pl.ds(g, 1), :] = value
+                    for left, pieces, prof, k0 in (
+                        (left_x, pieces_y, prof_x, 0),
+                        (left_y, pieces_x, prof_y, 3),
+                    ):
+                        by = times(left, pieces[s, :, span])
+                        for n in range(here):
+                            c = first + n
+                            found = moments(prof[s * COMPS + c] * by[:, n * 128 : (n + 1) * 128])
+                            for k, value in enumerate(found):
+                                sums[k0 + k, c, pl.ds(g, 1), :] = value
             return carry
 
         lax.fori_loop(0, trips, pull, 0)

time: 86.7 us -> 85.6 us (0.987)
  Pallas kernels: 28.7 us -> 22.4 us
  starting transfers between devices: 25.1 us -> 28.3 us
  waiting for transfers between devices: 30 us -> 32 us
    pallas_call x2, Pallas kernels: 26.5 us -> 20.2 us  [step_gradient(): pl.pallas_call(functools.partial(step_kernel, layout, later), out_shape=[...]
    ppermute x9, starting transfers between devices: 14.1 us -> 17.3 us  [round_tiles(): lax.ppermute(arrays[k], 'tile', [(i, (i + k) % owners) for i in range(own...]
    ppermute x9, waiting for transfers between devices: 14.1 us -> 16.2 us  [round_tiles(): lax.ppermute(arrays[k], 'tile', [(i, (i + k) % owners) for i in range(own...]
where the time goes in v12:
time: 85.6 us; the launch traced here: 85.1 us
  waiting for transfers between devices  32 us (37%)
  starting transfers between devices  28.3 us (33%)
  Pallas kernels  22.4 us (26%)
  local copies, waits for them, and re-layouts  1.63 us (2%)
    pallas_call x2, Pallas kernels, step_gradient(): pl.pallas_call(functools.partial(step_kernel, layout, later), out_shape=[...  20.2 us
    ppermute x9, starting transfers between devices, round_tiles(): lax.ppermute(arrays[k], 'tile', [(i, (i + k) % owners) for i in range(own...  17.3 us
    ppermute x9, waiting for transfers between devices, round_tiles(): lax.ppermute(arrays[k], 'tile', [(i, (i + k) % owners) for i in range(own...  16.2 us
    ppermute x10, waiting for transfers between devices, to_peers(): kept.append(lax.ppermute(other[k], ('epoch', 'band'), pairs))  14.1 us
    ppermute x10, starting transfers between devices, to_peers(): kept.append(lax.ppermute(other[k], ('epoch', 'band'), pairs))  5.53 us
    ppermute x5, starting transfers between devices, to_peers(): lax.ppermute(same[k], 'epoch', [(i, (i + k) % epochs) for i in range(epoc...  5.43 us
    ppermute x5, waiting for transfers between devices, to_peers(): lax.ppermute(same[k], 'epoch', [(i, (i + k) % epochs) for i in range(epoc...  1.74 us
  transfers between devices with their start and end apart: 24, of which 15 were waited for; matrix products, arithmetic and copies ran while one was open for 0% of the time, Pallas kernels for 0%

profile of v12, /device:TPU:0, one launch (start us, length us, event | category | flops | bytes accessed | tf_op | source)
XLA Modules:
  0.0 85.1 jit_solution(17910476167839995919)
XLA Ops:
  2.2 5.1 %collective-permute-start.2 = (f32[12,8,128]{2,1,0:T(8,128)S(1)}, f32[12,8,128]{2,1,0:T(8,128)S(1)}, u32[]{:S(2)}, u32[]{:S(2)}) collective-permute-start(f32[12,8,128]{2,1,0:T(8,128)S(1)} %pack.1.refs_0_), channel_id=1, source_target_pairs={{0,12},{4,0},{8,4},{12,8},{1,13},{5,1},{9,5},{13,9},{2,14},{6,2},{... | collective-permute-start | bytes 147464 | tf_op jit(solution)/shard_map/ppermute | solution.py:440
  7.3 1.0 %collective-permute-start = (f32[12,8,128]{2,1,0:T(8,128)S(1)}, f32[12,8,128]{2,1,0:T(8,128)S(1)}, u32[]{:S(2)}, u32[]{:S(2)}) collective-permute-start(f32[12,8,128]{2,1,0:T(8,128)S(1)} %pack.1.refs_0_), channel_id=1, source_target_pairs={{0,4},{4,8},{8,12},{12,0},{1,5},{5,9},{9,13},{13,1},{2,6},{6,10},{... | collective-permute-start | bytes 147464 | tf_op jit(solution)/shard_map/ppermute | solution.py:440
  8.3 1.0 %collective-permute-done.2.refs_3_ = f32[12,8,128]{2,1,0:T(8,128)S(1)} collective-permute-done((f32[12,8,128]{2,1,0:T(8,128)S(1)}, f32[12,8,128]{2,1,0:T(8,128)S(1)}, u32[]{:S(2)}, u32[]{:S(2)}) %collective-permute-start.2) | collective-permute-done | bytes 49184 | tf_op jit(solution)/shard_map/ppermute | solution.py:440
  9.4 2.9 %collective-permute-done.1.refs_2_ = f32[12,8,128]{2,1,0:T(8,128)S(1)} collective-permute-done((f32[12,8,128]{2,1,0:T(8,128)S(1)}, f32[12,8,128]{2,1,0:T(8,128)S(1)}, u32[]{:S(2)}, u32[]{:S(2)}) %collective-permute-start.1) | collective-permute-done | bytes 49184 | tf_op jit(solution)/shard_map/ppermute | solution.py:440
  13.5 1.5 %collective-permute-start.3 = (f32[11,16,128]{2,1,0:T(8,128)S(1)}, f32[11,16,128]{2,1,0:T(8,128)S(1)}, u32[]{:S(2)}, u32[]{:S(2)}) collective-permute-start(f32[11,16,128]{2,1,0:T(8,128)S(1)} %get-tuple-element.25.refs_0_), channel_id=1, source_target_pairs={{0,2},{2,0},{1,3},{3,1},{4,6},{6,4},{5,7},{7,5},{8,10},{10,8},{9,1... | collective-permute-start | bytes 270344 | tf_op jit(solution)/shard_map/ppermute | solution.py:428
  16.4 2.9 %collective-permute-done.5.refs_3_ = f32[7,16,128]{2,1,0:T(8,128)S(1)} collective-permute-done((f32[7,16,128]{2,1,0:T(8,128)S(1)}, f32[7,16,128]{2,1,0:T(8,128)S(1)}, u32[]{:S(2)}, u32[]{:S(2)}) %collective-permute-start.5) | collective-permute-done | bytes 57376 | tf_op jit(solution)/shard_map/ppermute | solution.py:435
  19.3 10.1 %first_step.1 = (f32[11,16,128]{2,1,0:T(8,128)S(1)}, f32[11,16,128]{2,1,0:T(8,128)S(1)}, f32[7,16,128]{2,1,0:T(8,128)S(1)}, f32[7,16,128]{2,1,0:T(8,128)S(1)}) custom-call(s32[2]{0:T(128)S(1)} %copy-done.5, s32[2,2,8]{2,1,0:T(2,128)S(1)} %bitcast.5, f32[1,1]{1,0:T(1,128)S(6)} %copy.8.psf_ref, f32[2,1,1,128,128]{4,3,2,1,0:T(8,128)S(1)} %copy-done.2, ...), custom_call_target="tpu_custom_call" | custom-call | tf_op jit(solution)/shard_map/first_step/pallas_call | solution.py:347
  30.5 1.1 %collective-permute-start.8 = (f32[7,16,128]{2,1,0:T(8,128)S(1)}, f32[7,16,128]{2,1,0:T(8,128)S(1)}, u32[]{:S(2)}, u32[]{:S(2)}) collective-permute-start(f32[7,16,128]{2,1,0:T(8,128)S(1)} %get-tuple-element.30), channel_id=1, source_target_pairs={{0,3},{1,2},{2,1},{3,0},{4,7},{5,6},{6,5},{7,4},{8,11},{9,10},{10,... | collective-permute-start | bytes 172040 | tf_op jit(solution)/shard_map/ppermute | solution.py:435
  31.6 3.1 %collective-permute-done.8 = f32[7,16,128]{2,1,0:T(8,128)S(1)} collective-permute-done((f32[7,16,128]{2,1,0:T(8,128)S(1)}, f32[7,16,128]{2,1,0:T(8,128)S(1)}, u32[]{:S(2)}, u32[]{:S(2)}) %collective-permute-start.8) | collective-permute-done | bytes 57376 | tf_op jit(solution)/shard_map/ppermute | solution.py:435
  34.7 4.3 %collective-permute-start.11 = (f32[11,16,128]{2,1,0:T(8,128)S(1)}, f32[11,16,128]{2,1,0:T(8,128)S(1)}, u32[]{:S(2)}, u32[]{:S(2)}) collective-permute-start(f32[11,16,128]{2,1,0:T(8,128)S(1)} %pad_add_fusion.1.refs_0_), channel_id=1, source_target_pairs={{0,12},{4,0},{8,4},{12,8},{1,13},{5,1},{9,5},{13,9},{2,14},{6,2},{... | collective-permute-start | bytes 270344 | tf_op jit(solution)/shard_map/ppermute | solution.py:440
  39.6 2.3 %collective-permute-done.11.refs_3_ = f32[11,16,128]{2,1,0:T(8,128)S(1)} collective-permute-done((f32[11,16,128]{2,1,0:T(8,128)S(1)}, f32[11,16,128]{2,1,0:T(8,128)S(1)}, u32[]{:S(2)}, u32[]{:S(2)}) %collective-permute-start.11) | collective-permute-done | bytes 90144 | tf_op jit(solution)/shard_map/ppermute | solution.py:440
  42.0 6.1 %collective-permute-done.10.refs_2_ = f32[11,16,128]{2,1,0:T(8,128)S(1)} collective-permute-done((f32[11,16,128]{2,1,0:T(8,128)S(1)}, f32[11,16,128]{2,1,0:T(8,128)S(1)}, u32[]{:S(2)}, u32[]{:S(2)}) %collective-permute-start.10) | collective-permute-done | bytes 90144 | tf_op jit(solution)/shard_map/ppermute | solution.py:440
  48.4 1.2 %collective-permute-start.12 = (f32[11,16,128]{2,1,0:T(8,128)S(1)}, f32[11,16,128]{2,1,0:T(8,128)S(1)}, u32[]{:S(2)}, u32[]{:S(2)}) collective-permute-start(f32[11,16,128]{2,1,0:T(8,128)S(1)} %get-tuple-element.33.refs_4_), channel_id=1, source_target_pairs={{0,2},{2,0},{1,3},{3,1},{4,6},{6,4},{5,7},{7,5},{8,10},{10,8},{9,1... | collective-permute-start | bytes 270344 | tf_op jit(solution)/shard_map/ppermute | solution.py:428
  50.6 3.2 %collective-permute-done.14.refs_7_ = f32[7,16,128]{2,1,0:T(8,128)S(1)} collective-permute-done((f32[7,16,128]{2,1,0:T(8,128)S(1)}, f32[7,16,128]{2,1,0:T(8,128)S(1)}, u32[]{:S(2)}, u32[]{:S(2)}) %collective-permute-start.14) | collective-permute-done | bytes 57376 | tf_op jit(solution)/shard_map/ppermute | solution.py:435
  53.8 10.1 %later_step.1 = (f32[11,16,128]{2,1,0:T(8,128)S(1)}, f32[11,16,128]{2,1,0:T(8,128)S(1)}, f32[7,16,128]{2,1,0:T(8,128)S(1)}, f32[7,16,128]{2,1,0:T(8,128)S(1)}) custom-call(s32[2]{0:T(128)S(1)} %copy-done.5, s32[2,2,8]{2,1,0:T(2,128)S(1)} %bitcast.6, f32[1,1]{1,0:T(1,128)S(6)} %copy.8.psf_ref, f32[2,1,1,128,128]{4,3,2,1,0:T(8,128)S(1)} %copy-done.2, ...), custom_call_target="tpu_custom_call" | custom-call | tf_op jit(solution)/shard_map/later_step/pallas_call | solution.py:347
  63.9 1.1 %collective-permute-start.15 = (f32[11,16,128]{2,1,0:T(8,128)S(1)}, f32[11,16,128]{2,1,0:T(8,128)S(1)}, u32[]{:S(2)}, u32[]{:S(2)}) collective-permute-start(f32[11,16,128]{2,1,0:T(8,128)S(1)} %get-tuple-element.36), channel_id=1, source_target_pairs={{0,2},{2,0},{1,3},{3,1},{4,6},{6,4},{5,7},{7,5},{8,10},{10,8},{9,1... | collective-permute-start | bytes 270344 | tf_op jit(solution)/shard_map/ppermute | solution.py:428
  66.2 3.1 %collective-permute-done.17 = f32[7,16,128]{2,1,0:T(8,128)S(1)} collective-permute-done((f32[7,16,128]{2,1,0:T(8,128)S(1)}, f32[7,16,128]{2,1,0:T(8,128)S(1)}, u32[]{:S(2)}, u32[]{:S(2)}) %collective-permute-start.17) | collective-permute-done | bytes 57376 | tf_op jit(solution)/shard_map/ppermute | solution.py:435
  69.6 2.9 %collective-permute-start.18 = (f32[11,8,128]{2,1,0:T(8,128)S(1)}, f32[11,8,128]{2,1,0:T(8,128)S(1)}, u32[]{:S(2)}, u32[]{:S(2)}) collective-permute-start(f32[11,8,128]{2,1,0:T(8,128)S(1)} %get-tuple-element.40), channel_id=1, source_target_pairs={{0,4},{4,8},{8,12},{12,0},{1,5},{5,9},{9,13},{13,1},{2,6},{6,10},{... | collective-permute-start | bytes 135176 | tf_op jit(solution)/shard_map/ppermute | solution.py:440
  72.5 2.1 %collective-permute-start.19 = (f32[11,8,128]{2,1,0:T(8,128)S(1)}, f32[11,8,128]{2,1,0:T(8,128)S(1)}, u32[]{:S(2)}, u32[]{:S(2)}) collective-permute-start(f32[11,8,128]{2,1,0:T(8,128)S(1)} %get-tuple-element.41), channel_id=1, source_target_pairs={{0,8},{4,12},{8,0},{12,4},{1,9},{5,13},{9,1},{13,5},{2,10},{6,14},... | collective-permute-start | bytes 135176 | tf_op jit(solution)/shard_map/ppermute | solution.py:440
  74.6 1.3 %collective-permute-start.20 = (f32[11,8,128]{2,1,0:T(8,128)S(1)}, f32[11,8,128]{2,1,0:T(8,128)S(1)}, u32[]{:S(2)}, u32[]{:S(2)}) collective-permute-start(f32[11,8,128]{2,1,0:T(8,128)S(1)} %get-tuple-element.42), channel_id=1, source_target_pairs={{0,12},{4,0},{8,4},{12,8},{1,13},{5,1},{9,5},{13,9},{2,14},{6,2},{... | collective-permute-start | bytes 135176 | tf_op jit(solution)/shard_map/ppermute | solution.py:440
  76.3 2.2 %collective-permute-done.19 = f32[11,8,128]{2,1,0:T(8,128)S(1)} collective-permute-done((f32[11,8,128]{2,1,0:T(8,128)S(1)}, f32[11,8,128]{2,1,0:T(8,128)S(1)}, u32[]{:S(2)}, u32[]{:S(2)}) %collective-permute-start.19) | collective-permute-done | bytes 45088 | tf_op jit(solution)/shard_map/ppermute | solution.py:440
  79.2 1.2 %collective-permute-start.22 = (f32[11,8,128]{2,1,0:T(8,128)S(1)}, f32[11,8,128]{2,1,0:T(8,128)S(1)}, u32[]{:S(2)}, u32[]{:S(2)}) collective-permute-start(f32[11,8,128]{2,1,0:T(8,128)S(1)} %add_add_fusion.refs_0_), channel_id=1, source_target_pairs={{0,1},{1,0},{2,3},{3,2},{4,5},{5,4},{6,7},{7,6},{8,9},{9,8},{10,11... | collective-permute-start | bytes 135176 | tf_op jit(solution)/shard_map/ppermute | solution.py:435
  81.0 1.7 %collective-permute-done.23.refs_3_ = f32[11,8,128]{2,1,0:T(8,128)S(1)} collective-permute-done((f32[11,8,128]{2,1,0:T(8,128)S(1)}, f32[11,8,128]{2,1,0:T(8,128)S(1)}, u32[]{:S(2)}, u32[]{:S(2)}) %collective-permute-start.23) | collective-permute-done | bytes 45088 | tf_op jit(solution)/shard_map/ppermute | solution.py:435
  82.8 1.6 %collective-permute-done.21.refs_1_ = f32[11,8,128]{2,1,0:T(8,128)S(1)} collective-permute-done((f32[11,8,128]{2,1,0:T(8,128)S(1)}, f32[11,8,128]{2,1,0:T(8,128)S(1)}, u32[]{:S(2)}, u32[]{:S(2)}) %collective-permute-start.21) | collective-permute-done | bytes 45088 | tf_op jit(solution)/shard_map/ppermute | solution.py:428
  (50 shorter events, 11.2 us)
Async XLA Ops:
  2.2 7.2 %collective-permute-start.2 = (f32[12,8,128]{2,1,0:T(8,128)S(1)}, f32[12,8,128]{2,1,0:T(8,128)S(1)}, u32[]{:S(2)}, u32[]{:S(2)}) collective-permute-start(f32[12,8,128]{2,1,0:T(8,128)S(1)} %pack.1.refs_0_), channel_id=1, source_target_pairs={{0,12},{4,0},{8,4},{12,8},{1,13},{5,1},{9,5},{13,9},{2,14},{6,2},{... | collective-permute-start | bytes 147464 | tf_op jit(solution)/shard_map/ppermute | solution.py:440
  7.3 5.0 %collective-permute-start.1 = (f32[12,8,128]{2,1,0:T(8,128)S(1)}, f32[12,8,128]{2,1,0:T(8,128)S(1)}, u32[]{:S(2)}, u32[]{:S(2)}) collective-permute-start(f32[12,8,128]{2,1,0:T(8,128)S(1)} %pack.1.refs_0_), channel_id=1, source_target_pairs={{0,8},{4,12},{8,0},{12,4},{1,9},{5,13},{9,1},{13,5},{2,10},{6,14},... | collective-permute-start | bytes 147464 | tf_op jit(solution)/shard_map/ppermute | solution.py:440
  7.3 5.9 %collective-permute-start = (f32[12,8,128]{2,1,0:T(8,128)S(1)}, f32[12,8,128]{2,1,0:T(8,128)S(1)}, u32[]{:S(2)}, u32[]{:S(2)}) collective-permute-start(f32[12,8,128]{2,1,0:T(8,128)S(1)} %pack.1.refs_0_), channel_id=1, source_target_pairs={{0,4},{4,8},{8,12},{12,0},{1,5},{5,9},{9,13},{13,1},{2,6},{6,10},{... | collective-permute-start | bytes 147464 | tf_op jit(solution)/shard_map/ppermute | solution.py:440
  13.5 5.7 %collective-permute-start.3 = (f32[11,16,128]{2,1,0:T(8,128)S(1)}, f32[11,16,128]{2,1,0:T(8,128)S(1)}, u32[]{:S(2)}, u32[]{:S(2)}) collective-permute-start(f32[11,16,128]{2,1,0:T(8,128)S(1)} %get-tuple-element.25.refs_0_), channel_id=1, source_target_pairs={{0,2},{2,0},{1,3},{3,1},{4,6},{6,4},{5,7},{7,5},{8,10},{10,8},{9,1... | collective-permute-start | bytes 270344 | tf_op jit(solution)/shard_map/ppermute | solution.py:428
  15.1 4.2 %collective-permute-start.5 = (f32[7,16,128]{2,1,0:T(8,128)S(1)}, f32[7,16,128]{2,1,0:T(8,128)S(1)}, u32[]{:S(2)}, u32[]{:S(2)}) collective-permute-start(f32[7,16,128]{2,1,0:T(8,128)S(1)} %get-tuple-element.26), channel_id=1, source_target_pairs={{0,3},{1,2},{2,1},{3,0},{4,7},{5,6},{6,5},{7,4},{8,11},{9,10},{10,... | collective-permute-start | bytes 172040 | tf_op jit(solution)/shard_map/ppermute | solution.py:435
  15.1 4.2 %collective-permute-start.4 = (f32[7,16,128]{2,1,0:T(8,128)S(1)}, f32[7,16,128]{2,1,0:T(8,128)S(1)}, u32[]{:S(2)}, u32[]{:S(2)}) collective-permute-start(f32[7,16,128]{2,1,0:T(8,128)S(1)} %get-tuple-element.26), channel_id=1, source_target_pairs={{0,1},{1,0},{2,3},{3,2},{4,5},{5,4},{6,7},{7,6},{8,9},{9,8},{10,11... | collective-permute-start | bytes 172040 | tf_op jit(solution)/shard_map/ppermute | solution.py:435
  29.4 5.3 %collective-permute-start.6 = (f32[11,16,128]{2,1,0:T(8,128)S(1)}, f32[11,16,128]{2,1,0:T(8,128)S(1)}, u32[]{:S(2)}, u32[]{:S(2)}) collective-permute-start(f32[11,16,128]{2,1,0:T(8,128)S(1)} %get-tuple-element.28), channel_id=1, source_target_pairs={{0,2},{2,0},{1,3},{3,1},{4,6},{6,4},{5,7},{7,5},{8,10},{10,8},{9,1... | collective-permute-start | bytes 270344 | tf_op jit(solution)/shard_map/ppermute | solution.py:428
  30.3 1.3 %collective-permute-start.7 = (f32[7,16,128]{2,1,0:T(8,128)S(1)}, f32[7,16,128]{2,1,0:T(8,128)S(1)}, u32[]{:S(2)}, u32[]{:S(2)}) collective-permute-start(f32[7,16,128]{2,1,0:T(8,128)S(1)} %get-tuple-element.29), channel_id=1, source_target_pairs={{0,1},{1,0},{2,3},{3,2},{4,5},{5,4},{6,7},{7,6},{8,9},{9,8},{10,11... | collective-permute-start | bytes 172040 | tf_op jit(solution)/shard_map/ppermute | solution.py:435
  30.5 4.1 %collective-permute-start.8 = (f32[7,16,128]{2,1,0:T(8,128)S(1)}, f32[7,16,128]{2,1,0:T(8,128)S(1)}, u32[]{:S(2)}, u32[]{:S(2)}) collective-permute-start(f32[7,16,128]{2,1,0:T(8,128)S(1)} %get-tuple-element.30), channel_id=1, source_target_pairs={{0,3},{1,2},{2,1},{3,0},{4,7},{5,6},{6,5},{7,4},{8,11},{9,10},{10,... | collective-permute-start | bytes 172040 | tf_op jit(solution)/shard_map/ppermute | solution.py:435
  34.7 7.3 %collective-permute-start.11 = (f32[11,16,128]{2,1,0:T(8,128)S(1)}, f32[11,16,128]{2,1,0:T(8,128)S(1)}, u32[]{:S(2)}, u32[]{:S(2)}) collective-permute-start(f32[11,16,128]{2,1,0:T(8,128)S(1)} %pad_add_fusion.1.refs_0_), channel_id=1, source_target_pairs={{0,12},{4,0},{8,4},{12,8},{1,13},{5,1},{9,5},{13,9},{2,14},{6,2},{... | collective-permute-start | bytes 270344 | tf_op jit(solution)/shard_map/ppermute | solution.py:440
  39.0 9.0 %collective-permute-start.10 = (f32[11,16,128]{2,1,0:T(8,128)S(1)}, f32[11,16,128]{2,1,0:T(8,128)S(1)}, u32[]{:S(2)}, u32[]{:S(2)}) collective-permute-start(f32[11,16,128]{2,1,0:T(8,128)S(1)} %pad_add_fusion.1.refs_0_), channel_id=1, source_target_pairs={{0,8},{4,12},{8,0},{12,4},{1,9},{5,13},{9,1},{13,5},{2,10},{6,14},... | collective-permute-start | bytes 270344 | tf_op jit(solution)/shard_map/ppermute | solution.py:440
  39.0 9.0 %collective-permute-start.9 = (f32[11,16,128]{2,1,0:T(8,128)S(1)}, f32[11,16,128]{2,1,0:T(8,128)S(1)}, u32[]{:S(2)}, u32[]{:S(2)}) collective-permute-start(f32[11,16,128]{2,1,0:T(8,128)S(1)} %pad_add_fusion.1.refs_0_), channel_id=1, source_target_pairs={{0,4},{4,8},{8,12},{12,0},{1,5},{5,9},{9,13},{13,1},{2,6},{6,10},{... | collective-permute-start | bytes 270344 | tf_op jit(solution)/shard_map/ppermute | solution.py:440
  48.4 5.4 %collective-permute-start.12 = (f32[11,16,128]{2,1,0:T(8,128)S(1)}, f32[11,16,128]{2,1,0:T(8,128)S(1)}, u32[]{:S(2)}, u32[]{:S(2)}) collective-permute-start(f32[11,16,128]{2,1,0:T(8,128)S(1)} %get-tuple-element.33.refs_4_), channel_id=1, source_target_pairs={{0,2},{2,0},{1,3},{3,1},{4,6},{6,4},{5,7},{7,5},{8,10},{10,8},{9,1... | collective-permute-start | bytes 270344 | tf_op jit(solution)/shard_map/ppermute | solution.py:428
  49.6 4.2 %collective-permute-start.14 = (f32[7,16,128]{2,1,0:T(8,128)S(1)}, f32[7,16,128]{2,1,0:T(8,128)S(1)}, u32[]{:S(2)}, u32[]{:S(2)}) collective-permute-start(f32[7,16,128]{2,1,0:T(8,128)S(1)} %get-tuple-element.34), channel_id=1, source_target_pairs={{0,3},{1,2},{2,1},{3,0},{4,7},{5,6},{6,5},{7,4},{8,11},{9,10},{10,... | collective-permute-start | bytes 172040 | tf_op jit(solution)/shard_map/ppermute | solution.py:435
  49.8 4.0 %collective-permute-start.13 = (f32[7,16,128]{2,1,0:T(8,128)S(1)}, f32[7,16,128]{2,1,0:T(8,128)S(1)}, u32[]{:S(2)}, u32[]{:S(2)}) collective-permute-start(f32[7,16,128]{2,1,0:T(8,128)S(1)} %get-tuple-element.34), channel_id=1, source_target_pairs={{0,1},{1,0},{2,3},{3,2},{4,5},{5,4},{6,7},{7,6},{8,9},{9,8},{10,11... | collective-permute-start | bytes 172040 | tf_op jit(solution)/shard_map/ppermute | solution.py:435
  63.9 5.4 %collective-permute-start.15 = (f32[11,16,128]{2,1,0:T(8,128)S(1)}, f32[11,16,128]{2,1,0:T(8,128)S(1)}, u32[]{:S(2)}, u32[]{:S(2)}) collective-permute-start(f32[11,16,128]{2,1,0:T(8,128)S(1)} %get-tuple-element.36), channel_id=1, source_target_pairs={{0,2},{2,0},{1,3},{3,1},{4,6},{6,4},{5,7},{7,5},{8,10},{10,8},{9,1... | collective-permute-start | bytes 270344 | tf_op jit(solution)/shard_map/ppermute | solution.py:428
  65.0 1.2 %collective-permute-start.16 = (f32[7,16,128]{2,1,0:T(8,128)S(1)}, f32[7,16,128]{2,1,0:T(8,128)S(1)}, u32[]{:S(2)}, u32[]{:S(2)}) collective-permute-start(f32[7,16,128]{2,1,0:T(8,128)S(1)} %get-tuple-element.37), channel_id=1, source_target_pairs={{0,1},{1,0},{2,3},{3,2},{4,5},{5,4},{6,7},{7,6},{8,9},{9,8},{10,11... | collective-permute-start | bytes 172040 | tf_op jit(solution)/shard_map/ppermute | solution.py:435
  65.2 4.2 %collective-permute-start.17 = (f32[7,16,128]{2,1,0:T(8,128)S(1)}, f32[7,16,128]{2,1,0:T(8,128)S(1)}, u32[]{:S(2)}, u32[]{:S(2)}) collective-permute-start(f32[7,16,128]{2,1,0:T(8,128)S(1)} %get-tuple-element.38), channel_id=1, source_target_pairs={{0,3},{1,2},{2,1},{3,0},{4,7},{5,6},{6,5},{7,4},{8,11},{9,10},{10,... | collective-permute-start | bytes 172040 | tf_op jit(solution)/shard_map/ppermute | solution.py:435
  69.6 6.7 %collective-permute-start.18 = (f32[11,8,128]{2,1,0:T(8,128)S(1)}, f32[11,8,128]{2,1,0:T(8,128)S(1)}, u32[]{:S(2)}, u32[]{:S(2)}) collective-permute-start(f32[11,8,128]{2,1,0:T(8,128)S(1)} %get-tuple-element.40), channel_id=1, source_target_pairs={{0,4},{4,8},{8,12},{12,0},{1,5},{5,9},{9,13},{13,1},{2,6},{6,10},{... | collective-permute-start | bytes 135176 | tf_op jit(solution)/shard_map/ppermute | solution.py:440
  72.5 6.0 %collective-permute-start.19 = (f32[11,8,128]{2,1,0:T(8,128)S(1)}, f32[11,8,128]{2,1,0:T(8,128)S(1)}, u32[]{:S(2)}, u32[]{:S(2)}) collective-permute-start(f32[11,8,128]{2,1,0:T(8,128)S(1)} %get-tuple-element.41), channel_id=1, source_target_pairs={{0,8},{4,12},{8,0},{12,4},{1,9},{5,13},{9,1},{13,5},{2,10},{6,14},... | collective-permute-start | bytes 135176 | tf_op jit(solution)/shard_map/ppermute | solution.py:440
  74.6 4.2 %collective-permute-start.20 = (f32[11,8,128]{2,1,0:T(8,128)S(1)}, f32[11,8,128]{2,1,0:T(8,128)S(1)}, u32[]{:S(2)}, u32[]{:S(2)}) collective-permute-start(f32[11,8,128]{2,1,0:T(8,128)S(1)} %get-tuple-element.42), channel_id=1, source_target_pairs={{0,12},{4,0},{8,4},{12,8},{1,13},{5,1},{9,5},{13,9},{2,14},{6,2},{... | collective-permute-start | bytes 135176 | tf_op jit(solution)/shard_map/ppermute | solution.py:440
  78.8 3.9 %collective-permute-start.23 = (f32[11,8,128]{2,1,0:T(8,128)S(1)}, f32[11,8,128]{2,1,0:T(8,128)S(1)}, u32[]{:S(2)}, u32[]{:S(2)}) collective-permute-start(f32[11,8,128]{2,1,0:T(8,128)S(1)} %add_add_fusion.refs_0_), channel_id=1, source_target_pairs={{0,3},{1,2},{2,1},{3,0},{4,7},{5,6},{6,5},{7,4},{8,11},{9,10},{10,... | collective-permute-start | bytes 135176 | tf_op jit(solution)/shard_map/ppermute | solution.py:435
  79.2 3.6 %collective-permute-start.22 = (f32[11,8,128]{2,1,0:T(8,128)S(1)}, f32[11,8,128]{2,1,0:T(8,128)S(1)}, u32[]{:S(2)}, u32[]{:S(2)}) collective-permute-start(f32[11,8,128]{2,1,0:T(8,128)S(1)} %add_add_fusion.refs_0_), channel_id=1, source_target_pairs={{0,1},{1,0},{2,3},{3,2},{4,5},{5,4},{6,7},{7,6},{8,9},{9,8},{10,11... | collective-permute-start | bytes 135176 | tf_op jit(solution)/shard_map/ppermute | solution.py:435
  80.4 4.0 %collective-permute-start.21 = (f32[11,8,128]{2,1,0:T(8,128)S(1)}, f32[11,8,128]{2,1,0:T(8,128)S(1)}, u32[]{:S(2)}, u32[]{:S(2)}) collective-permute-start(f32[11,8,128]{2,1,0:T(8,128)S(1)} %add_add_fusion.refs_0_), channel_id=1, source_target_pairs={{0,2},{2,0},{1,3},{3,1},{4,6},{6,4},{5,7},{7,5},{8,10},{10,8},{9,1... | collective-permute-start | bytes 135176 | tf_op jit(solution)/shard_map/ppermute | solution.py:428
  (7 other events, 58.5 us)

commit v13 on v11

--- a/solution.py
+++ b/solution.py
@@ -102,7 +102,7 @@
 
 def select_kernel(layout, wide, *refs):
     shared_rows, rows, pieces = layout
-    got, (out_ref, short_ref, match_ref, place_ref) = refs[:-4], refs[-4:]
+    got, (out_ref, match_ref, place_ref) = refs[:-3], refs[-3:]
     owners = len(got)
     blocks = got[0].shape[1]
     me = lax.axis_index("tile")
@@ -114,10 +114,7 @@
     held = lax.rem(me - lane // blocks + owners, owners) * blocks + lane % blocks
     choose = (own_column[:, : owners * blocks] == held.astype(F32)).astype(F32)
     for p in range(rows):
-        chosen = pick(choose, jnp.concatenate([ref[p] for ref in got], axis=0))
-        out_ref[p] = chosen
-        if p < shared_rows:
-            short_ref[p] = chosen
+        out_ref[p] = pick(choose, jnp.concatenate([ref[p] for ref in got], axis=0))
 
     lists = jnp.concatenate([ref[rows, :1, :wide] for ref in got], axis=1)
     match_ref[:wide] = (own_column[:, :1] == lists).astype(F32)
@@ -134,7 +131,7 @@
     for k in range(epochs):
         q = lax.rem(epoch - k + epochs, epochs)
         half[q] = ins[k][...]
-        other[q] = ins[epochs + k][...]
+        other[q] = ins[epochs][k]
     for q, piece in enumerate(pieces):
         for p, entry in enumerate(piece):
             if entry is None:
@@ -150,9 +147,10 @@
 def step_kernel(layout, later, counts_ref, offsets_ref, psf_ref, data_ref, weight_ref, *refs):
     shared_rows, rows, pieces = layout
     epochs = len(pieces)
-    taken = 2 * epochs * (2 if later else 1)
+    arrays = epochs + 1
+    taken = arrays * (2 if later else 1)
     ins, refs = refs[:taken], refs[taken:]
-    outs, refs = refs[: 2 * epochs], refs[2 * epochs :]
+    outs, refs = refs[:arrays], refs[arrays:]
     shared, amps, derived, prof_x, prof_y, pieces_x, pieces_y, image, sums, half, other = refs[:11]
     band, epoch = lax.axis_index("band"), lax.axis_index("epoch")
     tiles = data_ref.shape[0]
@@ -161,7 +159,7 @@
     slots = wide // tiles
     spacing = pixels / 8.0
 
-    put_together(layout, band, epoch, ins[: 2 * epochs], half, other, shared, amps)
+    put_together(layout, band, epoch, ins[:arrays], half, other, shared, amps)
 
     def row(k, c):
         r = k * COMPS + c
@@ -169,7 +167,7 @@
 
     if later:
         moved, moved_amps = refs[11:]
-        put_together(layout, band, epoch, ins[2 * epochs :], half, other, moved, moved_amps)
+        put_together(layout, band, epoch, ins[arrays:], half, other, moved, moved_amps)
         for k in range(4):
             shift = 0.0
             if k < 2:
@@ -323,7 +321,7 @@
                 other[q, p] = shared[1 - band, entry[1]] if is_shared else none
     for k in range(epochs):
         outs[k][...] = half[lax.rem(epoch + k, epochs)]
-        outs[epochs + k][...] = other[lax.rem(epoch + k, epochs)]
+        outs[epochs][k] = other[lax.rem(epoch + k, epochs)]
 
 
 def step_gradient(layout, counts, offsets, psf, data, weight, slot_rows, moved):
@@ -333,7 +331,7 @@
     tiles, _, slots = offsets.shape
     pixels = data.shape[-1]
     wide = tiles * slots
-    shapes = [(rows, wide, 128)] * epochs + [(shared_rows, wide, 128)] * epochs
+    shapes = [(rows, wide, 128)] * epochs + [(epochs, shared_rows, wide, 128)]
     ins = slot_rows + (moved or [])
     together = [pltpu.VMEM((BANDS, HALF, wide, 128), F32), pltpu.VMEM((COMPS, wide, 128), F32)]
     return pl.pallas_call(
@@ -361,14 +359,12 @@
 
 def combine_kernel(layout, match_ref, *refs):
     shared_rows, rows, pieces = layout
-    got, (out_ref, short_ref, own_ref) = refs[:-3], refs[-3:]
+    got, (out_ref, own_ref) = refs[:-2], refs[-2:]
     wide = out_ref.shape[1]
     match = match_ref[...]
     for p in range(rows):
         both = pick(match, jnp.concatenate([ref[p] for ref in got], axis=0))
         out_ref[p] = both[:wide]
-        if p < shared_rows:
-            short_ref[p] = both[:wide]
         own_ref[p] = both[wide:]
 
 
@@ -384,12 +380,12 @@
 def final_kernel(layout, spacing, params_ref, *refs):
     shared_rows, rows, pieces = layout
     epochs = len(pieces)
-    ins, (out_ref, held) = refs[: 2 * epochs], refs[2 * epochs :]
+    ins, (out_ref, held) = refs[: epochs + 1], refs[epochs + 1 :]
     band, epoch = lax.axis_index("band"), lax.axis_index("epoch")
     for k in range(epochs):
         q = lax.rem(epoch - k + epochs, epochs)
         held[band, q] = ins[k][...]
-        held[1 - band, q] = ins[epochs + k][...]
+        held[1 - band, q] = ins[epochs][k]
     shift = [0.0, 0.0]
     for b in range(BANDS):
         for q, piece in enumerate(pieces):
@@ -414,18 +410,11 @@
     layout = quarter_layout(epochs)
     shared_rows, rows, pieces = layout
 
-    def to_peers(same, other):
-        kept = [same[0]]
-        for k in range(1, epochs):
-            kept.append(lax.ppermute(same[k], "epoch", [(i, (i + k) % epochs) for i in range(epochs)]))
-        for k in range(epochs):
-            pairs = [
-                (i * BANDS + b, (i + k) % epochs * BANDS + 1 - b)
-                for i in range(epochs)
-                for b in range(BANDS)
-            ]
-            kept.append(lax.ppermute(other[k], ("epoch", "band"), pairs))
-        return kept
+    def to_epoch(x, k):
+        return lax.ppermute(x, "epoch", [(i, (i + k) % epochs) for i in range(epochs)])
+
+    def to_other_band(x):
+        return lax.ppermute(x, "band", [(b, 1 - b) for b in range(BANDS)])
 
     def round_tiles(arrays):
         return [arrays[0]] + [
@@ -433,13 +422,17 @@
             for k in range(1, owners)
         ]
 
-    def spread(piece, other):
-        return to_peers([piece] * epochs, [other] * epochs)
+    def spread(piece, count):
+        got = [piece] + [to_epoch(piece, k) for k in range(1, epochs)]
+        return got + [to_other_band(jnp.stack([x[:count] for x in got]))]
 
     def summed(parts):
-        near = functools.reduce(lambda a, b: a + b, parts[:epochs])
-        far = functools.reduce(lambda a, b: a + b, parts[epochs:])
-        return near + jnp.pad(far, ((0, rows - shared_rows), (0, 0), (0, 0)))
+        far = to_other_band(parts[epochs])
+        missing = ((0, rows - shared_rows), (0, 0), (0, 0))
+        halves = [parts[k] + jnp.pad(far[k], missing) for k in range(epochs)]
+        return functools.reduce(
+            lambda a, b: a + b, [to_epoch(halves[k], k) for k in range(1, epochs)], halves[0]
+        )
 
     by_row = jnp.transpose(source_params, (1, 0, 2))
     offsets = jnp.transpose(block_offsets, (0, 2, 1))
@@ -452,37 +445,35 @@
         name="pack",
     )(block_lists, by_row)
     got = round_tiles([packed] * owners)
-    slot_piece, slot_short, match, place = pl.pallas_call(
+    slot_piece, match, place = pl.pallas_call(
         functools.partial(select_kernel, layout, wide),
         out_shape=[
             f32(rows, wide, sources),
-            f32(shared_rows, wide, sources),
             f32(wide + blocks, owners * wide),
             f32(owners * blocks, wide),
         ],
         in_specs=[vmem()] * owners,
-        out_specs=[vmem()] * 4,
+        out_specs=[vmem()] * 3,
         compiler_params=params(),
         name="select",
     )(*got)
-    slot_rows = spread(slot_piece, slot_short)
+    slot_rows = spread(slot_piece, shared_rows)
 
     def gradient(moved):
         parts = step_gradient(
             layout, block_counts, offsets, psf_width, pixel_data, pixel_weight, slot_rows, moved
         )
-        return summed(to_peers(parts[:epochs], parts[epochs:]))
+        return summed(parts)
 
     got = round_tiles([gradient(None)] * owners)
-    slot_piece, slot_short, own_first = pl.pallas_call(
+    slot_piece, own_first = pl.pallas_call(
         functools.partial(combine_kernel, layout),
         out_shape=[
             f32(rows, wide, sources),
-            f32(shared_rows, wide, sources),
             f32(rows, blocks, sources),
         ],
         in_specs=[vmem()] * (1 + owners),
-        out_specs=[vmem()] * 3,
+        out_specs=[vmem()] * 2,
         compiler_params=params(),
         name="combine",
     )(match, *got)
@@ -494,17 +485,17 @@
         out_specs=[vmem()] * owners,
         compiler_params=params(),
         name="dense",
-    )(place, gradient(spread(slot_piece, slot_short)))
+    )(place, gradient(spread(slot_piece, shared_rows)))
     own = functools.reduce(lambda a, b: a + b, round_tiles(dense), own_first)
     whole = pl.pallas_call(
         functools.partial(final_kernel, layout, spacing),
         out_shape=f32(param_rows, blocks, sources),
-        in_specs=[vmem()] * (1 + 2 * epochs),
+        in_specs=[vmem()] * (2 + epochs),
         out_specs=vmem(),
         scratch_shapes=[pltpu.VMEM((BANDS, epochs, rows, blocks, sources), F32)],
         compiler_params=params(),
         name="final",
-    )(by_row, *spread(own, own))
+    )(by_row, *spread(own, rows))
     return jnp.transpose(whole, (1, 0, 2))
 
 

time: 86.7 us -> 86.9 us (level)
  Pallas kernels: 28.7 us -> 22.6 us
  waiting for transfers between devices: 30 us -> 36 us
  starting transfers between devices: 25.1 us -> 26.1 us
    pallas_call x2, Pallas kernels: 26.5 us -> 20.4 us  [step_gradient(): pl.pallas_call(functools.partial(step_kernel, layout, later), out_shape=[...]
    ppermute x15 -> x10, waiting for transfers between devices: 15.9 us -> 20.5 us  [the longest x5 15.2 us: to_epoch(): lax.ppermute(x, 'epoch', [(i, (i + k) % epochs) for i in range(epochs)])]
    ppermute x9, starting transfers between devices: 14.1 us -> 17.4 us  [round_tiles(): lax.ppermute(arrays[k], 'tile', [(i, (i + k) % owners) for i in range(own...]
    ppermute x15 -> x10, starting transfers between devices: 11 us -> 8.67 us  [the longest x5 7.73 us: to_epoch(): lax.ppermute(x, 'epoch', [(i, (i + k) % epochs) for i in range(epochs)])]
    ppermute x9, waiting for transfers between devices: 14.1 us -> 15.5 us  [round_tiles(): lax.ppermute(arrays[k], 'tile', [(i, (i + k) % owners) for i in range(own...]
  transfers between devices with their start and end apart: 24 -> 19, of which waited for: 15 -> 18; matrix products, arithmetic and copies ran while one was open for 0% -> 0% of each run, Pallas kernels for 0% -> 0%
where the time goes in v13:
time: 86.9 us; the launch traced here: 87.2 us
  waiting for transfers between devices  36 us (41%)
  starting transfers between devices  26.1 us (30%)
  Pallas kernels  22.6 us (26%)
  local copies, waits for them, and re-layouts  1.7 us (2%)
    pallas_call x2, Pallas kernels, step_gradient(): pl.pallas_call(functools.partial(step_kernel, layout, later), out_shape=[...  20.4 us
    ppermute x9, starting transfers between devices, round_tiles(): lax.ppermute(arrays[k], 'tile', [(i, (i + k) % owners) for i in range(own...  17.4 us
    ppermute x9, waiting for transfers between devices, round_tiles(): lax.ppermute(arrays[k], 'tile', [(i, (i + k) % owners) for i in range(own...  15.5 us
    ppermute x5, waiting for transfers between devices, to_epoch(): lax.ppermute(x, 'epoch', [(i, (i + k) % epochs) for i in range(epochs)])  15.2 us
    ppermute x5, starting transfers between devices, to_epoch(): lax.ppermute(x, 'epoch', [(i, (i + k) % epochs) for i in range(epochs)])  7.73 us
    ppermute x5, waiting for transfers between devices, to_other_band(): return lax.ppermute(x, 'band', [(b, 1 - b) for b in range(BANDS)])  5.34 us
  transfers between devices with their start and end apart: 19, of which 18 were waited for; matrix products, arithmetic and copies ran while one was open for 0% of the time, Pallas kernels for 0%

profile of v13, /device:TPU:0, one launch (start us, length us, event | category | flops | bytes accessed | tf_op | source)
XLA Modules:
  0.0 87.2 jit_solution(5835575615756549460)
XLA Ops:
  2.2 5.1 %collective-permute-start.2 = (f32[12,8,128]{2,1,0:T(8,128)S(1)}, f32[12,8,128]{2,1,0:T(8,128)S(1)}, u32[]{:S(2)}, u32[]{:S(2)}) collective-permute-start(f32[12,8,128]{2,1,0:T(8,128)S(1)} %pack.1.refs_0_), channel_id=1, source_target_pairs={{0,12},{4,0},{8,4},{12,8},{1,13},{5,1},{9,5},{13,9},{2,14},{6,2},{... | collective-permute-start | bytes 147464 | tf_op jit(solution)/shard_map/ppermute | solution.py:421
  8.3 1.0 %collective-permute-done.2.refs_3_ = f32[12,8,128]{2,1,0:T(8,128)S(1)} collective-permute-done((f32[12,8,128]{2,1,0:T(8,128)S(1)}, f32[12,8,128]{2,1,0:T(8,128)S(1)}, u32[]{:S(2)}, u32[]{:S(2)}) %collective-permute-start.2) | collective-permute-done | bytes 49184 | tf_op jit(solution)/shard_map/ppermute | solution.py:421
  9.4 2.9 %collective-permute-done.1.refs_2_ = f32[12,8,128]{2,1,0:T(8,128)S(1)} collective-permute-done((f32[12,8,128]{2,1,0:T(8,128)S(1)}, f32[12,8,128]{2,1,0:T(8,128)S(1)}, u32[]{:S(2)}, u32[]{:S(2)}) %collective-permute-start.1) | collective-permute-done | bytes 49184 | tf_op jit(solution)/shard_map/ppermute | solution.py:421
  13.5 1.5 %collective-permute-start.3 = (f32[11,16,128]{2,1,0:T(8,128)S(1)}, f32[11,16,128]{2,1,0:T(8,128)S(1)}, u32[]{:S(2)}, u32[]{:S(2)}) collective-permute-start(f32[11,16,128]{2,1,0:T(8,128)S(1)} %get-tuple-element.21.refs_0_), channel_id=1, source_target_pairs={{0,2},{2,0},{1,3},{3,1},{4,6},{6,4},{5,7},{7,5},{8,10},{10,8},{9,1... | collective-permute-start | bytes 270344 | tf_op jit(solution)/shard_map/ppermute | solution.py:414
  15.0 3.0 %collective-permute-done.3.refs_1_ = f32[11,16,128]{2,1,0:T(8,128)S(1)} collective-permute-done((f32[11,16,128]{2,1,0:T(8,128)S(1)}, f32[11,16,128]{2,1,0:T(8,128)S(1)}, u32[]{:S(2)}, u32[]{:S(2)}) %collective-permute-start.3) | collective-permute-done | bytes 90144 | tf_op jit(solution)/shard_map/ppermute | solution.py:414
  19.6 10.1 %first_step.1 = (f32[11,16,128]{2,1,0:T(8,128)S(1)}, f32[11,16,128]{2,1,0:T(8,128)S(1)}, f32[2,7,16,128]{3,2,1,0:T(8,128)S(1)}) custom-call(s32[2]{0:T(128)S(1)} %copy-done.5, s32[2,2,8]{2,1,0:T(2,128)S(1)} %bitcast.25, f32[1,1]{1,0:T(1,128)S(6)} %copy.8.psf_ref, f32[2,1,1,128,128]{4,3,2,1,0:T(8,128)S(1)} %copy-done.2, f32[2,1,1,128,128]{4,3,2,1,0:T(8,128)S(1)} %copy-done.3, ...), custom_call_target="tpu_custom_call" | custom-call | tf_op jit(solution)/shard_map/first_step/pallas_call | solution.py:337
  31.2 1.6 %collective-permute-start.6 = (f32[11,16,128]{2,1,0:T(8,128)S(1)}, f32[11,16,128]{2,1,0:T(8,128)S(1)}, u32[]{:S(2)}, u32[]{:S(2)}) collective-permute-start(f32[11,16,128]{2,1,0:T(8,128)S(1)} %pad_add_fusion.1), channel_id=1, source_target_pairs={{0,2},{2,0},{1,3},{3,1},{4,6},{6,4},{5,7},{7,5},{8,10},{10,8},{9,1... | collective-permute-start | bytes 270344 | tf_op jit(solution)/shard_map/ppermute | solution.py:414
  32.8 3.4 %collective-permute-done.6 = f32[11,16,128]{2,1,0:T(8,128)S(1)} collective-permute-done((f32[11,16,128]{2,1,0:T(8,128)S(1)}, f32[11,16,128]{2,1,0:T(8,128)S(1)}, u32[]{:S(2)}, u32[]{:S(2)}) %collective-permute-start.6) | collective-permute-done | bytes 90144 | tf_op jit(solution)/shard_map/ppermute | solution.py:414
  36.2 4.3 %collective-permute-start.9 = (f32[11,16,128]{2,1,0:T(8,128)S(1)}, f32[11,16,128]{2,1,0:T(8,128)S(1)}, u32[]{:S(2)}, u32[]{:S(2)}) collective-permute-start(f32[11,16,128]{2,1,0:T(8,128)S(1)} %add_add_fusion.1.refs_0_), channel_id=1, source_target_pairs={{0,12},{4,0},{8,4},{12,8},{1,13},{5,1},{9,5},{13,9},{2,14},{6,2},{... | collective-permute-start | bytes 270344 | tf_op jit(solution)/shard_map/ppermute | solution.py:421
  41.1 2.4 %collective-permute-done.9.refs_3_ = f32[11,16,128]{2,1,0:T(8,128)S(1)} collective-permute-done((f32[11,16,128]{2,1,0:T(8,128)S(1)}, f32[11,16,128]{2,1,0:T(8,128)S(1)}, u32[]{:S(2)}, u32[]{:S(2)}) %collective-permute-start.9) | collective-permute-done | bytes 90144 | tf_op jit(solution)/shard_map/ppermute | solution.py:421
  43.6 5.1 %collective-permute-done.8.refs_2_ = f32[11,16,128]{2,1,0:T(8,128)S(1)} collective-permute-done((f32[11,16,128]{2,1,0:T(8,128)S(1)}, f32[11,16,128]{2,1,0:T(8,128)S(1)}, u32[]{:S(2)}, u32[]{:S(2)}) %collective-permute-start.8) | collective-permute-done | bytes 90144 | tf_op jit(solution)/shard_map/ppermute | solution.py:421
  49.0 1.5 %collective-permute-start.10 = (f32[11,16,128]{2,1,0:T(8,128)S(1)}, f32[11,16,128]{2,1,0:T(8,128)S(1)}, u32[]{:S(2)}, u32[]{:S(2)}) collective-permute-start(f32[11,16,128]{2,1,0:T(8,128)S(1)} %get-tuple-element.27.refs_3_), channel_id=1, source_target_pairs={{0,2},{2,0},{1,3},{3,1},{4,6},{6,4},{5,7},{7,5},{8,10},{10,8},{9,1... | collective-permute-start | bytes 270344 | tf_op jit(solution)/shard_map/ppermute | solution.py:414
  50.5 3.0 %collective-permute-done.10.refs_4_ = f32[11,16,128]{2,1,0:T(8,128)S(1)} collective-permute-done((f32[11,16,128]{2,1,0:T(8,128)S(1)}, f32[11,16,128]{2,1,0:T(8,128)S(1)}, u32[]{:S(2)}, u32[]{:S(2)}) %collective-permute-start.10) | collective-permute-done | bytes 90144 | tf_op jit(solution)/shard_map/ppermute | solution.py:414
  53.6 1.3 %collective-permute-done.11.refs_5_ = f32[2,7,16,128]{3,2,1,0:T(8,128)S(1)} collective-permute-done((f32[2,7,16,128]{3,2,1,0:T(8,128)S(1)}, f32[2,7,16,128]{3,2,1,0:T(8,128)S(1)}, u32[]{:S(2)}, u32[]{:S(2)}) %collective-permute-start.11) | collective-permute-done | bytes 114720 | tf_op jit(solution)/shard_map/ppermute | solution.py:417
  54.9 10.2 %later_step.1 = (f32[11,16,128]{2,1,0:T(8,128)S(1)}, f32[11,16,128]{2,1,0:T(8,128)S(1)}, f32[2,7,16,128]{3,2,1,0:T(8,128)S(1)}) custom-call(s32[2]{0:T(128)S(1)} %copy-done.5, s32[2,2,8]{2,1,0:T(2,128)S(1)} %bitcast.26, f32[1,1]{1,0:T(1,128)S(6)} %copy.8.psf_ref, f32[2,1,1,128,128]{4,3,2,1,0:T(8,128)S(1)} %copy-done.2, f32[2,1,1,128,128]{4,3,2,1,0:T(8,128)S(1)} %copy-done.3, ...), custom_call_target="tpu_custom_call" | custom-call | tf_op jit(solution)/shard_map/later_step/pallas_call | solution.py:337
  65.4 1.2 %collective-permute-done.12 = f32[2,7,16,128]{3,2,1,0:T(8,128)S(1)} collective-permute-done((f32[2,7,16,128]{3,2,1,0:T(8,128)S(1)}, f32[2,7,16,128]{3,2,1,0:T(8,128)S(1)}, u32[]{:S(2)}, u32[]{:S(2)}) %collective-permute-start.12) | collective-permute-done | bytes 114720 | tf_op jit(solution)/shard_map/ppermute | solution.py:417
  66.6 1.6 %collective-permute-start.13 = (f32[11,16,128]{2,1,0:T(8,128)S(1)}, f32[11,16,128]{2,1,0:T(8,128)S(1)}, u32[]{:S(2)}, u32[]{:S(2)}) collective-permute-start(f32[11,16,128]{2,1,0:T(8,128)S(1)} %pad_add_fusion), channel_id=1, source_target_pairs={{0,2},{2,0},{1,3},{3,1},{4,6},{6,4},{5,7},{7,5},{8,10},{10,8},{9,1... | collective-permute-start | bytes 270344 | tf_op jit(solution)/shard_map/ppermute | solution.py:414
  68.2 3.2 %collective-permute-done.13 = f32[11,16,128]{2,1,0:T(8,128)S(1)} collective-permute-done((f32[11,16,128]{2,1,0:T(8,128)S(1)}, f32[11,16,128]{2,1,0:T(8,128)S(1)}, u32[]{:S(2)}, u32[]{:S(2)}) %collective-permute-start.13) | collective-permute-done | bytes 90144 | tf_op jit(solution)/shard_map/ppermute | solution.py:414
  71.6 3.0 %collective-permute-start.14 = (f32[11,8,128]{2,1,0:T(8,128)S(1)}, f32[11,8,128]{2,1,0:T(8,128)S(1)}, u32[]{:S(2)}, u32[]{:S(2)}) collective-permute-start(f32[11,8,128]{2,1,0:T(8,128)S(1)} %get-tuple-element.32), channel_id=1, source_target_pairs={{0,4},{4,8},{8,12},{12,0},{1,5},{5,9},{9,13},{13,1},{2,6},{6,10},{... | collective-permute-start | bytes 135176 | tf_op jit(solution)/shard_map/ppermute | solution.py:421
  74.6 2.4 %collective-permute-start.15 = (f32[11,8,128]{2,1,0:T(8,128)S(1)}, f32[11,8,128]{2,1,0:T(8,128)S(1)}, u32[]{:S(2)}, u32[]{:S(2)}) collective-permute-start(f32[11,8,128]{2,1,0:T(8,128)S(1)} %get-tuple-element.33), channel_id=1, source_target_pairs={{0,8},{4,12},{8,0},{12,4},{1,9},{5,13},{9,1},{13,5},{2,10},{6,14},... | collective-permute-start | bytes 135176 | tf_op jit(solution)/shard_map/ppermute | solution.py:421
  79.5 1.5 %collective-permute-done.16 = f32[11,8,128]{2,1,0:T(8,128)S(1)} collective-permute-done((f32[11,8,128]{2,1,0:T(8,128)S(1)}, f32[11,8,128]{2,1,0:T(8,128)S(1)}, u32[]{:S(2)}, u32[]{:S(2)}) %collective-permute-start.16) | collective-permute-done | bytes 45088 | tf_op jit(solution)/shard_map/ppermute | solution.py:421
  81.0 1.6 %collective-permute-start.17 = (f32[11,8,128]{2,1,0:T(8,128)S(1)}, f32[11,8,128]{2,1,0:T(8,128)S(1)}, u32[]{:S(2)}, u32[]{:S(2)}) collective-permute-start(f32[11,8,128]{2,1,0:T(8,128)S(1)} %add_add_fusion.2.refs_0_), channel_id=1, source_target_pairs={{0,2},{2,0},{1,3},{3,1},{4,6},{6,4},{5,7},{7,5},{8,10},{10,8},{9,1... | collective-permute-start | bytes 135176 | tf_op jit(solution)/shard_map/ppermute | solution.py:414
  82.6 2.5 %collective-permute-done.17.refs_1_ = f32[11,8,128]{2,1,0:T(8,128)S(1)} collective-permute-done((f32[11,8,128]{2,1,0:T(8,128)S(1)}, f32[11,8,128]{2,1,0:T(8,128)S(1)}, u32[]{:S(2)}, u32[]{:S(2)}) %collective-permute-start.17) | collective-permute-done | bytes 45088 | tf_op jit(solution)/shard_map/ppermute | solution.py:414
  85.2 1.3 %collective-permute-done.18.refs_2_ = f32[2,11,8,128]{3,2,1,0:T(8,128)S(1)} collective-permute-done((f32[2,11,8,128]{3,2,1,0:T(8,128)S(1)}, f32[2,11,8,128]{3,2,1,0:T(8,128)S(1)}, u32[]{:S(2)}, u32[]{:S(2)}) %collective-permute-start.18) | collective-permute-done | bytes 90144 | tf_op jit(solution)/shard_map/ppermute | solution.py:417
  (49 shorter events, 11.6 us)
Async XLA Ops:
  0.7 0.9 %copy-start = (f32[8,44,128]{2,0,1:T(8,128)S(1)}, f32[8,44,128]{2,0,1:T(8,128)}, u32[]{:S(2)}) copy-start(f32[8,44,128]{2,0,1:T(8,128)} %param.7) | copy-start | bytes 540676
  2.2 7.2 %collective-permute-start.2 = (f32[12,8,128]{2,1,0:T(8,128)S(1)}, f32[12,8,128]{2,1,0:T(8,128)S(1)}, u32[]{:S(2)}, u32[]{:S(2)}) collective-permute-start(f32[12,8,128]{2,1,0:T(8,128)S(1)} %pack.1.refs_0_), channel_id=1, source_target_pairs={{0,12},{4,0},{8,4},{12,8},{1,13},{5,1},{9,5},{13,9},{2,14},{6,2},{... | collective-permute-start | bytes 147464 | tf_op jit(solution)/shard_map/ppermute | solution.py:421
  7.3 5.0 %collective-permute-start.1 = (f32[12,8,128]{2,1,0:T(8,128)S(1)}, f32[12,8,128]{2,1,0:T(8,128)S(1)}, u32[]{:S(2)}, u32[]{:S(2)}) collective-permute-start(f32[12,8,128]{2,1,0:T(8,128)S(1)} %pack.1.refs_0_), channel_id=1, source_target_pairs={{0,8},{4,12},{8,0},{12,4},{1,9},{5,13},{9,1},{13,5},{2,10},{6,14},... | collective-permute-start | bytes 147464 | tf_op jit(solution)/shard_map/ppermute | solution.py:421
  7.3 5.9 %collective-permute-start = (f32[12,8,128]{2,1,0:T(8,128)S(1)}, f32[12,8,128]{2,1,0:T(8,128)S(1)}, u32[]{:S(2)}, u32[]{:S(2)}) collective-permute-start(f32[12,8,128]{2,1,0:T(8,128)S(1)} %pack.1.refs_0_), channel_id=1, source_target_pairs={{0,4},{4,8},{8,12},{12,0},{1,5},{5,9},{9,13},{13,1},{2,6},{6,10},{... | collective-permute-start | bytes 147464 | tf_op jit(solution)/shard_map/ppermute | solution.py:421
  13.5 4.6 %collective-permute-start.3 = (f32[11,16,128]{2,1,0:T(8,128)S(1)}, f32[11,16,128]{2,1,0:T(8,128)S(1)}, u32[]{:S(2)}, u32[]{:S(2)}) collective-permute-start(f32[11,16,128]{2,1,0:T(8,128)S(1)} %get-tuple-element.21.refs_0_), channel_id=1, source_target_pairs={{0,2},{2,0},{1,3},{3,1},{4,6},{6,4},{5,7},{7,5},{8,10},{10,8},{9,1... | collective-permute-start | bytes 270344 | tf_op jit(solution)/shard_map/ppermute | solution.py:414
  18.1 1.4 %copy-start.3 = (f32[2,1,1,128,128]{4,3,2,1,0:T(8,128)S(1)}, f32[2,1,1,128,128]{4,3,2,1,0:T(8,128)}, u32[]{:S(2)}) copy-start(f32[2,1,1,128,128]{4,3,2,1,0:T(8,128)} %weight_ref.3) | copy-start | bytes 393220
  18.1 1.4 %copy-start.2 = (f32[2,1,1,128,128]{4,3,2,1,0:T(8,128)S(1)}, f32[2,1,1,128,128]{4,3,2,1,0:T(8,128)}, u32[]{:S(2)}) copy-start(f32[2,1,1,128,128]{4,3,2,1,0:T(8,128)} %data_ref.3) | copy-start | bytes 393220
  18.1 1.4 %copy-start.4 = (s32[2,8,2]{1,2,0:T(2,128)S(1)}, s32[2,8,2]{1,2,0:T(2,128)}, u32[]{:S(2)}) copy-start(s32[2,8,2]{1,2,0:T(2,128)} %param.13) | copy-start | bytes 388
  18.1 1.4 %collective-permute-start.4 = (f32[2,7,16,128]{3,2,1,0:T(8,128)S(1)}, f32[2,7,16,128]{3,2,1,0:T(8,128)S(1)}, u32[]{:S(2)}, u32[]{:S(2)}) collective-permute-start(f32[2,7,16,128]{3,2,1,0:T(8,128)S(1)} %pad_maximum_fusion), channel_id=1, source_target_pairs={{0,1},{1,0},{2,3},{3,2},{4,5},{5,4},{6,7},{7,6},{8,9},{9,8},{10,11... | collective-permute-start | bytes 344072 | tf_op jit(solution)/shard_map/ppermute | solution.py:417
  29.7 1.5 %collective-permute-start.5 = (f32[2,7,16,128]{3,2,1,0:T(8,128)S(1)}, f32[2,7,16,128]{3,2,1,0:T(8,128)S(1)}, u32[]{:S(2)}, u32[]{:S(2)}) collective-permute-start(f32[2,7,16,128]{3,2,1,0:T(8,128)S(1)} %get-tuple-element.23), channel_id=1, source_target_pairs={{0,1},{1,0},{2,3},{3,2},{4,5},{5,4},{6,7},{7,6},{8,9},{9,8},{10,11... | collective-permute-start | bytes 344072 | tf_op jit(solution)/shard_map/ppermute | solution.py:417
  31.2 4.9 %collective-permute-start.6 = (f32[11,16,128]{2,1,0:T(8,128)S(1)}, f32[11,16,128]{2,1,0:T(8,128)S(1)}, u32[]{:S(2)}, u32[]{:S(2)}) collective-permute-start(f32[11,16,128]{2,1,0:T(8,128)S(1)} %pad_add_fusion.1), channel_id=1, source_target_pairs={{0,2},{2,0},{1,3},{3,1},{4,6},{6,4},{5,7},{7,5},{8,10},{10,8},{9,1... | collective-permute-start | bytes 270344 | tf_op jit(solution)/shard_map/ppermute | solution.py:414
  36.2 7.4 %collective-permute-start.9 = (f32[11,16,128]{2,1,0:T(8,128)S(1)}, f32[11,16,128]{2,1,0:T(8,128)S(1)}, u32[]{:S(2)}, u32[]{:S(2)}) collective-permute-start(f32[11,16,128]{2,1,0:T(8,128)S(1)} %add_add_fusion.1.refs_0_), channel_id=1, source_target_pairs={{0,12},{4,0},{8,4},{12,8},{1,13},{5,1},{9,5},{13,9},{2,14},{6,2},{... | collective-permute-start | bytes 270344 | tf_op jit(solution)/shard_map/ppermute | solution.py:421
  40.5 8.1 %collective-permute-start.8 = (f32[11,16,128]{2,1,0:T(8,128)S(1)}, f32[11,16,128]{2,1,0:T(8,128)S(1)}, u32[]{:S(2)}, u32[]{:S(2)}) collective-permute-start(f32[11,16,128]{2,1,0:T(8,128)S(1)} %add_add_fusion.1.refs_0_), channel_id=1, source_target_pairs={{0,8},{4,12},{8,0},{12,4},{1,9},{5,13},{9,1},{13,5},{2,10},{6,14},... | collective-permute-start | bytes 270344 | tf_op jit(solution)/shard_map/ppermute | solution.py:421
  40.5 8.1 %collective-permute-start.7 = (f32[11,16,128]{2,1,0:T(8,128)S(1)}, f32[11,16,128]{2,1,0:T(8,128)S(1)}, u32[]{:S(2)}, u32[]{:S(2)}) collective-permute-start(f32[11,16,128]{2,1,0:T(8,128)S(1)} %add_add_fusion.1.refs_0_), channel_id=1, source_target_pairs={{0,4},{4,8},{8,12},{12,0},{1,5},{5,9},{9,13},{13,1},{2,6},{6,10},{... | collective-permute-start | bytes 270344 | tf_op jit(solution)/shard_map/ppermute | solution.py:421
  49.0 4.5 %collective-permute-start.10 = (f32[11,16,128]{2,1,0:T(8,128)S(1)}, f32[11,16,128]{2,1,0:T(8,128)S(1)}, u32[]{:S(2)}, u32[]{:S(2)}) collective-permute-start(f32[11,16,128]{2,1,0:T(8,128)S(1)} %get-tuple-element.27.refs_3_), channel_id=1, source_target_pairs={{0,2},{2,0},{1,3},{3,1},{4,6},{6,4},{5,7},{7,5},{8,10},{10,8},{9,1... | collective-permute-start | bytes 270344 | tf_op jit(solution)/shard_map/ppermute | solution.py:414
  53.6 1.4 %collective-permute-start.11 = (f32[2,7,16,128]{3,2,1,0:T(8,128)S(1)}, f32[2,7,16,128]{3,2,1,0:T(8,128)S(1)}, u32[]{:S(2)}, u32[]{:S(2)}) collective-permute-start(f32[2,7,16,128]{3,2,1,0:T(8,128)S(1)} %pad_maximum_fusion.1), channel_id=1, source_target_pairs={{0,1},{1,0},{2,3},{3,2},{4,5},{5,4},{6,7},{7,6},{8,9},{9,8},{10,11... | collective-permute-start | bytes 344072 | tf_op jit(solution)/shard_map/ppermute | solution.py:417
  65.2 1.4 %collective-permute-start.12 = (f32[2,7,16,128]{3,2,1,0:T(8,128)S(1)}, f32[2,7,16,128]{3,2,1,0:T(8,128)S(1)}, u32[]{:S(2)}, u32[]{:S(2)}) collective-permute-start(f32[2,7,16,128]{3,2,1,0:T(8,128)S(1)} %get-tuple-element.29), channel_id=1, source_target_pairs={{0,1},{1,0},{2,3},{3,2},{4,5},{5,4},{6,7},{7,6},{8,9},{9,8},{10,11... | collective-permute-start | bytes 344072 | tf_op jit(solution)/shard_map/ppermute | solution.py:417
  66.6 4.7 %collective-permute-start.13 = (f32[11,16,128]{2,1,0:T(8,128)S(1)}, f32[11,16,128]{2,1,0:T(8,128)S(1)}, u32[]{:S(2)}, u32[]{:S(2)}) collective-permute-start(f32[11,16,128]{2,1,0:T(8,128)S(1)} %pad_add_fusion), channel_id=1, source_target_pairs={{0,2},{2,0},{1,3},{3,1},{4,6},{6,4},{5,7},{7,5},{8,10},{10,8},{9,1... | collective-permute-start | bytes 270344 | tf_op jit(solution)/shard_map/ppermute | solution.py:414
  71.6 7.1 %collective-permute-start.14 = (f32[11,8,128]{2,1,0:T(8,128)S(1)}, f32[11,8,128]{2,1,0:T(8,128)S(1)}, u32[]{:S(2)}, u32[]{:S(2)}) collective-permute-start(f32[11,8,128]{2,1,0:T(8,128)S(1)} %get-tuple-element.32), channel_id=1, source_target_pairs={{0,4},{4,8},{8,12},{12,0},{1,5},{5,9},{9,13},{13,1},{2,6},{6,10},{... | collective-permute-start | bytes 135176 | tf_op jit(solution)/shard_map/ppermute | solution.py:421
  74.6 5.0 %collective-permute-start.15 = (f32[11,8,128]{2,1,0:T(8,128)S(1)}, f32[11,8,128]{2,1,0:T(8,128)S(1)}, u32[]{:S(2)}, u32[]{:S(2)}) collective-permute-start(f32[11,8,128]{2,1,0:T(8,128)S(1)} %get-tuple-element.33), channel_id=1, source_target_pairs={{0,8},{4,12},{8,0},{12,4},{1,9},{5,13},{9,1},{13,5},{2,10},{6,14},... | collective-permute-start | bytes 135176 | tf_op jit(solution)/shard_map/ppermute | solution.py:421
  77.0 4.0 %collective-permute-start.16 = (f32[11,8,128]{2,1,0:T(8,128)S(1)}, f32[11,8,128]{2,1,0:T(8,128)S(1)}, u32[]{:S(2)}, u32[]{:S(2)}) collective-permute-start(f32[11,8,128]{2,1,0:T(8,128)S(1)} %get-tuple-element.34), channel_id=1, source_target_pairs={{0,12},{4,0},{8,4},{12,8},{1,13},{5,1},{9,5},{13,9},{2,14},{6,2},{... | collective-permute-start | bytes 135176 | tf_op jit(solution)/shard_map/ppermute | solution.py:421
  81.0 5.5 %copy-start.1 = (f32[8,44,128]{2,0,1:T(8,128)S(1)}, f32[8,44,128]{2,0,1:T(8,128)}, u32[]{:S(2)}) copy-start(f32[8,44,128]{2,0,1:T(8,128)} %param.7) | copy-start | bytes 540676
  81.0 4.1 %collective-permute-start.17 = (f32[11,8,128]{2,1,0:T(8,128)S(1)}, f32[11,8,128]{2,1,0:T(8,128)S(1)}, u32[]{:S(2)}, u32[]{:S(2)}) collective-permute-start(f32[11,8,128]{2,1,0:T(8,128)S(1)} %add_add_fusion.2.refs_0_), channel_id=1, source_target_pairs={{0,2},{2,0},{1,3},{3,1},{4,6},{6,4},{5,7},{7,5},{8,10},{10,8},{9,1... | collective-permute-start | bytes 135176 | tf_op jit(solution)/shard_map/ppermute | solution.py:414
  85.2 1.4 %collective-permute-start.18 = (f32[2,11,8,128]{3,2,1,0:T(8,128)S(1)}, f32[2,11,8,128]{3,2,1,0:T(8,128)S(1)}, u32[]{:S(2)}, u32[]{:S(2)}) collective-permute-start(f32[2,11,8,128]{3,2,1,0:T(8,128)S(1)} %pad_maximum_fusion.2), channel_id=1, source_target_pairs={{0,1},{1,0},{2,3},{3,2},{4,5},{5,4},{6,7},{7,6},{8,9},{9,8},{10,11... | collective-permute-start | bytes 270344 | tf_op jit(solution)/shard_map/ppermute | solution.py:417
  (2 other events, 1.4 us)

commit v14 on v11

--- a/solution.py
+++ b/solution.py
@@ -73,23 +73,22 @@
     return pltpu.CompilerParams(vmem_limit_bytes=mib * MIB)
 
 
-def pack_kernel(layout, spacing, lists_ref, params_ref, out_ref):
-    shared_rows, rows, pieces = layout
-    band, epoch = lax.axis_index("band"), lax.axis_index("epoch")
+def half_rows():
+    return [("s", i) for i in range(HALF)] + [("a", j) for j in range(COMPS)]
+
+
+def pack_kernel(spacing, lists_ref, params_ref, out_ref):
+    band = lax.axis_index("band")
     for b in range(BANDS):
-        for q in range(len(pieces)):
-
-            @pl.when((band == b) & (epoch == q))
-            def _():
-                for p, entry in enumerate(pieces[q]):
-                    if entry is None:
-                        out_ref[p] = jnp.zeros(out_ref.shape[1:], F32)
-                        continue
-                    row, position = row_of(b, entry)
-                    value = params_ref[row]
-                    if position is not None:
-                        value = spacing * params_ref[position] + value
-                    out_ref[p] = value
+
+        @pl.when(band == b)
+        def _():
+            for p, entry in enumerate(half_rows()):
+                row, position = row_of(b, entry)
+                value = params_ref[row]
+                if position is not None:
+                    value = spacing * params_ref[position] + value
+                out_ref[p] = value
 
     tiles, slots = lists_ref.shape
     lane = lax.broadcasted_iota(jnp.int32, (8, 128), 1)
@@ -97,11 +96,11 @@
     for t in range(tiles):
         for s in range(slots):
             ids = jnp.where(lane == t * slots + s, lists_ref[t, s], ids)
-    out_ref[rows] = ids.astype(F32)
-
-
-def select_kernel(layout, wide, *refs):
-    shared_rows, rows, pieces = layout
+    out_ref[HALF + COMPS] = ids.astype(F32)
+
+
+def select_kernel(wide, *refs):
+    rows = HALF + COMPS
     got, (out_ref, short_ref, match_ref, place_ref) = refs[:-4], refs[-4:]
     owners = len(got)
     blocks = got[0].shape[1]
@@ -116,7 +115,7 @@
     for p in range(rows):
         chosen = pick(choose, jnp.concatenate([ref[p] for ref in got], axis=0))
         out_ref[p] = chosen
-        if p < shared_rows:
+        if p < HALF:
             short_ref[p] = chosen
 
     lists = jnp.concatenate([ref[rows, :1, :wide] for ref in got], axis=1)
@@ -150,7 +149,8 @@
 def step_kernel(layout, later, counts_ref, offsets_ref, psf_ref, data_ref, weight_ref, *refs):
     shared_rows, rows, pieces = layout
     epochs = len(pieces)
-    taken = 2 * epochs * (2 if later else 1)
+    (mine, others), refs = refs[:2], refs[2:]
+    taken = 2 * epochs if later else 0
     ins, refs = refs[:taken], refs[taken:]
     outs, refs = refs[: 2 * epochs], refs[2 * epochs :]
     shared, amps, derived, prof_x, prof_y, pieces_x, pieces_y, image, sums, half, other = refs[:11]
@@ -161,7 +161,9 @@
     slots = wide // tiles
     spacing = pixels / 8.0
 
-    put_together(layout, band, epoch, ins[: 2 * epochs], half, other, shared, amps)
+    shared[band] = mine[:HALF]
+    shared[1 - band] = others[...]
+    amps[...] = mine[HALF:]
 
     def row(k, c):
         r = k * COMPS + c
@@ -169,7 +171,7 @@
 
     if later:
         moved, moved_amps = refs[11:]
-        put_together(layout, band, epoch, ins[2 * epochs :], half, other, moved, moved_amps)
+        put_together(layout, band, epoch, ins, half, other, moved, moved_amps)
         for k in range(4):
             shift = 0.0
             if k < 2:
@@ -444,19 +446,19 @@
     by_row = jnp.transpose(source_params, (1, 0, 2))
     offsets = jnp.transpose(block_offsets, (0, 2, 1))
     packed = pl.pallas_call(
-        functools.partial(pack_kernel, layout, spacing),
-        out_shape=f32(rows + 1, blocks, sources),
+        functools.partial(pack_kernel, spacing),
+        out_shape=f32(HALF + COMPS + 1, blocks, sources),
         in_specs=[smem(), vmem()],
         out_specs=vmem(),
         compiler_params=params(),
         name="pack",
     )(block_lists, by_row)
     got = round_tiles([packed] * owners)
-    slot_piece, slot_short, match, place = pl.pallas_call(
-        functools.partial(select_kernel, layout, wide),
+    slot_half, slot_short, match, place = pl.pallas_call(
+        functools.partial(select_kernel, wide),
         out_shape=[
-            f32(rows, wide, sources),
-            f32(shared_rows, wide, sources),
+            f32(HALF + COMPS, wide, sources),
+            f32(HALF, wide, sources),
             f32(wide + blocks, owners * wide),
             f32(owners * blocks, wide),
         ],
@@ -465,7 +467,7 @@
         compiler_params=params(),
         name="select",
     )(*got)
-    slot_rows = spread(slot_piece, slot_short)
+    slot_rows = [slot_half, lax.ppermute(slot_short, "band", [(b, 1 - b) for b in range(BANDS)])]
 
     def gradient(moved):
         parts = step_gradient(

time: 86.7 us -> 85.8 us (0.990)
  starting transfers between devices: 25.1 us -> 23.2 us
  waiting for transfers between devices: 30 us -> 31.2 us
    ppermute x9, waiting for transfers between devices: 14.1 us -> 16.9 us  [round_tiles(): lax.ppermute(arrays[k], 'tile', [(i, (i + k) % owners) for i in range(own...]
    ppermute x10 -> x8, waiting for transfers between devices: 14.1 us -> 11.5 us  [to_peers(): kept.append(lax.ppermute(other[k], ('epoch', 'band'), pairs))]
    ppermute x10 -> x8, starting transfers between devices: 5.64 us -> 4.35 us  [to_peers(): kept.append(lax.ppermute(other[k], ('epoch', 'band'), pairs))]
    ppermute x5 -> x4, starting transfers between devices: 5.32 us -> 4.42 us  [to_peers(): lax.ppermute(same[k], 'epoch', [(i, (i + k) % epochs) for i in range(epoc...]
    ppermute x5 -> x4, waiting for transfers between devices: 1.86 us -> 2.07 us  [to_peers(): lax.ppermute(same[k], 'epoch', [(i, (i + k) % epochs) for i in range(epoc...]
  transfers between devices with their start and end apart: 24 -> 22, of which waited for: 15 -> 15; matrix products, arithmetic and copies ran while one was open for 0% -> 0% of each run, Pallas kernels for 0% -> 0%
where the time goes in v14:
time: 85.8 us; the launch traced here: 86.1 us
  waiting for transfers between devices  31.2 us (36%)
  Pallas kernels  28.6 us (33%)
  starting transfers between devices  23.2 us (27%)
  local copies, waits for them, and re-layouts  2.27 us (3%)
    pallas_call x2, Pallas kernels, step_gradient(): pl.pallas_call(functools.partial(step_kernel, layout, later), out_shape=[...  26.4 us
    ppermute x9, waiting for transfers between devices, round_tiles(): lax.ppermute(arrays[k], 'tile', [(i, (i + k) % owners) for i in range(own...  16.9 us
    ppermute x9, starting transfers between devices, round_tiles(): lax.ppermute(arrays[k], 'tile', [(i, (i + k) % owners) for i in range(own...  14.4 us
    ppermute x8, waiting for transfers between devices, to_peers(): kept.append(lax.ppermute(other[k], ('epoch', 'band'), pairs))  11.5 us
    ppermute x4, starting transfers between devices, to_peers(): lax.ppermute(same[k], 'epoch', [(i, (i + k) % epochs) for i in range(epoc...  4.42 us
    ppermute x8, starting transfers between devices, to_peers(): kept.append(lax.ppermute(other[k], ('epoch', 'band'), pairs))  4.35 us
    unnamed x14, local copies, waits for them, and re-layouts  2.27 us
    ppermute x4, waiting for transfers between devices, to_peers(): lax.ppermute(same[k], 'epoch', [(i, (i + k) % epochs) for i in range(epoc...  2.07 us
  transfers between devices with their start and end apart: 22, of which 15 were waited for; matrix products, arithmetic and copies ran while one was open for 0% of the time, Pallas kernels for 0%

profile of v14, /device:TPU:0, one launch (start us, length us, event | category | flops | bytes accessed | tf_op | source)
XLA Modules:
  0.0 86.1 jit_solution(17289862026274095777)
XLA Ops:
  0.7 0.9 %copy-done = f32[8,44,128]{2,0,1:T(8,128)S(1)} copy-done((f32[8,44,128]{2,0,1:T(8,128)S(1)}, f32[8,44,128]{2,0,1:T(8,128)}, u32[]{:S(2)}) %copy-start) | copy-done | bytes 180248
  2.2 5.1 %collective-permute-start.2 = (f32[22,8,128]{2,1,0:T(8,128)S(1)}, f32[22,8,128]{2,1,0:T(8,128)S(1)}, u32[]{:S(2)}, u32[]{:S(2)}) collective-permute-start(f32[22,8,128]{2,1,0:T(8,128)S(1)} %pack.1.refs_0_), channel_id=1, source_target_pairs={{0,12},{4,0},{8,4},{12,8},{1,13},{5,1},{9,5},{13,9},{2,14},{6,2},{... | collective-permute-start | bytes 270344 | tf_op jit(solution)/shard_map/ppermute | solution.py:434
  7.3 1.0 %collective-permute-start = (f32[22,8,128]{2,1,0:T(8,128)S(1)}, f32[22,8,128]{2,1,0:T(8,128)S(1)}, u32[]{:S(2)}, u32[]{:S(2)}) collective-permute-start(f32[22,8,128]{2,1,0:T(8,128)S(1)} %pack.1.refs_0_), channel_id=1, source_target_pairs={{0,4},{4,8},{8,12},{12,0},{1,5},{5,9},{9,13},{13,1},{2,6},{6,10},{... | collective-permute-start | bytes 270344 | tf_op jit(solution)/shard_map/ppermute | solution.py:434
  8.3 2.0 %collective-permute-done.2.refs_3_ = f32[22,8,128]{2,1,0:T(8,128)S(1)} collective-permute-done((f32[22,8,128]{2,1,0:T(8,128)S(1)}, f32[22,8,128]{2,1,0:T(8,128)S(1)}, u32[]{:S(2)}, u32[]{:S(2)}) %collective-permute-start.2) | collective-permute-done | bytes 90144 | tf_op jit(solution)/shard_map/ppermute | solution.py:434
  10.3 5.1 %collective-permute-done.1.refs_2_ = f32[22,8,128]{2,1,0:T(8,128)S(1)} collective-permute-done((f32[22,8,128]{2,1,0:T(8,128)S(1)}, f32[22,8,128]{2,1,0:T(8,128)S(1)}, u32[]{:S(2)}, u32[]{:S(2)}) %collective-permute-start.1) | collective-permute-done | bytes 90144 | tf_op jit(solution)/shard_map/ppermute | solution.py:434
  17.9 13.1 %first_step.1 = (f32[11,16,128]{2,1,0:T(8,128)S(1)}, f32[11,16,128]{2,1,0:T(8,128)S(1)}, f32[7,16,128]{2,1,0:T(8,128)S(1)}, f32[7,16,128]{2,1,0:T(8,128)S(1)}) custom-call(s32[2]{0:T(128)S(1)} %copy-done.5, s32[2,2,8]{2,1,0:T(2,128)S(1)} %bitcast.5, f32[1,1]{1,0:T(1,128)S(6)} %copy.8.psf_ref, f32[2,1,1,128,128]{4,3,2,1,0:T(8,128)S(1)} %copy-done.2, ...), custom_call_target="tpu_custom_call" | custom-call | tf_op jit(solution)/shard_map/first_step/pallas_call | solution.py:341
  31.0 1.5 %collective-permute-start.4 = (f32[11,16,128]{2,1,0:T(8,128)S(1)}, f32[11,16,128]{2,1,0:T(8,128)S(1)}, u32[]{:S(2)}, u32[]{:S(2)}) collective-permute-start(f32[11,16,128]{2,1,0:T(8,128)S(1)} %get-tuple-element.28), channel_id=1, source_target_pairs={{0,2},{2,0},{1,3},{3,1},{4,6},{6,4},{5,7},{7,5},{8,10},{10,8},{9,1... | collective-permute-start | bytes 270344 | tf_op jit(solution)/shard_map/ppermute | solution.py:422
  33.8 2.7 %collective-permute-done.6 = f32[7,16,128]{2,1,0:T(8,128)S(1)} collective-permute-done((f32[7,16,128]{2,1,0:T(8,128)S(1)}, f32[7,16,128]{2,1,0:T(8,128)S(1)}, u32[]{:S(2)}, u32[]{:S(2)}) %collective-permute-start.6) | collective-permute-done | bytes 57376 | tf_op jit(solution)/shard_map/ppermute | solution.py:429
  37.1 1.7 %collective-permute-start.8 = (f32[11,16,128]{2,1,0:T(8,128)S(1)}, f32[11,16,128]{2,1,0:T(8,128)S(1)}, u32[]{:S(2)}, u32[]{:S(2)}) collective-permute-start(f32[11,16,128]{2,1,0:T(8,128)S(1)} %pad_add_fusion.1.refs_0_), channel_id=1, source_target_pairs={{0,8},{4,12},{8,0},{12,4},{1,9},{5,13},{9,1},{13,5},{2,10},{6,14},... | collective-permute-start | bytes 270344 | tf_op jit(solution)/shard_map/ppermute | solution.py:434
  38.9 1.9 %collective-permute-start.7 = (f32[11,16,128]{2,1,0:T(8,128)S(1)}, f32[11,16,128]{2,1,0:T(8,128)S(1)}, u32[]{:S(2)}, u32[]{:S(2)}) collective-permute-start(f32[11,16,128]{2,1,0:T(8,128)S(1)} %pad_add_fusion.1.refs_0_), channel_id=1, source_target_pairs={{0,4},{4,8},{8,12},{12,0},{1,5},{5,9},{9,13},{13,1},{2,6},{6,10},{... | collective-permute-start | bytes 270344 | tf_op jit(solution)/shard_map/ppermute | solution.py:434
  41.4 6.2 %collective-permute-done.8.refs_2_ = f32[11,16,128]{2,1,0:T(8,128)S(1)} collective-permute-done((f32[11,16,128]{2,1,0:T(8,128)S(1)}, f32[11,16,128]{2,1,0:T(8,128)S(1)}, u32[]{:S(2)}, u32[]{:S(2)}) %collective-permute-start.8) | collective-permute-done | bytes 90144 | tf_op jit(solution)/shard_map/ppermute | solution.py:434
  48.0 1.5 %collective-permute-start.10 = (f32[11,16,128]{2,1,0:T(8,128)S(1)}, f32[11,16,128]{2,1,0:T(8,128)S(1)}, u32[]{:S(2)}, u32[]{:S(2)}) collective-permute-start(f32[11,16,128]{2,1,0:T(8,128)S(1)} %get-tuple-element.33.refs_2_), channel_id=1, source_target_pairs={{0,2},{2,0},{1,3},{3,1},{4,6},{6,4},{5,7},{7,5},{8,10},{10,8},{9,1... | collective-permute-start | bytes 270344 | tf_op jit(solution)/shard_map/ppermute | solution.py:422
  50.2 3.6 %collective-permute-done.12.refs_5_ = f32[7,16,128]{2,1,0:T(8,128)S(1)} collective-permute-done((f32[7,16,128]{2,1,0:T(8,128)S(1)}, f32[7,16,128]{2,1,0:T(8,128)S(1)}, u32[]{:S(2)}, u32[]{:S(2)}) %collective-permute-start.12) | collective-permute-done | bytes 57376 | tf_op jit(solution)/shard_map/ppermute | solution.py:429
  53.7 13.2 %later_step.1 = (f32[11,16,128]{2,1,0:T(8,128)S(1)}, f32[11,16,128]{2,1,0:T(8,128)S(1)}, f32[7,16,128]{2,1,0:T(8,128)S(1)}, f32[7,16,128]{2,1,0:T(8,128)S(1)}) custom-call(s32[2]{0:T(128)S(1)} %copy-done.5, s32[2,2,8]{2,1,0:T(2,128)S(1)} %bitcast.6, f32[1,1]{1,0:T(1,128)S(6)} %copy.8.psf_ref, f32[2,1,1,128,128]{4,3,2,1,0:T(8,128)S(1)} %copy-done.2, ...), custom_call_target="tpu_custom_call" | custom-call | tf_op jit(solution)/shard_map/later_step/pallas_call | solution.py:341
  67.0 0.9 %collective-permute-start.13 = (f32[11,16,128]{2,1,0:T(8,128)S(1)}, f32[11,16,128]{2,1,0:T(8,128)S(1)}, u32[]{:S(2)}, u32[]{:S(2)}) collective-permute-start(f32[11,16,128]{2,1,0:T(8,128)S(1)} %get-tuple-element.36), channel_id=1, source_target_pairs={{0,2},{2,0},{1,3},{3,1},{4,6},{6,4},{5,7},{7,5},{8,10},{10,8},{9,1... | collective-permute-start | bytes 270344 | tf_op jit(solution)/shard_map/ppermute | solution.py:422
  68.1 1.1 %collective-permute-start.15 = (f32[7,16,128]{2,1,0:T(8,128)S(1)}, f32[7,16,128]{2,1,0:T(8,128)S(1)}, u32[]{:S(2)}, u32[]{:S(2)}) collective-permute-start(f32[7,16,128]{2,1,0:T(8,128)S(1)} %get-tuple-element.38), channel_id=1, source_target_pairs={{0,3},{1,2},{2,1},{3,0},{4,7},{5,6},{6,5},{7,4},{8,11},{9,10},{10,... | collective-permute-start | bytes 172040 | tf_op jit(solution)/shard_map/ppermute | solution.py:429
  69.2 3.0 %collective-permute-done.15 = f32[7,16,128]{2,1,0:T(8,128)S(1)} collective-permute-done((f32[7,16,128]{2,1,0:T(8,128)S(1)}, f32[7,16,128]{2,1,0:T(8,128)S(1)}, u32[]{:S(2)}, u32[]{:S(2)}) %collective-permute-start.15) | collective-permute-done | bytes 57376 | tf_op jit(solution)/shard_map/ppermute | solution.py:429
  72.6 1.1 %collective-permute-start.17 = (f32[11,8,128]{2,1,0:T(8,128)S(1)}, f32[11,8,128]{2,1,0:T(8,128)S(1)}, u32[]{:S(2)}, u32[]{:S(2)}) collective-permute-start(f32[11,8,128]{2,1,0:T(8,128)S(1)} %get-tuple-element.41), channel_id=1, source_target_pairs={{0,8},{4,12},{8,0},{12,4},{1,9},{5,13},{9,1},{13,5},{2,10},{6,14},... | collective-permute-start | bytes 135176 | tf_op jit(solution)/shard_map/ppermute | solution.py:434
  73.7 2.8 %collective-permute-start.18 = (f32[11,8,128]{2,1,0:T(8,128)S(1)}, f32[11,8,128]{2,1,0:T(8,128)S(1)}, u32[]{:S(2)}, u32[]{:S(2)}) collective-permute-start(f32[11,8,128]{2,1,0:T(8,128)S(1)} %get-tuple-element.42), channel_id=1, source_target_pairs={{0,12},{4,0},{8,4},{12,8},{1,13},{5,1},{9,5},{13,9},{2,14},{6,2},{... | collective-permute-start | bytes 135176 | tf_op jit(solution)/shard_map/ppermute | solution.py:434
  76.6 2.4 %collective-permute-done.16 = f32[11,8,128]{2,1,0:T(8,128)S(1)} collective-permute-done((f32[11,8,128]{2,1,0:T(8,128)S(1)}, f32[11,8,128]{2,1,0:T(8,128)S(1)}, u32[]{:S(2)}, u32[]{:S(2)}) %collective-permute-start.16) | collective-permute-done | bytes 45088 | tf_op jit(solution)/shard_map/ppermute | solution.py:434
  80.1 1.2 %collective-permute-start.20 = (f32[11,8,128]{2,1,0:T(8,128)S(1)}, f32[11,8,128]{2,1,0:T(8,128)S(1)}, u32[]{:S(2)}, u32[]{:S(2)}) collective-permute-start(f32[11,8,128]{2,1,0:T(8,128)S(1)} %add_add_fusion.refs_0_), channel_id=1, source_target_pairs={{0,1},{1,0},{2,3},{3,2},{4,5},{5,4},{6,7},{7,6},{8,9},{9,8},{10,11... | collective-permute-start | bytes 135176 | tf_op jit(solution)/shard_map/ppermute | solution.py:429
  81.8 1.6 %collective-permute-done.21.refs_3_ = f32[11,8,128]{2,1,0:T(8,128)S(1)} collective-permute-done((f32[11,8,128]{2,1,0:T(8,128)S(1)}, f32[11,8,128]{2,1,0:T(8,128)S(1)}, u32[]{:S(2)}, u32[]{:S(2)}) %collective-permute-start.21) | collective-permute-done | bytes 45088 | tf_op jit(solution)/shard_map/ppermute | solution.py:429
  83.4 2.0 %collective-permute-done.19.refs_1_ = f32[11,8,128]{2,1,0:T(8,128)S(1)} collective-permute-done((f32[11,8,128]{2,1,0:T(8,128)S(1)}, f32[11,8,128]{2,1,0:T(8,128)S(1)}, u32[]{:S(2)}, u32[]{:S(2)}) %collective-permute-start.19) | collective-permute-done | bytes 45088 | tf_op jit(solution)/shard_map/ppermute | solution.py:422
  85.4 0.7 final.1
  (46 shorter events, 8.6 us)
Async XLA Ops:
  2.2 15.0 %copy-start.2 = (f32[2,1,1,128,128]{4,3,2,1,0:T(8,128)S(1)}, f32[2,1,1,128,128]{4,3,2,1,0:T(8,128)}, u32[]{:S(2)}) copy-start(f32[2,1,1,128,128]{4,3,2,1,0:T(8,128)} %data_ref.3) | copy-start | bytes 393220
  2.2 15.0 %copy-start.3 = (f32[2,1,1,128,128]{4,3,2,1,0:T(8,128)S(1)}, f32[2,1,1,128,128]{4,3,2,1,0:T(8,128)}, u32[]{:S(2)}) copy-start(f32[2,1,1,128,128]{4,3,2,1,0:T(8,128)} %weight_ref.3) | copy-start | bytes 393220
  2.2 8.1 %collective-permute-start.2 = (f32[22,8,128]{2,1,0:T(8,128)S(1)}, f32[22,8,128]{2,1,0:T(8,128)S(1)}, u32[]{:S(2)}, u32[]{:S(2)}) collective-permute-start(f32[22,8,128]{2,1,0:T(8,128)S(1)} %pack.1.refs_0_), channel_id=1, source_target_pairs={{0,12},{4,0},{8,4},{12,8},{1,13},{5,1},{9,5},{13,9},{2,14},{6,2},{... | collective-permute-start | bytes 270344 | tf_op jit(solution)/shard_map/ppermute | solution.py:434
  7.3 8.1 %collective-permute-start.1 = (f32[22,8,128]{2,1,0:T(8,128)S(1)}, f32[22,8,128]{2,1,0:T(8,128)S(1)}, u32[]{:S(2)}, u32[]{:S(2)}) collective-permute-start(f32[22,8,128]{2,1,0:T(8,128)S(1)} %pack.1.refs_0_), channel_id=1, source_target_pairs={{0,8},{4,12},{8,0},{12,4},{1,9},{5,13},{9,1},{13,5},{2,10},{6,14},... | collective-permute-start | bytes 270344 | tf_op jit(solution)/shard_map/ppermute | solution.py:434
  7.3 8.1 %collective-permute-start = (f32[22,8,128]{2,1,0:T(8,128)S(1)}, f32[22,8,128]{2,1,0:T(8,128)S(1)}, u32[]{:S(2)}, u32[]{:S(2)}) collective-permute-start(f32[22,8,128]{2,1,0:T(8,128)S(1)} %pack.1.refs_0_), channel_id=1, source_target_pairs={{0,4},{4,8},{8,12},{12,0},{1,5},{5,9},{9,13},{13,1},{2,6},{6,10},{... | collective-permute-start | bytes 270344 | tf_op jit(solution)/shard_map/ppermute | solution.py:434
  15.8 1.4 %collective-permute-start.3 = (f32[14,16,128]{2,1,0:T(8,128)S(1)}, f32[14,16,128]{2,1,0:T(8,128)S(1)}, u32[]{:S(2)}, u32[]{:S(2)}) collective-permute-start(f32[14,16,128]{2,1,0:T(8,128)S(1)} %get-tuple-element.26), channel_id=1, source_target_pairs={{0,1},{1,0},{2,3},{3,2},{4,5},{5,4},{6,7},{7,6},{8,9},{9,8},{10,11... | collective-permute-start | bytes 344072 | tf_op jit(solution)/shard_map/ppermute | solution.py:470
  31.0 5.5 %collective-permute-start.4 = (f32[11,16,128]{2,1,0:T(8,128)S(1)}, f32[11,16,128]{2,1,0:T(8,128)S(1)}, u32[]{:S(2)}, u32[]{:S(2)}) collective-permute-start(f32[11,16,128]{2,1,0:T(8,128)S(1)} %get-tuple-element.28), channel_id=1, source_target_pairs={{0,2},{2,0},{1,3},{3,1},{4,6},{6,4},{5,7},{7,5},{8,10},{10,8},{9,1... | collective-permute-start | bytes 270344 | tf_op jit(solution)/shard_map/ppermute | solution.py:422
  32.5 1.2 %collective-permute-start.5 = (f32[7,16,128]{2,1,0:T(8,128)S(1)}, f32[7,16,128]{2,1,0:T(8,128)S(1)}, u32[]{:S(2)}, u32[]{:S(2)}) collective-permute-start(f32[7,16,128]{2,1,0:T(8,128)S(1)} %get-tuple-element.29), channel_id=1, source_target_pairs={{0,1},{1,0},{2,3},{3,2},{4,5},{5,4},{6,7},{7,6},{8,9},{9,8},{10,11... | collective-permute-start | bytes 172040 | tf_op jit(solution)/shard_map/ppermute | solution.py:429
  32.5 4.0 %collective-permute-start.6 = (f32[7,16,128]{2,1,0:T(8,128)S(1)}, f32[7,16,128]{2,1,0:T(8,128)S(1)}, u32[]{:S(2)}, u32[]{:S(2)}) collective-permute-start(f32[7,16,128]{2,1,0:T(8,128)S(1)} %get-tuple-element.30), channel_id=1, source_target_pairs={{0,3},{1,2},{2,1},{3,0},{4,7},{5,6},{6,5},{7,4},{8,11},{9,10},{10,... | collective-permute-start | bytes 172040 | tf_op jit(solution)/shard_map/ppermute | solution.py:429
  36.5 4.9 %collective-permute-start.9 = (f32[11,16,128]{2,1,0:T(8,128)S(1)}, f32[11,16,128]{2,1,0:T(8,128)S(1)}, u32[]{:S(2)}, u32[]{:S(2)}) collective-permute-start(f32[11,16,128]{2,1,0:T(8,128)S(1)} %pad_add_fusion.1.refs_0_), channel_id=1, source_target_pairs={{0,12},{4,0},{8,4},{12,8},{1,13},{5,1},{9,5},{13,9},{2,14},{6,2},{... | collective-permute-start | bytes 270344 | tf_op jit(solution)/shard_map/ppermute | solution.py:434
  37.1 10.5 %collective-permute-start.8 = (f32[11,16,128]{2,1,0:T(8,128)S(1)}, f32[11,16,128]{2,1,0:T(8,128)S(1)}, u32[]{:S(2)}, u32[]{:S(2)}) collective-permute-start(f32[11,16,128]{2,1,0:T(8,128)S(1)} %pad_add_fusion.1.refs_0_), channel_id=1, source_target_pairs={{0,8},{4,12},{8,0},{12,4},{1,9},{5,13},{9,1},{13,5},{2,10},{6,14},... | collective-permute-start | bytes 270344 | tf_op jit(solution)/shard_map/ppermute | solution.py:434
  38.9 8.8 %collective-permute-start.7 = (f32[11,16,128]{2,1,0:T(8,128)S(1)}, f32[11,16,128]{2,1,0:T(8,128)S(1)}, u32[]{:S(2)}, u32[]{:S(2)}) collective-permute-start(f32[11,16,128]{2,1,0:T(8,128)S(1)} %pad_add_fusion.1.refs_0_), channel_id=1, source_target_pairs={{0,4},{4,8},{8,12},{12,0},{1,5},{5,9},{9,13},{13,1},{2,6},{6,10},{... | collective-permute-start | bytes 270344 | tf_op jit(solution)/shard_map/ppermute | solution.py:434
  48.0 5.7 %collective-permute-start.10 = (f32[11,16,128]{2,1,0:T(8,128)S(1)}, f32[11,16,128]{2,1,0:T(8,128)S(1)}, u32[]{:S(2)}, u32[]{:S(2)}) collective-permute-start(f32[11,16,128]{2,1,0:T(8,128)S(1)} %get-tuple-element.33.refs_2_), channel_id=1, source_target_pairs={{0,2},{2,0},{1,3},{3,1},{4,6},{6,4},{5,7},{7,5},{8,10},{10,8},{9,1... | collective-permute-start | bytes 270344 | tf_op jit(solution)/shard_map/ppermute | solution.py:422
  49.5 4.2 %collective-permute-start.12 = (f32[7,16,128]{2,1,0:T(8,128)S(1)}, f32[7,16,128]{2,1,0:T(8,128)S(1)}, u32[]{:S(2)}, u32[]{:S(2)}) collective-permute-start(f32[7,16,128]{2,1,0:T(8,128)S(1)} %get-tuple-element.34), channel_id=1, source_target_pairs={{0,3},{1,2},{2,1},{3,0},{4,7},{5,6},{6,5},{7,4},{8,11},{9,10},{10,... | collective-permute-start | bytes 172040 | tf_op jit(solution)/shard_map/ppermute | solution.py:429
  49.5 4.2 %collective-permute-start.11 = (f32[7,16,128]{2,1,0:T(8,128)S(1)}, f32[7,16,128]{2,1,0:T(8,128)S(1)}, u32[]{:S(2)}, u32[]{:S(2)}) collective-permute-start(f32[7,16,128]{2,1,0:T(8,128)S(1)} %get-tuple-element.34), channel_id=1, source_target_pairs={{0,1},{1,0},{2,3},{3,2},{4,5},{5,4},{6,7},{7,6},{8,9},{9,8},{10,11... | collective-permute-start | bytes 172040 | tf_op jit(solution)/shard_map/ppermute | solution.py:429
  67.0 5.3 %collective-permute-start.13 = (f32[11,16,128]{2,1,0:T(8,128)S(1)}, f32[11,16,128]{2,1,0:T(8,128)S(1)}, u32[]{:S(2)}, u32[]{:S(2)}) collective-permute-start(f32[11,16,128]{2,1,0:T(8,128)S(1)} %get-tuple-element.36), channel_id=1, source_target_pairs={{0,2},{2,0},{1,3},{3,1},{4,6},{6,4},{5,7},{7,5},{8,10},{10,8},{9,1... | collective-permute-start | bytes 270344 | tf_op jit(solution)/shard_map/ppermute | solution.py:422
  67.9 1.3 %collective-permute-start.14 = (f32[7,16,128]{2,1,0:T(8,128)S(1)}, f32[7,16,128]{2,1,0:T(8,128)S(1)}, u32[]{:S(2)}, u32[]{:S(2)}) collective-permute-start(f32[7,16,128]{2,1,0:T(8,128)S(1)} %get-tuple-element.37), channel_id=1, source_target_pairs={{0,1},{1,0},{2,3},{3,2},{4,5},{5,4},{6,7},{7,6},{8,9},{9,8},{10,11... | collective-permute-start | bytes 172040 | tf_op jit(solution)/shard_map/ppermute | solution.py:429
  68.1 4.1 %collective-permute-start.15 = (f32[7,16,128]{2,1,0:T(8,128)S(1)}, f32[7,16,128]{2,1,0:T(8,128)S(1)}, u32[]{:S(2)}, u32[]{:S(2)}) collective-permute-start(f32[7,16,128]{2,1,0:T(8,128)S(1)} %get-tuple-element.38), channel_id=1, source_target_pairs={{0,3},{1,2},{2,1},{3,0},{4,7},{5,6},{6,5},{7,4},{8,11},{9,10},{10,... | collective-permute-start | bytes 172040 | tf_op jit(solution)/shard_map/ppermute | solution.py:429
  72.5 6.4 %collective-permute-start.16 = (f32[11,8,128]{2,1,0:T(8,128)S(1)}, f32[11,8,128]{2,1,0:T(8,128)S(1)}, u32[]{:S(2)}, u32[]{:S(2)}) collective-permute-start(f32[11,8,128]{2,1,0:T(8,128)S(1)} %get-tuple-element.40), channel_id=1, source_target_pairs={{0,4},{4,8},{8,12},{12,0},{1,5},{5,9},{9,13},{13,1},{2,6},{6,10},{... | collective-permute-start | bytes 135176 | tf_op jit(solution)/shard_map/ppermute | solution.py:434
  72.6 6.6 %collective-permute-start.17 = (f32[11,8,128]{2,1,0:T(8,128)S(1)}, f32[11,8,128]{2,1,0:T(8,128)S(1)}, u32[]{:S(2)}, u32[]{:S(2)}) collective-permute-start(f32[11,8,128]{2,1,0:T(8,128)S(1)} %get-tuple-element.41), channel_id=1, source_target_pairs={{0,8},{4,12},{8,0},{12,4},{1,9},{5,13},{9,1},{13,5},{2,10},{6,14},... | collective-permute-start | bytes 135176 | tf_op jit(solution)/shard_map/ppermute | solution.py:434
  73.7 5.8 %collective-permute-start.18 = (f32[11,8,128]{2,1,0:T(8,128)S(1)}, f32[11,8,128]{2,1,0:T(8,128)S(1)}, u32[]{:S(2)}, u32[]{:S(2)}) collective-permute-start(f32[11,8,128]{2,1,0:T(8,128)S(1)} %get-tuple-element.42), channel_id=1, source_target_pairs={{0,12},{4,0},{8,4},{12,8},{1,13},{5,1},{9,5},{13,9},{2,14},{6,2},{... | collective-permute-start | bytes 135176 | tf_op jit(solution)/shard_map/ppermute | solution.py:434
  79.6 3.8 %collective-permute-start.21 = (f32[11,8,128]{2,1,0:T(8,128)S(1)}, f32[11,8,128]{2,1,0:T(8,128)S(1)}, u32[]{:S(2)}, u32[]{:S(2)}) collective-permute-start(f32[11,8,128]{2,1,0:T(8,128)S(1)} %add_add_fusion.refs_0_), channel_id=1, source_target_pairs={{0,3},{1,2},{2,1},{3,0},{4,7},{5,6},{6,5},{7,4},{8,11},{9,10},{10,... | collective-permute-start | bytes 135176 | tf_op jit(solution)/shard_map/ppermute | solution.py:429
  80.1 3.3 %collective-permute-start.20 = (f32[11,8,128]{2,1,0:T(8,128)S(1)}, f32[11,8,128]{2,1,0:T(8,128)S(1)}, u32[]{:S(2)}, u32[]{:S(2)}) collective-permute-start(f32[11,8,128]{2,1,0:T(8,128)S(1)} %add_add_fusion.refs_0_), channel_id=1, source_target_pairs={{0,1},{1,0},{2,3},{3,2},{4,5},{5,4},{6,7},{7,6},{8,9},{9,8},{10,11... | collective-permute-start | bytes 135176 | tf_op jit(solution)/shard_map/ppermute | solution.py:429
  81.4 4.0 %collective-permute-start.19 = (f32[11,8,128]{2,1,0:T(8,128)S(1)}, f32[11,8,128]{2,1,0:T(8,128)S(1)}, u32[]{:S(2)}, u32[]{:S(2)}) collective-permute-start(f32[11,8,128]{2,1,0:T(8,128)S(1)} %add_add_fusion.refs_0_), channel_id=1, source_target_pairs={{0,2},{2,0},{1,3},{3,1},{4,6},{6,4},{5,7},{7,5},{8,10},{10,8},{9,1... | collective-permute-start | bytes 135176 | tf_op jit(solution)/shard_map/ppermute | solution.py:422
  (5 other events, 16.1 us)

commit v15 on v14

--- a/solution.py
+++ b/solution.py
@@ -146,7 +146,16 @@
                 amps[i] = half[q, p]
 
 
-def step_kernel(layout, later, counts_ref, offsets_ref, psf_ref, data_ref, weight_ref, *refs):
+def step_kernel(layout, later, counts_any, offsets_any, psf_ref, data_ref, weight_ref, *refs):
+    refs, (counts_ref, offsets_ref, sems) = refs[:-3], refs[-3:]
+    copies = [
+        pltpu.make_async_copy(source, target, sems.at[n])
+        for n, (source, target) in enumerate(
+            [(counts_any, counts_ref), (offsets_any, offsets_ref)]
+        )
+    ]
+    for copy in copies:
+        copy.start()
     shared_rows, rows, pieces = layout
     epochs = len(pieces)
     (mine, others), refs = refs[:2], refs[2:]
@@ -182,6 +191,8 @@
         for c in range(COMPS):
             amps[c] = amps[c] - STEP * moved_amps[c]
 
+    for copy in copies:
+        copy.wait()
     psf = psf_ref[0, 0]
     line_of = lax.broadcasted_iota(jnp.int32, (wide, 128), 0)
     live = jnp.zeros((wide, 128), jnp.bool_)
@@ -341,7 +352,7 @@
     return pl.pallas_call(
         functools.partial(step_kernel, layout, later),
         out_shape=[f32(*s) for s in shapes],
-        in_specs=[smem()] * 3 + [vmem()] * (2 + len(ins)),
+        in_specs=[pl.BlockSpec(memory_space=pl.ANY)] * 2 + [smem()] + [vmem()] * (2 + len(ins)),
         out_specs=[vmem()] * len(shapes),
         scratch_shapes=together
         + [
@@ -355,7 +366,12 @@
             pltpu.VMEM((epochs, rows, wide, 128), F32),
             pltpu.VMEM((epochs, shared_rows, wide, 128), F32),
         ]
-        + (together if later else []),
+        + (together if later else [])
+        + [
+            pltpu.SMEM((tiles,), jnp.int32),
+            pltpu.SMEM((tiles, 2, slots), jnp.int32),
+            pltpu.SemaphoreType.DMA((2,)),
+        ],
         compiler_params=params(40),
         name="later_step" if later else "first_step",
     )(counts, offsets, psf, data, weight, *ins)

time: 85.8 us -> 85.9 us (level); the launches traced: 86.1 us -> 85.4 us
  starting transfers between devices: 23.2 us -> 21.6 us
  waiting for transfers between devices: 31.2 us -> 32.1 us
    ppermute x9, starting transfers between devices: 14.4 us -> 12.7 us  [round_tiles(): lax.ppermute(arrays[k], 'tile', [(i, (i + k) % owners) for i in range(own...]
    ppermute x9, waiting for transfers between devices: 16.9 us -> 17.8 us  [round_tiles(): lax.ppermute(arrays[k], 'tile', [(i, (i + k) % owners) for i in range(own...]
  transfers between devices with their start and end apart: 22 -> 22, of which waited for: 15 -> 14; matrix products, arithmetic and copies ran while one was open for 0% -> 0% of each run, Pallas kernels for 0% -> 0%
where the time goes in v15:
time: 85.9 us; the launch traced here: 85.4 us
  waiting for transfers between devices  32.1 us (37%)
  Pallas kernels  28.6 us (33%)
  starting transfers between devices  21.6 us (25%)
  local copies, waits for them, and re-layouts  2.27 us (3%)
    pallas_call x2, Pallas kernels, step_gradient(): pl.pallas_call(functools.partial(step_kernel, layout, later), out_shape=[...  26.3 us
    ppermute x9, waiting for transfers between devices, round_tiles(): lax.ppermute(arrays[k], 'tile', [(i, (i + k) % owners) for i in range(own...  17.8 us
    ppermute x9, starting transfers between devices, round_tiles(): lax.ppermute(arrays[k], 'tile', [(i, (i + k) % owners) for i in range(own...  12.7 us
    ppermute x8, waiting for transfers between devices, to_peers(): kept.append(lax.ppermute(other[k], ('epoch', 'band'), pairs))  11.5 us
    ppermute x8, starting transfers between devices, to_peers(): kept.append(lax.ppermute(other[k], ('epoch', 'band'), pairs))  4.4 us
    ppermute x4, starting transfers between devices, to_peers(): lax.ppermute(same[k], 'epoch', [(i, (i + k) % epochs) for i in range(epoc...  4.37 us
    unnamed x14, local copies, waits for them, and re-layouts  2.27 us
    ppermute x4, waiting for transfers between devices, to_peers(): lax.ppermute(same[k], 'epoch', [(i, (i + k) % epochs) for i in range(epoc...  2.14 us
  transfers between devices with their start and end apart: 22, of which 14 were waited for; matrix products, arithmetic and copies ran while one was open for 0% of the time, Pallas kernels for 0%

profile of v15, /device:TPU:0, one launch (start us, length us, event | category | flops | bytes accessed | tf_op | source)
XLA Modules:
  0.0 85.4 jit_solution(18381636987248253613)
XLA Ops:
  0.7 0.9 %copy-done = f32[8,44,128]{2,0,1:T(8,128)S(1)} copy-done((f32[8,44,128]{2,0,1:T(8,128)S(1)}, f32[8,44,128]{2,0,1:T(8,128)}, u32[]{:S(2)}) %copy-start) | copy-done | bytes 180248
  2.2 5.1 %collective-permute-start.2 = (f32[22,8,128]{2,1,0:T(8,128)S(1)}, f32[22,8,128]{2,1,0:T(8,128)S(1)}, u32[]{:S(2)}, u32[]{:S(2)}) collective-permute-start(f32[22,8,128]{2,1,0:T(8,128)S(1)} %pack.1.refs_0_), channel_id=1, source_target_pairs={{0,12},{4,0},{8,4},{12,8},{1,13},{5,1},{9,5},{13,9},{2,14},{6,2},{... | collective-permute-start | bytes 270344 | tf_op jit(solution)/shard_map/ppermute | solution.py:450
  7.3 1.0 %collective-permute-start = (f32[22,8,128]{2,1,0:T(8,128)S(1)}, f32[22,8,128]{2,1,0:T(8,128)S(1)}, u32[]{:S(2)}, u32[]{:S(2)}) collective-permute-start(f32[22,8,128]{2,1,0:T(8,128)S(1)} %pack.1.refs_0_), channel_id=1, source_target_pairs={{0,4},{4,8},{8,12},{12,0},{1,5},{5,9},{9,13},{13,1},{2,6},{6,10},{... | collective-permute-start | bytes 270344 | tf_op jit(solution)/shard_map/ppermute | solution.py:450
  8.3 2.0 %collective-permute-done.2.refs_3_ = f32[22,8,128]{2,1,0:T(8,128)S(1)} collective-permute-done((f32[22,8,128]{2,1,0:T(8,128)S(1)}, f32[22,8,128]{2,1,0:T(8,128)S(1)}, u32[]{:S(2)}, u32[]{:S(2)}) %collective-permute-start.2) | collective-permute-done | bytes 90144 | tf_op jit(solution)/shard_map/ppermute | solution.py:450
  10.3 5.1 %collective-permute-done.1.refs_2_ = f32[22,8,128]{2,1,0:T(8,128)S(1)} collective-permute-done((f32[22,8,128]{2,1,0:T(8,128)S(1)}, f32[22,8,128]{2,1,0:T(8,128)S(1)}, u32[]{:S(2)}, u32[]{:S(2)}) %collective-permute-start.1) | collective-permute-done | bytes 90144 | tf_op jit(solution)/shard_map/ppermute | solution.py:450
  17.9 13.1 %first_step.1 = (f32[11,16,128]{2,1,0:T(8,128)S(1)}, f32[11,16,128]{2,1,0:T(8,128)S(1)}, f32[7,16,128]{2,1,0:T(8,128)S(1)}, f32[7,16,128]{2,1,0:T(8,128)S(1)}) custom-call(s32[2]{0:T(128)S(1)} %copy-done.5, s32[2,2,8]{2,1,0:T(2,128)S(1)} %bitcast.5, f32[1,1]{1,0:T(1,128)S(6)} %copy.8.psf_ref, f32[2,1,1,128,128]{4,3,2,1,0:T(8,128)S(1)} %copy-done.2, ...), custom_call_target="tpu_custom_call" | custom-call | tf_op jit(solution)/shard_map/first_step/pallas_call | solution.py:352
  31.0 1.5 %collective-permute-start.4 = (f32[11,16,128]{2,1,0:T(8,128)S(1)}, f32[11,16,128]{2,1,0:T(8,128)S(1)}, u32[]{:S(2)}, u32[]{:S(2)}) collective-permute-start(f32[11,16,128]{2,1,0:T(8,128)S(1)} %get-tuple-element.28), channel_id=1, source_target_pairs={{0,2},{2,0},{1,3},{3,1},{4,6},{6,4},{5,7},{7,5},{8,10},{10,8},{9,1... | collective-permute-start | bytes 270344 | tf_op jit(solution)/shard_map/ppermute | solution.py:438
  33.8 2.7 %collective-permute-done.6 = f32[7,16,128]{2,1,0:T(8,128)S(1)} collective-permute-done((f32[7,16,128]{2,1,0:T(8,128)S(1)}, f32[7,16,128]{2,1,0:T(8,128)S(1)}, u32[]{:S(2)}, u32[]{:S(2)}) %collective-permute-start.6) | collective-permute-done | bytes 57376 | tf_op jit(solution)/shard_map/ppermute | solution.py:445
  36.6 1.7 %collective-permute-start.8 = (f32[11,16,128]{2,1,0:T(8,128)S(1)}, f32[11,16,128]{2,1,0:T(8,128)S(1)}, u32[]{:S(2)}, u32[]{:S(2)}) collective-permute-start(f32[11,16,128]{2,1,0:T(8,128)S(1)} %pad_add_fusion.1.refs_0_), channel_id=1, source_target_pairs={{0,8},{4,12},{8,0},{12,4},{1,9},{5,13},{9,1},{13,5},{2,10},{6,14},... | collective-permute-start | bytes 270344 | tf_op jit(solution)/shard_map/ppermute | solution.py:450
  38.3 1.0 %collective-permute-start.7 = (f32[11,16,128]{2,1,0:T(8,128)S(1)}, f32[11,16,128]{2,1,0:T(8,128)S(1)}, u32[]{:S(2)}, u32[]{:S(2)}) collective-permute-start(f32[11,16,128]{2,1,0:T(8,128)S(1)} %pad_add_fusion.1.refs_0_), channel_id=1, source_target_pairs={{0,4},{4,8},{8,12},{12,0},{1,5},{5,9},{9,13},{13,1},{2,6},{6,10},{... | collective-permute-start | bytes 270344 | tf_op jit(solution)/shard_map/ppermute | solution.py:450
  39.3 2.7 %collective-permute-done.9.refs_3_ = f32[11,16,128]{2,1,0:T(8,128)S(1)} collective-permute-done((f32[11,16,128]{2,1,0:T(8,128)S(1)}, f32[11,16,128]{2,1,0:T(8,128)S(1)}, u32[]{:S(2)}, u32[]{:S(2)}) %collective-permute-start.9) | collective-permute-done | bytes 90144 | tf_op jit(solution)/shard_map/ppermute | solution.py:450
  42.0 4.9 %collective-permute-done.8.refs_2_ = f32[11,16,128]{2,1,0:T(8,128)S(1)} collective-permute-done((f32[11,16,128]{2,1,0:T(8,128)S(1)}, f32[11,16,128]{2,1,0:T(8,128)S(1)}, u32[]{:S(2)}, u32[]{:S(2)}) %collective-permute-start.8) | collective-permute-done | bytes 90144 | tf_op jit(solution)/shard_map/ppermute | solution.py:450
  47.3 1.5 %collective-permute-start.10 = (f32[11,16,128]{2,1,0:T(8,128)S(1)}, f32[11,16,128]{2,1,0:T(8,128)S(1)}, u32[]{:S(2)}, u32[]{:S(2)}) collective-permute-start(f32[11,16,128]{2,1,0:T(8,128)S(1)} %get-tuple-element.33.refs_2_), channel_id=1, source_target_pairs={{0,2},{2,0},{1,3},{3,1},{4,6},{6,4},{5,7},{7,5},{8,10},{10,8},{9,1... | collective-permute-start | bytes 270344 | tf_op jit(solution)/shard_map/ppermute | solution.py:438
  49.4 3.5 %collective-permute-done.12.refs_5_ = f32[7,16,128]{2,1,0:T(8,128)S(1)} collective-permute-done((f32[7,16,128]{2,1,0:T(8,128)S(1)}, f32[7,16,128]{2,1,0:T(8,128)S(1)}, u32[]{:S(2)}, u32[]{:S(2)}) %collective-permute-start.12) | collective-permute-done | bytes 57376 | tf_op jit(solution)/shard_map/ppermute | solution.py:445
  53.0 13.2 %later_step.1 = (f32[11,16,128]{2,1,0:T(8,128)S(1)}, f32[11,16,128]{2,1,0:T(8,128)S(1)}, f32[7,16,128]{2,1,0:T(8,128)S(1)}, f32[7,16,128]{2,1,0:T(8,128)S(1)}) custom-call(s32[2]{0:T(128)S(1)} %copy-done.5, s32[2,2,8]{2,1,0:T(2,128)S(1)} %bitcast.6, f32[1,1]{1,0:T(1,128)S(6)} %copy.8.psf_ref, f32[2,1,1,128,128]{4,3,2,1,0:T(8,128)S(1)} %copy-done.2, ...), custom_call_target="tpu_custom_call" | custom-call | tf_op jit(solution)/shard_map/later_step/pallas_call | solution.py:352
  66.1 1.0 %collective-permute-start.13 = (f32[11,16,128]{2,1,0:T(8,128)S(1)}, f32[11,16,128]{2,1,0:T(8,128)S(1)}, u32[]{:S(2)}, u32[]{:S(2)}) collective-permute-start(f32[11,16,128]{2,1,0:T(8,128)S(1)} %get-tuple-element.36), channel_id=1, source_target_pairs={{0,2},{2,0},{1,3},{3,1},{4,6},{6,4},{5,7},{7,5},{8,10},{10,8},{9,1... | collective-permute-start | bytes 270344 | tf_op jit(solution)/shard_map/ppermute | solution.py:438
  67.3 1.1 %collective-permute-start.15 = (f32[7,16,128]{2,1,0:T(8,128)S(1)}, f32[7,16,128]{2,1,0:T(8,128)S(1)}, u32[]{:S(2)}, u32[]{:S(2)}) collective-permute-start(f32[7,16,128]{2,1,0:T(8,128)S(1)} %get-tuple-element.38), channel_id=1, source_target_pairs={{0,3},{1,2},{2,1},{3,0},{4,7},{5,6},{6,5},{7,4},{8,11},{9,10},{10,... | collective-permute-start | bytes 172040 | tf_op jit(solution)/shard_map/ppermute | solution.py:445
  68.4 3.1 %collective-permute-done.15 = f32[7,16,128]{2,1,0:T(8,128)S(1)} collective-permute-done((f32[7,16,128]{2,1,0:T(8,128)S(1)}, f32[7,16,128]{2,1,0:T(8,128)S(1)}, u32[]{:S(2)}, u32[]{:S(2)}) %collective-permute-start.15) | collective-permute-done | bytes 57376 | tf_op jit(solution)/shard_map/ppermute | solution.py:445
  71.9 3.7 %collective-permute-start.18 = (f32[11,8,128]{2,1,0:T(8,128)S(1)}, f32[11,8,128]{2,1,0:T(8,128)S(1)}, u32[]{:S(2)}, u32[]{:S(2)}) collective-permute-start(f32[11,8,128]{2,1,0:T(8,128)S(1)} %get-tuple-element.42), channel_id=1, source_target_pairs={{0,12},{4,0},{8,4},{12,8},{1,13},{5,1},{9,5},{13,9},{2,14},{6,2},{... | collective-permute-start | bytes 135176 | tf_op jit(solution)/shard_map/ppermute | solution.py:450
  75.6 2.5 %collective-permute-done.16 = f32[11,8,128]{2,1,0:T(8,128)S(1)} collective-permute-done((f32[11,8,128]{2,1,0:T(8,128)S(1)}, f32[11,8,128]{2,1,0:T(8,128)S(1)}, u32[]{:S(2)}, u32[]{:S(2)}) %collective-permute-start.16) | collective-permute-done | bytes 45088 | tf_op jit(solution)/shard_map/ppermute | solution.py:450
  79.3 1.2 %collective-permute-start.20 = (f32[11,8,128]{2,1,0:T(8,128)S(1)}, f32[11,8,128]{2,1,0:T(8,128)S(1)}, u32[]{:S(2)}, u32[]{:S(2)}) collective-permute-start(f32[11,8,128]{2,1,0:T(8,128)S(1)} %add_add_fusion.refs_0_), channel_id=1, source_target_pairs={{0,1},{1,0},{2,3},{3,2},{4,5},{5,4},{6,7},{7,6},{8,9},{9,8},{10,11... | collective-permute-start | bytes 135176 | tf_op jit(solution)/shard_map/ppermute | solution.py:445
  80.9 1.6 %collective-permute-done.21.refs_3_ = f32[11,8,128]{2,1,0:T(8,128)S(1)} collective-permute-done((f32[11,8,128]{2,1,0:T(8,128)S(1)}, f32[11,8,128]{2,1,0:T(8,128)S(1)}, u32[]{:S(2)}, u32[]{:S(2)}) %collective-permute-start.21) | collective-permute-done | bytes 45088 | tf_op jit(solution)/shard_map/ppermute | solution.py:445
  82.5 2.1 %collective-permute-done.19.refs_1_ = f32[11,8,128]{2,1,0:T(8,128)S(1)} collective-permute-done((f32[11,8,128]{2,1,0:T(8,128)S(1)}, f32[11,8,128]{2,1,0:T(8,128)S(1)}, u32[]{:S(2)}, u32[]{:S(2)}) %collective-permute-start.19) | collective-permute-done | bytes 45088 | tf_op jit(solution)/shard_map/ppermute | solution.py:438
  84.6 0.7 final.1
  (46 shorter events, 7.6 us)
Async XLA Ops:
  2.2 15.0 %copy-start.2 = (f32[2,1,1,128,128]{4,3,2,1,0:T(8,128)S(1)}, f32[2,1,1,128,128]{4,3,2,1,0:T(8,128)}, u32[]{:S(2)}) copy-start(f32[2,1,1,128,128]{4,3,2,1,0:T(8,128)} %data_ref.3) | copy-start | bytes 393220
  2.2 15.0 %copy-start.3 = (f32[2,1,1,128,128]{4,3,2,1,0:T(8,128)S(1)}, f32[2,1,1,128,128]{4,3,2,1,0:T(8,128)}, u32[]{:S(2)}) copy-start(f32[2,1,1,128,128]{4,3,2,1,0:T(8,128)} %weight_ref.3) | copy-start | bytes 393220
  2.2 8.1 %collective-permute-start.2 = (f32[22,8,128]{2,1,0:T(8,128)S(1)}, f32[22,8,128]{2,1,0:T(8,128)S(1)}, u32[]{:S(2)}, u32[]{:S(2)}) collective-permute-start(f32[22,8,128]{2,1,0:T(8,128)S(1)} %pack.1.refs_0_), channel_id=1, source_target_pairs={{0,12},{4,0},{8,4},{12,8},{1,13},{5,1},{9,5},{13,9},{2,14},{6,2},{... | collective-permute-start | bytes 270344 | tf_op jit(solution)/shard_map/ppermute | solution.py:450
  7.3 8.1 %collective-permute-start.1 = (f32[22,8,128]{2,1,0:T(8,128)S(1)}, f32[22,8,128]{2,1,0:T(8,128)S(1)}, u32[]{:S(2)}, u32[]{:S(2)}) collective-permute-start(f32[22,8,128]{2,1,0:T(8,128)S(1)} %pack.1.refs_0_), channel_id=1, source_target_pairs={{0,8},{4,12},{8,0},{12,4},{1,9},{5,13},{9,1},{13,5},{2,10},{6,14},... | collective-permute-start | bytes 270344 | tf_op jit(solution)/shard_map/ppermute | solution.py:450
  7.3 8.1 %collective-permute-start = (f32[22,8,128]{2,1,0:T(8,128)S(1)}, f32[22,8,128]{2,1,0:T(8,128)S(1)}, u32[]{:S(2)}, u32[]{:S(2)}) collective-permute-start(f32[22,8,128]{2,1,0:T(8,128)S(1)} %pack.1.refs_0_), channel_id=1, source_target_pairs={{0,4},{4,8},{8,12},{12,0},{1,5},{5,9},{9,13},{13,1},{2,6},{6,10},{... | collective-permute-start | bytes 270344 | tf_op jit(solution)/shard_map/ppermute | solution.py:450
  15.8 1.4 %collective-permute-start.3 = (f32[14,16,128]{2,1,0:T(8,128)S(1)}, f32[14,16,128]{2,1,0:T(8,128)S(1)}, u32[]{:S(2)}, u32[]{:S(2)}) collective-permute-start(f32[14,16,128]{2,1,0:T(8,128)S(1)} %get-tuple-element.26), channel_id=1, source_target_pairs={{0,1},{1,0},{2,3},{3,2},{4,5},{5,4},{6,7},{7,6},{8,9},{9,8},{10,11... | collective-permute-start | bytes 344072 | tf_op jit(solution)/shard_map/ppermute | solution.py:486
  31.0 5.5 %collective-permute-start.4 = (f32[11,16,128]{2,1,0:T(8,128)S(1)}, f32[11,16,128]{2,1,0:T(8,128)S(1)}, u32[]{:S(2)}, u32[]{:S(2)}) collective-permute-start(f32[11,16,128]{2,1,0:T(8,128)S(1)} %get-tuple-element.28), channel_id=1, source_target_pairs={{0,2},{2,0},{1,3},{3,1},{4,6},{6,4},{5,7},{7,5},{8,10},{10,8},{9,1... | collective-permute-start | bytes 270344 | tf_op jit(solution)/shard_map/ppermute | solution.py:438
  32.6 1.2 %collective-permute-start.5 = (f32[7,16,128]{2,1,0:T(8,128)S(1)}, f32[7,16,128]{2,1,0:T(8,128)S(1)}, u32[]{:S(2)}, u32[]{:S(2)}) collective-permute-start(f32[7,16,128]{2,1,0:T(8,128)S(1)} %get-tuple-element.29), channel_id=1, source_target_pairs={{0,1},{1,0},{2,3},{3,2},{4,5},{5,4},{6,7},{7,6},{8,9},{9,8},{10,11... | collective-permute-start | bytes 172040 | tf_op jit(solution)/shard_map/ppermute | solution.py:445
  32.6 4.0 %collective-permute-start.6 = (f32[7,16,128]{2,1,0:T(8,128)S(1)}, f32[7,16,128]{2,1,0:T(8,128)S(1)}, u32[]{:S(2)}, u32[]{:S(2)}) collective-permute-start(f32[7,16,128]{2,1,0:T(8,128)S(1)} %get-tuple-element.30), channel_id=1, source_target_pairs={{0,3},{1,2},{2,1},{3,0},{4,7},{5,6},{6,5},{7,4},{8,11},{9,10},{10,... | collective-permute-start | bytes 172040 | tf_op jit(solution)/shard_map/ppermute | solution.py:445
  36.6 5.5 %collective-permute-start.9 = (f32[11,16,128]{2,1,0:T(8,128)S(1)}, f32[11,16,128]{2,1,0:T(8,128)S(1)}, u32[]{:S(2)}, u32[]{:S(2)}) collective-permute-start(f32[11,16,128]{2,1,0:T(8,128)S(1)} %pad_add_fusion.1.refs_0_), channel_id=1, source_target_pairs={{0,12},{4,0},{8,4},{12,8},{1,13},{5,1},{9,5},{13,9},{2,14},{6,2},{... | collective-permute-start | bytes 270344 | tf_op jit(solution)/shard_map/ppermute | solution.py:450
  36.6 10.3 %collective-permute-start.8 = (f32[11,16,128]{2,1,0:T(8,128)S(1)}, f32[11,16,128]{2,1,0:T(8,128)S(1)}, u32[]{:S(2)}, u32[]{:S(2)}) collective-permute-start(f32[11,16,128]{2,1,0:T(8,128)S(1)} %pad_add_fusion.1.refs_0_), channel_id=1, source_target_pairs={{0,8},{4,12},{8,0},{12,4},{1,9},{5,13},{9,1},{13,5},{2,10},{6,14},... | collective-permute-start | bytes 270344 | tf_op jit(solution)/shard_map/ppermute | solution.py:450
  38.3 8.6 %collective-permute-start.7 = (f32[11,16,128]{2,1,0:T(8,128)S(1)}, f32[11,16,128]{2,1,0:T(8,128)S(1)}, u32[]{:S(2)}, u32[]{:S(2)}) collective-permute-start(f32[11,16,128]{2,1,0:T(8,128)S(1)} %pad_add_fusion.1.refs_0_), channel_id=1, source_target_pairs={{0,4},{4,8},{8,12},{12,0},{1,5},{5,9},{9,13},{13,1},{2,6},{6,10},{... | collective-permute-start | bytes 270344 | tf_op jit(solution)/shard_map/ppermute | solution.py:450
  47.3 5.7 %collective-permute-start.10 = (f32[11,16,128]{2,1,0:T(8,128)S(1)}, f32[11,16,128]{2,1,0:T(8,128)S(1)}, u32[]{:S(2)}, u32[]{:S(2)}) collective-permute-start(f32[11,16,128]{2,1,0:T(8,128)S(1)} %get-tuple-element.33.refs_2_), channel_id=1, source_target_pairs={{0,2},{2,0},{1,3},{3,1},{4,6},{6,4},{5,7},{7,5},{8,10},{10,8},{9,1... | collective-permute-start | bytes 270344 | tf_op jit(solution)/shard_map/ppermute | solution.py:438
  48.8 4.2 %collective-permute-start.12 = (f32[7,16,128]{2,1,0:T(8,128)S(1)}, f32[7,16,128]{2,1,0:T(8,128)S(1)}, u32[]{:S(2)}, u32[]{:S(2)}) collective-permute-start(f32[7,16,128]{2,1,0:T(8,128)S(1)} %get-tuple-element.34), channel_id=1, source_target_pairs={{0,3},{1,2},{2,1},{3,0},{4,7},{5,6},{6,5},{7,4},{8,11},{9,10},{10,... | collective-permute-start | bytes 172040 | tf_op jit(solution)/shard_map/ppermute | solution.py:445
  48.8 4.2 %collective-permute-start.11 = (f32[7,16,128]{2,1,0:T(8,128)S(1)}, f32[7,16,128]{2,1,0:T(8,128)S(1)}, u32[]{:S(2)}, u32[]{:S(2)}) collective-permute-start(f32[7,16,128]{2,1,0:T(8,128)S(1)} %get-tuple-element.34), channel_id=1, source_target_pairs={{0,1},{1,0},{2,3},{3,2},{4,5},{5,4},{6,7},{7,6},{8,9},{9,8},{10,11... | collective-permute-start | bytes 172040 | tf_op jit(solution)/shard_map/ppermute | solution.py:445
  66.1 5.3 %collective-permute-start.13 = (f32[11,16,128]{2,1,0:T(8,128)S(1)}, f32[11,16,128]{2,1,0:T(8,128)S(1)}, u32[]{:S(2)}, u32[]{:S(2)}) collective-permute-start(f32[11,16,128]{2,1,0:T(8,128)S(1)} %get-tuple-element.36), channel_id=1, source_target_pairs={{0,2},{2,0},{1,3},{3,1},{4,6},{6,4},{5,7},{7,5},{8,10},{10,8},{9,1... | collective-permute-start | bytes 270344 | tf_op jit(solution)/shard_map/ppermute | solution.py:438
  67.1 1.3 %collective-permute-start.14 = (f32[7,16,128]{2,1,0:T(8,128)S(1)}, f32[7,16,128]{2,1,0:T(8,128)S(1)}, u32[]{:S(2)}, u32[]{:S(2)}) collective-permute-start(f32[7,16,128]{2,1,0:T(8,128)S(1)} %get-tuple-element.37), channel_id=1, source_target_pairs={{0,1},{1,0},{2,3},{3,2},{4,5},{5,4},{6,7},{7,6},{8,9},{9,8},{10,11... | collective-permute-start | bytes 172040 | tf_op jit(solution)/shard_map/ppermute | solution.py:445
  67.3 4.1 %collective-permute-start.15 = (f32[7,16,128]{2,1,0:T(8,128)S(1)}, f32[7,16,128]{2,1,0:T(8,128)S(1)}, u32[]{:S(2)}, u32[]{:S(2)}) collective-permute-start(f32[7,16,128]{2,1,0:T(8,128)S(1)} %get-tuple-element.38), channel_id=1, source_target_pairs={{0,3},{1,2},{2,1},{3,0},{4,7},{5,6},{6,5},{7,4},{8,11},{9,10},{10,... | collective-permute-start | bytes 172040 | tf_op jit(solution)/shard_map/ppermute | solution.py:445
  71.7 6.4 %collective-permute-start.16 = (f32[11,8,128]{2,1,0:T(8,128)S(1)}, f32[11,8,128]{2,1,0:T(8,128)S(1)}, u32[]{:S(2)}, u32[]{:S(2)}) collective-permute-start(f32[11,8,128]{2,1,0:T(8,128)S(1)} %get-tuple-element.40), channel_id=1, source_target_pairs={{0,4},{4,8},{8,12},{12,0},{1,5},{5,9},{9,13},{13,1},{2,6},{6,10},{... | collective-permute-start | bytes 135176 | tf_op jit(solution)/shard_map/ppermute | solution.py:450
  71.8 6.6 %collective-permute-start.17 = (f32[11,8,128]{2,1,0:T(8,128)S(1)}, f32[11,8,128]{2,1,0:T(8,128)S(1)}, u32[]{:S(2)}, u32[]{:S(2)}) collective-permute-start(f32[11,8,128]{2,1,0:T(8,128)S(1)} %get-tuple-element.41), channel_id=1, source_target_pairs={{0,8},{4,12},{8,0},{12,4},{1,9},{5,13},{9,1},{13,5},{2,10},{6,14},... | collective-permute-start | bytes 135176 | tf_op jit(solution)/shard_map/ppermute | solution.py:450
  71.9 6.8 %collective-permute-start.18 = (f32[11,8,128]{2,1,0:T(8,128)S(1)}, f32[11,8,128]{2,1,0:T(8,128)S(1)}, u32[]{:S(2)}, u32[]{:S(2)}) collective-permute-start(f32[11,8,128]{2,1,0:T(8,128)S(1)} %get-tuple-element.42), channel_id=1, source_target_pairs={{0,12},{4,0},{8,4},{12,8},{1,13},{5,1},{9,5},{13,9},{2,14},{6,2},{... | collective-permute-start | bytes 135176 | tf_op jit(solution)/shard_map/ppermute | solution.py:450
  78.7 3.8 %collective-permute-start.21 = (f32[11,8,128]{2,1,0:T(8,128)S(1)}, f32[11,8,128]{2,1,0:T(8,128)S(1)}, u32[]{:S(2)}, u32[]{:S(2)}) collective-permute-start(f32[11,8,128]{2,1,0:T(8,128)S(1)} %add_add_fusion.refs_0_), channel_id=1, source_target_pairs={{0,3},{1,2},{2,1},{3,0},{4,7},{5,6},{6,5},{7,4},{8,11},{9,10},{10,... | collective-permute-start | bytes 135176 | tf_op jit(solution)/shard_map/ppermute | solution.py:445
  79.3 3.2 %collective-permute-start.20 = (f32[11,8,128]{2,1,0:T(8,128)S(1)}, f32[11,8,128]{2,1,0:T(8,128)S(1)}, u32[]{:S(2)}, u32[]{:S(2)}) collective-permute-start(f32[11,8,128]{2,1,0:T(8,128)S(1)} %add_add_fusion.refs_0_), channel_id=1, source_target_pairs={{0,1},{1,0},{2,3},{3,2},{4,5},{5,4},{6,7},{7,6},{8,9},{9,8},{10,11... | collective-permute-start | bytes 135176 | tf_op jit(solution)/shard_map/ppermute | solution.py:445
  80.6 4.0 %collective-permute-start.19 = (f32[11,8,128]{2,1,0:T(8,128)S(1)}, f32[11,8,128]{2,1,0:T(8,128)S(1)}, u32[]{:S(2)}, u32[]{:S(2)}) collective-permute-start(f32[11,8,128]{2,1,0:T(8,128)S(1)} %add_add_fusion.refs_0_), channel_id=1, source_target_pairs={{0,2},{2,0},{1,3},{3,1},{4,6},{6,4},{5,7},{7,5},{8,10},{10,8},{9,1... | collective-permute-start | bytes 135176 | tf_op jit(solution)/shard_map/ppermute | solution.py:438
  (5 other events, 16.1 us)

commit v16 on v14

--- a/solution.py
+++ b/solution.py
@@ -13,6 +13,7 @@
 POSITION_RATE = 1.0 / 64.0
 COMPS = 7
 BANDS = 2
+TOGETHER = 2
 SHARED = 4 * COMPS
 HALF = SHARED // BANDS
 SPLIT_UNIT = 49152.0
@@ -153,9 +154,10 @@
     taken = 2 * epochs if later else 0
     ins, refs = refs[:taken], refs[taken:]
     outs, refs = refs[: 2 * epochs], refs[2 * epochs :]
-    shared, amps, derived, prof_x, prof_y, pieces_x, pieces_y, image, sums, half, other = refs[:11]
+    shared, amps, derived, image, left_x, left_y, sums, half, other = refs[:9]
+    tiles = data_ref.shape[0]
+    prof_x, prof_y, pieces_x, pieces_y = (refs[9 + n * tiles : 9 + (n + 1) * tiles] for n in range(4))
     band, epoch = lax.axis_index("band"), lax.axis_index("epoch")
-    tiles = data_ref.shape[0]
     pixels = data_ref.shape[-1]
     wide = shared.shape[2]
     slots = wide // tiles
@@ -170,7 +172,7 @@
         return r // HALF, r % HALF
 
     if later:
-        moved, moved_amps = refs[11:]
+        moved, moved_amps = refs[9 + 4 * tiles :]
         put_together(layout, band, epoch, ins, half, other, moved, moved_amps)
         for k in range(4):
             shift = 0.0
@@ -242,56 +244,68 @@
     def line(index, c, s):
         return derived[index, c, pl.ds(s, 1), :]
 
-    together = 2
+    def profiles(t, s, c):
+        g = t * slots + s
+        at = slice(c * 128, (c + 1) * 128)
+        d = grid - line(0, c, g)
+        e = jnp.exp2(d * d * line(2, c, g))
+        prof_x[t][s * COMPS + c] = e
+        pieces_x[t][s, :, at] = cut(e, SPLIT_UNIT)
+        d = grid - line(1, c, g)
+        e = jnp.exp2(d * d * line(3, c, g))
+        prof_y[t][s * COMPS + c] = e
+        pieces_y[t][s, :, at] = cut(e * line(4, c, g), line(5, c, g))
+
+    def add_image(t, s):
+        image[...] += lax.dot_general(
+            pieces_x[t][s], pieces_y[t][s], (((1,), (1,)), ((), ())), preferred_element_type=F32
+        )
+
+    def pull_pair(t, s, first):
+        g = t * slots + s
+        here = min(2, COMPS - first)
+        span = slice(first * 128, (first + here) * 128)
+        by_x = times(left_x[...], pieces_y[t][s, :, span])
+        by_y = times(left_y[...], pieces_x[t][s, :, span])
+        for n in range(here):
+            c = first + n
+            at = slice(n * 128, (n + 1) * 128)
+            for k, value in enumerate(moments(prof_x[t][s * COMPS + c] * by_x[:, at])):
+                sums[k, c, pl.ds(g, 1), :] = value
+            for k, value in enumerate(moments(prof_y[t][s * COMPS + c] * by_y[:, at])):
+                sums[3 + k, c, pl.ds(g, 1), :] = value
+
+    def loop(first, last, rendered=None, pulled=None):
+        def body(i, carry):
+            for u in range(TOGETHER):
+                s = i * TOGETHER + u
+                for c in range(COMPS):
+                    if rendered is not None:
+                        profiles(rendered, s, c)
+                    if pulled is not None and c % 2 == 0:
+                        pull_pair(pulled, s, c)
+                if rendered is not None:
+                    add_image(rendered, s)
+            return carry
+
+        lax.fori_loop(first, last, body, 0)
+
+    trips = [(counts_ref[t] + TOGETHER - 1) // TOGETHER for t in range(tiles)]
     for t in range(tiles):
-        trips = (counts_ref[t] + together - 1) // together
         image[...] = jnp.zeros_like(image)
-
-        def render(i, carry):
-            for u in range(together):
-                s = i * together + u
-                g = t * slots + s
-                for c in range(COMPS):
-                    d = grid - line(0, c, g)
-                    e = jnp.exp2(d * d * line(2, c, g))
-                    prof_x[s * COMPS + c] = e
-                    pieces_x[s, :, c * 128 : (c + 1) * 128] = cut(e, SPLIT_UNIT)
-                    d = grid - line(1, c, g)
-                    e = jnp.exp2(d * d * line(3, c, g))
-                    prof_y[s * COMPS + c] = e
-                    pieces_y[s, :, c * 128 : (c + 1) * 128] = cut(e * line(4, c, g), line(5, c, g))
-                image[...] += lax.dot_general(
-                    pieces_x[s], pieces_y[s], (((1,), (1,)), ((), ())), preferred_element_type=F32
-                )
-            return carry
-
-        lax.fori_loop(0, trips, render, 0)
-
+        common = 0
+        if t > 0:
+            common = jnp.minimum(trips[t - 1], trips[t])
+            loop(0, common, rendered=t, pulled=t - 1)
+            loop(common, trips[t - 1], pulled=t - 1)
+        loop(common, trips[t], rendered=t)
         model = (image[:pixels, :pixels] + image[pixels:, pixels:]) + (
             image[:pixels, pixels:] + image[pixels:, :pixels]
         )
         cotangent = weight_ref[t, 0, 0] * (model - data_ref[t, 0, 0])
-        left_x, left_y = stack(cotangent), stack(cotangent.T)
-
-        def pull(i, carry):
-            for u in range(together):
-                s = i * together + u
-                g = t * slots + s
-                for first in range(0, COMPS, 2):
-                    here = min(2, COMPS - first)
-                    span = pl.ds(first * 128, 128 * here)
-                    by_x = times(left_x, pieces_y[s, :, span])
-                    by_y = times(left_y, pieces_x[s, :, span])
-                    for n in range(here):
-                        c = first + n
-                        at = slice(n * 128, (n + 1) * 128)
-                        for k, value in enumerate(moments(prof_x[s * COMPS + c] * by_x[:, at])):
-                            sums[k, c, pl.ds(g, 1), :] = value
-                        for k, value in enumerate(moments(prof_y[s * COMPS + c] * by_y[:, at])):
-                            sums[3 + k, c, pl.ds(g, 1), :] = value
-            return carry
-
-        lax.fori_loop(0, trips, pull, 0)
+        left_x[...] = stack(cotangent)
+        left_y[...] = stack(cotangent.T)
+    loop(0, trips[tiles - 1], pulled=tiles - 1)
 
     def keep(x):
         return jnp.where(live, x, 0.0)
@@ -346,17 +360,17 @@
         scratch_shapes=together
         + [
             pltpu.VMEM((6, COMPS, wide, 128), F32),
-            pltpu.VMEM((slots * COMPS, pixels, 128), F32),
-            pltpu.VMEM((slots * COMPS, pixels, 128), F32),
-            pltpu.VMEM((slots, 2 * pixels, COMPS * 128), F32),
-            pltpu.VMEM((slots, 2 * pixels, COMPS * 128), F32),
             pltpu.VMEM((2 * pixels, 2 * pixels), F32),
+            pltpu.VMEM((pixels, 3 * pixels), F32),
+            pltpu.VMEM((pixels, 3 * pixels), F32),
             pltpu.VMEM((6, COMPS, wide, 128), F32),
             pltpu.VMEM((epochs, rows, wide, 128), F32),
             pltpu.VMEM((epochs, shared_rows, wide, 128), F32),
         ]
+        + [pltpu.VMEM((slots * COMPS, pixels, 128), F32)] * (2 * tiles)
+        + [pltpu.VMEM((slots, 2 * pixels, COMPS * 128), F32)] * (2 * tiles)
         + (together if later else []),
-        compiler_params=params(40),
+        compiler_params=params(52),
         name="later_step" if later else "first_step",
     )(counts, offsets, psf, data, weight, *ins)
 

time: 85.8 us -> 85.3 us (level)
  Pallas kernels: 28.6 us -> 25.8 us
  waiting for transfers between devices: 31.2 us -> 33.1 us
    pallas_call x2, Pallas kernels: 26.4 us -> 23.6 us  [step_gradient(): pl.pallas_call(functools.partial(step_kernel, layout, later), out_shape=[...]
    ppermute x9, waiting for transfers between devices: 16.9 us -> 19.1 us  [round_tiles(): lax.ppermute(arrays[k], 'tile', [(i, (i + k) % owners) for i in range(own...]
  transfers between devices with their start and end apart: 22 -> 22, of which waited for: 15 -> 14; matrix products, arithmetic and copies ran while one was open for 0% -> 0% of each run, Pallas kernels for 0% -> 0%
where the time goes in v16:
time: 85.3 us; the launch traced here: 85.1 us
  waiting for transfers between devices  33.1 us (39%)
  Pallas kernels  25.8 us (30%)
  starting transfers between devices  23.1 us (27%)
  local copies, waits for them, and re-layouts  2.27 us (3%)
    pallas_call x2, Pallas kernels, step_gradient(): pl.pallas_call(functools.partial(step_kernel, layout, later), out_shape=[...  23.6 us
    ppermute x9, waiting for transfers between devices, round_tiles(): lax.ppermute(arrays[k], 'tile', [(i, (i + k) % owners) for i in range(own...  19.1 us
    ppermute x9, starting transfers between devices, round_tiles(): lax.ppermute(arrays[k], 'tile', [(i, (i + k) % owners) for i in range(own...  14.2 us
    ppermute x8, waiting for transfers between devices, to_peers(): kept.append(lax.ppermute(other[k], ('epoch', 'band'), pairs))  11.7 us
    ppermute x4, starting transfers between devices, to_peers(): lax.ppermute(same[k], 'epoch', [(i, (i + k) % epochs) for i in range(epoc...  4.79 us
    ppermute x8, starting transfers between devices, to_peers(): kept.append(lax.ppermute(other[k], ('epoch', 'band'), pairs))  3.98 us
    unnamed x14, local copies, waits for them, and re-layouts  2.27 us
  transfers between devices with their start and end apart: 22, of which 14 were waited for; matrix products, arithmetic and copies ran while one was open for 0% of the time, Pallas kernels for 0%

profile of v16, /device:TPU:0, one launch (start us, length us, event | category | flops | bytes accessed | tf_op | source)
XLA Modules:
  0.0 85.1 jit_solution(1410600970234176266)
XLA Ops:
  0.7 0.9 %copy-done = f32[8,44,128]{2,0,1:T(8,128)S(1)} copy-done((f32[8,44,128]{2,0,1:T(8,128)S(1)}, f32[8,44,128]{2,0,1:T(8,128)}, u32[]{:S(2)}) %copy-start) | copy-done | bytes 180248
  2.2 5.1 %collective-permute-start.2 = (f32[22,8,128]{2,1,0:T(8,128)S(1)}, f32[22,8,128]{2,1,0:T(8,128)S(1)}, u32[]{:S(2)}, u32[]{:S(2)}) collective-permute-start(f32[22,8,128]{2,1,0:T(8,128)S(1)} %pack.1.refs_0_), channel_id=1, source_target_pairs={{0,12},{4,0},{8,4},{12,8},{1,13},{5,1},{9,5},{13,9},{2,14},{6,2},{... | collective-permute-start | bytes 270344 | tf_op jit(solution)/shard_map/ppermute | solution.py:448
  7.3 1.0 %collective-permute-start = (f32[22,8,128]{2,1,0:T(8,128)S(1)}, f32[22,8,128]{2,1,0:T(8,128)S(1)}, u32[]{:S(2)}, u32[]{:S(2)}) collective-permute-start(f32[22,8,128]{2,1,0:T(8,128)S(1)} %pack.1.refs_0_), channel_id=1, source_target_pairs={{0,4},{4,8},{8,12},{12,0},{1,5},{5,9},{9,13},{13,1},{2,6},{6,10},{... | collective-permute-start | bytes 270344 | tf_op jit(solution)/shard_map/ppermute | solution.py:448
  8.3 2.0 %collective-permute-done.2.refs_3_ = f32[22,8,128]{2,1,0:T(8,128)S(1)} collective-permute-done((f32[22,8,128]{2,1,0:T(8,128)S(1)}, f32[22,8,128]{2,1,0:T(8,128)S(1)}, u32[]{:S(2)}, u32[]{:S(2)}) %collective-permute-start.2) | collective-permute-done | bytes 90144 | tf_op jit(solution)/shard_map/ppermute | solution.py:448
  10.3 5.1 %collective-permute-done.1.refs_2_ = f32[22,8,128]{2,1,0:T(8,128)S(1)} collective-permute-done((f32[22,8,128]{2,1,0:T(8,128)S(1)}, f32[22,8,128]{2,1,0:T(8,128)S(1)}, u32[]{:S(2)}, u32[]{:S(2)}) %collective-permute-start.1) | collective-permute-done | bytes 90144 | tf_op jit(solution)/shard_map/ppermute | solution.py:448
  17.9 11.7 %first_step.1 = (f32[11,16,128]{2,1,0:T(8,128)S(1)}, f32[11,16,128]{2,1,0:T(8,128)S(1)}, f32[7,16,128]{2,1,0:T(8,128)S(1)}, f32[7,16,128]{2,1,0:T(8,128)S(1)}) custom-call(s32[2]{0:T(128)S(1)} %copy-done.5, s32[2,2,8]{2,1,0:T(2,128)S(1)} %bitcast.5, f32[1,1]{1,0:T(1,128)S(6)} %copy.8.psf_ref, f32[2,1,1,128,128]{4,3,2,1,0:T(8,128)S(1)} %copy-done.2, ...), custom_call_target="tpu_custom_call" | custom-call | tf_op jit(solution)/shard_map/first_step/pallas_call | solution.py:355
  29.6 1.6 %collective-permute-start.4 = (f32[11,16,128]{2,1,0:T(8,128)S(1)}, f32[11,16,128]{2,1,0:T(8,128)S(1)}, u32[]{:S(2)}, u32[]{:S(2)}) collective-permute-start(f32[11,16,128]{2,1,0:T(8,128)S(1)} %get-tuple-element.28), channel_id=1, source_target_pairs={{0,2},{2,0},{1,3},{3,1},{4,6},{6,4},{5,7},{7,5},{8,10},{10,8},{9,1... | collective-permute-start | bytes 270344 | tf_op jit(solution)/shard_map/ppermute | solution.py:436
  32.4 2.7 %collective-permute-done.6 = f32[7,16,128]{2,1,0:T(8,128)S(1)} collective-permute-done((f32[7,16,128]{2,1,0:T(8,128)S(1)}, f32[7,16,128]{2,1,0:T(8,128)S(1)}, u32[]{:S(2)}, u32[]{:S(2)}) %collective-permute-start.6) | collective-permute-done | bytes 57376 | tf_op jit(solution)/shard_map/ppermute | solution.py:443
  35.1 3.6 %collective-permute-start.9 = (f32[11,16,128]{2,1,0:T(8,128)S(1)}, f32[11,16,128]{2,1,0:T(8,128)S(1)}, u32[]{:S(2)}, u32[]{:S(2)}) collective-permute-start(f32[11,16,128]{2,1,0:T(8,128)S(1)} %pad_add_fusion.1.refs_0_), channel_id=1, source_target_pairs={{0,12},{4,0},{8,4},{12,8},{1,13},{5,1},{9,5},{13,9},{2,14},{6,2},{... | collective-permute-start | bytes 270344 | tf_op jit(solution)/shard_map/ppermute | solution.py:448
  39.4 2.4 %collective-permute-done.9.refs_3_ = f32[11,16,128]{2,1,0:T(8,128)S(1)} collective-permute-done((f32[11,16,128]{2,1,0:T(8,128)S(1)}, f32[11,16,128]{2,1,0:T(8,128)S(1)}, u32[]{:S(2)}, u32[]{:S(2)}) %collective-permute-start.9) | collective-permute-done | bytes 90144 | tf_op jit(solution)/shard_map/ppermute | solution.py:448
  41.8 5.8 %collective-permute-done.8.refs_2_ = f32[11,16,128]{2,1,0:T(8,128)S(1)} collective-permute-done((f32[11,16,128]{2,1,0:T(8,128)S(1)}, f32[11,16,128]{2,1,0:T(8,128)S(1)}, u32[]{:S(2)}, u32[]{:S(2)}) %collective-permute-start.8) | collective-permute-done | bytes 90144 | tf_op jit(solution)/shard_map/ppermute | solution.py:448
  48.0 1.5 %collective-permute-start.10 = (f32[11,16,128]{2,1,0:T(8,128)S(1)}, f32[11,16,128]{2,1,0:T(8,128)S(1)}, u32[]{:S(2)}, u32[]{:S(2)}) collective-permute-start(f32[11,16,128]{2,1,0:T(8,128)S(1)} %get-tuple-element.33.refs_2_), channel_id=1, source_target_pairs={{0,2},{2,0},{1,3},{3,1},{4,6},{6,4},{5,7},{7,5},{8,10},{10,8},{9,1... | collective-permute-start | bytes 270344 | tf_op jit(solution)/shard_map/ppermute | solution.py:436
  50.1 3.6 %collective-permute-done.12.refs_5_ = f32[7,16,128]{2,1,0:T(8,128)S(1)} collective-permute-done((f32[7,16,128]{2,1,0:T(8,128)S(1)}, f32[7,16,128]{2,1,0:T(8,128)S(1)}, u32[]{:S(2)}, u32[]{:S(2)}) %collective-permute-start.12) | collective-permute-done | bytes 57376 | tf_op jit(solution)/shard_map/ppermute | solution.py:443
  53.7 11.8 %later_step.1 = (f32[11,16,128]{2,1,0:T(8,128)S(1)}, f32[11,16,128]{2,1,0:T(8,128)S(1)}, f32[7,16,128]{2,1,0:T(8,128)S(1)}, f32[7,16,128]{2,1,0:T(8,128)S(1)}) custom-call(s32[2]{0:T(128)S(1)} %copy-done.5, s32[2,2,8]{2,1,0:T(2,128)S(1)} %bitcast.6, f32[1,1]{1,0:T(1,128)S(6)} %copy.8.psf_ref, f32[2,1,1,128,128]{4,3,2,1,0:T(8,128)S(1)} %copy-done.2, ...), custom_call_target="tpu_custom_call" | custom-call | tf_op jit(solution)/shard_map/later_step/pallas_call | solution.py:355
  65.5 1.0 %collective-permute-start.13 = (f32[11,16,128]{2,1,0:T(8,128)S(1)}, f32[11,16,128]{2,1,0:T(8,128)S(1)}, u32[]{:S(2)}, u32[]{:S(2)}) collective-permute-start(f32[11,16,128]{2,1,0:T(8,128)S(1)} %get-tuple-element.36), channel_id=1, source_target_pairs={{0,2},{2,0},{1,3},{3,1},{4,6},{6,4},{5,7},{7,5},{8,10},{10,8},{9,1... | collective-permute-start | bytes 270344 | tf_op jit(solution)/shard_map/ppermute | solution.py:436
  66.7 1.0 %collective-permute-start.15 = (f32[7,16,128]{2,1,0:T(8,128)S(1)}, f32[7,16,128]{2,1,0:T(8,128)S(1)}, u32[]{:S(2)}, u32[]{:S(2)}) collective-permute-start(f32[7,16,128]{2,1,0:T(8,128)S(1)} %get-tuple-element.38), channel_id=1, source_target_pairs={{0,3},{1,2},{2,1},{3,0},{4,7},{5,6},{6,5},{7,4},{8,11},{9,10},{10,... | collective-permute-start | bytes 172040 | tf_op jit(solution)/shard_map/ppermute | solution.py:443
  67.8 3.1 %collective-permute-done.15 = f32[7,16,128]{2,1,0:T(8,128)S(1)} collective-permute-done((f32[7,16,128]{2,1,0:T(8,128)S(1)}, f32[7,16,128]{2,1,0:T(8,128)S(1)}, u32[]{:S(2)}, u32[]{:S(2)}) %collective-permute-start.15) | collective-permute-done | bytes 57376 | tf_op jit(solution)/shard_map/ppermute | solution.py:443
  71.2 3.3 %collective-permute-start.17 = (f32[11,8,128]{2,1,0:T(8,128)S(1)}, f32[11,8,128]{2,1,0:T(8,128)S(1)}, u32[]{:S(2)}, u32[]{:S(2)}) collective-permute-start(f32[11,8,128]{2,1,0:T(8,128)S(1)} %get-tuple-element.41), channel_id=1, source_target_pairs={{0,8},{4,12},{8,0},{12,4},{1,9},{5,13},{9,1},{13,5},{2,10},{6,14},... | collective-permute-start | bytes 135176 | tf_op jit(solution)/shard_map/ppermute | solution.py:448
  75.0 2.5 %collective-permute-done.16 = f32[11,8,128]{2,1,0:T(8,128)S(1)} collective-permute-done((f32[11,8,128]{2,1,0:T(8,128)S(1)}, f32[11,8,128]{2,1,0:T(8,128)S(1)}, u32[]{:S(2)}, u32[]{:S(2)}) %collective-permute-start.16) | collective-permute-done | bytes 45088 | tf_op jit(solution)/shard_map/ppermute | solution.py:448
  77.6 1.3 %collective-permute-done.17 = f32[11,8,128]{2,1,0:T(8,128)S(1)} collective-permute-done((f32[11,8,128]{2,1,0:T(8,128)S(1)}, f32[11,8,128]{2,1,0:T(8,128)S(1)}, u32[]{:S(2)}, u32[]{:S(2)}) %collective-permute-start.17) | collective-permute-done | bytes 45088 | tf_op jit(solution)/shard_map/ppermute | solution.py:448
  79.0 1.3 %collective-permute-start.20 = (f32[11,8,128]{2,1,0:T(8,128)S(1)}, f32[11,8,128]{2,1,0:T(8,128)S(1)}, u32[]{:S(2)}, u32[]{:S(2)}) collective-permute-start(f32[11,8,128]{2,1,0:T(8,128)S(1)} %add_add_fusion.refs_0_), channel_id=1, source_target_pairs={{0,1},{1,0},{2,3},{3,2},{4,5},{5,4},{6,7},{7,6},{8,9},{9,8},{10,11... | collective-permute-start | bytes 135176 | tf_op jit(solution)/shard_map/ppermute | solution.py:443
  81.1 1.7 %collective-permute-done.21.refs_3_ = f32[11,8,128]{2,1,0:T(8,128)S(1)} collective-permute-done((f32[11,8,128]{2,1,0:T(8,128)S(1)}, f32[11,8,128]{2,1,0:T(8,128)S(1)}, u32[]{:S(2)}, u32[]{:S(2)}) %collective-permute-start.21) | collective-permute-done | bytes 45088 | tf_op jit(solution)/shard_map/ppermute | solution.py:443
  82.8 1.6 %collective-permute-done.19.refs_1_ = f32[11,8,128]{2,1,0:T(8,128)S(1)} collective-permute-done((f32[11,8,128]{2,1,0:T(8,128)S(1)}, f32[11,8,128]{2,1,0:T(8,128)S(1)}, u32[]{:S(2)}, u32[]{:S(2)}) %collective-permute-start.19) | collective-permute-done | bytes 45088 | tf_op jit(solution)/shard_map/ppermute | solution.py:436
  84.4 0.7 final.1
  (46 shorter events, 7.9 us)
Async XLA Ops:
  2.2 15.0 %copy-start.2 = (f32[2,1,1,128,128]{4,3,2,1,0:T(8,128)S(1)}, f32[2,1,1,128,128]{4,3,2,1,0:T(8,128)}, u32[]{:S(2)}) copy-start(f32[2,1,1,128,128]{4,3,2,1,0:T(8,128)} %data_ref.3) | copy-start | bytes 393220
  2.2 15.0 %copy-start.3 = (f32[2,1,1,128,128]{4,3,2,1,0:T(8,128)S(1)}, f32[2,1,1,128,128]{4,3,2,1,0:T(8,128)}, u32[]{:S(2)}) copy-start(f32[2,1,1,128,128]{4,3,2,1,0:T(8,128)} %weight_ref.3) | copy-start | bytes 393220
  2.2 8.1 %collective-permute-start.2 = (f32[22,8,128]{2,1,0:T(8,128)S(1)}, f32[22,8,128]{2,1,0:T(8,128)S(1)}, u32[]{:S(2)}, u32[]{:S(2)}) collective-permute-start(f32[22,8,128]{2,1,0:T(8,128)S(1)} %pack.1.refs_0_), channel_id=1, source_target_pairs={{0,12},{4,0},{8,4},{12,8},{1,13},{5,1},{9,5},{13,9},{2,14},{6,2},{... | collective-permute-start | bytes 270344 | tf_op jit(solution)/shard_map/ppermute | solution.py:448
  7.3 8.1 %collective-permute-start.1 = (f32[22,8,128]{2,1,0:T(8,128)S(1)}, f32[22,8,128]{2,1,0:T(8,128)S(1)}, u32[]{:S(2)}, u32[]{:S(2)}) collective-permute-start(f32[22,8,128]{2,1,0:T(8,128)S(1)} %pack.1.refs_0_), channel_id=1, source_target_pairs={{0,8},{4,12},{8,0},{12,4},{1,9},{5,13},{9,1},{13,5},{2,10},{6,14},... | collective-permute-start | bytes 270344 | tf_op jit(solution)/shard_map/ppermute | solution.py:448
  7.3 8.1 %collective-permute-start = (f32[22,8,128]{2,1,0:T(8,128)S(1)}, f32[22,8,128]{2,1,0:T(8,128)S(1)}, u32[]{:S(2)}, u32[]{:S(2)}) collective-permute-start(f32[22,8,128]{2,1,0:T(8,128)S(1)} %pack.1.refs_0_), channel_id=1, source_target_pairs={{0,4},{4,8},{8,12},{12,0},{1,5},{5,9},{9,13},{13,1},{2,6},{6,10},{... | collective-permute-start | bytes 270344 | tf_op jit(solution)/shard_map/ppermute | solution.py:448
  15.8 1.4 %collective-permute-start.3 = (f32[14,16,128]{2,1,0:T(8,128)S(1)}, f32[14,16,128]{2,1,0:T(8,128)S(1)}, u32[]{:S(2)}, u32[]{:S(2)}) collective-permute-start(f32[14,16,128]{2,1,0:T(8,128)S(1)} %get-tuple-element.26), channel_id=1, source_target_pairs={{0,1},{1,0},{2,3},{3,2},{4,5},{5,4},{6,7},{7,6},{8,9},{9,8},{10,11... | collective-permute-start | bytes 344072 | tf_op jit(solution)/shard_map/ppermute | solution.py:484
  29.6 5.5 %collective-permute-start.4 = (f32[11,16,128]{2,1,0:T(8,128)S(1)}, f32[11,16,128]{2,1,0:T(8,128)S(1)}, u32[]{:S(2)}, u32[]{:S(2)}) collective-permute-start(f32[11,16,128]{2,1,0:T(8,128)S(1)} %get-tuple-element.28), channel_id=1, source_target_pairs={{0,2},{2,0},{1,3},{3,1},{4,6},{6,4},{5,7},{7,5},{8,10},{10,8},{9,1... | collective-permute-start | bytes 270344 | tf_op jit(solution)/shard_map/ppermute | solution.py:436
  31.1 1.2 %collective-permute-start.5 = (f32[7,16,128]{2,1,0:T(8,128)S(1)}, f32[7,16,128]{2,1,0:T(8,128)S(1)}, u32[]{:S(2)}, u32[]{:S(2)}) collective-permute-start(f32[7,16,128]{2,1,0:T(8,128)S(1)} %get-tuple-element.29), channel_id=1, source_target_pairs={{0,1},{1,0},{2,3},{3,2},{4,5},{5,4},{6,7},{7,6},{8,9},{9,8},{10,11... | collective-permute-start | bytes 172040 | tf_op jit(solution)/shard_map/ppermute | solution.py:443
  31.1 4.0 %collective-permute-start.6 = (f32[7,16,128]{2,1,0:T(8,128)S(1)}, f32[7,16,128]{2,1,0:T(8,128)S(1)}, u32[]{:S(2)}, u32[]{:S(2)}) collective-permute-start(f32[7,16,128]{2,1,0:T(8,128)S(1)} %get-tuple-element.30), channel_id=1, source_target_pairs={{0,3},{1,2},{2,1},{3,0},{4,7},{5,6},{6,5},{7,4},{8,11},{9,10},{10,... | collective-permute-start | bytes 172040 | tf_op jit(solution)/shard_map/ppermute | solution.py:443
  35.1 6.6 %collective-permute-start.9 = (f32[11,16,128]{2,1,0:T(8,128)S(1)}, f32[11,16,128]{2,1,0:T(8,128)S(1)}, u32[]{:S(2)}, u32[]{:S(2)}) collective-permute-start(f32[11,16,128]{2,1,0:T(8,128)S(1)} %pad_add_fusion.1.refs_0_), channel_id=1, source_target_pairs={{0,12},{4,0},{8,4},{12,8},{1,13},{5,1},{9,5},{13,9},{2,14},{6,2},{... | collective-permute-start | bytes 270344 | tf_op jit(solution)/shard_map/ppermute | solution.py:448
  38.7 8.9 %collective-permute-start.8 = (f32[11,16,128]{2,1,0:T(8,128)S(1)}, f32[11,16,128]{2,1,0:T(8,128)S(1)}, u32[]{:S(2)}, u32[]{:S(2)}) collective-permute-start(f32[11,16,128]{2,1,0:T(8,128)S(1)} %pad_add_fusion.1.refs_0_), channel_id=1, source_target_pairs={{0,8},{4,12},{8,0},{12,4},{1,9},{5,13},{9,1},{13,5},{2,10},{6,14},... | collective-permute-start | bytes 270344 | tf_op jit(solution)/shard_map/ppermute | solution.py:448
  38.8 8.9 %collective-permute-start.7 = (f32[11,16,128]{2,1,0:T(8,128)S(1)}, f32[11,16,128]{2,1,0:T(8,128)S(1)}, u32[]{:S(2)}, u32[]{:S(2)}) collective-permute-start(f32[11,16,128]{2,1,0:T(8,128)S(1)} %pad_add_fusion.1.refs_0_), channel_id=1, source_target_pairs={{0,4},{4,8},{8,12},{12,0},{1,5},{5,9},{9,13},{13,1},{2,6},{6,10},{... | collective-permute-start | bytes 270344 | tf_op jit(solution)/shard_map/ppermute | solution.py:448
  48.0 5.7 %collective-permute-start.10 = (f32[11,16,128]{2,1,0:T(8,128)S(1)}, f32[11,16,128]{2,1,0:T(8,128)S(1)}, u32[]{:S(2)}, u32[]{:S(2)}) collective-permute-start(f32[11,16,128]{2,1,0:T(8,128)S(1)} %get-tuple-element.33.refs_2_), channel_id=1, source_target_pairs={{0,2},{2,0},{1,3},{3,1},{4,6},{6,4},{5,7},{7,5},{8,10},{10,8},{9,1... | collective-permute-start | bytes 270344 | tf_op jit(solution)/shard_map/ppermute | solution.py:436
  49.5 4.2 %collective-permute-start.12 = (f32[7,16,128]{2,1,0:T(8,128)S(1)}, f32[7,16,128]{2,1,0:T(8,128)S(1)}, u32[]{:S(2)}, u32[]{:S(2)}) collective-permute-start(f32[7,16,128]{2,1,0:T(8,128)S(1)} %get-tuple-element.34), channel_id=1, source_target_pairs={{0,3},{1,2},{2,1},{3,0},{4,7},{5,6},{6,5},{7,4},{8,11},{9,10},{10,... | collective-permute-start | bytes 172040 | tf_op jit(solution)/shard_map/ppermute | solution.py:443
  49.5 4.2 %collective-permute-start.11 = (f32[7,16,128]{2,1,0:T(8,128)S(1)}, f32[7,16,128]{2,1,0:T(8,128)S(1)}, u32[]{:S(2)}, u32[]{:S(2)}) collective-permute-start(f32[7,16,128]{2,1,0:T(8,128)S(1)} %get-tuple-element.34), channel_id=1, source_target_pairs={{0,1},{1,0},{2,3},{3,2},{4,5},{5,4},{6,7},{7,6},{8,9},{9,8},{10,11... | collective-permute-start | bytes 172040 | tf_op jit(solution)/shard_map/ppermute | solution.py:443
  65.5 5.3 %collective-permute-start.13 = (f32[11,16,128]{2,1,0:T(8,128)S(1)}, f32[11,16,128]{2,1,0:T(8,128)S(1)}, u32[]{:S(2)}, u32[]{:S(2)}) collective-permute-start(f32[11,16,128]{2,1,0:T(8,128)S(1)} %get-tuple-element.36), channel_id=1, source_target_pairs={{0,2},{2,0},{1,3},{3,1},{4,6},{6,4},{5,7},{7,5},{8,10},{10,8},{9,1... | collective-permute-start | bytes 270344 | tf_op jit(solution)/shard_map/ppermute | solution.py:436
  66.6 1.2 %collective-permute-start.14 = (f32[7,16,128]{2,1,0:T(8,128)S(1)}, f32[7,16,128]{2,1,0:T(8,128)S(1)}, u32[]{:S(2)}, u32[]{:S(2)}) collective-permute-start(f32[7,16,128]{2,1,0:T(8,128)S(1)} %get-tuple-element.37), channel_id=1, source_target_pairs={{0,1},{1,0},{2,3},{3,2},{4,5},{5,4},{6,7},{7,6},{8,9},{9,8},{10,11... | collective-permute-start | bytes 172040 | tf_op jit(solution)/shard_map/ppermute | solution.py:443
  66.7 4.1 %collective-permute-start.15 = (f32[7,16,128]{2,1,0:T(8,128)S(1)}, f32[7,16,128]{2,1,0:T(8,128)S(1)}, u32[]{:S(2)}, u32[]{:S(2)}) collective-permute-start(f32[7,16,128]{2,1,0:T(8,128)S(1)} %get-tuple-element.38), channel_id=1, source_target_pairs={{0,3},{1,2},{2,1},{3,0},{4,7},{5,6},{6,5},{7,4},{8,11},{9,10},{10,... | collective-permute-start | bytes 172040 | tf_op jit(solution)/shard_map/ppermute | solution.py:443
  71.2 6.4 %collective-permute-start.16 = (f32[11,8,128]{2,1,0:T(8,128)S(1)}, f32[11,8,128]{2,1,0:T(8,128)S(1)}, u32[]{:S(2)}, u32[]{:S(2)}) collective-permute-start(f32[11,8,128]{2,1,0:T(8,128)S(1)} %get-tuple-element.40), channel_id=1, source_target_pairs={{0,4},{4,8},{8,12},{12,0},{1,5},{5,9},{9,13},{13,1},{2,6},{6,10},{... | collective-permute-start | bytes 135176 | tf_op jit(solution)/shard_map/ppermute | solution.py:448
  71.2 7.6 %collective-permute-start.17 = (f32[11,8,128]{2,1,0:T(8,128)S(1)}, f32[11,8,128]{2,1,0:T(8,128)S(1)}, u32[]{:S(2)}, u32[]{:S(2)}) collective-permute-start(f32[11,8,128]{2,1,0:T(8,128)S(1)} %get-tuple-element.41), channel_id=1, source_target_pairs={{0,8},{4,12},{8,0},{12,4},{1,9},{5,13},{9,1},{13,5},{2,10},{6,14},... | collective-permute-start | bytes 135176 | tf_op jit(solution)/shard_map/ppermute | solution.py:448
  74.5 4.3 %collective-permute-start.18 = (f32[11,8,128]{2,1,0:T(8,128)S(1)}, f32[11,8,128]{2,1,0:T(8,128)S(1)}, u32[]{:S(2)}, u32[]{:S(2)}) collective-permute-start(f32[11,8,128]{2,1,0:T(8,128)S(1)} %get-tuple-element.42), channel_id=1, source_target_pairs={{0,12},{4,0},{8,4},{12,8},{1,13},{5,1},{9,5},{13,9},{2,14},{6,2},{... | collective-permute-start | bytes 135176 | tf_op jit(solution)/shard_map/ppermute | solution.py:448
  78.9 3.9 %collective-permute-start.21 = (f32[11,8,128]{2,1,0:T(8,128)S(1)}, f32[11,8,128]{2,1,0:T(8,128)S(1)}, u32[]{:S(2)}, u32[]{:S(2)}) collective-permute-start(f32[11,8,128]{2,1,0:T(8,128)S(1)} %add_add_fusion.refs_0_), channel_id=1, source_target_pairs={{0,3},{1,2},{2,1},{3,0},{4,7},{5,6},{6,5},{7,4},{8,11},{9,10},{10,... | collective-permute-start | bytes 135176 | tf_op jit(solution)/shard_map/ppermute | solution.py:443
  79.0 3.7 %collective-permute-start.20 = (f32[11,8,128]{2,1,0:T(8,128)S(1)}, f32[11,8,128]{2,1,0:T(8,128)S(1)}, u32[]{:S(2)}, u32[]{:S(2)}) collective-permute-start(f32[11,8,128]{2,1,0:T(8,128)S(1)} %add_add_fusion.refs_0_), channel_id=1, source_target_pairs={{0,1},{1,0},{2,3},{3,2},{4,5},{5,4},{6,7},{7,6},{8,9},{9,8},{10,11... | collective-permute-start | bytes 135176 | tf_op jit(solution)/shard_map/ppermute | solution.py:443
  80.4 4.0 %collective-permute-start.19 = (f32[11,8,128]{2,1,0:T(8,128)S(1)}, f32[11,8,128]{2,1,0:T(8,128)S(1)}, u32[]{:S(2)}, u32[]{:S(2)}) collective-permute-start(f32[11,8,128]{2,1,0:T(8,128)S(1)} %add_add_fusion.refs_0_), channel_id=1, source_target_pairs={{0,2},{2,0},{1,3},{3,1},{4,6},{6,4},{5,7},{7,5},{8,10},{10,8},{9,1... | collective-permute-start | bytes 135176 | tf_op jit(solution)/shard_map/ppermute | solution.py:436
  (5 other events, 16.4 us)

commit v17 on v16

--- a/solution.py
+++ b/solution.py
@@ -257,8 +257,11 @@
         pieces_y[t][s, :, at] = cut(e * line(4, c, g), line(5, c, g))
 
     def add_image(t, s):
-        image[...] += lax.dot_general(
-            pieces_x[t][s], pieces_y[t][s], (((1,), (1,)), ((), ())), preferred_element_type=F32
+        lanes = (((1,), (1,)), ((), ()))
+        hi, lo = pieces_x[t][s, :pixels], pieces_x[t][s, pixels:]
+        image[:, : 2 * pixels] += lax.dot_general(hi, pieces_y[t][s], lanes, preferred_element_type=F32)
+        image[:, 2 * pixels :] += lax.dot_general(
+            lo, pieces_y[t][s, :pixels], lanes, preferred_element_type=F32
         )
 
     def pull_pair(t, s, first):
@@ -299,9 +302,7 @@
             loop(0, common, rendered=t, pulled=t - 1)
             loop(common, trips[t - 1], pulled=t - 1)
         loop(common, trips[t], rendered=t)
-        model = (image[:pixels, :pixels] + image[pixels:, pixels:]) + (
-            image[:pixels, pixels:] + image[pixels:, :pixels]
-        )
+        model = image[:, :pixels] + (image[:, pixels : 2 * pixels] + image[:, 2 * pixels :])
         cotangent = weight_ref[t, 0, 0] * (model - data_ref[t, 0, 0])
         left_x[...] = stack(cotangent)
         left_y[...] = stack(cotangent.T)
@@ -360,7 +361,7 @@
         scratch_shapes=together
         + [
             pltpu.VMEM((6, COMPS, wide, 128), F32),
-            pltpu.VMEM((2 * pixels, 2 * pixels), F32),
+            pltpu.VMEM((pixels, 3 * pixels), F32),
             pltpu.VMEM((pixels, 3 * pixels), F32),
             pltpu.VMEM((pixels, 3 * pixels), F32),
             pltpu.VMEM((6, COMPS, wide, 128), F32),

time: 85.3 us -> 86.4 us (1.013); the launches traced: 85.1 us -> 87.3 us
  Pallas kernels: 25.8 us -> 29.7 us
  waiting for transfers between devices: 33.1 us -> 30 us
  starting transfers between devices: 23.1 us -> 24.5 us
    pallas_call x2, Pallas kernels: 23.6 us -> 27.4 us  [step_gradient(): pl.pallas_call(functools.partial(step_kernel, layout, later), out_shape=[...]
    ppermute x9, waiting for transfers between devices: 19.1 us -> 16 us  [round_tiles(): lax.ppermute(arrays[k], 'tile', [(i, (i + k) % owners) for i in range(own...]
    ppermute x9, starting transfers between devices: 14.2 us -> 15.7 us  [round_tiles(): lax.ppermute(arrays[k], 'tile', [(i, (i + k) % owners) for i in range(own...]
where the time goes in v17:
time: 86.4 us; the launch traced here: 87.3 us
  waiting for transfers between devices  30 us (35%)
  Pallas kernels  29.7 us (34%)
  starting transfers between devices  24.5 us (28%)
  local copies, waits for them, and re-layouts  2.27 us (3%)
    pallas_call x2, Pallas kernels, step_gradient(): pl.pallas_call(functools.partial(step_kernel, layout, later), out_shape=[...  27.4 us
    ppermute x9, waiting for transfers between devices, round_tiles(): lax.ppermute(arrays[k], 'tile', [(i, (i + k) % owners) for i in range(own...  16 us
    ppermute x9, starting transfers between devices, round_tiles(): lax.ppermute(arrays[k], 'tile', [(i, (i + k) % owners) for i in range(own...  15.7 us
    ppermute x8, waiting for transfers between devices, to_peers(): kept.append(lax.ppermute(other[k], ('epoch', 'band'), pairs))  11.5 us
    ppermute x4, starting transfers between devices, to_peers(): lax.ppermute(same[k], 'epoch', [(i, (i + k) % epochs) for i in range(epoc...  4.62 us
    ppermute x8, starting transfers between devices, to_peers(): kept.append(lax.ppermute(other[k], ('epoch', 'band'), pairs))  4.15 us
    unnamed x14, local copies, waits for them, and re-layouts  2.27 us
    ppermute x4, waiting for transfers between devices, to_peers(): lax.ppermute(same[k], 'epoch', [(i, (i + k) % epochs) for i in range(epoc...  1.88 us
  transfers between devices with their start and end apart: 22, of which 14 were waited for; matrix products, arithmetic and copies ran while one was open for 0% of the time, Pallas kernels for 0%

profile of v17, /device:TPU:0, one launch (start us, length us, event | category | flops | bytes accessed | tf_op | source)
XLA Modules:
  0.0 87.3 jit_solution(1264894582034120892)
XLA Ops:
  0.7 0.9 %copy-done = f32[8,44,128]{2,0,1:T(8,128)S(1)} copy-done((f32[8,44,128]{2,0,1:T(8,128)S(1)}, f32[8,44,128]{2,0,1:T(8,128)}, u32[]{:S(2)}) %copy-start) | copy-done | bytes 180248
  2.2 5.1 %collective-permute-start.2 = (f32[22,8,128]{2,1,0:T(8,128)S(1)}, f32[22,8,128]{2,1,0:T(8,128)S(1)}, u32[]{:S(2)}, u32[]{:S(2)}) collective-permute-start(f32[22,8,128]{2,1,0:T(8,128)S(1)} %pack.1.refs_0_), channel_id=1, source_target_pairs={{0,12},{4,0},{8,4},{12,8},{1,13},{5,1},{9,5},{13,9},{2,14},{6,2},{... | collective-permute-start | bytes 270344 | tf_op jit(solution)/shard_map/ppermute | solution.py:449
  7.3 1.0 %collective-permute-start = (f32[22,8,128]{2,1,0:T(8,128)S(1)}, f32[22,8,128]{2,1,0:T(8,128)S(1)}, u32[]{:S(2)}, u32[]{:S(2)}) collective-permute-start(f32[22,8,128]{2,1,0:T(8,128)S(1)} %pack.1.refs_0_), channel_id=1, source_target_pairs={{0,4},{4,8},{8,12},{12,0},{1,5},{5,9},{9,13},{13,1},{2,6},{6,10},{... | collective-permute-start | bytes 270344 | tf_op jit(solution)/shard_map/ppermute | solution.py:449
  8.3 2.0 %collective-permute-done.2.refs_3_ = f32[22,8,128]{2,1,0:T(8,128)S(1)} collective-permute-done((f32[22,8,128]{2,1,0:T(8,128)S(1)}, f32[22,8,128]{2,1,0:T(8,128)S(1)}, u32[]{:S(2)}, u32[]{:S(2)}) %collective-permute-start.2) | collective-permute-done | bytes 90144 | tf_op jit(solution)/shard_map/ppermute | solution.py:449
  10.3 5.1 %collective-permute-done.1.refs_2_ = f32[22,8,128]{2,1,0:T(8,128)S(1)} collective-permute-done((f32[22,8,128]{2,1,0:T(8,128)S(1)}, f32[22,8,128]{2,1,0:T(8,128)S(1)}, u32[]{:S(2)}, u32[]{:S(2)}) %collective-permute-start.1) | collective-permute-done | bytes 90144 | tf_op jit(solution)/shard_map/ppermute | solution.py:449
  17.9 13.7 %first_step.1 = (f32[11,16,128]{2,1,0:T(8,128)S(1)}, f32[11,16,128]{2,1,0:T(8,128)S(1)}, f32[7,16,128]{2,1,0:T(8,128)S(1)}, f32[7,16,128]{2,1,0:T(8,128)S(1)}) custom-call(s32[2]{0:T(128)S(1)} %copy-done.5, s32[2,2,8]{2,1,0:T(2,128)S(1)} %bitcast.5, f32[1,1]{1,0:T(1,128)S(6)} %copy.8.psf_ref, f32[2,1,1,128,128]{4,3,2,1,0:T(8,128)S(1)} %copy-done.2, ...), custom_call_target="tpu_custom_call" | custom-call | tf_op jit(solution)/shard_map/first_step/pallas_call | solution.py:356
  31.5 1.6 %collective-permute-start.4 = (f32[11,16,128]{2,1,0:T(8,128)S(1)}, f32[11,16,128]{2,1,0:T(8,128)S(1)}, u32[]{:S(2)}, u32[]{:S(2)}) collective-permute-start(f32[11,16,128]{2,1,0:T(8,128)S(1)} %get-tuple-element.28), channel_id=1, source_target_pairs={{0,2},{2,0},{1,3},{3,1},{4,6},{6,4},{5,7},{7,5},{8,10},{10,8},{9,1... | collective-permute-start | bytes 270344 | tf_op jit(solution)/shard_map/ppermute | solution.py:437
  34.3 2.7 %collective-permute-done.6 = f32[7,16,128]{2,1,0:T(8,128)S(1)} collective-permute-done((f32[7,16,128]{2,1,0:T(8,128)S(1)}, f32[7,16,128]{2,1,0:T(8,128)S(1)}, u32[]{:S(2)}, u32[]{:S(2)}) %collective-permute-start.6) | collective-permute-done | bytes 57376 | tf_op jit(solution)/shard_map/ppermute | solution.py:444
  37.0 2.1 %collective-permute-start.9 = (f32[11,16,128]{2,1,0:T(8,128)S(1)}, f32[11,16,128]{2,1,0:T(8,128)S(1)}, u32[]{:S(2)}, u32[]{:S(2)}) collective-permute-start(f32[11,16,128]{2,1,0:T(8,128)S(1)} %pad_add_fusion.1.refs_0_), channel_id=1, source_target_pairs={{0,12},{4,0},{8,4},{12,8},{1,13},{5,1},{9,5},{13,9},{2,14},{6,2},{... | collective-permute-start | bytes 270344 | tf_op jit(solution)/shard_map/ppermute | solution.py:449
  39.4 1.9 %collective-permute-start.7 = (f32[11,16,128]{2,1,0:T(8,128)S(1)}, f32[11,16,128]{2,1,0:T(8,128)S(1)}, u32[]{:S(2)}, u32[]{:S(2)}) collective-permute-start(f32[11,16,128]{2,1,0:T(8,128)S(1)} %pad_add_fusion.1.refs_0_), channel_id=1, source_target_pairs={{0,4},{4,8},{8,12},{12,0},{1,5},{5,9},{9,13},{13,1},{2,6},{6,10},{... | collective-permute-start | bytes 270344 | tf_op jit(solution)/shard_map/ppermute | solution.py:449
  41.3 0.9 collective-permute-done.9.refs_3_
  42.2 6.3 %collective-permute-done.8.refs_2_ = f32[11,16,128]{2,1,0:T(8,128)S(1)} collective-permute-done((f32[11,16,128]{2,1,0:T(8,128)S(1)}, f32[11,16,128]{2,1,0:T(8,128)S(1)}, u32[]{:S(2)}, u32[]{:S(2)}) %collective-permute-start.8) | collective-permute-done | bytes 90144 | tf_op jit(solution)/shard_map/ppermute | solution.py:449
  48.8 1.5 %collective-permute-start.10 = (f32[11,16,128]{2,1,0:T(8,128)S(1)}, f32[11,16,128]{2,1,0:T(8,128)S(1)}, u32[]{:S(2)}, u32[]{:S(2)}) collective-permute-start(f32[11,16,128]{2,1,0:T(8,128)S(1)} %get-tuple-element.33.refs_2_), channel_id=1, source_target_pairs={{0,2},{2,0},{1,3},{3,1},{4,6},{6,4},{5,7},{7,5},{8,10},{10,8},{9,1... | collective-permute-start | bytes 270344 | tf_op jit(solution)/shard_map/ppermute | solution.py:437
  51.0 3.5 %collective-permute-done.12.refs_5_ = f32[7,16,128]{2,1,0:T(8,128)S(1)} collective-permute-done((f32[7,16,128]{2,1,0:T(8,128)S(1)}, f32[7,16,128]{2,1,0:T(8,128)S(1)}, u32[]{:S(2)}, u32[]{:S(2)}) %collective-permute-start.12) | collective-permute-done | bytes 57376 | tf_op jit(solution)/shard_map/ppermute | solution.py:444
  54.5 13.8 %later_step.1 = (f32[11,16,128]{2,1,0:T(8,128)S(1)}, f32[11,16,128]{2,1,0:T(8,128)S(1)}, f32[7,16,128]{2,1,0:T(8,128)S(1)}, f32[7,16,128]{2,1,0:T(8,128)S(1)}) custom-call(s32[2]{0:T(128)S(1)} %copy-done.5, s32[2,2,8]{2,1,0:T(2,128)S(1)} %bitcast.6, f32[1,1]{1,0:T(1,128)S(6)} %copy.8.psf_ref, f32[2,1,1,128,128]{4,3,2,1,0:T(8,128)S(1)} %copy-done.2, ...), custom_call_target="tpu_custom_call" | custom-call | tf_op jit(solution)/shard_map/later_step/pallas_call | solution.py:356
  68.3 1.0 %collective-permute-start.13 = (f32[11,16,128]{2,1,0:T(8,128)S(1)}, f32[11,16,128]{2,1,0:T(8,128)S(1)}, u32[]{:S(2)}, u32[]{:S(2)}) collective-permute-start(f32[11,16,128]{2,1,0:T(8,128)S(1)} %get-tuple-element.36), channel_id=1, source_target_pairs={{0,2},{2,0},{1,3},{3,1},{4,6},{6,4},{5,7},{7,5},{8,10},{10,8},{9,1... | collective-permute-start | bytes 270344 | tf_op jit(solution)/shard_map/ppermute | solution.py:437
  69.4 1.1 %collective-permute-start.15 = (f32[7,16,128]{2,1,0:T(8,128)S(1)}, f32[7,16,128]{2,1,0:T(8,128)S(1)}, u32[]{:S(2)}, u32[]{:S(2)}) collective-permute-start(f32[7,16,128]{2,1,0:T(8,128)S(1)} %get-tuple-element.38), channel_id=1, source_target_pairs={{0,3},{1,2},{2,1},{3,0},{4,7},{5,6},{6,5},{7,4},{8,11},{9,10},{10,... | collective-permute-start | bytes 172040 | tf_op jit(solution)/shard_map/ppermute | solution.py:444
  70.5 3.1 %collective-permute-done.15 = f32[7,16,128]{2,1,0:T(8,128)S(1)} collective-permute-done((f32[7,16,128]{2,1,0:T(8,128)S(1)}, f32[7,16,128]{2,1,0:T(8,128)S(1)}, u32[]{:S(2)}, u32[]{:S(2)}) %collective-permute-start.15) | collective-permute-done | bytes 57376 | tf_op jit(solution)/shard_map/ppermute | solution.py:444
  73.9 2.4 %collective-permute-start.17 = (f32[11,8,128]{2,1,0:T(8,128)S(1)}, f32[11,8,128]{2,1,0:T(8,128)S(1)}, u32[]{:S(2)}, u32[]{:S(2)}) collective-permute-start(f32[11,8,128]{2,1,0:T(8,128)S(1)} %get-tuple-element.41), channel_id=1, source_target_pairs={{0,8},{4,12},{8,0},{12,4},{1,9},{5,13},{9,1},{13,5},{2,10},{6,14},... | collective-permute-start | bytes 135176 | tf_op jit(solution)/shard_map/ppermute | solution.py:449
  76.3 2.8 %collective-permute-start.18 = (f32[11,8,128]{2,1,0:T(8,128)S(1)}, f32[11,8,128]{2,1,0:T(8,128)S(1)}, u32[]{:S(2)}, u32[]{:S(2)}) collective-permute-start(f32[11,8,128]{2,1,0:T(8,128)S(1)} %get-tuple-element.42), channel_id=1, source_target_pairs={{0,12},{4,0},{8,4},{12,8},{1,13},{5,1},{9,5},{13,9},{2,14},{6,2},{... | collective-permute-start | bytes 135176 | tf_op jit(solution)/shard_map/ppermute | solution.py:449
  79.1 0.8 collective-permute-done.16
  80.9 1.1 %collective-permute-start.21 = (f32[11,8,128]{2,1,0:T(8,128)S(1)}, f32[11,8,128]{2,1,0:T(8,128)S(1)}, u32[]{:S(2)}, u32[]{:S(2)}) collective-permute-start(f32[11,8,128]{2,1,0:T(8,128)S(1)} %add_add_fusion.refs_0_), channel_id=1, source_target_pairs={{0,3},{1,2},{2,1},{3,0},{4,7},{5,6},{6,5},{7,4},{8,11},{9,10},{10,... | collective-permute-start | bytes 135176 | tf_op jit(solution)/shard_map/ppermute | solution.py:444
  83.1 1.6 %collective-permute-done.21.refs_3_ = f32[11,8,128]{2,1,0:T(8,128)S(1)} collective-permute-done((f32[11,8,128]{2,1,0:T(8,128)S(1)}, f32[11,8,128]{2,1,0:T(8,128)S(1)}, u32[]{:S(2)}, u32[]{:S(2)}) %collective-permute-start.21) | collective-permute-done | bytes 45088 | tf_op jit(solution)/shard_map/ppermute | solution.py:444
  84.7 1.9 %collective-permute-done.19.refs_1_ = f32[11,8,128]{2,1,0:T(8,128)S(1)} collective-permute-done((f32[11,8,128]{2,1,0:T(8,128)S(1)}, f32[11,8,128]{2,1,0:T(8,128)S(1)}, u32[]{:S(2)}, u32[]{:S(2)}) %collective-permute-start.19) | collective-permute-done | bytes 45088 | tf_op jit(solution)/shard_map/ppermute | solution.py:437
  (46 shorter events, 8.8 us)
Async XLA Ops:
  2.2 15.0 %copy-start.2 = (f32[2,1,1,128,128]{4,3,2,1,0:T(8,128)S(1)}, f32[2,1,1,128,128]{4,3,2,1,0:T(8,128)}, u32[]{:S(2)}) copy-start(f32[2,1,1,128,128]{4,3,2,1,0:T(8,128)} %data_ref.3) | copy-start | bytes 393220
  2.2 15.0 %copy-start.3 = (f32[2,1,1,128,128]{4,3,2,1,0:T(8,128)S(1)}, f32[2,1,1,128,128]{4,3,2,1,0:T(8,128)}, u32[]{:S(2)}) copy-start(f32[2,1,1,128,128]{4,3,2,1,0:T(8,128)} %weight_ref.3) | copy-start | bytes 393220
  2.2 8.1 %collective-permute-start.2 = (f32[22,8,128]{2,1,0:T(8,128)S(1)}, f32[22,8,128]{2,1,0:T(8,128)S(1)}, u32[]{:S(2)}, u32[]{:S(2)}) collective-permute-start(f32[22,8,128]{2,1,0:T(8,128)S(1)} %pack.1.refs_0_), channel_id=1, source_target_pairs={{0,12},{4,0},{8,4},{12,8},{1,13},{5,1},{9,5},{13,9},{2,14},{6,2},{... | collective-permute-start | bytes 270344 | tf_op jit(solution)/shard_map/ppermute | solution.py:449
  7.3 8.1 %collective-permute-start.1 = (f32[22,8,128]{2,1,0:T(8,128)S(1)}, f32[22,8,128]{2,1,0:T(8,128)S(1)}, u32[]{:S(2)}, u32[]{:S(2)}) collective-permute-start(f32[22,8,128]{2,1,0:T(8,128)S(1)} %pack.1.refs_0_), channel_id=1, source_target_pairs={{0,8},{4,12},{8,0},{12,4},{1,9},{5,13},{9,1},{13,5},{2,10},{6,14},... | collective-permute-start | bytes 270344 | tf_op jit(solution)/shard_map/ppermute | solution.py:449
  7.3 8.1 %collective-permute-start = (f32[22,8,128]{2,1,0:T(8,128)S(1)}, f32[22,8,128]{2,1,0:T(8,128)S(1)}, u32[]{:S(2)}, u32[]{:S(2)}) collective-permute-start(f32[22,8,128]{2,1,0:T(8,128)S(1)} %pack.1.refs_0_), channel_id=1, source_target_pairs={{0,4},{4,8},{8,12},{12,0},{1,5},{5,9},{9,13},{13,1},{2,6},{6,10},{... | collective-permute-start | bytes 270344 | tf_op jit(solution)/shard_map/ppermute | solution.py:449
  15.8 1.4 %collective-permute-start.3 = (f32[14,16,128]{2,1,0:T(8,128)S(1)}, f32[14,16,128]{2,1,0:T(8,128)S(1)}, u32[]{:S(2)}, u32[]{:S(2)}) collective-permute-start(f32[14,16,128]{2,1,0:T(8,128)S(1)} %get-tuple-element.26), channel_id=1, source_target_pairs={{0,1},{1,0},{2,3},{3,2},{4,5},{5,4},{6,7},{7,6},{8,9},{9,8},{10,11... | collective-permute-start | bytes 344072 | tf_op jit(solution)/shard_map/ppermute | solution.py:485
  31.5 5.5 %collective-permute-start.4 = (f32[11,16,128]{2,1,0:T(8,128)S(1)}, f32[11,16,128]{2,1,0:T(8,128)S(1)}, u32[]{:S(2)}, u32[]{:S(2)}) collective-permute-start(f32[11,16,128]{2,1,0:T(8,128)S(1)} %get-tuple-element.28), channel_id=1, source_target_pairs={{0,2},{2,0},{1,3},{3,1},{4,6},{6,4},{5,7},{7,5},{8,10},{10,8},{9,1... | collective-permute-start | bytes 270344 | tf_op jit(solution)/shard_map/ppermute | solution.py:437
  33.1 1.2 %collective-permute-start.5 = (f32[7,16,128]{2,1,0:T(8,128)S(1)}, f32[7,16,128]{2,1,0:T(8,128)S(1)}, u32[]{:S(2)}, u32[]{:S(2)}) collective-permute-start(f32[7,16,128]{2,1,0:T(8,128)S(1)} %get-tuple-element.29), channel_id=1, source_target_pairs={{0,1},{1,0},{2,3},{3,2},{4,5},{5,4},{6,7},{7,6},{8,9},{9,8},{10,11... | collective-permute-start | bytes 172040 | tf_op jit(solution)/shard_map/ppermute | solution.py:444
  33.1 3.9 %collective-permute-start.6 = (f32[7,16,128]{2,1,0:T(8,128)S(1)}, f32[7,16,128]{2,1,0:T(8,128)S(1)}, u32[]{:S(2)}, u32[]{:S(2)}) collective-permute-start(f32[7,16,128]{2,1,0:T(8,128)S(1)} %get-tuple-element.30), channel_id=1, source_target_pairs={{0,3},{1,2},{2,1},{3,0},{4,7},{5,6},{6,5},{7,4},{8,11},{9,10},{10,... | collective-permute-start | bytes 172040 | tf_op jit(solution)/shard_map/ppermute | solution.py:444
  37.0 5.1 %collective-permute-start.9 = (f32[11,16,128]{2,1,0:T(8,128)S(1)}, f32[11,16,128]{2,1,0:T(8,128)S(1)}, u32[]{:S(2)}, u32[]{:S(2)}) collective-permute-start(f32[11,16,128]{2,1,0:T(8,128)S(1)} %pad_add_fusion.1.refs_0_), channel_id=1, source_target_pairs={{0,12},{4,0},{8,4},{12,8},{1,13},{5,1},{9,5},{13,9},{2,14},{6,2},{... | collective-permute-start | bytes 270344 | tf_op jit(solution)/shard_map/ppermute | solution.py:449
  39.2 9.3 %collective-permute-start.8 = (f32[11,16,128]{2,1,0:T(8,128)S(1)}, f32[11,16,128]{2,1,0:T(8,128)S(1)}, u32[]{:S(2)}, u32[]{:S(2)}) collective-permute-start(f32[11,16,128]{2,1,0:T(8,128)S(1)} %pad_add_fusion.1.refs_0_), channel_id=1, source_target_pairs={{0,8},{4,12},{8,0},{12,4},{1,9},{5,13},{9,1},{13,5},{2,10},{6,14},... | collective-permute-start | bytes 270344 | tf_op jit(solution)/shard_map/ppermute | solution.py:449
  39.4 9.1 %collective-permute-start.7 = (f32[11,16,128]{2,1,0:T(8,128)S(1)}, f32[11,16,128]{2,1,0:T(8,128)S(1)}, u32[]{:S(2)}, u32[]{:S(2)}) collective-permute-start(f32[11,16,128]{2,1,0:T(8,128)S(1)} %pad_add_fusion.1.refs_0_), channel_id=1, source_target_pairs={{0,4},{4,8},{8,12},{12,0},{1,5},{5,9},{9,13},{13,1},{2,6},{6,10},{... | collective-permute-start | bytes 270344 | tf_op jit(solution)/shard_map/ppermute | solution.py:449
  48.8 5.7 %collective-permute-start.10 = (f32[11,16,128]{2,1,0:T(8,128)S(1)}, f32[11,16,128]{2,1,0:T(8,128)S(1)}, u32[]{:S(2)}, u32[]{:S(2)}) collective-permute-start(f32[11,16,128]{2,1,0:T(8,128)S(1)} %get-tuple-element.33.refs_2_), channel_id=1, source_target_pairs={{0,2},{2,0},{1,3},{3,1},{4,6},{6,4},{5,7},{7,5},{8,10},{10,8},{9,1... | collective-permute-start | bytes 270344 | tf_op jit(solution)/shard_map/ppermute | solution.py:437
  50.3 4.2 %collective-permute-start.12 = (f32[7,16,128]{2,1,0:T(8,128)S(1)}, f32[7,16,128]{2,1,0:T(8,128)S(1)}, u32[]{:S(2)}, u32[]{:S(2)}) collective-permute-start(f32[7,16,128]{2,1,0:T(8,128)S(1)} %get-tuple-element.34), channel_id=1, source_target_pairs={{0,3},{1,2},{2,1},{3,0},{4,7},{5,6},{6,5},{7,4},{8,11},{9,10},{10,... | collective-permute-start | bytes 172040 | tf_op jit(solution)/shard_map/ppermute | solution.py:444
  50.3 4.2 %collective-permute-start.11 = (f32[7,16,128]{2,1,0:T(8,128)S(1)}, f32[7,16,128]{2,1,0:T(8,128)S(1)}, u32[]{:S(2)}, u32[]{:S(2)}) collective-permute-start(f32[7,16,128]{2,1,0:T(8,128)S(1)} %get-tuple-element.34), channel_id=1, source_target_pairs={{0,1},{1,0},{2,3},{3,2},{4,5},{5,4},{6,7},{7,6},{8,9},{9,8},{10,11... | collective-permute-start | bytes 172040 | tf_op jit(solution)/shard_map/ppermute | solution.py:444
  68.3 5.3 %collective-permute-start.13 = (f32[11,16,128]{2,1,0:T(8,128)S(1)}, f32[11,16,128]{2,1,0:T(8,128)S(1)}, u32[]{:S(2)}, u32[]{:S(2)}) collective-permute-start(f32[11,16,128]{2,1,0:T(8,128)S(1)} %get-tuple-element.36), channel_id=1, source_target_pairs={{0,2},{2,0},{1,3},{3,1},{4,6},{6,4},{5,7},{7,5},{8,10},{10,8},{9,1... | collective-permute-start | bytes 270344 | tf_op jit(solution)/shard_map/ppermute | solution.py:437
  69.3 1.2 %collective-permute-start.14 = (f32[7,16,128]{2,1,0:T(8,128)S(1)}, f32[7,16,128]{2,1,0:T(8,128)S(1)}, u32[]{:S(2)}, u32[]{:S(2)}) collective-permute-start(f32[7,16,128]{2,1,0:T(8,128)S(1)} %get-tuple-element.37), channel_id=1, source_target_pairs={{0,1},{1,0},{2,3},{3,2},{4,5},{5,4},{6,7},{7,6},{8,9},{9,8},{10,11... | collective-permute-start | bytes 172040 | tf_op jit(solution)/shard_map/ppermute | solution.py:444
  69.4 4.1 %collective-permute-start.15 = (f32[7,16,128]{2,1,0:T(8,128)S(1)}, f32[7,16,128]{2,1,0:T(8,128)S(1)}, u32[]{:S(2)}, u32[]{:S(2)}) collective-permute-start(f32[7,16,128]{2,1,0:T(8,128)S(1)} %get-tuple-element.38), channel_id=1, source_target_pairs={{0,3},{1,2},{2,1},{3,0},{4,7},{5,6},{6,5},{7,4},{8,11},{9,10},{10,... | collective-permute-start | bytes 172040 | tf_op jit(solution)/shard_map/ppermute | solution.py:444
  73.9 6.1 %collective-permute-start.16 = (f32[11,8,128]{2,1,0:T(8,128)S(1)}, f32[11,8,128]{2,1,0:T(8,128)S(1)}, u32[]{:S(2)}, u32[]{:S(2)}) collective-permute-start(f32[11,8,128]{2,1,0:T(8,128)S(1)} %get-tuple-element.40), channel_id=1, source_target_pairs={{0,4},{4,8},{8,12},{12,0},{1,5},{5,9},{9,13},{13,1},{2,6},{6,10},{... | collective-permute-start | bytes 135176 | tf_op jit(solution)/shard_map/ppermute | solution.py:449
  73.9 6.5 %collective-permute-start.17 = (f32[11,8,128]{2,1,0:T(8,128)S(1)}, f32[11,8,128]{2,1,0:T(8,128)S(1)}, u32[]{:S(2)}, u32[]{:S(2)}) collective-permute-start(f32[11,8,128]{2,1,0:T(8,128)S(1)} %get-tuple-element.41), channel_id=1, source_target_pairs={{0,8},{4,12},{8,0},{12,4},{1,9},{5,13},{9,1},{13,5},{2,10},{6,14},... | collective-permute-start | bytes 135176 | tf_op jit(solution)/shard_map/ppermute | solution.py:449
  76.3 4.6 %collective-permute-start.18 = (f32[11,8,128]{2,1,0:T(8,128)S(1)}, f32[11,8,128]{2,1,0:T(8,128)S(1)}, u32[]{:S(2)}, u32[]{:S(2)}) collective-permute-start(f32[11,8,128]{2,1,0:T(8,128)S(1)} %get-tuple-element.42), channel_id=1, source_target_pairs={{0,12},{4,0},{8,4},{12,8},{1,13},{5,1},{9,5},{13,9},{2,14},{6,2},{... | collective-permute-start | bytes 135176 | tf_op jit(solution)/shard_map/ppermute | solution.py:449
  80.9 3.8 %collective-permute-start.21 = (f32[11,8,128]{2,1,0:T(8,128)S(1)}, f32[11,8,128]{2,1,0:T(8,128)S(1)}, u32[]{:S(2)}, u32[]{:S(2)}) collective-permute-start(f32[11,8,128]{2,1,0:T(8,128)S(1)} %add_add_fusion.refs_0_), channel_id=1, source_target_pairs={{0,3},{1,2},{2,1},{3,0},{4,7},{5,6},{6,5},{7,4},{8,11},{9,10},{10,... | collective-permute-start | bytes 135176 | tf_op jit(solution)/shard_map/ppermute | solution.py:444
  82.0 2.7 %collective-permute-start.20 = (f32[11,8,128]{2,1,0:T(8,128)S(1)}, f32[11,8,128]{2,1,0:T(8,128)S(1)}, u32[]{:S(2)}, u32[]{:S(2)}) collective-permute-start(f32[11,8,128]{2,1,0:T(8,128)S(1)} %add_add_fusion.refs_0_), channel_id=1, source_target_pairs={{0,1},{1,0},{2,3},{3,2},{4,5},{5,4},{6,7},{7,6},{8,9},{9,8},{10,11... | collective-permute-start | bytes 135176 | tf_op jit(solution)/shard_map/ppermute | solution.py:444
  82.5 4.0 %collective-permute-start.19 = (f32[11,8,128]{2,1,0:T(8,128)S(1)}, f32[11,8,128]{2,1,0:T(8,128)S(1)}, u32[]{:S(2)}, u32[]{:S(2)}) collective-permute-start(f32[11,8,128]{2,1,0:T(8,128)S(1)} %add_add_fusion.refs_0_), channel_id=1, source_target_pairs={{0,2},{2,0},{1,3},{3,1},{4,6},{6,4},{5,7},{7,5},{8,10},{10,8},{9,1... | collective-permute-start | bytes 135176 | tf_op jit(solution)/shard_map/ppermute | solution.py:437
  (5 other events, 15.9 us)

commit v18 on v16

--- a/solution.py
+++ b/solution.py
@@ -244,48 +244,48 @@
     def line(index, c, s):
         return derived[index, c, pl.ds(s, 1), :]
 
-    def profiles(t, s, c):
-        g = t * slots + s
-        at = slice(c * 128, (c + 1) * 128)
+    columns = TOGETHER * COMPS
+
+    def profiles(t, i, n):
+        c = n % COMPS
+        g = t * slots + i * TOGETHER + n // COMPS
+        at = slice(n * 128, (n + 1) * 128)
         d = grid - line(0, c, g)
         e = jnp.exp2(d * d * line(2, c, g))
-        prof_x[t][s * COMPS + c] = e
-        pieces_x[t][s, :, at] = cut(e, SPLIT_UNIT)
+        prof_x[t][i * columns + n] = e
+        pieces_x[t][i, :, at] = cut(e, SPLIT_UNIT)
         d = grid - line(1, c, g)
         e = jnp.exp2(d * d * line(3, c, g))
-        prof_y[t][s * COMPS + c] = e
-        pieces_y[t][s, :, at] = cut(e * line(4, c, g), line(5, c, g))
-
-    def add_image(t, s):
+        prof_y[t][i * columns + n] = e
+        pieces_y[t][i, :, at] = cut(e * line(4, c, g), line(5, c, g))
+
+    def add_image(t, i):
         image[...] += lax.dot_general(
-            pieces_x[t][s], pieces_y[t][s], (((1,), (1,)), ((), ())), preferred_element_type=F32
+            pieces_x[t][i], pieces_y[t][i], (((1,), (1,)), ((), ())), preferred_element_type=F32
         )
 
-    def pull_pair(t, s, first):
-        g = t * slots + s
-        here = min(2, COMPS - first)
-        span = slice(first * 128, (first + here) * 128)
-        by_x = times(left_x[...], pieces_y[t][s, :, span])
-        by_y = times(left_y[...], pieces_x[t][s, :, span])
-        for n in range(here):
-            c = first + n
-            at = slice(n * 128, (n + 1) * 128)
-            for k, value in enumerate(moments(prof_x[t][s * COMPS + c] * by_x[:, at])):
+    def pull_pair(t, i, first):
+        span = slice(first * 128, (first + 2) * 128)
+        by_x = times(left_x[...], pieces_y[t][i, :, span])
+        by_y = times(left_y[...], pieces_x[t][i, :, span])
+        for n in (first, first + 1):
+            c = n % COMPS
+            g = t * slots + i * TOGETHER + n // COMPS
+            at = slice((n - first) * 128, (n - first + 1) * 128)
+            for k, value in enumerate(moments(prof_x[t][i * columns + n] * by_x[:, at])):
                 sums[k, c, pl.ds(g, 1), :] = value
-            for k, value in enumerate(moments(prof_y[t][s * COMPS + c] * by_y[:, at])):
+            for k, value in enumerate(moments(prof_y[t][i * columns + n] * by_y[:, at])):
                 sums[3 + k, c, pl.ds(g, 1), :] = value
 
     def loop(first, last, rendered=None, pulled=None):
         def body(i, carry):
-            for u in range(TOGETHER):
-                s = i * TOGETHER + u
-                for c in range(COMPS):
-                    if rendered is not None:
-                        profiles(rendered, s, c)
-                    if pulled is not None and c % 2 == 0:
-                        pull_pair(pulled, s, c)
+            for n in range(columns):
                 if rendered is not None:
-                    add_image(rendered, s)
+                    profiles(rendered, i, n)
+                if pulled is not None and n % 2 == 0:
+                    pull_pair(pulled, i, n)
+            if rendered is not None:
+                add_image(rendered, i)
             return carry
 
         lax.fori_loop(first, last, body, 0)
@@ -368,7 +368,7 @@
             pltpu.VMEM((epochs, shared_rows, wide, 128), F32),
         ]
         + [pltpu.VMEM((slots * COMPS, pixels, 128), F32)] * (2 * tiles)
-        + [pltpu.VMEM((slots, 2 * pixels, COMPS * 128), F32)] * (2 * tiles)
+        + [pltpu.VMEM((slots // TOGETHER, 2 * pixels, TOGETHER * COMPS * 128), F32)] * (2 * tiles)
         + (together if later else []),
         compiler_params=params(52),
         name="later_step" if later else "first_step",

time: 85.3 us -> 85.5 us (level)
  starting transfers between devices: 23.1 us -> 29.1 us
  Pallas kernels: 25.8 us -> 20.1 us
    ppermute x9, starting transfers between devices: 14.2 us -> 20.3 us  [round_tiles(): lax.ppermute(arrays[k], 'tile', [(i, (i + k) % owners) for i in range(own...]
    pallas_call x2, Pallas kernels: 23.6 us -> 17.8 us  [step_gradient(): pl.pallas_call(functools.partial(step_kernel, layout, later), out_shape=[...]
  transfers between devices with their start and end apart: 22 -> 22, of which waited for: 14 -> 15; matrix products, arithmetic and copies ran while one was open for 0% -> 0% of each run, Pallas kernels for 0% -> 0%
where the time goes in v18:
time: 85.5 us; the launch traced here: 85.3 us
  waiting for transfers between devices  33.1 us (39%)
  starting transfers between devices  29.1 us (34%)
  Pallas kernels  20.1 us (24%)
  local copies, waits for them, and re-layouts  2.27 us (3%)
    ppermute x9, starting transfers between devices, round_tiles(): lax.ppermute(arrays[k], 'tile', [(i, (i + k) % owners) for i in range(own...  20.3 us
    ppermute x9, waiting for transfers between devices, round_tiles(): lax.ppermute(arrays[k], 'tile', [(i, (i + k) % owners) for i in range(own...  19.1 us
    pallas_call x2, Pallas kernels, step_gradient(): pl.pallas_call(functools.partial(step_kernel, layout, later), out_shape=[...  17.8 us
    ppermute x8, waiting for transfers between devices, to_peers(): kept.append(lax.ppermute(other[k], ('epoch', 'band'), pairs))  11.8 us
    ppermute x4, starting transfers between devices, to_peers(): lax.ppermute(same[k], 'epoch', [(i, (i + k) % epochs) for i in range(epoc...  4.86 us
    ppermute x8, starting transfers between devices, to_peers(): kept.append(lax.ppermute(other[k], ('epoch', 'band'), pairs))  3.91 us
    unnamed x14, local copies, waits for them, and re-layouts  2.27 us
  transfers between devices with their start and end apart: 22, of which 15 were waited for; matrix products, arithmetic and copies ran while one was open for 0% of the time, Pallas kernels for 0%

profile of v18, /device:TPU:0, one launch (start us, length us, event | category | flops | bytes accessed | tf_op | source)
XLA Modules:
  0.0 85.3 jit_solution(4601902395636689846)
XLA Ops:
  0.7 0.9 %copy-done = f32[8,44,128]{2,0,1:T(8,128)S(1)} copy-done((f32[8,44,128]{2,0,1:T(8,128)S(1)}, f32[8,44,128]{2,0,1:T(8,128)}, u32[]{:S(2)}) %copy-start) | copy-done | bytes 180248
  2.2 5.1 %collective-permute-start.2 = (f32[22,8,128]{2,1,0:T(8,128)S(1)}, f32[22,8,128]{2,1,0:T(8,128)S(1)}, u32[]{:S(2)}, u32[]{:S(2)}) collective-permute-start(f32[22,8,128]{2,1,0:T(8,128)S(1)} %pack.1.refs_0_), channel_id=1, source_target_pairs={{0,12},{4,0},{8,4},{12,8},{1,13},{5,1},{9,5},{13,9},{2,14},{6,2},{... | collective-permute-start | bytes 270344 | tf_op jit(solution)/shard_map/ppermute | solution.py:448
  7.3 1.0 %collective-permute-start = (f32[22,8,128]{2,1,0:T(8,128)S(1)}, f32[22,8,128]{2,1,0:T(8,128)S(1)}, u32[]{:S(2)}, u32[]{:S(2)}) collective-permute-start(f32[22,8,128]{2,1,0:T(8,128)S(1)} %pack.1.refs_0_), channel_id=1, source_target_pairs={{0,4},{4,8},{8,12},{12,0},{1,5},{5,9},{9,13},{13,1},{2,6},{6,10},{... | collective-permute-start | bytes 270344 | tf_op jit(solution)/shard_map/ppermute | solution.py:448
  8.3 2.0 %collective-permute-done.2.refs_3_ = f32[22,8,128]{2,1,0:T(8,128)S(1)} collective-permute-done((f32[22,8,128]{2,1,0:T(8,128)S(1)}, f32[22,8,128]{2,1,0:T(8,128)S(1)}, u32[]{:S(2)}, u32[]{:S(2)}) %collective-permute-start.2) | collective-permute-done | bytes 90144 | tf_op jit(solution)/shard_map/ppermute | solution.py:448
  10.3 5.1 %collective-permute-done.1.refs_2_ = f32[22,8,128]{2,1,0:T(8,128)S(1)} collective-permute-done((f32[22,8,128]{2,1,0:T(8,128)S(1)}, f32[22,8,128]{2,1,0:T(8,128)S(1)}, u32[]{:S(2)}, u32[]{:S(2)}) %collective-permute-start.1) | collective-permute-done | bytes 90144 | tf_op jit(solution)/shard_map/ppermute | solution.py:448
  17.9 8.9 %first_step.1 = (f32[11,16,128]{2,1,0:T(8,128)S(1)}, f32[11,16,128]{2,1,0:T(8,128)S(1)}, f32[7,16,128]{2,1,0:T(8,128)S(1)}, f32[7,16,128]{2,1,0:T(8,128)S(1)}) custom-call(s32[2]{0:T(128)S(1)} %copy-done.5, s32[2,2,8]{2,1,0:T(2,128)S(1)} %bitcast.5, f32[1,1]{1,0:T(1,128)S(6)} %copy.8.psf_ref, f32[2,1,1,128,128]{4,3,2,1,0:T(8,128)S(1)} %copy-done.2, ...), custom_call_target="tpu_custom_call" | custom-call | tf_op jit(solution)/shard_map/first_step/pallas_call | solution.py:355
  26.7 1.6 %collective-permute-start.4 = (f32[11,16,128]{2,1,0:T(8,128)S(1)}, f32[11,16,128]{2,1,0:T(8,128)S(1)}, u32[]{:S(2)}, u32[]{:S(2)}) collective-permute-start(f32[11,16,128]{2,1,0:T(8,128)S(1)} %get-tuple-element.28), channel_id=1, source_target_pairs={{0,2},{2,0},{1,3},{3,1},{4,6},{6,4},{5,7},{7,5},{8,10},{10,8},{9,1... | collective-permute-start | bytes 270344 | tf_op jit(solution)/shard_map/ppermute | solution.py:436
  29.5 2.7 %collective-permute-done.6 = f32[7,16,128]{2,1,0:T(8,128)S(1)} collective-permute-done((f32[7,16,128]{2,1,0:T(8,128)S(1)}, f32[7,16,128]{2,1,0:T(8,128)S(1)}, u32[]{:S(2)}, u32[]{:S(2)}) %collective-permute-start.6) | collective-permute-done | bytes 57376 | tf_op jit(solution)/shard_map/ppermute | solution.py:443
  32.3 6.6 %collective-permute-start.9 = (f32[11,16,128]{2,1,0:T(8,128)S(1)}, f32[11,16,128]{2,1,0:T(8,128)S(1)}, u32[]{:S(2)}, u32[]{:S(2)}) collective-permute-start(f32[11,16,128]{2,1,0:T(8,128)S(1)} %pad_add_fusion.1.refs_0_), channel_id=1, source_target_pairs={{0,12},{4,0},{8,4},{12,8},{1,13},{5,1},{9,5},{13,9},{2,14},{6,2},{... | collective-permute-start | bytes 270344 | tf_op jit(solution)/shard_map/ppermute | solution.py:448
  39.6 2.4 %collective-permute-done.9.refs_3_ = f32[11,16,128]{2,1,0:T(8,128)S(1)} collective-permute-done((f32[11,16,128]{2,1,0:T(8,128)S(1)}, f32[11,16,128]{2,1,0:T(8,128)S(1)}, u32[]{:S(2)}, u32[]{:S(2)}) %collective-permute-start.9) | collective-permute-done | bytes 90144 | tf_op jit(solution)/shard_map/ppermute | solution.py:448
  41.9 5.8 %collective-permute-done.8.refs_2_ = f32[11,16,128]{2,1,0:T(8,128)S(1)} collective-permute-done((f32[11,16,128]{2,1,0:T(8,128)S(1)}, f32[11,16,128]{2,1,0:T(8,128)S(1)}, u32[]{:S(2)}, u32[]{:S(2)}) %collective-permute-start.8) | collective-permute-done | bytes 90144 | tf_op jit(solution)/shard_map/ppermute | solution.py:448
  48.1 1.5 %collective-permute-start.10 = (f32[11,16,128]{2,1,0:T(8,128)S(1)}, f32[11,16,128]{2,1,0:T(8,128)S(1)}, u32[]{:S(2)}, u32[]{:S(2)}) collective-permute-start(f32[11,16,128]{2,1,0:T(8,128)S(1)} %get-tuple-element.33.refs_2_), channel_id=1, source_target_pairs={{0,2},{2,0},{1,3},{3,1},{4,6},{6,4},{5,7},{7,5},{8,10},{10,8},{9,1... | collective-permute-start | bytes 270344 | tf_op jit(solution)/shard_map/ppermute | solution.py:436
  50.3 3.5 %collective-permute-done.12.refs_5_ = f32[7,16,128]{2,1,0:T(8,128)S(1)} collective-permute-done((f32[7,16,128]{2,1,0:T(8,128)S(1)}, f32[7,16,128]{2,1,0:T(8,128)S(1)}, u32[]{:S(2)}, u32[]{:S(2)}) %collective-permute-start.12) | collective-permute-done | bytes 57376 | tf_op jit(solution)/shard_map/ppermute | solution.py:443
  53.8 8.9 %later_step.1 = (f32[11,16,128]{2,1,0:T(8,128)S(1)}, f32[11,16,128]{2,1,0:T(8,128)S(1)}, f32[7,16,128]{2,1,0:T(8,128)S(1)}, f32[7,16,128]{2,1,0:T(8,128)S(1)}) custom-call(s32[2]{0:T(128)S(1)} %copy-done.5, s32[2,2,8]{2,1,0:T(2,128)S(1)} %bitcast.6, f32[1,1]{1,0:T(1,128)S(6)} %copy.8.psf_ref, f32[2,1,1,128,128]{4,3,2,1,0:T(8,128)S(1)} %copy-done.2, ...), custom_call_target="tpu_custom_call" | custom-call | tf_op jit(solution)/shard_map/later_step/pallas_call | solution.py:355
  62.8 1.0 %collective-permute-start.13 = (f32[11,16,128]{2,1,0:T(8,128)S(1)}, f32[11,16,128]{2,1,0:T(8,128)S(1)}, u32[]{:S(2)}, u32[]{:S(2)}) collective-permute-start(f32[11,16,128]{2,1,0:T(8,128)S(1)} %get-tuple-element.36), channel_id=1, source_target_pairs={{0,2},{2,0},{1,3},{3,1},{4,6},{6,4},{5,7},{7,5},{8,10},{10,8},{9,1... | collective-permute-start | bytes 270344 | tf_op jit(solution)/shard_map/ppermute | solution.py:436
  64.0 1.0 %collective-permute-start.15 = (f32[7,16,128]{2,1,0:T(8,128)S(1)}, f32[7,16,128]{2,1,0:T(8,128)S(1)}, u32[]{:S(2)}, u32[]{:S(2)}) collective-permute-start(f32[7,16,128]{2,1,0:T(8,128)S(1)} %get-tuple-element.38), channel_id=1, source_target_pairs={{0,3},{1,2},{2,1},{3,0},{4,7},{5,6},{6,5},{7,4},{8,11},{9,10},{10,... | collective-permute-start | bytes 172040 | tf_op jit(solution)/shard_map/ppermute | solution.py:443
  65.1 3.1 %collective-permute-done.15 = f32[7,16,128]{2,1,0:T(8,128)S(1)} collective-permute-done((f32[7,16,128]{2,1,0:T(8,128)S(1)}, f32[7,16,128]{2,1,0:T(8,128)S(1)}, u32[]{:S(2)}, u32[]{:S(2)}) %collective-permute-start.15) | collective-permute-done | bytes 57376 | tf_op jit(solution)/shard_map/ppermute | solution.py:443
  68.4 4.4 %collective-permute-start.16 = (f32[11,8,128]{2,1,0:T(8,128)S(1)}, f32[11,8,128]{2,1,0:T(8,128)S(1)}, u32[]{:S(2)}, u32[]{:S(2)}) collective-permute-start(f32[11,8,128]{2,1,0:T(8,128)S(1)} %get-tuple-element.40), channel_id=1, source_target_pairs={{0,4},{4,8},{8,12},{12,0},{1,5},{5,9},{9,13},{13,1},{2,6},{6,10},{... | collective-permute-start | bytes 135176 | tf_op jit(solution)/shard_map/ppermute | solution.py:448
  72.9 1.9 %collective-permute-start.17 = (f32[11,8,128]{2,1,0:T(8,128)S(1)}, f32[11,8,128]{2,1,0:T(8,128)S(1)}, u32[]{:S(2)}, u32[]{:S(2)}) collective-permute-start(f32[11,8,128]{2,1,0:T(8,128)S(1)} %get-tuple-element.41), channel_id=1, source_target_pairs={{0,8},{4,12},{8,0},{12,4},{1,9},{5,13},{9,1},{13,5},{2,10},{6,14},... | collective-permute-start | bytes 135176 | tf_op jit(solution)/shard_map/ppermute | solution.py:448
  75.3 1.3 %collective-permute-done.16 = f32[11,8,128]{2,1,0:T(8,128)S(1)} collective-permute-done((f32[11,8,128]{2,1,0:T(8,128)S(1)}, f32[11,8,128]{2,1,0:T(8,128)S(1)}, u32[]{:S(2)}, u32[]{:S(2)}) %collective-permute-start.16) | collective-permute-done | bytes 45088 | tf_op jit(solution)/shard_map/ppermute | solution.py:448
  76.6 1.9 %collective-permute-done.17 = f32[11,8,128]{2,1,0:T(8,128)S(1)} collective-permute-done((f32[11,8,128]{2,1,0:T(8,128)S(1)}, f32[11,8,128]{2,1,0:T(8,128)S(1)}, u32[]{:S(2)}, u32[]{:S(2)}) %collective-permute-start.17) | collective-permute-done | bytes 45088 | tf_op jit(solution)/shard_map/ppermute | solution.py:448
  79.8 0.8 collective-permute-start.20
  81.3 1.8 %collective-permute-done.21.refs_3_ = f32[11,8,128]{2,1,0:T(8,128)S(1)} collective-permute-done((f32[11,8,128]{2,1,0:T(8,128)S(1)}, f32[11,8,128]{2,1,0:T(8,128)S(1)}, u32[]{:S(2)}, u32[]{:S(2)}) %collective-permute-start.21) | collective-permute-done | bytes 45088 | tf_op jit(solution)/shard_map/ppermute | solution.py:443
  83.1 1.5 %collective-permute-done.19.refs_1_ = f32[11,8,128]{2,1,0:T(8,128)S(1)} collective-permute-done((f32[11,8,128]{2,1,0:T(8,128)S(1)}, f32[11,8,128]{2,1,0:T(8,128)S(1)}, u32[]{:S(2)}, u32[]{:S(2)}) %collective-permute-start.19) | collective-permute-done | bytes 45088 | tf_op jit(solution)/shard_map/ppermute | solution.py:436
  (46 shorter events, 9.7 us)
Async XLA Ops:
  2.2 15.0 %copy-start.2 = (f32[2,1,1,128,128]{4,3,2,1,0:T(8,128)S(1)}, f32[2,1,1,128,128]{4,3,2,1,0:T(8,128)}, u32[]{:S(2)}) copy-start(f32[2,1,1,128,128]{4,3,2,1,0:T(8,128)} %data_ref.3) | copy-start | bytes 393220
  2.2 8.1 %collective-permute-start.2 = (f32[22,8,128]{2,1,0:T(8,128)S(1)}, f32[22,8,128]{2,1,0:T(8,128)S(1)}, u32[]{:S(2)}, u32[]{:S(2)}) collective-permute-start(f32[22,8,128]{2,1,0:T(8,128)S(1)} %pack.1.refs_0_), channel_id=1, source_target_pairs={{0,12},{4,0},{8,4},{12,8},{1,13},{5,1},{9,5},{13,9},{2,14},{6,2},{... | collective-permute-start | bytes 270344 | tf_op jit(solution)/shard_map/ppermute | solution.py:448
  7.3 8.1 %collective-permute-start.1 = (f32[22,8,128]{2,1,0:T(8,128)S(1)}, f32[22,8,128]{2,1,0:T(8,128)S(1)}, u32[]{:S(2)}, u32[]{:S(2)}) collective-permute-start(f32[22,8,128]{2,1,0:T(8,128)S(1)} %pack.1.refs_0_), channel_id=1, source_target_pairs={{0,8},{4,12},{8,0},{12,4},{1,9},{5,13},{9,1},{13,5},{2,10},{6,14},... | collective-permute-start | bytes 270344 | tf_op jit(solution)/shard_map/ppermute | solution.py:448
  7.3 8.1 %collective-permute-start = (f32[22,8,128]{2,1,0:T(8,128)S(1)}, f32[22,8,128]{2,1,0:T(8,128)S(1)}, u32[]{:S(2)}, u32[]{:S(2)}) collective-permute-start(f32[22,8,128]{2,1,0:T(8,128)S(1)} %pack.1.refs_0_), channel_id=1, source_target_pairs={{0,4},{4,8},{8,12},{12,0},{1,5},{5,9},{9,13},{13,1},{2,6},{6,10},{... | collective-permute-start | bytes 270344 | tf_op jit(solution)/shard_map/ppermute | solution.py:448
  15.8 1.4 %collective-permute-start.3 = (f32[14,16,128]{2,1,0:T(8,128)S(1)}, f32[14,16,128]{2,1,0:T(8,128)S(1)}, u32[]{:S(2)}, u32[]{:S(2)}) collective-permute-start(f32[14,16,128]{2,1,0:T(8,128)S(1)} %get-tuple-element.26), channel_id=1, source_target_pairs={{0,1},{1,0},{2,3},{3,2},{4,5},{5,4},{6,7},{7,6},{8,9},{9,8},{10,11... | collective-permute-start | bytes 344072 | tf_op jit(solution)/shard_map/ppermute | solution.py:484
  26.7 5.5 %collective-permute-start.4 = (f32[11,16,128]{2,1,0:T(8,128)S(1)}, f32[11,16,128]{2,1,0:T(8,128)S(1)}, u32[]{:S(2)}, u32[]{:S(2)}) collective-permute-start(f32[11,16,128]{2,1,0:T(8,128)S(1)} %get-tuple-element.28), channel_id=1, source_target_pairs={{0,2},{2,0},{1,3},{3,1},{4,6},{6,4},{5,7},{7,5},{8,10},{10,8},{9,1... | collective-permute-start | bytes 270344 | tf_op jit(solution)/shard_map/ppermute | solution.py:436
  28.3 1.2 %collective-permute-start.5 = (f32[7,16,128]{2,1,0:T(8,128)S(1)}, f32[7,16,128]{2,1,0:T(8,128)S(1)}, u32[]{:S(2)}, u32[]{:S(2)}) collective-permute-start(f32[7,16,128]{2,1,0:T(8,128)S(1)} %get-tuple-element.29), channel_id=1, source_target_pairs={{0,1},{1,0},{2,3},{3,2},{4,5},{5,4},{6,7},{7,6},{8,9},{9,8},{10,11... | collective-permute-start | bytes 172040 | tf_op jit(solution)/shard_map/ppermute | solution.py:443
  28.3 4.0 %collective-permute-start.6 = (f32[7,16,128]{2,1,0:T(8,128)S(1)}, f32[7,16,128]{2,1,0:T(8,128)S(1)}, u32[]{:S(2)}, u32[]{:S(2)}) collective-permute-start(f32[7,16,128]{2,1,0:T(8,128)S(1)} %get-tuple-element.30), channel_id=1, source_target_pairs={{0,3},{1,2},{2,1},{3,0},{4,7},{5,6},{6,5},{7,4},{8,11},{9,10},{10,... | collective-permute-start | bytes 172040 | tf_op jit(solution)/shard_map/ppermute | solution.py:443
  32.3 9.7 %collective-permute-start.9 = (f32[11,16,128]{2,1,0:T(8,128)S(1)}, f32[11,16,128]{2,1,0:T(8,128)S(1)}, u32[]{:S(2)}, u32[]{:S(2)}) collective-permute-start(f32[11,16,128]{2,1,0:T(8,128)S(1)} %pad_add_fusion.1.refs_0_), channel_id=1, source_target_pairs={{0,12},{4,0},{8,4},{12,8},{1,13},{5,1},{9,5},{13,9},{2,14},{6,2},{... | collective-permute-start | bytes 270344 | tf_op jit(solution)/shard_map/ppermute | solution.py:448
  38.9 8.9 %collective-permute-start.8 = (f32[11,16,128]{2,1,0:T(8,128)S(1)}, f32[11,16,128]{2,1,0:T(8,128)S(1)}, u32[]{:S(2)}, u32[]{:S(2)}) collective-permute-start(f32[11,16,128]{2,1,0:T(8,128)S(1)} %pad_add_fusion.1.refs_0_), channel_id=1, source_target_pairs={{0,8},{4,12},{8,0},{12,4},{1,9},{5,13},{9,1},{13,5},{2,10},{6,14},... | collective-permute-start | bytes 270344 | tf_op jit(solution)/shard_map/ppermute | solution.py:448
  38.9 8.9 %collective-permute-start.7 = (f32[11,16,128]{2,1,0:T(8,128)S(1)}, f32[11,16,128]{2,1,0:T(8,128)S(1)}, u32[]{:S(2)}, u32[]{:S(2)}) collective-permute-start(f32[11,16,128]{2,1,0:T(8,128)S(1)} %pad_add_fusion.1.refs_0_), channel_id=1, source_target_pairs={{0,4},{4,8},{8,12},{12,0},{1,5},{5,9},{9,13},{13,1},{2,6},{6,10},{... | collective-permute-start | bytes 270344 | tf_op jit(solution)/shard_map/ppermute | solution.py:448
  48.1 5.7 %collective-permute-start.10 = (f32[11,16,128]{2,1,0:T(8,128)S(1)}, f32[11,16,128]{2,1,0:T(8,128)S(1)}, u32[]{:S(2)}, u32[]{:S(2)}) collective-permute-start(f32[11,16,128]{2,1,0:T(8,128)S(1)} %get-tuple-element.33.refs_2_), channel_id=1, source_target_pairs={{0,2},{2,0},{1,3},{3,1},{4,6},{6,4},{5,7},{7,5},{8,10},{10,8},{9,1... | collective-permute-start | bytes 270344 | tf_op jit(solution)/shard_map/ppermute | solution.py:436
  49.6 4.2 %collective-permute-start.12 = (f32[7,16,128]{2,1,0:T(8,128)S(1)}, f32[7,16,128]{2,1,0:T(8,128)S(1)}, u32[]{:S(2)}, u32[]{:S(2)}) collective-permute-start(f32[7,16,128]{2,1,0:T(8,128)S(1)} %get-tuple-element.34), channel_id=1, source_target_pairs={{0,3},{1,2},{2,1},{3,0},{4,7},{5,6},{6,5},{7,4},{8,11},{9,10},{10,... | collective-permute-start | bytes 172040 | tf_op jit(solution)/shard_map/ppermute | solution.py:443
  49.6 4.2 %collective-permute-start.11 = (f32[7,16,128]{2,1,0:T(8,128)S(1)}, f32[7,16,128]{2,1,0:T(8,128)S(1)}, u32[]{:S(2)}, u32[]{:S(2)}) collective-permute-start(f32[7,16,128]{2,1,0:T(8,128)S(1)} %get-tuple-element.34), channel_id=1, source_target_pairs={{0,1},{1,0},{2,3},{3,2},{4,5},{5,4},{6,7},{7,6},{8,9},{9,8},{10,11... | collective-permute-start | bytes 172040 | tf_op jit(solution)/shard_map/ppermute | solution.py:443
  62.8 5.4 %collective-permute-start.13 = (f32[11,16,128]{2,1,0:T(8,128)S(1)}, f32[11,16,128]{2,1,0:T(8,128)S(1)}, u32[]{:S(2)}, u32[]{:S(2)}) collective-permute-start(f32[11,16,128]{2,1,0:T(8,128)S(1)} %get-tuple-element.36), channel_id=1, source_target_pairs={{0,2},{2,0},{1,3},{3,1},{4,6},{6,4},{5,7},{7,5},{8,10},{10,8},{9,1... | collective-permute-start | bytes 270344 | tf_op jit(solution)/shard_map/ppermute | solution.py:436
  63.8 1.2 %collective-permute-start.14 = (f32[7,16,128]{2,1,0:T(8,128)S(1)}, f32[7,16,128]{2,1,0:T(8,128)S(1)}, u32[]{:S(2)}, u32[]{:S(2)}) collective-permute-start(f32[7,16,128]{2,1,0:T(8,128)S(1)} %get-tuple-element.37), channel_id=1, source_target_pairs={{0,1},{1,0},{2,3},{3,2},{4,5},{5,4},{6,7},{7,6},{8,9},{9,8},{10,11... | collective-permute-start | bytes 172040 | tf_op jit(solution)/shard_map/ppermute | solution.py:443
  64.0 4.1 %collective-permute-start.15 = (f32[7,16,128]{2,1,0:T(8,128)S(1)}, f32[7,16,128]{2,1,0:T(8,128)S(1)}, u32[]{:S(2)}, u32[]{:S(2)}) collective-permute-start(f32[7,16,128]{2,1,0:T(8,128)S(1)} %get-tuple-element.38), channel_id=1, source_target_pairs={{0,3},{1,2},{2,1},{3,0},{4,7},{5,6},{6,5},{7,4},{8,11},{9,10},{10,... | collective-permute-start | bytes 172040 | tf_op jit(solution)/shard_map/ppermute | solution.py:443
  68.2 16.4 %copy-start.1 = (f32[8,44,128]{2,0,1:T(8,128)S(1)}, f32[8,44,128]{2,0,1:T(8,128)}, u32[]{:S(2)}) copy-start(f32[8,44,128]{2,0,1:T(8,128)} %param.7) | copy-start | bytes 540676
  68.4 8.2 %collective-permute-start.16 = (f32[11,8,128]{2,1,0:T(8,128)S(1)}, f32[11,8,128]{2,1,0:T(8,128)S(1)}, u32[]{:S(2)}, u32[]{:S(2)}) collective-permute-start(f32[11,8,128]{2,1,0:T(8,128)S(1)} %get-tuple-element.40), channel_id=1, source_target_pairs={{0,4},{4,8},{8,12},{12,0},{1,5},{5,9},{9,13},{13,1},{2,6},{6,10},{... | collective-permute-start | bytes 135176 | tf_op jit(solution)/shard_map/ppermute | solution.py:448
  72.9 5.6 %collective-permute-start.17 = (f32[11,8,128]{2,1,0:T(8,128)S(1)}, f32[11,8,128]{2,1,0:T(8,128)S(1)}, u32[]{:S(2)}, u32[]{:S(2)}) collective-permute-start(f32[11,8,128]{2,1,0:T(8,128)S(1)} %get-tuple-element.41), channel_id=1, source_target_pairs={{0,8},{4,12},{8,0},{12,4},{1,9},{5,13},{9,1},{13,5},{2,10},{6,14},... | collective-permute-start | bytes 135176 | tf_op jit(solution)/shard_map/ppermute | solution.py:448
  74.8 4.3 %collective-permute-start.18 = (f32[11,8,128]{2,1,0:T(8,128)S(1)}, f32[11,8,128]{2,1,0:T(8,128)S(1)}, u32[]{:S(2)}, u32[]{:S(2)}) collective-permute-start(f32[11,8,128]{2,1,0:T(8,128)S(1)} %get-tuple-element.42), channel_id=1, source_target_pairs={{0,12},{4,0},{8,4},{12,8},{1,13},{5,1},{9,5},{13,9},{2,14},{6,2},{... | collective-permute-start | bytes 135176 | tf_op jit(solution)/shard_map/ppermute | solution.py:448
  79.1 4.0 %collective-permute-start.21 = (f32[11,8,128]{2,1,0:T(8,128)S(1)}, f32[11,8,128]{2,1,0:T(8,128)S(1)}, u32[]{:S(2)}, u32[]{:S(2)}) collective-permute-start(f32[11,8,128]{2,1,0:T(8,128)S(1)} %add_add_fusion.refs_0_), channel_id=1, source_target_pairs={{0,3},{1,2},{2,1},{3,0},{4,7},{5,6},{6,5},{7,4},{8,11},{9,10},{10,... | collective-permute-start | bytes 135176 | tf_op jit(solution)/shard_map/ppermute | solution.py:443
  79.8 3.3 %collective-permute-start.20 = (f32[11,8,128]{2,1,0:T(8,128)S(1)}, f32[11,8,128]{2,1,0:T(8,128)S(1)}, u32[]{:S(2)}, u32[]{:S(2)}) collective-permute-start(f32[11,8,128]{2,1,0:T(8,128)S(1)} %add_add_fusion.refs_0_), channel_id=1, source_target_pairs={{0,1},{1,0},{2,3},{3,2},{4,5},{5,4},{6,7},{7,6},{8,9},{9,8},{10,11... | collective-permute-start | bytes 135176 | tf_op jit(solution)/shard_map/ppermute | solution.py:443
  80.6 4.0 %collective-permute-start.19 = (f32[11,8,128]{2,1,0:T(8,128)S(1)}, f32[11,8,128]{2,1,0:T(8,128)S(1)}, u32[]{:S(2)}, u32[]{:S(2)}) collective-permute-start(f32[11,8,128]{2,1,0:T(8,128)S(1)} %add_add_fusion.refs_0_), channel_id=1, source_target_pairs={{0,2},{2,0},{1,3},{3,1},{4,6},{6,4},{5,7},{7,5},{8,10},{10,8},{9,1... | collective-permute-start | bytes 135176 | tf_op jit(solution)/shard_map/ppermute | solution.py:436
  (5 other events, 17.9 us)
